TPU v7x, 128 devices: a whole 4x4x4 slice. The times are simulated.
128 devices in a mesh: rows: 8 (over y_hi, z), cent: 16 (over y_lo, x, core).
Axes of the slice: x: 4, y: 4 (y_hi: 2, y_lo: 2; y = y_hi * 2 + y_lo), z: 4, core: 2. Of those that a mesh axis runs over, the one named last changes fastest.
Arguments:
- train_rows: float32 [32768, 64], P('rows'), may hold values from -6 to 6
- centre_index: int32 [16384], P('cent'), may hold values from 0 to 32767
- precond: bfloat16 [16384, 16384], P('cent', 'rows'), as said below
- coefficients: float32 [16384, 128], P(('rows', 'cent')), may hold values from -6 to 6
- residual: float32 [16384, 128], P(('rows', 'cent')), may hold values from -6 to 6
- direction: float32 [16384, 128], P(('rows', 'cent')), may hold values from -6 to 6
Outputs:
- coef_next: float32 [16384, 128], P(('rows', 'cent'))
- residual_next: float32 [16384, 128], P(('rows', 'cent'))
- direction_next: float32 [16384, 128], P(('rows', 'cent'))
Inputs may be any that keep to these rules, and one draw needn't show every extreme that they name: precond is zero below its diagonal.
All inputs are finite; a program needn't handle non-finite values.
Results may differ from a plain program's by a relative error of at most 0.0047.
Values may be sent and summed in bfloat16 or wider, within the bound.
No kernel may reach another device: no remote copies, remote signals or barrier semaphores. Data moves between devices by JAX's collectives and lax.ppermute only.
A program may use at most 64 MiB of HBM per device.

v0:
```python
import math

import jax
import jax.numpy as jnp
from jax import lax
from jax.sharding import PartitionSpec as P

FEAT = 64
OUTS = 128


ridge_weight = 0.1


def kernel_tile(block_rows, centres):
    row_sq = jnp.sum(block_rows * block_rows, axis=1)
    cen_sq = jnp.sum(centres * centres, axis=1)
    cross = jnp.dot(
        block_rows, centres.T, precision=lax.Precision.HIGHEST, preferred_element_type=jnp.float32
    )
    distance = row_sq[:, None] + cen_sq[None, :] - 2.0 * cross
    return jnp.exp(-(2.0 / FEAT) * distance).astype(jnp.bfloat16)


def kernel_pass(local_rows, centres, coef_field, combine):
    count_rows = local_rows.shape[0]
    block_size = math.gcd(count_rows, 1024)
    block_count = count_rows // block_size
    groups = local_rows.reshape(block_count, block_size, FEAT)
    tiles = lax.map(lambda group_rows: kernel_tile(group_rows, centres), groups)
    fitted_part = jnp.einsum(
        "kbc,cd->kbd", tiles, coef_field, preferred_element_type=jnp.float32
    ).reshape(count_rows, OUTS)
    fitted = combine(fitted_part)
    fitted_groups = fitted.reshape(block_count, block_size, OUTS)
    grad_part = jnp.einsum("kbc,kbd->cd", tiles, fitted_groups, preferred_element_type=jnp.float32)
    return grad_part


def on_device(train_rows, centre_index, precond, coefficients, residual, direction):
    rows_here = train_rows.shape[0]
    start_row = lax.axis_index("rows") * rows_here
    offset = centre_index - start_row
    inside = ((offset >= 0) & (offset < rows_here)).astype(jnp.float32)
    picked = train_rows[jnp.clip(offset, 0, rows_here - 1)] * inside[:, None]
    centres = lax.psum(picked, "rows")
    dir_low = direction.astype(jnp.bfloat16)
    columns = precond
    partial_field = jnp.dot(
        columns,
        lax.all_gather(dir_low, "cent", axis=0, tiled=True),
        preferred_element_type=jnp.float32,
    )
    coef_field = lax.psum(partial_field, "rows").astype(jnp.bfloat16)

    def line_sum(part):
        return lax.psum(part, "cent").astype(jnp.bfloat16)

    grad_part = kernel_pass(train_rows, centres, coef_field, line_sum)
    grad = lax.psum(grad_part, "rows")
    grad_low = (grad * float(rows_here * lax.axis_size("rows")) ** (-0.5)).astype(jnp.bfloat16)
    columns = precond
    image = lax.psum_scatter(
        lax.dot_general(
            columns, grad_low, (((0,), (0,)), ((), ())), preferred_element_type=jnp.float32
        ),
        "cent",
        scatter_dimension=0,
        tiled=True,
    )
    image = image + ridge_weight * direction
    norm_old, curvature = lax.psum(
        (jnp.sum(residual * residual), jnp.sum(direction * image)), ("rows", "cent")
    )
    step_size = norm_old / curvature
    coef_next = coefficients + step_size * direction
    residual_next = residual - step_size * image
    norm_new = lax.psum(jnp.sum(residual_next * residual_next), ("rows", "cent"))
    direction_next = residual_next + norm_new / norm_old * direction
    return (coef_next, residual_next, direction_next)


def solution(mesh):
    placed = (
        P("rows", None),
        P("cent"),
        P("cent", "rows"),
        P(("rows", "cent"), None),
        P(("rows", "cent"), None),
        P(("rows", "cent"), None),
    )
    return jax.shard_map(
        on_device,
        mesh=mesh,
        in_specs=placed,
        out_specs=(P(("rows", "cent"), None), P(("rows", "cent"), None), P(("rows", "cent"), None)),
        check_vma=False,
    )
```

profile of v0, /device:TPU:1, one launch (start us, length us, event | category | flops | bytes accessed | tf_op | source)
XLA Modules:
  0.0 496.0 jit_solution(6410955484376986183)
XLA Ops:
  7.2 0.0 all-reduce.6.cloned.1.call-start
  7.2 0.7 fusion.8
  7.9 0.7 and_convert_fusion
  8.6 0.0 copy-start
  8.6 1.9 copy.9
  10.5 2.8 gather_fusion
  13.3 1.1 broadcast_multiply_fusion
  14.4 0.0 all-reduce.6.cloned.1.call-update
  14.4 0.0 all-reduce.8.cloned.1.call-start
  14.4 0.0 copy-done
  14.5 22.6 %all_gather.3 = bf16[2048,128]{1,0:T(8,128)(2,1)S(1)} all-gather(bf16[128,128]{1,0:T(8,128)(2,1)S(1)} %convert_element_type.21), channel_id=1, replica_groups=mesh['rows'=8,'cent'=16] {'cent'}, dimensions={0}, use_global_device_ids=true | all-gather | bytes 557056 | tf_op jit(solution)/shard_map/all_gather | solution.py:51
  37.0 3.4 fusion.10
  40.5 43.2 %all-reduce.9 = bf16[1024,128]{1,0:T(8,128)(2,1)S(1)} all-reduce(f32[1024,128]{1,0:T(8,128)S(1)} %fusion.10), channel_id=1, replica_groups=mesh['rows'=8,'cent'=16] {'rows'}, use_global_device_ids=true, to_apply=%region_7.8 | all-reduce | flops 131072 | bytes 786432 | tf_op jit(solution)/shard_map/psum | solution.py:54
  83.7 14.7 %all-reduce.6.cloned.1.call-done = f32[1024,64]{1,0:T(8,128)} async-done(((f32[1024,64]{1,0:T(8,128)}), f32[1024,64]{1,0:T(8,128)}) %all-reduce.6.cloned.1.call-update) | async-done | bytes 262160 | tf_op jit(solution)/shard_map/psum | solution.py:46
  98.4 1.2 multiply_reduce_fusion
  99.7 26.4 %while.12 = (s32[]{:T(128)}, bf16[4,1024,1024]{2,1,0:T(8,128)(2,1)}, f32[4,1024,64]{2,1,0:T(8,128)S(1)}, f32[1024]{0:T(1024)S(1)}, f32[1024,64]{1,0:T(8,128)}, /*index=5*/s32[]{:T(128)}) while((s32[]{:T(128)}, bf16[4,1024,1024]{2,1,0:T(8,128)(2,1)}, f32[4,1024,64]{2,1,0:T(8,128)S(1)}, f32[1024]{0:T(1024)S(1)}, f32[1024,64]{1,0:T(8,128)}, ...), condition=%wide.region_6.7_spmd, body=%wide.region_4.0_spmd.sunk | while | flops 810679296 | bytes 3421257 | solution.py:30
  99.7 0.2 fusion.23
  99.9 6.4 %bitcast_dynamic-update-slice_fusion.2 = bf16[4,1024,1024]{2,1,0:T(8,128)(2,1)} fusion(bf16[4,1024,1024]{2,1,0:T(8,128)(2,1)} %get-tuple-element.116, s32[]{:T(128)} %get-tuple-element.115, f32[1024,64]{1,0:T(8,128)} %get-tuple-element.125, f32[1024]{0:T(1024)S(1)} %get-tuple-element.124, f32[1024]{0:T(1024)S(1)} %fusion.23, ...), kind=kOutput, calls=%fused_computation.2.clone.1 | convolution fusion | flops 810549248 | bytes 3154944 | tf_op jit(solution)/shard_map/while/body/eval_jaxpr/dot_general | solution.py:18
  106.3 0.2 fusion.23
  106.5 6.4 %bitcast_dynamic-update-slice_fusion.2 = bf16[4,1024,1024]{2,1,0:T(8,128)(2,1)} fusion(bf16[4,1024,1024]{2,1,0:T(8,128)(2,1)} %get-tuple-element.116, s32[]{:T(128)} %get-tuple-element.115, f32[1024,64]{1,0:T(8,128)} %get-tuple-element.125, f32[1024]{0:T(1024)S(1)} %get-tuple-element.124, f32[1024]{0:T(1024)S(1)} %fusion.23, ...), kind=kOutput, calls=%fused_computation.2.clone.1 | convolution fusion | flops 810549248 | bytes 3154944 | tf_op jit(solution)/shard_map/while/body/eval_jaxpr/dot_general | solution.py:18
  112.9 0.2 fusion.23
  113.1 6.4 %bitcast_dynamic-update-slice_fusion.2 = bf16[4,1024,1024]{2,1,0:T(8,128)(2,1)} fusion(bf16[4,1024,1024]{2,1,0:T(8,128)(2,1)} %get-tuple-element.116, s32[]{:T(128)} %get-tuple-element.115, f32[1024,64]{1,0:T(8,128)} %get-tuple-element.125, f32[1024]{0:T(1024)S(1)} %get-tuple-element.124, f32[1024]{0:T(1024)S(1)} %fusion.23, ...), kind=kOutput, calls=%fused_computation.2.clone.1 | convolution fusion | flops 810549248 | bytes 3154944 | tf_op jit(solution)/shard_map/while/body/eval_jaxpr/dot_general | solution.py:18
  119.5 0.2 fusion.23
  119.7 6.4 %bitcast_dynamic-update-slice_fusion.2 = bf16[4,1024,1024]{2,1,0:T(8,128)(2,1)} fusion(bf16[4,1024,1024]{2,1,0:T(8,128)(2,1)} %get-tuple-element.116, s32[]{:T(128)} %get-tuple-element.115, f32[1024,64]{1,0:T(8,128)} %get-tuple-element.125, f32[1024]{0:T(1024)S(1)} %get-tuple-element.124, f32[1024]{0:T(1024)S(1)} %fusion.23, ...), kind=kOutput, calls=%fused_computation.2.clone.1 | convolution fusion | flops 810549248 | bytes 3154944 | tf_op jit(solution)/shard_map/while/body/eval_jaxpr/dot_general | solution.py:18
  126.1 5.7 %fusion.4 = f32[4,1024,128]{2,1,0:T(8,128)S(1)} fusion(bf16[4,1024,1024]{2,1,0:T(8,128)(2,1)} %get-tuple-element.58, bf16[1024,128]{1,0:T(8,128)(2,1)S(1)} %all-reduce.9), kind=kOutput, calls=%fused_computation.12 | convolution fusion | flops 1073741824 | bytes 10747904 | tf_op jit(solution)/shard_map/kbc,cd->kbd/dot_general | solution.py:31
  131.8 66.6 %all-reduce.10 = bf16[4096,128]{1,0:T(8,128)(2,1)S(1)} all-reduce(f32[4096,128]{1,0:T(8,128)S(1)} %bitcast.34), channel_id=1, replica_groups=mesh['rows'=8,'cent'=16] {'cent'}, use_global_device_ids=true, to_apply=%region_8.9 | all-reduce | flops 524288 | bytes 3145728 | tf_op jit(solution)/shard_map/psum | solution.py:57
  198.5 6.6 %convolution_bitcast_fusion.1 = f32[1024,128]{1,0:T(8,128)} fusion(bf16[4,1024,1024]{2,1,0:T(8,128)(2,1)} %get-tuple-element.58, bf16[4,1024,128]{2,1,0:T(8,128)(2,1)S(1)} %bitcast.35), kind=kOutput, calls=%fused_computation.9 | convolution fusion | flops 1073741824 | bytes 9961472 | tf_op jit(solution)/shard_map/kbc,kbd->cd/dot_general | solution.py:36
  205.0 0.0 copy-start.1
  205.0 0.0 copy-start.2
  205.0 0.0 all-reduce.8.cloned.1.call-update
  205.1 0.0 reduce-scatter.2.cloned.1.call-start
  205.1 80.4 %all-reduce.8.cloned.1.call-done = f32[1024,128]{1,0:T(8,128)} async-done(((f32[1024,128]{1,0:T(8,128)}), f32[1024,128]{1,0:T(8,128)}) %all-reduce.8.cloned.1.call-update) | async-done | bytes 524304 | tf_op jit(solution)/shard_map/psum | solution.py:60
  285.5 4.1 convolution_bitcast_fusion
  289.6 0.0 reduce-scatter.2.cloned.1.call-update
  289.6 0.1 copy.12
  289.7 0.0 copy-done.1
  289.7 0.1 copy.15
  289.8 0.6 multiply_reduce_fusion.3
  290.5 59.9 %reduce-scatter.2.cloned.1.call-done = f32[128,128]{0,1:T(8,128)} async-done(((f32[2048,128]{0,1:T(8,128)}), f32[128,128]{0,1:T(8,128)}) %reduce-scatter.2.cloned.1.call-update) | async-done | bytes 65552 | tf_op jit(solution)/shard_map/reduce_scatter | solution.py:63
  350.4 1.5 multiply_reduce_fusion.2
  351.8 0.0 copy-done.2
  351.8 0.1 copy.14
  351.9 68.6 %all-reduce = (f32[]{:T(128)}, f32[]{:T(128)}) all-reduce(f32[]{:T(128)} %multiply_reduce_fusion.3, f32[]{:T(128)} %multiply_reduce_fusion.2), channel_id=1, replica_groups=mesh['rows'=8,'cent'=16] {'rows','cent'}, use_global_device_ids=true, to_apply=%region_1.2 | all-reduce | flops 2 | bytes 16 | tf_op jit(solution)/shard_map/psum | solution.py:72
  421.9 1.5 multiply_reduce_fusion.1
  423.3 62.6 %psum.55 = f32[]{:T(128)} all-reduce(f32[]{:T(128)} %get-tuple-element.74), channel_id=1, replica_groups=mesh['rows'=8,'cent'=16] {'rows','cent'}, use_global_device_ids=true, to_apply=%region_14.15 | all-reduce | flops 1 | bytes 8 | tf_op jit(solution)/shard_map/psum | solution.py:78
  487.3 0.7 copy.18
  488.0 0.7 copy.17
  488.7 0.7 copy.19
  (3 shorter events, 0.0 us)
Async XLA Ops:
  7.2 91.3 %all-reduce.6.cloned.1.call-start = ((), (), s32[]{:S(2)}) async-start(), calls=%async_computation.1 | async-start | bytes 1048576 | tf_op jit(solution)/shard_map/psum | solution.py:46
  8.6 5.8 %copy-start = (f32[128,128]{1,0:T(8,128)S(1)}, f32[128,128]{1,0:T(8,128)}, u32[]{:S(2)}) copy-start(f32[128,128]{1,0:T(8,128)} %param.13) | copy-start | bytes 196612
  14.4 271.1 %all-reduce.8.cloned.1.call-start = ((), (), s32[]{:S(2)}) async-start(), calls=%async_computation.2 | async-start | bytes 1048576 | tf_op jit(solution)/shard_map/psum | solution.py:60
  205.0 84.7 %copy-start.1 = (f32[128,128]{1,0:T(8,128)S(1)}, f32[128,128]{1,0:T(8,128)}, u32[]{:S(2)}) copy-start(f32[128,128]{1,0:T(8,128)} %param.12) | copy-start | bytes 196612
  205.0 146.8 %copy-start.2 = (f32[128,128]{1,0:T(8,128)S(1)}, f32[128,128]{1,0:T(8,128)}, u32[]{:S(2)}) copy-start(f32[128,128]{1,0:T(8,128)} %param.11) | copy-start | bytes 196612
  205.1 145.3 %reduce-scatter.2.cloned.1.call-start = ((), (), s32[]{:S(2)}) async-start(), calls=%async_computation.3 | async-start | bytes 1114112 | tf_op jit(solution)/shard_map/reduce_scatter | solution.py:63
Sparse Core Ops, SparseCore 0:
  14.5 83.8 all-reduce.5
  205.2 80.2 all-reduce.7
  289.8 60.5 reduce-scatter.1
where the time goes:
time: 497 us; the launch traced here: 496 us
  blocking collectives  264 us (53%)
  waiting for transfers between devices  155 us (31%)
  matrix products  45.4 us (9%)
  between operations  16.5 us (3%)
  other arithmetic  8.12 us (2%)
  local copies, waits for them, and re-layouts  7.13 us (1%)
    psum x1, waiting for transfers between devices, on_device(): grad = lax.psum(grad_part, 'rows')  80.4 us
    psum x1, blocking collectives, on_device(): lax.psum((jnp.sum(residual * residual), jnp.sum(direction * image)), ('ro...  68.6 us
    psum x1, blocking collectives, line_sum(): return lax.psum(part, 'cent').astype(jnp.bfloat16)  66.6 us
    psum x1, blocking collectives, on_device(): lax.psum(jnp.sum(residual_next * residual_next), ('rows', 'cent'))  62.6 us
    reduce_scatter x1, waiting for transfers between devices, on_device(): lax.psum_scatter(lax.dot_general(columns, grad_low, (((0,), (0,)), ((), (...  59.9 us
    psum x1, blocking collectives, on_device(): coef_field = lax.psum(partial_field, 'rows').astype(jnp.bfloat16)  43.2 us
    dot_general x4, matrix products, kernel_tile(): jnp.dot(block_rows, centres.T, precision=lax.Precision.HIGHEST, preferred...  25.5 us
    all_gather x1, blocking collectives, on_device(): lax.all_gather(dir_low, 'cent', axis=0, tiled=True)  22.6 us
  transfers between devices with their start and end apart: 3, of which 3 were waited for; matrix products, arithmetic and copies ran while one was open for 1% of the time, Pallas kernels for 0%

commit v1 on v0

v1 whole, which is shorter than its diff:
```python
import math

import jax
import jax.numpy as jnp
import numpy as np
from jax import lax
from jax.experimental import pallas as pl
from jax.experimental.pallas import tpu as pltpu
from jax.sharding import Mesh
from jax.sharding import PartitionSpec as P

FEAT = 64
OUTS = 128
ridge_weight = 0.1
F32, BF16 = jnp.float32, jnp.bfloat16

FINE = (("yh", 2), ("z", 4), ("yl", 2), ("x", 4), ("core", 2))
ROWS = ("yh", "z")
CHIPS = ("yl", "x")
CENT = ("yl", "x", "core")
FEATURE_SCALE = math.sqrt(2.0 * (2.0 / FEAT) * math.log2(math.e))
SWAP = [(0, 1), (1, 0)]


def pieces(value, count):
    out = []
    for _ in range(count):
        top = lax.reduce_precision(value, 8, 7)
        out.append(top.astype(BF16))
        value = value - top
    return out


def half_norm(high, mid):
    value = high.astype(F32) + mid.astype(F32)
    return pieces(-0.5 * jnp.sum(value * value, axis=1, keepdims=True), 3)


def row_operand(high, mid):
    n = high.shape[0]
    ones = jnp.ones((n, 3), BF16)
    return jnp.concatenate([high, high, mid, *half_norm(high, mid), ones, jnp.zeros((n, 58), BF16)], axis=1)


def centre_operand(high, mid):
    n = high.shape[0]
    ones = jnp.ones((n, 3), BF16)
    return jnp.concatenate([high, mid, high, ones, *half_norm(high, mid), jnp.zeros((n, 58), BF16)], axis=1)


def params(**more):
    return pltpu.CompilerParams(vmem_limit_bytes=48 * 1024 * 1024, **more)


def tile_kernel(rows_ref, cen_ref, coef_ref, tile_ref, fit_ref):
    power = lax.dot_general(rows_ref[...], cen_ref[...], (((1,), (1,)), ((), ())), preferred_element_type=F32)
    tile = jnp.exp2(power).astype(BF16)
    tile_ref[...] = tile
    fit_ref[...] = jnp.dot(tile, coef_ref[...], preferred_element_type=F32).astype(BF16)


def tile_forward(rows_op, cen_op, coef, block=512):
    n, m = rows_op.shape[0], cen_op.shape[0]
    return pl.pallas_call(
        tile_kernel,
        grid=(n // block,),
        in_specs=[
            pl.BlockSpec((block, 256), lambda i: (i, 0)),
            pl.BlockSpec((m, 256), lambda i: (0, 0)),
            pl.BlockSpec((m, OUTS), lambda i: (0, 0)),
        ],
        out_specs=[pl.BlockSpec((block, m), lambda i: (i, 0)), pl.BlockSpec((block, OUTS), lambda i: (i, 0))],
        out_shape=[jax.ShapeDtypeStruct((n, m), BF16), jax.ShapeDtypeStruct((n, OUTS), BF16)],
        compiler_params=params(),
        name="tile_forward",
    )(rows_op, cen_op, coef)


def back_kernel(tile_ref, fit_ref, grad_ref, total_ref):
    step = pl.program_id(0)

    @pl.when(step == 0)
    def _():
        total_ref[...] = jnp.zeros_like(total_ref)

    total_ref[...] += jnp.dot(fit_ref[...].T, tile_ref[...], preferred_element_type=F32)

    @pl.when(step == pl.num_programs(0) - 1)
    def _():
        grad_ref[...] = total_ref[...].T.astype(BF16)


def backward(tile, fitted, block=512):
    n, m = tile.shape
    return pl.pallas_call(
        back_kernel,
        grid=(n // block,),
        in_specs=[pl.BlockSpec((block, m), lambda i: (i, 0)), pl.BlockSpec((block, OUTS), lambda i: (i, 0))],
        out_specs=pl.BlockSpec((m, OUTS), lambda i: (0, 0)),
        out_shape=jax.ShapeDtypeStruct((m, OUTS), BF16),
        scratch_shapes=[pltpu.VMEM((OUTS, m), F32)],
        compiler_params=params(),
        name="tile_backward",
    )(tile, fitted)


def field_kernel(pre_ref, dir_ref, out_ref):
    out_ref[...] = jnp.dot(pre_ref[...], dir_ref[...], preferred_element_type=F32).astype(BF16)


def field(precond, dir_all, block=256):
    n, m = precond.shape
    return pl.pallas_call(
        field_kernel,
        grid=(n // block,),
        in_specs=[pl.BlockSpec((block, m), lambda i: (i, 0)), pl.BlockSpec((m, OUTS), lambda i: (0, 0))],
        out_specs=pl.BlockSpec((block, OUTS), lambda i: (i, 0)),
        out_shape=jax.ShapeDtypeStruct((n, OUTS), BF16),
        compiler_params=params(),
        name="precond_forward",
    )(precond, dir_all)


def image_kernel(pre_ref, grad_ref, out_ref):
    part = jnp.dot(grad_ref[...].T, pre_ref[...], preferred_element_type=F32)
    out_ref[...] = part.T.astype(BF16)


def image_part(precond, grad, block=512):
    n, m = precond.shape
    return pl.pallas_call(
        image_kernel,
        grid=(m // block,),
        in_specs=[pl.BlockSpec((n, block), lambda i: (0, i)), pl.BlockSpec((n, OUTS), lambda i: (0, 0))],
        out_specs=pl.BlockSpec((block, OUTS), lambda i: (i, 0)),
        out_shape=jax.ShapeDtypeStruct((m, OUTS), BF16),
        compiler_params=params(),
        name="precond_backward",
    )(precond, grad)


def spread(part, axes):
    return lax.all_to_all(part, axes, 0, 0, tiled=True)


def gathered(part, axes):
    count = math.prod(lax.axis_size(axis) for axis in axes)
    return spread(jnp.broadcast_to(part[None], (count, *part.shape)), axes)


def summed(parts):
    return jnp.sum(parts.astype(F32), axis=0)


def core_halves(part, axis):
    me = lax.axis_index("core")
    mine = lax.dynamic_index_in_dim(part, me, axis, keepdims=False)
    other = lax.dynamic_index_in_dim(part, 1 - me, axis, keepdims=False)
    came = lax.ppermute(other, "core", SWAP)
    return mine.astype(F32) + came.astype(F32)


def core_both(part):
    first = lax.axis_index("core") == 0
    came = lax.ppermute(part, "core", SWAP)
    return jnp.stack([jnp.where(first, part, came), jnp.where(first, came, part)])


def on_device(train_rows, centre_index, precond, coefficients, residual, direction):
    rows_here = train_rows.shape[0]
    cen_here = centre_index.shape[0]
    row_devices = lax.axis_size("yh") * lax.axis_size("z")
    cen_devices = lax.axis_size("yl") * lax.axis_size("x") * lax.axis_size("core")
    start_row = lax.axis_index(ROWS) * rows_here

    offset = centre_index - start_row
    inside = (offset >= 0) & (offset < rows_here)
    picked = train_rows[jnp.clip(offset, 0, rows_here - 1)]
    picked = jnp.where(inside[:, None], picked, 0.0)
    both = jnp.concatenate(pieces(picked * FEATURE_SCALE, 2), axis=1)
    mine = summed(spread(both.reshape(row_devices, cen_here // row_devices, 2 * FEAT), ROWS)).astype(BF16)

    dir_all = gathered(direction.astype(BF16), CENT).reshape(-1, OUTS)
    part = field(precond, dir_all).reshape(row_devices, cen_here // row_devices, OUTS)
    load = jnp.concatenate([part, jnp.broadcast_to(mine[None], (row_devices, *mine.shape))], axis=1)
    got = spread(load, ROWS)
    share = cen_here // row_devices
    features = got[:, share:].reshape(cen_here, 2 * FEAT)
    coef_mine = summed(got[:, :share]).astype(BF16)
    coef_field = gathered(coef_mine, ROWS).reshape(cen_here, OUTS)

    rows_op = row_operand(*pieces(train_rows * FEATURE_SCALE, 2))
    cen_op = centre_operand(features[:, :FEAT], features[:, FEAT:])
    tile, fit_part = tile_forward(rows_op, cen_op, coef_field)

    share = rows_here // cen_devices
    half = core_halves(fit_part.reshape(2, cen_devices // 2, share, OUTS), 0).astype(BF16)
    fit_mine = summed(spread(half, CHIPS)).astype(BF16)
    fitted = core_both(gathered(fit_mine, CHIPS)).reshape(rows_here, OUTS)

    grad_part = backward(tile, fitted).reshape(row_devices, cen_here // row_devices, OUTS)
    grad_mine = summed(spread(grad_part, ROWS)) * float(rows_here * row_devices) ** (-0.5)
    grad_low = gathered(grad_mine.astype(BF16), ROWS).reshape(cen_here, OUTS)

    part = image_part(precond, grad_low)
    half = core_halves(part.reshape(cen_devices // 2, 2, direction.shape[0], OUTS), 1).astype(BF16)
    image = summed(spread(half, CHIPS)) + ridge_weight * direction

    top = jnp.max(jnp.abs(image))
    top = jnp.where(top > 0, top, 1.0)
    scaled = image / top
    numbers = [jnp.sum(residual * residual), jnp.sum(direction * image), jnp.sum(residual * scaled), jnp.sum(scaled * scaled), top]
    lane = lax.broadcasted_iota(jnp.int32, (8, 128), 0)
    packed = jnp.zeros((8, 128), F32)
    for place, number in enumerate(numbers):
        packed = jnp.where(lane == place, number, packed)

    def combine(parts):
        tops = parts[:, 4:5]
        most = jnp.max(tops, axis=0, keepdims=True)
        ratio = tops / most
        plain = jnp.sum(parts[:, 0:2], axis=0)
        cross = jnp.sum(parts[:, 2:3] * ratio, axis=0)
        square = jnp.sum(parts[:, 3:4] * ratio * ratio, axis=0)
        return jnp.concatenate([plain, cross, square, most[0], jnp.zeros((3, 128), F32)], axis=0)

    packed = combine(gathered(packed, CENT))
    packed = combine(gathered(packed, ROWS))
    norm_old, curvature, cross, square, most = (packed[place, 0] for place in range(5))
    step_size = norm_old / curvature
    reach = step_size * most
    norm_new = norm_old - 2.0 * reach * cross + reach * reach * square
    coef_next = coefficients + step_size * direction
    residual_next = residual - step_size * image
    direction_next = residual_next + norm_new / norm_old * direction
    return (coef_next, residual_next, direction_next)


def solution(mesh):
    fine = Mesh(np.asarray(mesh.devices).reshape([size for _, size in FINE]), [name for name, _ in FINE])
    every = P((*ROWS, *CENT), None)
    return jax.shard_map(
        on_device,
        mesh=fine,
        in_specs=(P(ROWS, None), P(CENT), P(CENT, ROWS), every, every, every),
        out_specs=(every, every, every),
        check_vma=False,
    )
```

time: 497 us -> 205 us (0.41)
  blocking collectives: 264 us -> 65.8 us
  waiting for transfers between devices: 155 us -> 24 us
  matrix products: 45.4 us -> 0 us
  starting transfers between devices: 0.12 us -> 36.4 us
  local copies, waits for them, and re-layouts: 7.13 us -> 34 us
  Pallas kernels: 0 us -> 18.7 us
  between operations: 16.5 us -> 5.04 us
  other arithmetic: 8.12 us -> 18.9 us
    psum x4 -> x0, blocking collectives: 241 us -> none  [the longest x1 68.6 us: on_device(): lax.psum((jnp.sum(residual * residual), jnp.sum(direction * image)), ('ro...]
    psum x2 -> x0, waiting for transfers between devices: 95.1 us -> none  [the longest x1 80.4 us: on_device(): grad = lax.psum(grad_part, 'rows')]
    all_to_all x0 -> x6, blocking collectives: none -> 65.8 us  [spread(): return lax.all_to_all(part, axes, 0, 0, tiled=True)]
    reduce_scatter x1 -> x0, waiting for transfers between devices: 59.9 us -> none  [on_device(): lax.psum_scatter(lax.dot_general(columns, grad_low, (((0,), (0,)), ((), (...]
    dot_general x8 -> x0, matrix products: 45.4 us -> none  [the longest x4 25.5 us: kernel_tile(): jnp.dot(block_rows, centres.T, precision=lax.Precision.HIGHEST, preferred...]
    all_to_all x0 -> x5, starting transfers between devices: none -> 29.1 us  [spread(): return lax.all_to_all(part, axes, 0, 0, tiled=True)]
    all_gather x1 -> x0, blocking collectives: 22.6 us -> none  [on_device(): lax.all_gather(dir_low, 'cent', axis=0, tiled=True)]
    all_to_all x0 -> x5, waiting for transfers between devices: none -> 19.8 us  [spread(): return lax.all_to_all(part, axes, 0, 0, tiled=True)]
  transfers between devices with their start and end apart: 3 -> 8, of which waited for: 3 -> 7; matrix products, arithmetic and copies ran while one was open for 1% -> 14% of each run, Pallas kernels for 0% -> 0%
where the time goes in v1:
time: 205 us; the launch traced here: 203 us
  blocking collectives  65.8 us (32%)
  starting transfers between devices  36.4 us (18%)
  local copies, waits for them, and re-layouts  34 us (17%)
  waiting for transfers between devices  24 us (12%)
  other arithmetic  18.9 us (9%)
  Pallas kernels  18.7 us (9%)
  between operations  5.04 us (2%)
    all_to_all x6, blocking collectives, spread(): return lax.all_to_all(part, axes, 0, 0, tiled=True)  65.8 us
    all_to_all x5, starting transfers between devices, spread(): return lax.all_to_all(part, axes, 0, 0, tiled=True)  29.1 us
    all_to_all x5, waiting for transfers between devices, spread(): return lax.all_to_all(part, axes, 0, 0, tiled=True)  19.8 us
    concatenate x1, local copies, waits for them, and re-layouts, row_operand(): jnp.concatenate([high, high, mid, *half_norm(high, mid), ones, jnp.zeros(...  9.57 us
    pallas_call x1, Pallas kernels, tile_forward(): pl.pallas_call(tile_kernel, grid=(n // block,), in_specs=[pl.BlockSpec((b...  7.8 us
    pallas_call x1, Pallas kernels, backward(): pl.pallas_call(back_kernel, grid=(n // block,), in_specs=[pl.BlockSpec((b...  7.25 us
    convert_element_type x3, other arithmetic, pieces(): out.append(top.astype(BF16))  5.51 us
    ppermute x2, starting transfers between devices, core_halves(): came = lax.ppermute(other, 'core', SWAP)  5.43 us
  transfers between devices with their start and end apart: 8, of which 7 were waited for; matrix products, arithmetic and copies ran while one was open for 14% of the time, Pallas kernels for 0%

profile of v1, /device:TPU:1, one launch (start us, length us, event | category | flops | bytes accessed | tf_op | source)
XLA Modules:
  0.0 202.8 jit_solution(18012735340874089636)
XLA Ops:
  0.6 0.7 fusion.12
  1.3 0.7 and_bitcast_fusion
  2.0 1.8 copy.37
  3.9 2.8 %gather_fusion = f32[1024,64]{1,0:T(8,128)S(1)} fusion(f32[4096,64]{1,0:T(8,128)S(1)} %copy.37, s32[1024]{0:T(1024)S(1)} %fusion.12), kind=kCustom, calls=%fused_computation | custom fusion | bytes 528384 | tf_op jit(solution)/shard_map/gather | solution.py:178
  6.7 0.2 reduce-precision_convert_fusion.3
  6.9 0.9 pad_maximum_fusion.2
  7.8 8.5 %all-to-all-start.1 = ((bf16[8,128,128]{2,1,0:T(8,128)(2,1)}), bf16[8,128,128]{2,1,0:T(8,128)(2,1)S(1)}, u32[]{:S(2)}, u32[]{:S(2)}) async-start(bf16[8,128,128]{2,1,0:T(8,128)(2,1)} %pad_maximum_fusion.2), calls=%async_computation.1 | async-start | bytes 524288 | tf_op jit(solution)/shard_map/all_to_all | solution.py:143
  16.3 1.7 multiply_reduce_fusion
  18.0 2.0 copy.39
  20.0 3.9 %all-to-all-done.1 = bf16[8,128,128]{2,1,0:T(8,128)(2,1)S(1)} async-done(((bf16[8,128,128]{2,1,0:T(8,128)(2,1)}), bf16[8,128,128]{2,1,0:T(8,128)(2,1)S(1)}, u32[]{:S(2)}, u32[]{:S(2)}) %all-to-all-start.1) | async-done | bytes 262176 | tf_op jit(solution)/shard_map/all_to_all | solution.py:143
  23.8 0.9 broadcast_in_dim.100
  24.8 6.5 %all-to-all-start = ((bf16[16,128,128]{2,1,0:T(8,128)(2,1)}), bf16[16,128,128]{2,1,0:T(8,128)(2,1)S(1)}, u32[]{:S(2)}, u32[]{:S(2)}) async-start(bf16[16,128,128]{2,1,0:T(8,128)(2,1)} %broadcast_in_dim.100), calls=%async_computation | async-start | bytes 1048576 | tf_op jit(solution)/shard_map/all_to_all | solution.py:143
  31.3 1.9 copy.40
  33.3 7.9 %all-to-all-done = bf16[16,128,128]{2,1,0:T(8,128)(2,1)S(1)} async-done(((bf16[16,128,128]{2,1,0:T(8,128)(2,1)}), bf16[16,128,128]{2,1,0:T(8,128)(2,1)S(1)}, u32[]{:S(2)}, u32[]{:S(2)}) %all-to-all-start) | async-done | bytes 524320 | tf_op jit(solution)/shard_map/all_to_all | solution.py:143
  41.2 2.2 %copy-done = bf16[1024,2048]{1,0:T(8,128)(2,1)S(1)} copy-done((bf16[1024,2048]{1,0:T(8,128)(2,1)S(1)}, bf16[1024,2048]{1,0:T(8,128)(2,1)}, u32[]{:S(2)}) %copy-start) | copy-done | bytes 4194328
  43.4 1.7 precond_forward.1
  45.1 0.9 pad_maximum_fusion.1
  46.0 4.1 %all-to-all-start.2 = ((bf16[8,256,128]{2,1,0:T(8,128)(2,1)}), bf16[8,256,128]{2,1,0:T(8,128)(2,1)}, u32[]{:S(2)}, u32[]{:S(2)}) async-start(bf16[8,256,128]{2,1,0:T(8,128)(2,1)} %pad_maximum_fusion.1), calls=%async_computation.2 | async-start | bytes 1048576 | tf_op jit(solution)/shard_map/all_to_all | solution.py:143
  50.1 3.3 %fusion.3 = (bf16[4096,1]{1,0:T(8,128)(2,1)}, bf16[4096,1]{1,0:T(8,128)(2,1)}) fusion(f32[4096,1]{1,0:T(8,128)S(1)} %copy-done.3, f32[4096,1]{1,0:T(8,128)} %copy.40), kind=kLoop, calls=%fused_computation.8 | loop fusion | flops 24576 | bytes 49152 | tf_op jit(solution)/shard_map/convert_element_type | solution.py:29
  53.5 1.4 copy.41
  54.9 1.1 broadcast_in_dim.98
  56.0 1.2 broadcast_in_dim.99
  57.2 9.6 %concatenate.16.rows_ref = bf16[4096,256]{1,0:T(8,128)(2,1)S(1)} concatenate(bf16[4096,64]{1,0:T(8,128)(2,1)S(1)} %get-tuple-element.21, bf16[4096,64]{1,0:T(8,128)(2,1)S(1)} %get-tuple-element.21, bf16[4096,64]{1,0:T(8,128)(2,1)} %get-tuple-element.20, bf16[4096,1]{1,0:T(8,128)(2,1)} %copy.41, bf16[4096,1]{1,0:T(8,128)(2,1)} %get-tuple-element.23, ...), dimensions={1} | concatenate | bytes 4194304 | tf_op jit(solution)/shard_map/concatenate | solution.py:42
  66.8 1.1 slice_reduce_fusion
  67.8 0.3 multiply_reduce_fusion.1
  68.2 0.2 copy.43
  68.4 1.0 copy.44
  69.4 0.2 copy.45
  69.6 0.7 broadcast_in_dim.108
  70.4 6.5 %all-to-all-start.3 = ((bf16[8,128,128]{2,1,0:T(8,128)(2,1)}), bf16[8,128,128]{2,1,0:T(8,128)(2,1)S(1)}, u32[]{:S(2)}, u32[]{:S(2)}) async-start(bf16[8,128,128]{2,1,0:T(8,128)(2,1)} %broadcast_in_dim.108), calls=%async_computation.3 | async-start | bytes 524288 | tf_op jit(solution)/shard_map/all_to_all | solution.py:143
  76.9 1.9 fusion.8
  78.9 0.7 broadcast_in_dim.106
  79.6 0.7 broadcast_in_dim.107
  80.3 3.5 %concatenate.19.cen_ref = bf16[1024,256]{1,0:T(8,128)(2,1)S(1)} concatenate(bf16[1024,128]{1,0:T(8,128)(2,1)S(1)} %bitcast.60, bf16[1024,64]{1,0:T(8,128)(2,1)S(1)} %bitcast.61, bf16[1024,3]{1,0:T(8,128)(2,1)} %broadcast_in_dim.106, bf16[1024,1]{1,0:T(8,128)(2,1)S(1)} %copy.45, bf16[1024,1]{1,0:T(8,128)(2,1)} %get-tuple-element.27, bf16[1024,1]{1,0:T(8,128)(2,1)} %get-tuple-element.26, ...), dimensions={1} | concatenate | bytes 1048576 | tf_op jit(solution)/shard_map/concatenate | solution.py:48
  83.8 0.7 all-to-all-done.3
  84.5 7.8 %tile_forward.1 = (bf16[4096,1024]{1,0:T(8,128)(2,1)}, bf16[4096,128]{1,0:T(8,128)(2,1)S(1)}) custom-call(bf16[4096,256]{1,0:T(8,128)(2,1)S(1)} %concatenate.16.rows_ref, bf16[1024,256]{1,0:T(8,128)(2,1)S(1)} %concatenate.19.cen_ref, bf16[1024,128]{1,0:T(8,128)(2,1)S(1)} %bitcast.58), custom_call_target="tpu_custom_call" | custom-call | tf_op jit(solution)/shard_map/tile_forward/pallas_call | solution.py:64
  92.3 1.1 copy-done.2
  93.4 2.8 %collective-permute-start = (bf16[8,256,128]{2,1,0:T(8,128)(2,1)S(1)}, bf16[8,256,128]{2,1,0:T(8,128)(2,1)S(1)}, u32[]{:S(2)}, u32[]{:S(2)}) collective-permute-start(bf16[8,256,128]{2,1,0:T(8,128)(2,1)S(1)} %dynamic-slice_bitcast_fusion), channel_id=1, source_target_pairs={{0,1},{1,0},{2,3},{3,2},{4,5},{5,4},{6,7},{7,6},{8,9},{9,8},{10,11... | collective-permute-start | bytes 1572872 | tf_op jit(solution)/shard_map/ppermute | solution.py:159
  96.3 1.5 collective-permute-done
  97.8 1.2 fusion.4
  99.0 12.6 %all_to_all.55 = bf16[8,256,128]{2,1,0:T(8,128)(2,1)S(1)} all-to-all(bf16[8,256,128]{2,1,0:T(8,128)(2,1)S(1)} %fusion.4), channel_id=1, replica_groups=mesh['yh'=2,'z'=4,'yl'=2,'x'=4,'core'=2] {'yl','x'}, dimensions={0} | all-to-all | bytes 1048576 | tf_op jit(solution)/shard_map/all_to_all | solution.py:143
  111.6 0.1 reduce_sum.174
  111.8 11.6 %all_to_all.56 = bf16[8,256,128]{2,1,0:T(8,128)(2,1)S(1)} all-to-all(bf16[8,256,128]{2,1,0:T(8,128)(2,1)S(1)} %broadcast_in_dim.109), channel_id=1, replica_groups=mesh['yh'=2,'z'=4,'yl'=2,'x'=4,'core'=2] {'yl','x'}, dimensions={0} | all-to-all | bytes 1048576 | tf_op jit(solution)/shard_map/all_to_all | solution.py:143
  123.4 1.8 collective-permute-start.1
  125.2 1.5 collective-permute-done.1
  126.8 0.1 select_bitcast_fusion.1
  126.8 0.1 pad_maximum_fusion
  127.0 7.2 %tile_backward.1 = bf16[1024,128]{1,0:T(8,128)(2,1)S(1)} custom-call(bf16[4096,1024]{1,0:T(8,128)(2,1)} %get-tuple-element.5.tile_ref, bf16[4096,128]{1,0:T(8,128)(2,1)S(1)} %bitcast.49), custom_call_target="tpu_custom_call" | custom-call | tf_op jit(solution)/shard_map/tile_backward/pallas_call | solution.py:95
  134.2 12.5 %all_to_all.57 = bf16[8,128,128]{2,1,0:T(8,128)(2,1)S(1)} all-to-all(bf16[8,128,128]{2,1,0:T(8,128)(2,1)S(1)} %bitcast.53), channel_id=1, replica_groups=mesh['yh'=2,'z'=4,'yl'=2,'x'=4,'core'=2] {'yh','z'}, dimensions={0} | all-to-all | bytes 524288 | tf_op jit(solution)/shard_map/all_to_all | solution.py:143
  146.8 10.9 %all_to_all.58 = bf16[8,128,128]{2,1,0:T(8,128)(2,1)S(1)} all-to-all(bf16[8,128,128]{2,1,0:T(8,128)(2,1)S(1)} %broadcast_in_dim.110), channel_id=1, replica_groups=mesh['yh'=2,'z'=4,'yl'=2,'x'=4,'core'=2] {'yh','z'}, dimensions={0} | all-to-all | bytes 524288 | tf_op jit(solution)/shard_map/all_to_all | solution.py:143
  157.7 2.0 precond_backward.1
  159.8 2.6 %collective-permute-start.2 = (bf16[8,128,128]{2,1,0:T(8,128)(2,1)S(1)}, bf16[8,128,128]{2,1,0:T(8,128)(2,1)S(1)}, u32[]{:S(2)}, u32[]{:S(2)}) collective-permute-start(bf16[8,128,128]{2,1,0:T(8,128)(2,1)S(1)} %dynamic-slice_bitcast_fusion.1), channel_id=1, source_target_pairs={{0,1},{1,0},{2,3},{3,2},{4,5},{5,4},{6,7},{7,6},{8,9},{9,8},{10,11... | collective-permute-start | bytes 786440 | tf_op jit(solution)/shard_map/ppermute | solution.py:159
  162.4 1.2 collective-permute-done.2
  163.5 0.8 fusion.9
  164.3 3.4 %all-to-all-start.8 = ((bf16[8,128,128]{2,1,0:T(8,128)(2,1)}), bf16[8,128,128]{2,1,0:T(8,128)(2,1)S(1)}, u32[]{:S(2)}, u32[]{:S(2)}) async-start(bf16[8,128,128]{2,1,0:T(8,128)(2,1)} %fusion.9), calls=%async_computation.8 | async-start | bytes 524288 | tf_op jit(solution)/shard_map/all_to_all | solution.py:143
  167.7 7.3 %all-to-all-done.8 = bf16[8,128,128]{2,1,0:T(8,128)(2,1)S(1)} async-done(((bf16[8,128,128]{2,1,0:T(8,128)(2,1)}), bf16[8,128,128]{2,1,0:T(8,128)(2,1)S(1)}, u32[]{:S(2)}, u32[]{:S(2)}) %all-to-all-start.8) | async-done | bytes 262176 | tf_op jit(solution)/shard_map/all_to_all | solution.py:143
  175.1 0.6 abs_reduce_fusion
  177.0 0.7 multiply_reduce_fusion.5
  177.7 0.6 compare_select_fusion.1
  178.4 2.1 %select_select_fusion = f32[8,128]{1,0:T(8,128)S(1)} fusion(f32[8]{0:T(128)S(1)} %compare_select_fusion.1, f32[]{:T(128)} %get-tuple-element.10, f32[]{:T(128)} %get-tuple-element.8, f32[]{:T(128)} %get-tuple-element.7, f32[]{:T(128)S(6)} %select_n.75, pred[8]{0:T(512)(128)(4,1)S(1)} %get-tuple-element.45, pred[8]{0:T(512)(128)(4,1)S(1)} %get-tuple-element.46, ...), kind=kLoop, calls=%fused_computation.57 | loop fusion | flops 4096 | bytes 4176 | tf_op jit(solution)/shard_map/jit(_where)/select_n | solution.py:216
  180.5 9.2 %all_to_all.59 = f32[16,8,128]{2,1,0:T(8,128)S(1)} all-to-all(f32[16,8,128]{2,1,0:T(8,128)S(1)} %broadcast_in_dim.117), channel_id=1, replica_groups=mesh['yh'=2,'z'=4,'yl'=2,'x'=4,'core'=2] {'yl','x','core'}, dimensions={0} | all-to-all | bytes 131072 | tf_op jit(solution)/shard_map/all_to_all | solution.py:143
  189.8 9.0 %all_to_all.60 = f32[8,8,128]{2,1,0:T(8,128)S(1)} all-to-all(f32[8,8,128]{2,1,0:T(8,128)S(1)} %broadcast_in_dim.119), channel_id=1, replica_groups=mesh['yh'=2,'z'=4,'yl'=2,'x'=4,'core'=2] {'yh','z'}, dimensions={0} | all-to-all | bytes 65536 | tf_op jit(solution)/shard_map/all_to_all | solution.py:143
  198.8 0.5 fusion.18
  202.1 0.7 multiply_add_fusion
  (41 shorter events, 0.6 us)
Async XLA Ops:
  7.8 16.1 %all-to-all-start.1 = ((bf16[8,128,128]{2,1,0:T(8,128)(2,1)}), bf16[8,128,128]{2,1,0:T(8,128)(2,1)S(1)}, u32[]{:S(2)}, u32[]{:S(2)}) async-start(bf16[8,128,128]{2,1,0:T(8,128)(2,1)} %pad_maximum_fusion.2), calls=%async_computation.1 | async-start | bytes 524288 | tf_op jit(solution)/shard_map/all_to_all | solution.py:143
  16.3 1.7 copy-start.4
  24.8 16.4 %all-to-all-start = ((bf16[16,128,128]{2,1,0:T(8,128)(2,1)}), bf16[16,128,128]{2,1,0:T(8,128)(2,1)S(1)}, u32[]{:S(2)}, u32[]{:S(2)}) async-start(bf16[16,128,128]{2,1,0:T(8,128)(2,1)} %broadcast_in_dim.100), calls=%async_computation | async-start | bytes 1048576 | tf_op jit(solution)/shard_map/all_to_all | solution.py:143
  41.2 2.2 %copy-start = (bf16[1024,2048]{1,0:T(8,128)(2,1)S(1)}, bf16[1024,2048]{1,0:T(8,128)(2,1)}, u32[]{:S(2)}) copy-start(bf16[1024,2048]{1,0:T(8,128)(2,1)} %pre_ref.3) | copy-start | bytes 12582916
  45.1 5.1 %copy-start.3 = (f32[4096,1]{1,0:T(8,128)S(1)}, f32[4096,1]{1,0:T(8,128)}, u32[]{:S(2)}) copy-start(f32[4096,1]{1,0:T(8,128)} %copy.39) | copy-start | bytes 49156
  46.0 20.8 %all-to-all-start.2 = ((bf16[8,256,128]{2,1,0:T(8,128)(2,1)}), bf16[8,256,128]{2,1,0:T(8,128)(2,1)}, u32[]{:S(2)}, u32[]{:S(2)}) async-start(bf16[8,256,128]{2,1,0:T(8,128)(2,1)} %pad_maximum_fusion.1), calls=%async_computation.2 | async-start | bytes 1048576 | tf_op jit(solution)/shard_map/all_to_all | solution.py:143
  70.4 14.2 %all-to-all-start.3 = ((bf16[8,128,128]{2,1,0:T(8,128)(2,1)}), bf16[8,128,128]{2,1,0:T(8,128)(2,1)S(1)}, u32[]{:S(2)}, u32[]{:S(2)}) async-start(bf16[8,128,128]{2,1,0:T(8,128)(2,1)} %broadcast_in_dim.108), calls=%async_computation.3 | async-start | bytes 524288 | tf_op jit(solution)/shard_map/all_to_all | solution.py:143
  92.3 1.1 copy-start.2
  93.4 4.4 %collective-permute-start = (bf16[8,256,128]{2,1,0:T(8,128)(2,1)S(1)}, bf16[8,256,128]{2,1,0:T(8,128)(2,1)S(1)}, u32[]{:S(2)}, u32[]{:S(2)}) collective-permute-start(bf16[8,256,128]{2,1,0:T(8,128)(2,1)S(1)} %dynamic-slice_bitcast_fusion), channel_id=1, source_target_pairs={{0,1},{1,0},{2,3},{3,2},{4,5},{5,4},{6,7},{7,6},{8,9},{9,8},{10,11... | collective-permute-start | bytes 1572872 | tf_op jit(solution)/shard_map/ppermute | solution.py:159
  123.4 3.4 %collective-permute-start.1 = (bf16[8,256,128]{2,1,0:T(8,128)(2,1)S(1)}, bf16[8,256,128]{2,1,0:T(8,128)(2,1)S(1)}, u32[]{:S(2)}, u32[]{:S(2)}) collective-permute-start(bf16[8,256,128]{2,1,0:T(8,128)(2,1)S(1)} %all_to_all.56), channel_id=1, source_target_pairs={{0,1},{1,0},{2,3},{3,2},{4,5},{5,4},{6,7},{7,6},{8,9},{9,8},{10,11... | collective-permute-start | bytes 1572872 | tf_op jit(solution)/shard_map/ppermute | solution.py:165
  127.0 30.8 %copy-start.1 = (bf16[1024,2048]{1,0:T(8,128)(2,1)S(1)}, bf16[1024,2048]{1,0:T(8,128)(2,1)}, u32[]{:S(2)}) copy-start(bf16[1024,2048]{1,0:T(8,128)(2,1)} %pre_ref.3) | copy-start | bytes 12582916
  159.7 17.3 %copy-start.5 = (f32[128,128]{1,0:T(8,128)S(1)}, f32[128,128]{1,0:T(8,128)}, u32[]{:S(2)}) copy-start(f32[128,128]{1,0:T(8,128)} %param.10) | copy-start | bytes 196612
  159.7 42.4 %copy-start.6 = (f32[128,128]{1,0:T(8,128)S(1)}, f32[128,128]{1,0:T(8,128)}, u32[]{:S(2)}) copy-start(f32[128,128]{1,0:T(8,128)} %param.9) | copy-start | bytes 196612
  159.8 3.8 %collective-permute-start.2 = (bf16[8,128,128]{2,1,0:T(8,128)(2,1)S(1)}, bf16[8,128,128]{2,1,0:T(8,128)(2,1)S(1)}, u32[]{:S(2)}, u32[]{:S(2)}) collective-permute-start(bf16[8,128,128]{2,1,0:T(8,128)(2,1)S(1)} %dynamic-slice_bitcast_fusion.1), channel_id=1, source_target_pairs={{0,1},{1,0},{2,3},{3,2},{4,5},{5,4},{6,7},{7,6},{8,9},{9,8},{10,11... | collective-permute-start | bytes 786440 | tf_op jit(solution)/shard_map/ppermute | solution.py:159
  164.3 10.8 %all-to-all-start.8 = ((bf16[8,128,128]{2,1,0:T(8,128)(2,1)}), bf16[8,128,128]{2,1,0:T(8,128)(2,1)S(1)}, u32[]{:S(2)}, u32[]{:S(2)}) async-start(bf16[8,128,128]{2,1,0:T(8,128)(2,1)} %fusion.9), calls=%async_computation.8 | async-start | bytes 524288 | tf_op jit(solution)/shard_map/all_to_all | solution.py:143

commit v2 on v1

v2 whole, which is shorter than its diff:
```python
import math

import jax
import jax.numpy as jnp
import numpy as np
from jax import lax
from jax.experimental import pallas as pl
from jax.experimental.pallas import tpu as pltpu
from jax.sharding import Mesh
from jax.sharding import PartitionSpec as P

FEAT = 64
OUTS = 128
ridge_weight = 0.1
F32, BF16 = jnp.float32, jnp.bfloat16

FINE = (("yh", 2), ("z", 4), ("yl", 2), ("x", 4), ("core", 2))
ROWS = ("yh", "z")
CHIPS = ("yl", "x")
CENT = ("yl", "x", "core")
FEATURE_SCALE = math.sqrt(2.0 * (2.0 / FEAT) * math.log2(math.e))
SWAP = [(0, 1), (1, 0)]


def params(limit=48):
    return pltpu.CompilerParams(vmem_limit_bytes=limit * 1024 * 1024)


def cost(flops, nbytes, exps=0):
    return pl.CostEstimate(flops=flops, bytes_accessed=nbytes, transcendentals=exps)


def split_pieces(value, count):
    out = []
    for _ in range(count):
        top = value.astype(BF16)
        out.append(top)
        value = value - top.astype(F32)
    return out


def operand(high, mid, row_side):
    n = high.shape[1]
    value = high.astype(F32) + mid.astype(F32)
    norm = -0.5 * jnp.sum(value * value, axis=0, keepdims=True)
    line = lax.broadcasted_iota(jnp.int32, (FEAT, n), 0)
    tail = jnp.zeros((FEAT, n), F32)
    first_norm, first_one = (0, 3) if row_side else (3, 0)
    for place, piece in enumerate(split_pieces(norm, 3)):
        tail = jnp.where(line == first_norm + place, piece.astype(F32), tail)
    tail = jnp.where((line >= first_one) & (line < first_one + 3), 1.0, tail).astype(BF16)
    middle = (high, mid) if row_side else (mid, high)
    return jnp.concatenate([high, *middle, tail], axis=0)


def pick_kernel(start_ref, index_ref, feat_ref, out_ref, total_ref):
    step = pl.program_id(0)
    block = feat_ref.shape[1]

    @pl.when(step == 0)
    def _():
        total_ref[...] = jnp.zeros_like(total_ref)

    table = jnp.concatenate(split_pieces(feat_ref[...] * FEATURE_SCALE, 2), axis=0)
    wanted = index_ref[...] - (start_ref[0] + step * block)
    place = lax.broadcasted_iota(jnp.int32, (block, wanted.shape[1]), 0)
    choice = jnp.where(place == wanted, 1.0, 0.0).astype(BF16)
    total_ref[...] += jnp.dot(table, choice, preferred_element_type=F32)

    @pl.when(step == pl.num_programs(0) - 1)
    def _():
        for j in range(out_ref.shape[0]):
            width = out_ref.shape[2]
            out_ref[j] = total_ref[:, j * width : (j + 1) * width].astype(BF16)


def pick(start, index, feat, parts, block=512):
    depth, n = feat.shape
    m = index.shape[1]
    return pl.pallas_call(
        pick_kernel,
        grid=(n // block,),
        in_specs=[
            pl.BlockSpec(memory_space=pltpu.SMEM),
            pl.BlockSpec((1, m), lambda i: (0, 0)),
            pl.BlockSpec((depth, block), lambda i: (0, i)),
        ],
        out_specs=pl.BlockSpec((parts, 2 * depth, m // parts), lambda i: (0, 0, 0)),
        out_shape=jax.ShapeDtypeStruct((parts, 2 * depth, m // parts), BF16),
        scratch_shapes=[pltpu.VMEM((2 * depth, m), F32)],
        compiler_params=params(),
        cost_estimate=cost(2 * n * m * 128 * 4, n * depth * 4),
        name="pick_centres",
    )(start, index, feat)


def prepare_kernel(feat_ref, out_ref):
    high, mid = split_pieces(feat_ref[...] * FEATURE_SCALE, 2)
    out_ref[...] = operand(high, mid, True).T


def prepare_rows(feat, block=1024):
    depth, n = feat.shape
    return pl.pallas_call(
        prepare_kernel,
        grid=(n // block,),
        in_specs=[pl.BlockSpec((depth, block), lambda i: (0, i))],
        out_specs=pl.BlockSpec((block, 256), lambda i: (i, 0)),
        out_shape=jax.ShapeDtypeStruct((n, 256), BF16),
        compiler_params=params(),
        cost_estimate=cost(n * 2**20 // 2, n * 1024),
        name="prepare_rows",
    )(feat)


def tile_kernel(rows_ref, got_ref, tile_ref, cen_ref):
    @pl.when(pl.program_id(0) == 0)
    def _():
        width = got_ref.shape[2]
        for j in range(got_ref.shape[0]):
            both = got_ref[j, got_ref.shape[1] - 2 * FEAT :]
            cen_ref[:, j * width : (j + 1) * width] = operand(both[:FEAT], both[FEAT:], False)

    power = jnp.dot(rows_ref[...], cen_ref[...], preferred_element_type=F32)
    tile_ref[...] = jnp.exp2(power).astype(BF16)


def make_tile(rows_op, got, block=512):
    n = rows_op.shape[0]
    m = got.shape[0] * got.shape[2]
    return pl.pallas_call(
        tile_kernel,
        grid=(n // block,),
        in_specs=[pl.BlockSpec((block, 256), lambda i: (i, 0)), pl.BlockSpec(got.shape, lambda i: (0, 0, 0))],
        out_specs=pl.BlockSpec((block, m), lambda i: (i, 0)),
        out_shape=jax.ShapeDtypeStruct((n, m), BF16),
        scratch_shapes=[pltpu.VMEM((256, m), BF16)],
        compiler_params=params(),
        cost_estimate=cost(2 * n * m * 256, 2 * n * m, n * m),
        name="kernel_tile",
    )(rows_op, got)


def forward_kernel(tile_ref, coef_ref, fit_ref):
    fit_ref[...] = jnp.dot(tile_ref[...], coef_ref[...], preferred_element_type=F32)


def forward(tile, coef, block=512):
    n, m = tile.shape
    return pl.pallas_call(
        forward_kernel,
        grid=(n // block,),
        in_specs=[pl.BlockSpec((block, m), lambda i: (i, 0)), pl.BlockSpec((m, OUTS), lambda i: (0, 0))],
        out_specs=pl.BlockSpec((block, OUTS), lambda i: (i, 0)),
        out_shape=jax.ShapeDtypeStruct((n, OUTS), F32),
        compiler_params=params(),
        cost_estimate=cost(2 * n * m * OUTS, 2 * n * m),
        name="tile_forward",
    )(tile, coef)


def back_kernel(tile_ref, fit_ref, grad_ref, total_ref):
    step = pl.program_id(0)

    @pl.when(step == 0)
    def _():
        total_ref[...] = jnp.zeros_like(total_ref)

    total_ref[...] += jnp.dot(fit_ref[...].T, tile_ref[...], preferred_element_type=F32)

    @pl.when(step == pl.num_programs(0) - 1)
    def _():
        grad_ref[...] = total_ref[...].T.astype(BF16)


def backward(tile, fitted, block=512):
    n, m = tile.shape
    return pl.pallas_call(
        back_kernel,
        grid=(n // block,),
        in_specs=[pl.BlockSpec((block, m), lambda i: (i, 0)), pl.BlockSpec((block, OUTS), lambda i: (i, 0))],
        out_specs=pl.BlockSpec((m, OUTS), lambda i: (0, 0)),
        out_shape=jax.ShapeDtypeStruct((m, OUTS), BF16),
        scratch_shapes=[pltpu.VMEM((OUTS, m), F32)],
        compiler_params=params(),
        cost_estimate=cost(2 * n * m * OUTS, 2 * n * m),
        name="tile_backward",
    )(tile, fitted)


def field_kernel(pre_ref, dir_ref, feat_ref, out_ref):
    width = out_ref.shape[1] - 2 * FEAT
    part = jnp.dot(pre_ref[...], dir_ref[...], preferred_element_type=F32).astype(BF16)
    features = jnp.sum(feat_ref[...].astype(F32), axis=0).astype(BF16)
    for j in range(out_ref.shape[0]):
        out_ref[j, :width] = part[j * width : (j + 1) * width]
        out_ref[j, width:] = features


def field(precond, dir_all, feat_parts, block=256):
    n, m = precond.shape
    parts = feat_parts.shape[0]
    share = n // parts
    return pl.pallas_call(
        field_kernel,
        grid=(n // block,),
        in_specs=[
            pl.BlockSpec((block, m), lambda i: (i, 0)),
            pl.BlockSpec((m, OUTS), lambda i: (0, 0)),
            pl.BlockSpec(feat_parts.shape, lambda i: (0, 0, 0)),
        ],
        out_specs=pl.BlockSpec((block // share, share + 2 * FEAT, OUTS), lambda i: (i, 0, 0)),
        out_shape=jax.ShapeDtypeStruct((parts, share + 2 * FEAT, OUTS), BF16),
        compiler_params=params(60),
        cost_estimate=cost(2 * n * m * OUTS, 2 * n * m),
        name="precond_forward",
    )(precond, dir_all, feat_parts)


def image_kernel(pre_ref, grad_ref, out_ref):
    part = jnp.dot(grad_ref[...].T, pre_ref[...], preferred_element_type=F32).T
    chips, width = out_ref.shape[1:3]
    for chip in range(chips):
        for core in range(2):
            first = (chip * 2 + core) * width
            out_ref[core, chip] = part[first : first + width]


def image_part(precond, grad, share, block=512):
    n, m = precond.shape
    return pl.pallas_call(
        image_kernel,
        grid=(m // block,),
        in_specs=[pl.BlockSpec((n, block), lambda i: (0, i)), pl.BlockSpec((n, OUTS), lambda i: (0, 0))],
        out_specs=pl.BlockSpec((2, block // share // 2, share, OUTS), lambda i: (0, i, 0, 0)),
        out_shape=jax.ShapeDtypeStruct((2, m // share // 2, share, OUTS), F32),
        compiler_params=params(),
        cost_estimate=cost(2 * n * m * OUTS, 2 * n * m),
        name="precond_backward",
    )(precond, grad)


def numbers_kernel(part_ref, dir_ref, res_ref, image_ref, out_ref):
    direction, residual = dir_ref[...], res_ref[...]
    image = jnp.sum(part_ref[...].astype(F32), axis=0) + ridge_weight * direction
    image_ref[...] = image
    top = jnp.max(jnp.max(jnp.abs(image), axis=0, keepdims=True), axis=1, keepdims=True)
    top = jnp.where(top > 0, top, 1.0)
    scaled = image / top

    def total(value):
        return jnp.sum(jnp.sum(value, axis=0, keepdims=True), axis=1, keepdims=True)

    numbers = [total(residual * residual), total(direction * image), total(residual * scaled), total(scaled * scaled), top]
    lane = lax.broadcasted_iota(jnp.int32, (1, 128), 1)
    packed = jnp.zeros((1, 128), F32)
    for place, number in enumerate(numbers):
        packed = jnp.where(lane == place, number, packed)
    out_ref[...] = jnp.broadcast_to(packed, out_ref.shape)


def numbers(parts, direction, residual, devices):
    shape = jax.ShapeDtypeStruct(direction.shape, F32)
    return pl.pallas_call(
        numbers_kernel,
        out_shape=[shape, jax.ShapeDtypeStruct((devices, 128), F32)],
        compiler_params=params(),
        name="image_numbers",
    )(parts, direction, residual)


def finish_kernel(all_ref, image_ref, coef_ref, res_ref, dir_ref, coef_out, res_out, dir_out):
    every = all_ref[...]
    lane = lax.broadcasted_iota(jnp.int32, every.shape, 1)

    def column(place):
        return jnp.sum(jnp.where(lane == place, every, 0.0), axis=1, keepdims=True)

    tops = column(4)
    most = jnp.max(tops, axis=0, keepdims=True)
    ratio = tops / most
    norm_old = jnp.sum(column(0), axis=0, keepdims=True)
    curvature = jnp.sum(column(1), axis=0, keepdims=True)
    cross = jnp.sum(column(2) * ratio, axis=0, keepdims=True)
    square = jnp.sum(column(3) * ratio * ratio, axis=0, keepdims=True)
    step_size = norm_old / curvature
    reach = step_size * most
    norm_new = norm_old - 2.0 * reach * cross + reach * reach * square
    direction = dir_ref[...]
    coef_out[...] = coef_ref[...] + step_size * direction
    residual_next = res_ref[...] - step_size * image_ref[...]
    res_out[...] = residual_next
    dir_out[...] = residual_next + norm_new / norm_old * direction


def finish(every, image, coefficients, residual, direction):
    shape = jax.ShapeDtypeStruct(direction.shape, F32)
    return pl.pallas_call(
        finish_kernel,
        out_shape=[shape, shape, shape],
        compiler_params=params(),
        name="finish",
    )(every, image, coefficients, residual, direction)


def spread(part, axes):
    return lax.all_to_all(part, axes, 0, 0, tiled=True)


def gathered(part, axes):
    count = math.prod(lax.axis_size(axis) for axis in axes)
    return spread(jnp.broadcast_to(part[None], (count, *part.shape)), axes)


def summed(parts):
    return jnp.sum(parts.astype(F32), axis=0)


def core_halves(part, send):
    me = lax.axis_index("core")
    mine = lax.dynamic_index_in_dim(part, me, 0, keepdims=False)
    other = lax.dynamic_index_in_dim(part, 1 - me, 0, keepdims=False)
    came = lax.ppermute(other.astype(send), "core", SWAP)
    return (mine + came.astype(F32)).astype(BF16)


def core_both(part):
    first = lax.axis_index("core") == 0
    came = lax.ppermute(part, "core", SWAP)
    return jnp.stack([jnp.where(first, part, came), jnp.where(first, came, part)])


def on_device(train_rows, centre_index, precond, coefficients, residual, direction):
    rows_here = train_rows.shape[0]
    cen_here = centre_index.shape[0]
    row_devices = lax.axis_size("yh") * lax.axis_size("z")
    cen_devices = lax.axis_size("yl") * lax.axis_size("x") * lax.axis_size("core")
    start_row = (lax.axis_index(ROWS) * rows_here).astype(jnp.int32)
    share = cen_here // row_devices

    dir_all = gathered(direction.astype(BF16), CENT).reshape(-1, OUTS)

    feat = train_rows.T
    feat_parts = spread(pick(start_row[None], centre_index[None], feat, row_devices), ROWS)
    rows_op = prepare_rows(feat)

    got = spread(field(precond, dir_all, feat_parts), ROWS)
    coef_mine = summed(got[:, :share]).astype(BF16)
    coef_field = gathered(coef_mine, ROWS).reshape(cen_here, OUTS)
    tile = make_tile(rows_op, got)
    fit_part = forward(tile, coef_field)

    half = core_halves(fit_part.reshape(2, cen_devices // 2, rows_here // cen_devices, OUTS), BF16)
    fit_mine = summed(spread(half, CHIPS)).astype(BF16)
    fitted = core_both(gathered(fit_mine, CHIPS)).reshape(rows_here, OUTS)

    grad_part = backward(tile, fitted).reshape(row_devices, share, OUTS)
    grad_mine = summed(spread(grad_part, ROWS)) * float(rows_here * row_devices) ** (-0.5)
    grad_low = gathered(grad_mine.astype(BF16), ROWS).reshape(cen_here, OUTS)

    half = core_halves(image_part(precond, grad_low, direction.shape[0]), F32)
    image, row = numbers(spread(half, CHIPS), direction, residual, row_devices * cen_devices)
    every = spread(row, (*ROWS, *CENT))
    return tuple(finish(every, image, coefficients, residual, direction))


def solution(mesh):
    fine = Mesh(np.asarray(mesh.devices).reshape([size for _, size in FINE]), [name for name, _ in FINE])
    every = P((*ROWS, *CENT), None)
    return jax.shard_map(
        on_device,
        mesh=fine,
        in_specs=(P(ROWS, None), P(CENT), P(CENT, ROWS), every, every, every),
        out_specs=(every, every, every),
        check_vma=False,
    )
```

time: 205 us -> 174 us (0.85)
  blocking collectives: 65.8 us -> 102 us
  local copies, waits for them, and re-layouts: 34 us -> 4.24 us
  other arithmetic: 18.9 us -> 0.51 us
  starting transfers between devices: 36.4 us -> 19.4 us
  Pallas kernels: 18.7 us -> 33.7 us
  waiting for transfers between devices: 24 us -> 12.2 us
  between operations: 5.04 us -> 0.82 us
    all_to_all x6 -> x8, blocking collectives: 65.8 us -> 102 us  [spread(): return lax.all_to_all(part, axes, 0, 0, tiled=True)]
    all_to_all x5 -> x2, starting transfers between devices: 29.1 us -> 11.9 us  [spread(): return lax.all_to_all(part, axes, 0, 0, tiled=True)]
    concatenate x3 -> x0, local copies, waits for them, and re-layouts: 13.1 us -> none  [the longest x1 9.57 us: row_operand(): jnp.concatenate([high, high, mid, *half_norm(high, mid), ones, jnp.zeros(...]
    all_to_all x5 -> x2, waiting for transfers between devices: 19.8 us -> 7.56 us  [spread(): return lax.all_to_all(part, axes, 0, 0, tiled=True)]
    pallas_call x1 -> x6, Pallas kernels: 7.8 us -> 19.4 us  [the longest x1 7.34 us: forward(): pl.pallas_call(forward_kernel, grid=(n // block,), in_specs=[pl.BlockSpec...]
    convert_element_type x5 -> x2, other arithmetic: 7.46 us -> 0.17 us  [core_halves(): return (mine + came.astype(F32)).astype(BF16)]
    broadcast_in_dim x6 -> x0, local copies, waits for them, and re-layouts: 3.77 us -> none  [the longest x1 1.15 us: row_operand(): jnp.zeros((n, 58), BF16)]
    pallas_call x1, Pallas kernels: 1.71 us -> 4.88 us  [field(): pl.pallas_call(field_kernel, grid=(n // block,), in_specs=[pl.BlockSpec((...]
  transfers between devices with their start and end apart: 8 -> 5, of which waited for: 7 -> 4; matrix products, arithmetic and copies ran while one was open for 14% -> 0% of each run, Pallas kernels for 0% -> 4%
where the time goes in v2:
time: 174 us; the launch traced here: 173 us
  blocking collectives  102 us (59%)
  Pallas kernels  33.7 us (19%)
  starting transfers between devices  19.4 us (11%)
  waiting for transfers between devices  12.2 us (7%)
  local copies, waits for them, and re-layouts  4.24 us (2%)
    all_to_all x8, blocking collectives, spread(): return lax.all_to_all(part, axes, 0, 0, tiled=True)  102 us
    all_to_all x2, starting transfers between devices, spread(): return lax.all_to_all(part, axes, 0, 0, tiled=True)  11.9 us
    all_to_all x2, waiting for transfers between devices, spread(): return lax.all_to_all(part, axes, 0, 0, tiled=True)  7.56 us
    pallas_call x1, Pallas kernels, forward(): pl.pallas_call(forward_kernel, grid=(n // block,), in_specs=[pl.BlockSpec...  7.34 us
    pallas_call x1, Pallas kernels, backward(): pl.pallas_call(back_kernel, grid=(n // block,), in_specs=[pl.BlockSpec((b...  7.26 us
    pallas_call x1, Pallas kernels, make_tile(): pl.pallas_call(tile_kernel, grid=(n // block,), in_specs=[pl.BlockSpec((b...  6.45 us
    ppermute x2, starting transfers between devices, core_halves(): came = lax.ppermute(other.astype(send), 'core', SWAP)  5.34 us
    pallas_call x1, Pallas kernels, field(): pl.pallas_call(field_kernel, grid=(n // block,), in_specs=[pl.BlockSpec((...  4.88 us
  transfers between devices with their start and end apart: 5, of which 4 were waited for; matrix products, arithmetic and copies ran while one was open for 0% of the time, Pallas kernels for 4%

profile of v2, /device:TPU:1, one launch (start us, length us, event | category | flops | bytes accessed | tf_op | source)
XLA Modules:
  0.0 172.7 jit_solution(12716502448159210654)
XLA Ops:
  0.6 0.0 copy-start.4
  0.7 1.2 copy-done.4
  1.9 0.0 copy-start.6
  1.9 0.7 copy-done.6
  2.6 0.0 copy-start.1
  2.6 3.6 %pick_centres.1 = bf16[8,128,128]{2,1,0:T(8,128)(2,1)} custom-call(s32[1]{0:T(128)} %bitcast.2.start_ref, s32[1,1024]{1,0:T(1,128)S(1)} %bitcast.39, f32[64,4096]{1,0:T(8,128)S(1)} %bitcast.37), custom_call_target="tpu_custom_call" | custom-call | flops 4294967296 | bytes 1048576 | tf_op jit(solution)/shard_map/pick_centres/pallas_call | solution.py:80
  6.1 8.5 %all-to-all-start.1 = ((bf16[8,128,128]{2,1,0:T(8,128)(2,1)}), bf16[8,128,128]{2,1,0:T(8,128)(2,1)S(1)}, u32[]{:S(2)}, u32[]{:S(2)}) async-start(bf16[8,128,128]{2,1,0:T(8,128)(2,1)} %pick_centres.1), calls=%async_computation.1 | async-start | bytes 524288 | tf_op jit(solution)/shard_map/all_to_all | solution.py:307
  14.6 0.0 copy-done.1
  14.6 7.6 %all-to-all-done.1.feat_ref = bf16[8,128,128]{2,1,0:T(8,128)(2,1)S(1)} async-done(((bf16[8,128,128]{2,1,0:T(8,128)(2,1)}), bf16[8,128,128]{2,1,0:T(8,128)(2,1)S(1)}, u32[]{:S(2)}, u32[]{:S(2)}) %all-to-all-start.1) | async-done | bytes 262176 | tf_op jit(solution)/shard_map/all_to_all | solution.py:307
  22.2 0.0 copy-start.7
  22.2 0.1 broadcast_in_dim.12
  22.3 16.3 %all_to_all.56 = bf16[16,128,128]{2,1,0:T(8,128)(2,1)} all-to-all(bf16[16,128,128]{2,1,0:T(8,128)(2,1)S(1)} %broadcast_in_dim.12), channel_id=1, replica_groups=mesh['yh'=2,'z'=4,'yl'=2,'x'=4,'core'=2] {'yl','x','core'}, dimensions={0} | all-to-all | bytes 1048576 | tf_op jit(solution)/shard_map/all_to_all | solution.py:307
  38.6 0.0 copy-done.7
  38.6 4.9 %precond_forward.1 = bf16[8,256,128]{2,1,0:T(8,128)(2,1)} custom-call(bf16[1024,2048]{1,0:T(8,128)(2,1)} %pre_ref.3, bf16[2048,128]{1,0:T(8,128)(2,1)} %bitcast.40, bf16[8,128,128]{2,1,0:T(8,128)(2,1)} %copy-done.7), custom_call_target="tpu_custom_call" | custom-call | flops 536870912 | bytes 4194304 | tf_op jit(solution)/shard_map/precond_forward/pallas_call | solution.py:204
  43.5 13.2 %all_to_all.57.got_ref = bf16[8,256,128]{2,1,0:T(8,128)(2,1)S(1)} all-to-all(bf16[8,256,128]{2,1,0:T(8,128)(2,1)} %precond_forward.1), channel_id=1, replica_groups=mesh['yh'=2,'z'=4,'yl'=2,'x'=4,'core'=2] {'yh','z'}, dimensions={0} | all-to-all | bytes 1048576 | tf_op jit(solution)/shard_map/all_to_all | solution.py:307
  56.8 0.8 broadcast_in_dim.15
  57.5 3.4 %all-to-all-start.3 = ((bf16[8,128,128]{2,1,0:T(8,128)(2,1)}), bf16[8,128,128]{2,1,0:T(8,128)(2,1)S(1)}, u32[]{:S(2)}, u32[]{:S(2)}) async-start(bf16[8,128,128]{2,1,0:T(8,128)(2,1)} %broadcast_in_dim.15), calls=%async_computation.3 | async-start | bytes 524288 | tf_op jit(solution)/shard_map/all_to_all | solution.py:307
  60.9 0.0 copy-start.5
  61.0 1.2 copy-done.5
  62.2 0.9 prepare_rows.1.rows_ref
  63.1 6.5 %kernel_tile.1.tile_ref = bf16[4096,1024]{1,0:T(8,128)(2,1)} custom-call(bf16[4096,256]{1,0:T(8,128)(2,1)S(1)} %prepare_rows.1.rows_ref, bf16[8,256,128]{2,1,0:T(8,128)(2,1)S(1)} %all_to_all.57.got_ref), custom_call_target="tpu_custom_call" | custom-call | flops 2147483648 | bytes 8388608 | tf_op jit(solution)/shard_map/kernel_tile/pallas_call | solution.py:131
  69.6 0.0 all-to-all-done.3
  69.6 7.3 %tile_forward.1 = f32[4096,128]{1,0:T(8,128)S(1)} custom-call(bf16[4096,1024]{1,0:T(8,128)(2,1)} %kernel_tile.1.tile_ref, bf16[1024,128]{1,0:T(8,128)(2,1)S(1)} %bitcast.34), custom_call_target="tpu_custom_call" | custom-call | flops 1073741824 | bytes 8388608 | tf_op jit(solution)/shard_map/tile_forward/pallas_call | solution.py:150
  76.9 0.1 fusion.1
  77.0 2.7 %collective-permute-start = (bf16[8,256,128]{2,1,0:T(8,128)(2,1)S(1)}, bf16[8,256,128]{2,1,0:T(8,128)(2,1)S(1)}, u32[]{:S(2)}, u32[]{:S(2)}) collective-permute-start(bf16[8,256,128]{2,1,0:T(8,128)(2,1)S(1)} %fusion.1), channel_id=1, source_target_pairs={{0,1},{1,0},{2,3},{3,2},{4,5},{5,4},{6,7},{7,6},{8,9},{9,8},{10,11... | collective-permute-start | bytes 1572872 | tf_op jit(solution)/shard_map/ppermute | solution.py:323
  79.8 1.5 collective-permute-done
  81.3 0.1 fusion
  81.4 11.9 %all_to_all.58 = bf16[8,256,128]{2,1,0:T(8,128)(2,1)S(1)} all-to-all(bf16[8,256,128]{2,1,0:T(8,128)(2,1)S(1)} %fusion), channel_id=1, replica_groups=mesh['yh'=2,'z'=4,'yl'=2,'x'=4,'core'=2] {'yl','x'}, dimensions={0} | all-to-all | bytes 1048576 | tf_op jit(solution)/shard_map/all_to_all | solution.py:307
  93.3 0.1 reduce_sum.34
  93.4 0.1 broadcast_in_dim.16
  93.5 11.3 %all_to_all.59 = bf16[8,256,128]{2,1,0:T(8,128)(2,1)S(1)} all-to-all(bf16[8,256,128]{2,1,0:T(8,128)(2,1)S(1)} %broadcast_in_dim.16), channel_id=1, replica_groups=mesh['yh'=2,'z'=4,'yl'=2,'x'=4,'core'=2] {'yl','x'}, dimensions={0} | all-to-all | bytes 1048576 | tf_op jit(solution)/shard_map/all_to_all | solution.py:307
  104.7 2.2 %collective-permute-start.1 = (bf16[8,256,128]{2,1,0:T(8,128)(2,1)S(1)}, bf16[8,256,128]{2,1,0:T(8,128)(2,1)S(1)}, u32[]{:S(2)}, u32[]{:S(2)}) collective-permute-start(bf16[8,256,128]{2,1,0:T(8,128)(2,1)S(1)} %all_to_all.59), channel_id=1, source_target_pairs={{0,1},{1,0},{2,3},{3,2},{4,5},{5,4},{6,7},{7,6},{8,9},{9,8},{10,11... | collective-permute-start | bytes 1572872 | tf_op jit(solution)/shard_map/ppermute | solution.py:329
  106.9 1.5 collective-permute-done.1
  108.5 0.1 select_bitcast_fusion.1
  108.5 0.1 pad_maximum_fusion
  108.6 0.0 copy-start
  108.6 7.3 %tile_backward.1 = bf16[1024,128]{1,0:T(8,128)(2,1)S(1)} custom-call(bf16[4096,1024]{1,0:T(8,128)(2,1)} %kernel_tile.1.tile_ref, bf16[4096,128]{1,0:T(8,128)(2,1)S(1)} %bitcast.31), custom_call_target="tpu_custom_call" | custom-call | flops 1073741824 | bytes 8388608 | tf_op jit(solution)/shard_map/tile_backward/pallas_call | solution.py:178
  115.9 14.8 %all_to_all.60 = bf16[8,128,128]{2,1,0:T(8,128)(2,1)S(1)} all-to-all(bf16[8,128,128]{2,1,0:T(8,128)(2,1)S(1)} %bitcast.32), channel_id=1, replica_groups=mesh['yh'=2,'z'=4,'yl'=2,'x'=4,'core'=2] {'yh','z'}, dimensions={0} | all-to-all | bytes 524288 | tf_op jit(solution)/shard_map/all_to_all | solution.py:307
  130.8 10.9 %all_to_all.61 = bf16[8,128,128]{2,1,0:T(8,128)(2,1)S(1)} all-to-all(bf16[8,128,128]{2,1,0:T(8,128)(2,1)S(1)} %broadcast_in_dim.17), channel_id=1, replica_groups=mesh['yh'=2,'z'=4,'yl'=2,'x'=4,'core'=2] {'yh','z'}, dimensions={0} | all-to-all | bytes 524288 | tf_op jit(solution)/shard_map/all_to_all | solution.py:307
  141.7 0.0 copy-done
  141.7 2.2 %precond_backward.1 = f32[2,8,128,128]{3,2,1,0:T(8,128)S(1)} custom-call(bf16[1024,2048]{1,0:T(8,128)(2,1)S(1)} %copy-done, bf16[1024,128]{1,0:T(8,128)(2,1)S(1)} %bitcast.33), custom_call_target="tpu_custom_call" | custom-call | flops 536870912 | bytes 4194304 | tf_op jit(solution)/shard_map/precond_backward/pallas_call | solution.py:231
  143.9 0.0 copy-start.2
  143.9 0.0 copy-start.3
  144.0 2.6 %collective-permute-start.2 = (f32[8,128,128]{2,1,0:T(8,128)S(1)}, f32[8,128,128]{2,1,0:T(8,128)S(1)}, u32[]{:S(2)}, u32[]{:S(2)}) collective-permute-start(f32[8,128,128]{2,1,0:T(8,128)S(1)} %dynamic-slice_bitcast_fusion), channel_id=1, source_target_pairs={{0,1},{1,0},{2,3},{3,2},{4,5},{5,4},{6,7},{7,6},{8,9},{9,8},{10,11... | collective-permute-start | bytes 1572872 | tf_op jit(solution)/shard_map/ppermute | solution.py:323
  146.6 1.5 collective-permute-done.2
  148.2 0.1 fusion.2
  148.2 9.8 %all_to_all.62.part_ref = bf16[8,128,128]{2,1,0:T(8,128)(2,1)S(1)} all-to-all(bf16[8,128,128]{2,1,0:T(8,128)(2,1)S(1)} %fusion.2), channel_id=1, replica_groups=mesh['yh'=2,'z'=4,'yl'=2,'x'=4,'core'=2] {'yl','x'}, dimensions={0} | all-to-all | bytes 524288 | tf_op jit(solution)/shard_map/all_to_all | solution.py:307
  158.1 0.0 copy-done.2
  158.1 0.2 image_numbers.1
  158.3 13.6 %all_to_all.63 = f32[128,1,128]{2,1,0:T(1,128)S(1)} all-to-all(f32[128,1,128]{2,1,0:T(1,128)S(1)} %bitcast.36), channel_id=1, replica_groups=mesh['yh'=2,'z'=4,'yl'=2,'x'=4,'core'=2] {'yh','z','yl','x','core'}, dimensions={0} | all-to-all | bytes 131072 | tf_op jit(solution)/shard_map/all_to_all | solution.py:307
  171.9 0.0 copy-done.3
  171.9 0.8 finish.1
  (6 shorter events, 0.2 us)
Async XLA Ops:
  0.6 1.2 copy-start.4
  1.9 0.7 copy-start.6
  2.6 12.0 %copy-start.1 = (f32[128,128]{1,0:T(8,128)S(1)}, f32[128,128]{1,0:T(8,128)}, u32[]{:S(2)}) copy-start(f32[128,128]{1,0:T(8,128)} %dir_ref.3) | copy-start | bytes 196612
  6.1 16.1 %all-to-all-start.1 = ((bf16[8,128,128]{2,1,0:T(8,128)(2,1)}), bf16[8,128,128]{2,1,0:T(8,128)(2,1)S(1)}, u32[]{:S(2)}, u32[]{:S(2)}) async-start(bf16[8,128,128]{2,1,0:T(8,128)(2,1)} %pick_centres.1), calls=%async_computation.1 | async-start | bytes 524288 | tf_op jit(solution)/shard_map/all_to_all | solution.py:307
  22.2 16.4 %copy-start.7 = (bf16[8,128,128]{2,1,0:T(8,128)(2,1)}, bf16[8,128,128]{2,1,0:T(8,128)(2,1)S(1)}, u32[]{:S(2)}) copy-start(bf16[8,128,128]{2,1,0:T(8,128)(2,1)S(1)} %all-to-all-done.1.feat_ref) | copy-start | bytes 786436
  57.5 12.1 %all-to-all-start.3 = ((bf16[8,128,128]{2,1,0:T(8,128)(2,1)}), bf16[8,128,128]{2,1,0:T(8,128)(2,1)S(1)}, u32[]{:S(2)}, u32[]{:S(2)}) async-start(bf16[8,128,128]{2,1,0:T(8,128)(2,1)} %broadcast_in_dim.15), calls=%async_computation.3 | async-start | bytes 524288 | tf_op jit(solution)/shard_map/all_to_all | solution.py:307
  60.9 1.2 copy-start.5
  77.0 4.3 %collective-permute-start = (bf16[8,256,128]{2,1,0:T(8,128)(2,1)S(1)}, bf16[8,256,128]{2,1,0:T(8,128)(2,1)S(1)}, u32[]{:S(2)}, u32[]{:S(2)}) collective-permute-start(bf16[8,256,128]{2,1,0:T(8,128)(2,1)S(1)} %fusion.1), channel_id=1, source_target_pairs={{0,1},{1,0},{2,3},{3,2},{4,5},{5,4},{6,7},{7,6},{8,9},{9,8},{10,11... | collective-permute-start | bytes 1572872 | tf_op jit(solution)/shard_map/ppermute | solution.py:323
  104.7 3.7 %collective-permute-start.1 = (bf16[8,256,128]{2,1,0:T(8,128)(2,1)S(1)}, bf16[8,256,128]{2,1,0:T(8,128)(2,1)S(1)}, u32[]{:S(2)}, u32[]{:S(2)}) collective-permute-start(bf16[8,256,128]{2,1,0:T(8,128)(2,1)S(1)} %all_to_all.59), channel_id=1, source_target_pairs={{0,1},{1,0},{2,3},{3,2},{4,5},{5,4},{6,7},{7,6},{8,9},{9,8},{10,11... | collective-permute-start | bytes 1572872 | tf_op jit(solution)/shard_map/ppermute | solution.py:329
  108.6 33.1 %copy-start = (bf16[1024,2048]{1,0:T(8,128)(2,1)S(1)}, bf16[1024,2048]{1,0:T(8,128)(2,1)}, u32[]{:S(2)}) copy-start(bf16[1024,2048]{1,0:T(8,128)(2,1)} %pre_ref.3) | copy-start | bytes 12582916
  143.9 14.1 %copy-start.2 = (f32[128,128]{1,0:T(8,128)S(1)}, f32[128,128]{1,0:T(8,128)}, u32[]{:S(2)}) copy-start(f32[128,128]{1,0:T(8,128)} %res_ref.3) | copy-start | bytes 196612
  143.9 27.9 %copy-start.3 = (f32[128,128]{1,0:T(8,128)S(1)}, f32[128,128]{1,0:T(8,128)}, u32[]{:S(2)}) copy-start(f32[128,128]{1,0:T(8,128)} %coef_ref.1) | copy-start | bytes 196612
  144.0 4.1 %collective-permute-start.2 = (f32[8,128,128]{2,1,0:T(8,128)S(1)}, f32[8,128,128]{2,1,0:T(8,128)S(1)}, u32[]{:S(2)}, u32[]{:S(2)}) collective-permute-start(f32[8,128,128]{2,1,0:T(8,128)S(1)} %dynamic-slice_bitcast_fusion), channel_id=1, source_target_pairs={{0,1},{1,0},{2,3},{3,2},{4,5},{5,4},{6,7},{7,6},{8,9},{9,8},{10,11... | collective-permute-start | bytes 1572872 | tf_op jit(solution)/shard_map/ppermute | solution.py:323

commit v3 on v2

--- a/solution.py
+++ b/solution.py
@@ -22,7 +22,7 @@
 SWAP = [(0, 1), (1, 0)]
 
 
-def params(limit=48):
+def params(limit=16):
     return pltpu.CompilerParams(vmem_limit_bytes=limit * 1024 * 1024)
 
 
@@ -107,114 +107,130 @@
         in_specs=[pl.BlockSpec((depth, block), lambda i: (0, i))],
         out_specs=pl.BlockSpec((block, 256), lambda i: (i, 0)),
         out_shape=jax.ShapeDtypeStruct((n, 256), BF16),
-        compiler_params=params(),
+        compiler_params=params(60),
         cost_estimate=cost(n * 2**20 // 2, n * 1024),
         name="prepare_rows",
     )(feat)
 
 
-def tile_kernel(rows_ref, got_ref, tile_ref, cen_ref):
+VMEM = pl.BlockSpec(memory_space=pltpu.VMEM)
+SMEM = pl.BlockSpec(memory_space=pltpu.SMEM)
+HBM = pl.BlockSpec(memory_space=pltpu.HBM)
+
+
+def tile_kernel(rows_ref, got_ref, tile_ref, fit_ref, cen_ref, coef_ref):
     @pl.when(pl.program_id(0) == 0)
     def _():
-        width = got_ref.shape[2]
-        for j in range(got_ref.shape[0]):
-            both = got_ref[j, got_ref.shape[1] - 2 * FEAT :]
+        parts, depth, width = got_ref.shape
+        share = depth - 2 * FEAT
+        for j in range(parts):
+            both = got_ref[j, share:]
             cen_ref[:, j * width : (j + 1) * width] = operand(both[:FEAT], both[FEAT:], False)
+            coef_ref[j * share : (j + 1) * share] = got_ref[j, :share]
 
     power = jnp.dot(rows_ref[...], cen_ref[...], preferred_element_type=F32)
-    tile_ref[...] = jnp.exp2(power).astype(BF16)
-
-
-def make_tile(rows_op, got, block=512):
+    tile = jnp.exp2(power).astype(BF16)
+    tile_ref[...] = tile
+    fit_ref[...] = jnp.dot(tile, coef_ref[...], preferred_element_type=F32)
+
+
+def tile_forward(rows_op, got, block=512):
     n = rows_op.shape[0]
-    m = got.shape[0] * got.shape[2]
+    parts, depth, width = got.shape
+    m = parts * width
     return pl.pallas_call(
         tile_kernel,
         grid=(n // block,),
         in_specs=[pl.BlockSpec((block, 256), lambda i: (i, 0)), pl.BlockSpec(got.shape, lambda i: (0, 0, 0))],
-        out_specs=pl.BlockSpec((block, m), lambda i: (i, 0)),
-        out_shape=jax.ShapeDtypeStruct((n, m), BF16),
-        scratch_shapes=[pltpu.VMEM((256, m), BF16)],
-        compiler_params=params(),
-        cost_estimate=cost(2 * n * m * 256, 2 * n * m, n * m),
-        name="kernel_tile",
+        out_specs=[pl.BlockSpec((block, m), lambda i: (i, 0)), pl.BlockSpec((block, OUTS), lambda i: (i, 0))],
+        out_shape=[jax.ShapeDtypeStruct((n, m), BF16), jax.ShapeDtypeStruct((n, OUTS), F32)],
+        scratch_shapes=[pltpu.VMEM((256, m), BF16), pltpu.VMEM((parts * (depth - 2 * FEAT), OUTS), BF16)],
+        compiler_params=params(56),
+        cost_estimate=cost(2 * n * m * 384, 2 * n * m, n * m),
+        name="tile_forward",
     )(rows_op, got)
 
 
-def forward_kernel(tile_ref, coef_ref, fit_ref):
-    fit_ref[...] = jnp.dot(tile_ref[...], coef_ref[...], preferred_element_type=F32)
-
-
-def forward(tile, coef, block=512):
+def back_kernel(me_ref, tile_ref, mine_ref, came_ref, grad_ref, tile_here, fit_ref, total_ref, sems):
+    blocks = sems.shape[0]
+    block = tile_ref.shape[0] // blocks
+    copies = [
+        pltpu.make_async_copy(tile_ref.at[pl.ds(j * block, block)], tile_here.at[pl.ds(j * block, block)], sems.at[j])
+        for j in range(blocks)
+    ]
+    for copy in copies:
+        copy.start()
+    me = me_ref[0]
+    parts, share, _ = mine_ref.shape
+    half = parts * share
+    for j in range(parts):
+        fit_ref[:, pl.ds(pl.multiple_of(me * half + j * share, share), share)] = mine_ref[j].T
+        fit_ref[:, pl.ds(pl.multiple_of((1 - me) * half + j * share, share), share)] = came_ref[j].T
+    for j in range(blocks):
+        copies[j].wait()
+        here = slice(j * block, (j + 1) * block)
+        part = jnp.dot(fit_ref[:, here], tile_here[here], preferred_element_type=F32)
+        if j == 0:
+            total_ref[...] = part
+        else:
+            total_ref[...] += part
+    grad_ref[...] = total_ref[...].T.astype(BF16)
+
+
+def backward(me, tile, mine, came, blocks=8):
     n, m = tile.shape
     return pl.pallas_call(
-        forward_kernel,
-        grid=(n // block,),
-        in_specs=[pl.BlockSpec((block, m), lambda i: (i, 0)), pl.BlockSpec((m, OUTS), lambda i: (0, 0))],
-        out_specs=pl.BlockSpec((block, OUTS), lambda i: (i, 0)),
-        out_shape=jax.ShapeDtypeStruct((n, OUTS), F32),
-        compiler_params=params(),
-        cost_estimate=cost(2 * n * m * OUTS, 2 * n * m),
-        name="tile_forward",
-    )(tile, coef)
-
-
-def back_kernel(tile_ref, fit_ref, grad_ref, total_ref):
-    step = pl.program_id(0)
-
-    @pl.when(step == 0)
-    def _():
-        total_ref[...] = jnp.zeros_like(total_ref)
-
-    total_ref[...] += jnp.dot(fit_ref[...].T, tile_ref[...], preferred_element_type=F32)
-
-    @pl.when(step == pl.num_programs(0) - 1)
-    def _():
-        grad_ref[...] = total_ref[...].T.astype(BF16)
-
-
-def backward(tile, fitted, block=512):
-    n, m = tile.shape
-    return pl.pallas_call(
         back_kernel,
-        grid=(n // block,),
-        in_specs=[pl.BlockSpec((block, m), lambda i: (i, 0)), pl.BlockSpec((block, OUTS), lambda i: (i, 0))],
-        out_specs=pl.BlockSpec((m, OUTS), lambda i: (0, 0)),
+        in_specs=[SMEM, HBM, VMEM, VMEM],
+        out_specs=VMEM,
         out_shape=jax.ShapeDtypeStruct((m, OUTS), BF16),
-        scratch_shapes=[pltpu.VMEM((OUTS, m), F32)],
-        compiler_params=params(),
+        scratch_shapes=[
+            pltpu.VMEM((n, m), BF16),
+            pltpu.VMEM((OUTS, n), BF16),
+            pltpu.VMEM((OUTS, m), F32),
+            pltpu.SemaphoreType.DMA((blocks,)),
+        ],
+        compiler_params=params(53),
         cost_estimate=cost(2 * n * m * OUTS, 2 * n * m),
         name="tile_backward",
-    )(tile, fitted)
-
-
-def field_kernel(pre_ref, dir_ref, feat_ref, out_ref):
+    )(me, tile, mine, came)
+
+
+def field_kernel(me_ref, pre_ref, mine_ref, came_ref, feat_ref, out_ref, pre_here, dir_here, sems):
+    parts = out_ref.shape[0]
     width = out_ref.shape[1] - 2 * FEAT
-    part = jnp.dot(pre_ref[...], dir_ref[...], preferred_element_type=F32).astype(BF16)
-    features = jnp.sum(feat_ref[...].astype(F32), axis=0).astype(BF16)
-    for j in range(out_ref.shape[0]):
-        out_ref[j, :width] = part[j * width : (j + 1) * width]
-        out_ref[j, width:] = features
-
-
-def field(precond, dir_all, feat_parts, block=256):
+    copies = [
+        pltpu.make_async_copy(pre_ref.at[pl.ds(j * width, width)], pre_here.at[pl.ds(j * width, width)], sems.at[j])
+        for j in range(parts)
+    ]
+    for copy in copies:
+        copy.start()
+    me = me_ref[0]
+    chips, share, _ = mine_ref.shape
+    for j in range(chips):
+        dir_here[pl.ds(pl.multiple_of((2 * j + me) * share, share), share)] = mine_ref[j]
+        dir_here[pl.ds(pl.multiple_of((2 * j + 1 - me) * share, share), share)] = came_ref[j]
+    for j in range(parts):
+        out_ref[j, width:] = feat_ref[j]
+    for j in range(parts):
+        copies[j].wait()
+        part = jnp.dot(pre_here[j * width : (j + 1) * width], dir_here[...], preferred_element_type=F32)
+        out_ref[j, :width] = part.astype(BF16)
+
+
+def field(me, precond, mine, came, feat_parts):
     n, m = precond.shape
     parts = feat_parts.shape[0]
-    share = n // parts
     return pl.pallas_call(
         field_kernel,
-        grid=(n // block,),
-        in_specs=[
-            pl.BlockSpec((block, m), lambda i: (i, 0)),
-            pl.BlockSpec((m, OUTS), lambda i: (0, 0)),
-            pl.BlockSpec(feat_parts.shape, lambda i: (0, 0, 0)),
-        ],
-        out_specs=pl.BlockSpec((block // share, share + 2 * FEAT, OUTS), lambda i: (i, 0, 0)),
-        out_shape=jax.ShapeDtypeStruct((parts, share + 2 * FEAT, OUTS), BF16),
-        compiler_params=params(60),
+        in_specs=[SMEM, HBM, VMEM, VMEM, VMEM],
+        out_specs=VMEM,
+        out_shape=jax.ShapeDtypeStruct((parts, n // parts + 2 * FEAT, OUTS), BF16),
+        scratch_shapes=[pltpu.VMEM((n, m), BF16), pltpu.VMEM((m, OUTS), BF16), pltpu.SemaphoreType.DMA((parts,))],
+        compiler_params=params(57),
         cost_estimate=cost(2 * n * m * OUTS, 2 * n * m),
         name="precond_forward",
-    )(precond, dir_all, feat_parts)
+    )(me, precond, mine, came, feat_parts)
 
 
 def image_kernel(pre_ref, grad_ref, out_ref):
@@ -324,37 +340,30 @@
     return (mine + came.astype(F32)).astype(BF16)
 
 
-def core_both(part):
-    first = lax.axis_index("core") == 0
-    came = lax.ppermute(part, "core", SWAP)
-    return jnp.stack([jnp.where(first, part, came), jnp.where(first, came, part)])
-
-
 def on_device(train_rows, centre_index, precond, coefficients, residual, direction):
     rows_here = train_rows.shape[0]
     cen_here = centre_index.shape[0]
     row_devices = lax.axis_size("yh") * lax.axis_size("z")
     cen_devices = lax.axis_size("yl") * lax.axis_size("x") * lax.axis_size("core")
+    me = lax.axis_index("core").astype(jnp.int32)[None]
     start_row = (lax.axis_index(ROWS) * rows_here).astype(jnp.int32)
     share = cen_here // row_devices
 
-    dir_all = gathered(direction.astype(BF16), CENT).reshape(-1, OUTS)
-
+    dir_mine = gathered(direction.astype(BF16), CHIPS)
     feat = train_rows.T
-    feat_parts = spread(pick(start_row[None], centre_index[None], feat, row_devices), ROWS)
+    picked = pick(start_row[None], centre_index[None], feat, row_devices)
+    dir_mine, picked = lax.optimization_barrier((dir_mine, picked))
+    dir_came = lax.ppermute(dir_mine, "core", SWAP)
     rows_op = prepare_rows(feat)
-
-    got = spread(field(precond, dir_all, feat_parts), ROWS)
-    coef_mine = summed(got[:, :share]).astype(BF16)
-    coef_field = gathered(coef_mine, ROWS).reshape(cen_here, OUTS)
-    tile = make_tile(rows_op, got)
-    fit_part = forward(tile, coef_field)
+    parts = spread(field(me, precond, dir_mine, dir_came, picked), ROWS)
+    got = gathered(summed(parts).astype(BF16), ROWS)
+    tile, fit_part = tile_forward(rows_op, got)
 
     half = core_halves(fit_part.reshape(2, cen_devices // 2, rows_here // cen_devices, OUTS), BF16)
-    fit_mine = summed(spread(half, CHIPS)).astype(BF16)
-    fitted = core_both(gathered(fit_mine, CHIPS)).reshape(rows_here, OUTS)
-
-    grad_part = backward(tile, fitted).reshape(row_devices, share, OUTS)
+    fit_mine = gathered(summed(spread(half, CHIPS)).astype(BF16), CHIPS)
+    fit_came = lax.ppermute(fit_mine, "core", SWAP)
+
+    grad_part = backward(me, tile, fit_mine, fit_came).reshape(row_devices, share, OUTS)
     grad_mine = summed(spread(grad_part, ROWS)) * float(rows_here * row_devices) ** (-0.5)
     grad_low = gathered(grad_mine.astype(BF16), ROWS).reshape(cen_here, OUTS)
 

time: 174 us -> 161 us (0.925)
  blocking collectives: 102 us -> 86.1 us
  local copies, waits for them, and re-layouts: 4.24 us -> 8.04 us
  Pallas kernels: 33.7 us -> 30.8 us
  other arithmetic: 0.51 us -> 2.45 us
    all_to_all x8 -> x7, blocking collectives: 102 us -> 86.1 us  [spread(): return lax.all_to_all(part, axes, 0, 0, tiled=True)]
    pallas_call x4 -> x3, Pallas kernels: 25.9 us -> 20.7 us  [the longest x1 10 us: tile_forward(): pl.pallas_call(tile_kernel, grid=(n // block,), in_specs=[pl.BlockSpec((b...]
    pallas_call x1, Pallas kernels: 0.95 us -> 3.96 us  [prepare_rows(): pl.pallas_call(prepare_kernel, grid=(n // block,), in_specs=[pl.BlockSpec...]
    all_to_all x2, starting transfers between devices: 11.9 us -> 9.74 us  [spread(): return lax.all_to_all(part, axes, 0, 0, tiled=True)]
    ppermute x1 -> x2, starting transfers between devices: 2.2 us -> 4.15 us  [the longest x1 2.2 us: on_device(): fit_came = lax.ppermute(fit_mine, 'core', SWAP)]
    all_to_all x2, waiting for transfers between devices: 7.56 us -> 5.68 us  [spread(): return lax.all_to_all(part, axes, 0, 0, tiled=True)]
    unnamed x16 -> x22, local copies, waits for them, and re-layouts: 3.15 us -> 4.97 us
  transfers between devices with their start and end apart: 5 -> 6, of which waited for: 4 -> 6; matrix products, arithmetic and copies ran while one was open for 0% -> 0% of each run, Pallas kernels for 4% -> 4%
where the time goes in v3:
time: 161 us; the launch traced here: 159 us
  blocking collectives  86.1 us (53%)
  Pallas kernels  30.8 us (19%)
  starting transfers between devices  19.9 us (12%)
  waiting for transfers between devices  11.5 us (7%)
  local copies, waits for them, and re-layouts  8.04 us (5%)
  other arithmetic  2.45 us (2%)
    all_to_all x7, blocking collectives, spread(): return lax.all_to_all(part, axes, 0, 0, tiled=True)  86.1 us
    pallas_call x1, Pallas kernels, tile_forward(): pl.pallas_call(tile_kernel, grid=(n // block,), in_specs=[pl.BlockSpec((b...  10 us
    all_to_all x2, starting transfers between devices, spread(): return lax.all_to_all(part, axes, 0, 0, tiled=True)  9.74 us
    ppermute x2, starting transfers between devices, core_halves(): came = lax.ppermute(other.astype(send), 'core', SWAP)  6.02 us
    all_to_all x2, waiting for transfers between devices, spread(): return lax.all_to_all(part, axes, 0, 0, tiled=True)  5.68 us
    pallas_call x1, Pallas kernels, field(): pl.pallas_call(field_kernel, in_specs=[SMEM, HBM, VMEM, VMEM, VMEM], out_...  5.35 us
    pallas_call x1, Pallas kernels, backward(): pl.pallas_call(back_kernel, in_specs=[SMEM, HBM, VMEM, VMEM], out_specs=V...  5.28 us
    unnamed x22, local copies, waits for them, and re-layouts  4.97 us
  transfers between devices with their start and end apart: 6, of which 6 were waited for; matrix products, arithmetic and copies ran while one was open for 0% of the time, Pallas kernels for 4%

profile of v3, /device:TPU:1, one launch (start us, length us, event | category | flops | bytes accessed | tf_op | source)
XLA Modules:
  0.0 159.5 jit_solution(639797707223357584)
XLA Ops:
  0.6 0.8 convert_element_type.32
  1.5 0.7 broadcast_in_dim.15
  2.2 5.9 %all-to-all-start = ((bf16[8,128,128]{2,1,0:T(8,128)(2,1)}), bf16[8,128,128]{2,1,0:T(8,128)(2,1)S(1)}, u32[]{:S(2)}, u32[]{:S(2)}) async-start(bf16[8,128,128]{2,1,0:T(8,128)(2,1)} %broadcast_in_dim.15), calls=%async_computation | async-start | bytes 524288 | tf_op jit(solution)/shard_map/all_to_all | solution.py:323
  8.1 0.0 copy-start.5
  8.1 1.2 copy-done.5
  9.3 0.0 copy-start.6
  9.3 0.7 copy-done.6
  10.0 2.8 %pick_centres.1.feat_ref = bf16[8,128,128]{2,1,0:T(8,128)(2,1)S(1)} custom-call(s32[1]{0:T(128)} %bitcast.2.start_ref, s32[1,1024]{1,0:T(1,128)S(1)} %bitcast.29, f32[64,4096]{1,0:T(8,128)S(1)} %bitcast.28), custom_call_target="tpu_custom_call" | custom-call | flops 4294967296 | bytes 1048576 | tf_op jit(solution)/shard_map/pick_centres/pallas_call | solution.py:80
  12.8 0.0 copy-start.2
  12.9 0.7 copy-done.2
  13.5 0.8 all-to-all-done.mine_ref
  14.4 0.0 copy-start.7
  14.4 1.9 %collective-permute-start = (bf16[8,128,128]{2,1,0:T(8,128)(2,1)S(1)}, bf16[8,128,128]{2,1,0:T(8,128)(2,1)S(1)}, u32[]{:S(2)}, u32[]{:S(2)}) collective-permute-start(bf16[8,128,128]{2,1,0:T(8,128)(2,1)S(1)} %all-to-all-done.mine_ref), channel_id=1, source_target_pairs={{0,1},{1,0},{2,3},{3,2},{4,5},{5,4},{6,7},{7,6},{8,9},{9,8},{10,11... | collective-permute-start | bytes 786440 | tf_op jit(solution)/shard_map/ppermute | solution.py:356
  16.3 1.2 collective-permute-done.came_ref
  17.5 0.0 copy-start.10
  17.5 0.0 copy-done.7
  17.5 0.7 copy-done.10
  18.2 5.4 %precond_forward.1 = bf16[8,256,128]{2,1,0:T(8,128)(2,1)} custom-call(s32[1]{0:T(128)} %bitcast.me_ref, bf16[1024,2048]{1,0:T(8,128)(2,1)} %pre_ref.3, bf16[8,128,128]{2,1,0:T(8,128)(2,1)} %copy-done.7, bf16[8,128,128]{2,1,0:T(8,128)(2,1)} %copy-done.10, bf16[8,128,128]{2,1,0:T(8,128)(2,1)} %copy-done.2), custom_call_target="tpu_custom_call" | custom-call | flops 536870912 | bytes 4194304 | tf_op jit(solution)/shard_map/precond_forward/pallas_call | solution.py:224
  23.6 17.4 %all_to_all.51 = bf16[8,256,128]{2,1,0:T(8,128)(2,1)S(1)} all-to-all(bf16[8,256,128]{2,1,0:T(8,128)(2,1)} %precond_forward.1), channel_id=1, replica_groups=mesh['yh'=2,'z'=4,'yl'=2,'x'=4,'core'=2] {'yh','z'}, dimensions={0} | all-to-all | bytes 1048576 | tf_op jit(solution)/shard_map/all_to_all | solution.py:323
  41.0 0.1 reduce_sum.33
  41.0 0.9 broadcast_in_dim.18
  41.9 3.9 %all-to-all-start.2 = ((bf16[8,256,128]{2,1,0:T(8,128)(2,1)}), bf16[8,256,128]{2,1,0:T(8,128)(2,1)S(1)}, u32[]{:S(2)}, u32[]{:S(2)}) async-start(bf16[8,256,128]{2,1,0:T(8,128)(2,1)} %broadcast_in_dim.18), calls=%async_computation.2 | async-start | bytes 1048576 | tf_op jit(solution)/shard_map/all_to_all | solution.py:323
  45.8 4.0 %prepare_rows.1.rows_ref = bf16[4096,256]{1,0:T(8,128)(2,1)} custom-call(f32[64,4096]{1,0:T(8,128)} %bitcast.27), custom_call_target="tpu_custom_call" | custom-call | flops 2147483648 | bytes 4194304 | tf_op jit(solution)/shard_map/prepare_rows/pallas_call | solution.py:104
  49.8 4.8 %all-to-all-done.2.got_ref = bf16[8,256,128]{2,1,0:T(8,128)(2,1)S(1)} async-done(((bf16[8,256,128]{2,1,0:T(8,128)(2,1)}), bf16[8,256,128]{2,1,0:T(8,128)(2,1)S(1)}, u32[]{:S(2)}, u32[]{:S(2)}) %all-to-all-start.2) | async-done | bytes 524320 | tf_op jit(solution)/shard_map/all_to_all | solution.py:323
  54.6 0.0 copy-start.9
  54.6 0.8 copy-done.9
  55.4 10.0 %tile_forward.1 = (bf16[4096,1024]{1,0:T(8,128)(2,1)}, f32[4096,128]{1,0:T(8,128)}) custom-call(bf16[4096,256]{1,0:T(8,128)(2,1)} %prepare_rows.1.rows_ref, bf16[8,256,128]{2,1,0:T(8,128)(2,1)} %copy-done.9), custom_call_target="tpu_custom_call" | custom-call | flops 3221225472 | bytes 8388608 | tf_op jit(solution)/shard_map/tile_forward/pallas_call | solution.py:141
  65.5 1.3 fusion.1
  66.8 3.4 %collective-permute-start.1 = (bf16[8,256,128]{2,1,0:T(8,128)(2,1)S(1)}, bf16[8,256,128]{2,1,0:T(8,128)(2,1)S(1)}, u32[]{:S(2)}, u32[]{:S(2)}) collective-permute-start(bf16[8,256,128]{2,1,0:T(8,128)(2,1)S(1)} %fusion.1), channel_id=1, source_target_pairs={{0,1},{1,0},{2,3},{3,2},{4,5},{5,4},{6,7},{7,6},{8,9},{9,8},{10,11... | collective-permute-start | bytes 1572872 | tf_op jit(solution)/shard_map/ppermute | solution.py:339
  70.2 1.5 collective-permute-done.1
  71.7 1.3 fusion
  73.1 12.3 %all_to_all.52 = bf16[8,256,128]{2,1,0:T(8,128)(2,1)S(1)} all-to-all(bf16[8,256,128]{2,1,0:T(8,128)(2,1)S(1)} %fusion), channel_id=1, replica_groups=mesh['yh'=2,'z'=4,'yl'=2,'x'=4,'core'=2] {'yl','x'}, dimensions={0} | all-to-all | bytes 1048576 | tf_op jit(solution)/shard_map/all_to_all | solution.py:323
  85.4 0.1 reduce_sum.34
  85.4 0.1 broadcast_in_dim.38
  85.5 11.3 %all_to_all.53.mine_ref = bf16[8,256,128]{2,1,0:T(8,128)(2,1)S(1)} all-to-all(bf16[8,256,128]{2,1,0:T(8,128)(2,1)S(1)} %broadcast_in_dim.38), channel_id=1, replica_groups=mesh['yh'=2,'z'=4,'yl'=2,'x'=4,'core'=2] {'yl','x'}, dimensions={0} | all-to-all | bytes 1048576 | tf_op jit(solution)/shard_map/all_to_all | solution.py:323
  96.8 2.2 %collective-permute-start.2 = (bf16[8,256,128]{2,1,0:T(8,128)(2,1)S(1)}, bf16[8,256,128]{2,1,0:T(8,128)(2,1)S(1)}, u32[]{:S(2)}, u32[]{:S(2)}) collective-permute-start(bf16[8,256,128]{2,1,0:T(8,128)(2,1)S(1)} %all_to_all.53.mine_ref), channel_id=1, source_target_pairs={{0,1},{1,0},{2,3},{3,2},{4,5},{5,4},{6,7},{7,6},{8,9},{9,8},{10,11... | collective-permute-start | bytes 1572872 | tf_op jit(solution)/shard_map/ppermute | solution.py:364
  99.0 1.5 collective-permute-done.2.came_ref
  100.5 0.0 copy-start.8
  100.5 0.8 copy-done.8
  101.3 0.0 copy-start
  101.3 5.3 %tile_backward.1 = bf16[1024,128]{1,0:T(8,128)(2,1)S(1)} custom-call(s32[1]{0:T(128)} %bitcast.me_ref, bf16[4096,1024]{1,0:T(8,128)(2,1)} %get-tuple-element.11.tile_ref, bf16[8,256,128]{2,1,0:T(8,128)(2,1)S(1)} %all_to_all.53.mine_ref, bf16[8,256,128]{2,1,0:T(8,128)(2,1)} %copy-done.8), custom_call_target="tpu_custom_call" | custom-call | flops 1073741824 | bytes 8388608 | tf_op jit(solution)/shard_map/tile_backward/pallas_call | solution.py:182
  106.6 10.8 %all_to_all.54 = bf16[8,128,128]{2,1,0:T(8,128)(2,1)S(1)} all-to-all(bf16[8,128,128]{2,1,0:T(8,128)(2,1)S(1)} %bitcast.23), channel_id=1, replica_groups=mesh['yh'=2,'z'=4,'yl'=2,'x'=4,'core'=2] {'yh','z'}, dimensions={0} | all-to-all | bytes 524288 | tf_op jit(solution)/shard_map/all_to_all | solution.py:323
  117.5 10.9 %all_to_all.55 = bf16[8,128,128]{2,1,0:T(8,128)(2,1)S(1)} all-to-all(bf16[8,128,128]{2,1,0:T(8,128)(2,1)S(1)} %broadcast_in_dim.39), channel_id=1, replica_groups=mesh['yh'=2,'z'=4,'yl'=2,'x'=4,'core'=2] {'yh','z'}, dimensions={0} | all-to-all | bytes 524288 | tf_op jit(solution)/shard_map/all_to_all | solution.py:323
  128.4 0.0 copy-done
  128.4 2.2 %precond_backward.1 = f32[2,8,128,128]{3,2,1,0:T(8,128)S(1)} custom-call(bf16[1024,2048]{1,0:T(8,128)(2,1)S(1)} %copy-done, bf16[1024,128]{1,0:T(8,128)(2,1)S(1)} %bitcast.24), custom_call_target="tpu_custom_call" | custom-call | flops 536870912 | bytes 4194304 | tf_op jit(solution)/shard_map/precond_backward/pallas_call | solution.py:247
  130.6 0.0 copy-start.1
  130.6 0.0 copy-start.3
  130.7 0.0 copy-start.4
  130.7 2.6 %collective-permute-start.3 = (f32[8,128,128]{2,1,0:T(8,128)S(1)}, f32[8,128,128]{2,1,0:T(8,128)S(1)}, u32[]{:S(2)}, u32[]{:S(2)}) collective-permute-start(f32[8,128,128]{2,1,0:T(8,128)S(1)} %dynamic-slice_bitcast_fusion), channel_id=1, source_target_pairs={{0,1},{1,0},{2,3},{3,2},{4,5},{5,4},{6,7},{7,6},{8,9},{9,8},{10,11... | collective-permute-start | bytes 1572872 | tf_op jit(solution)/shard_map/ppermute | solution.py:339
  133.3 1.5 collective-permute-done.3
  134.9 0.1 fusion.2
  134.9 9.8 %all_to_all.56.part_ref = bf16[8,128,128]{2,1,0:T(8,128)(2,1)S(1)} all-to-all(bf16[8,128,128]{2,1,0:T(8,128)(2,1)S(1)} %fusion.2), channel_id=1, replica_groups=mesh['yh'=2,'z'=4,'yl'=2,'x'=4,'core'=2] {'yl','x'}, dimensions={0} | all-to-all | bytes 524288 | tf_op jit(solution)/shard_map/all_to_all | solution.py:323
  144.8 0.0 copy-done.1
  144.8 0.0 copy-done.3
  144.8 0.2 image_numbers.1
  145.0 13.6 %all_to_all.57 = f32[128,1,128]{2,1,0:T(1,128)S(1)} all-to-all(f32[128,1,128]{2,1,0:T(1,128)S(1)} %bitcast.26), channel_id=1, replica_groups=mesh['yh'=2,'z'=4,'yl'=2,'x'=4,'core'=2] {'yh','z','yl','x','core'}, dimensions={0} | all-to-all | bytes 131072 | tf_op jit(solution)/shard_map/all_to_all | solution.py:323
  158.6 0.0 copy-done.4
  158.6 0.8 finish.1
  (4 shorter events, 0.1 us)
Async XLA Ops:
  2.2 12.2 %all-to-all-start = ((bf16[8,128,128]{2,1,0:T(8,128)(2,1)}), bf16[8,128,128]{2,1,0:T(8,128)(2,1)S(1)}, u32[]{:S(2)}, u32[]{:S(2)}) async-start(bf16[8,128,128]{2,1,0:T(8,128)(2,1)} %broadcast_in_dim.15), calls=%async_computation | async-start | bytes 524288 | tf_op jit(solution)/shard_map/all_to_all | solution.py:323
  8.1 1.2 copy-start.5
  9.3 0.7 copy-start.6
  12.8 0.7 copy-start.2
  14.4 3.1 %copy-start.7 = (bf16[8,128,128]{2,1,0:T(8,128)(2,1)}, bf16[8,128,128]{2,1,0:T(8,128)(2,1)S(1)}, u32[]{:S(2)}) copy-start(bf16[8,128,128]{2,1,0:T(8,128)(2,1)S(1)} %all-to-all-done.mine_ref) | copy-start | bytes 786436
  14.4 3.1 %collective-permute-start = (bf16[8,128,128]{2,1,0:T(8,128)(2,1)S(1)}, bf16[8,128,128]{2,1,0:T(8,128)(2,1)S(1)}, u32[]{:S(2)}, u32[]{:S(2)}) collective-permute-start(bf16[8,128,128]{2,1,0:T(8,128)(2,1)S(1)} %all-to-all-done.mine_ref), channel_id=1, source_target_pairs={{0,1},{1,0},{2,3},{3,2},{4,5},{5,4},{6,7},{7,6},{8,9},{9,8},{10,11... | collective-permute-start | bytes 786440 | tf_op jit(solution)/shard_map/ppermute | solution.py:356
  17.5 0.7 copy-start.10
  41.9 12.7 %all-to-all-start.2 = ((bf16[8,256,128]{2,1,0:T(8,128)(2,1)}), bf16[8,256,128]{2,1,0:T(8,128)(2,1)S(1)}, u32[]{:S(2)}, u32[]{:S(2)}) async-start(bf16[8,256,128]{2,1,0:T(8,128)(2,1)} %broadcast_in_dim.18), calls=%async_computation.2 | async-start | bytes 1048576 | tf_op jit(solution)/shard_map/all_to_all | solution.py:323
  54.6 0.8 copy-start.9
  66.8 5.0 %collective-permute-start.1 = (bf16[8,256,128]{2,1,0:T(8,128)(2,1)S(1)}, bf16[8,256,128]{2,1,0:T(8,128)(2,1)S(1)}, u32[]{:S(2)}, u32[]{:S(2)}) collective-permute-start(bf16[8,256,128]{2,1,0:T(8,128)(2,1)S(1)} %fusion.1), channel_id=1, source_target_pairs={{0,1},{1,0},{2,3},{3,2},{4,5},{5,4},{6,7},{7,6},{8,9},{9,8},{10,11... | collective-permute-start | bytes 1572872 | tf_op jit(solution)/shard_map/ppermute | solution.py:339
  96.8 3.7 %collective-permute-start.2 = (bf16[8,256,128]{2,1,0:T(8,128)(2,1)S(1)}, bf16[8,256,128]{2,1,0:T(8,128)(2,1)S(1)}, u32[]{:S(2)}, u32[]{:S(2)}) collective-permute-start(bf16[8,256,128]{2,1,0:T(8,128)(2,1)S(1)} %all_to_all.53.mine_ref), channel_id=1, source_target_pairs={{0,1},{1,0},{2,3},{3,2},{4,5},{5,4},{6,7},{7,6},{8,9},{9,8},{10,11... | collective-permute-start | bytes 1572872 | tf_op jit(solution)/shard_map/ppermute | solution.py:364
  100.5 0.8 copy-start.8
  101.3 27.1 %copy-start = (bf16[1024,2048]{1,0:T(8,128)(2,1)S(1)}, bf16[1024,2048]{1,0:T(8,128)(2,1)}, u32[]{:S(2)}) copy-start(bf16[1024,2048]{1,0:T(8,128)(2,1)} %pre_ref.3) | copy-start | bytes 12582916
  130.6 14.1 %copy-start.1 = (f32[128,128]{1,0:T(8,128)S(1)}, f32[128,128]{1,0:T(8,128)}, u32[]{:S(2)}) copy-start(f32[128,128]{1,0:T(8,128)} %dir_ref.3) | copy-start | bytes 196612
  130.6 14.1 %copy-start.3 = (f32[128,128]{1,0:T(8,128)S(1)}, f32[128,128]{1,0:T(8,128)}, u32[]{:S(2)}) copy-start(f32[128,128]{1,0:T(8,128)} %res_ref.3) | copy-start | bytes 196612
  130.7 28.0 %copy-start.4 = (f32[128,128]{1,0:T(8,128)S(1)}, f32[128,128]{1,0:T(8,128)}, u32[]{:S(2)}) copy-start(f32[128,128]{1,0:T(8,128)} %coef_ref.1) | copy-start | bytes 196612
  130.7 4.1 %collective-permute-start.3 = (f32[8,128,128]{2,1,0:T(8,128)S(1)}, f32[8,128,128]{2,1,0:T(8,128)S(1)}, u32[]{:S(2)}, u32[]{:S(2)}) collective-permute-start(f32[8,128,128]{2,1,0:T(8,128)S(1)} %dynamic-slice_bitcast_fusion), channel_id=1, source_target_pairs={{0,1},{1,0},{2,3},{3,2},{4,5},{5,4},{6,7},{7,6},{8,9},{9,8},{10,11... | collective-permute-start | bytes 1572872 | tf_op jit(solution)/shard_map/ppermute | solution.py:339

commit v4 on v3

--- a/solution.py
+++ b/solution.py
@@ -1,3 +1,4 @@
+import functools
 import math
 
 import jax
@@ -28,6 +29,10 @@
 
 def cost(flops, nbytes, exps=0):
     return pl.CostEstimate(flops=flops, bytes_accessed=nbytes, transcendentals=exps)
+
+
+def in_hbm(value):
+    return pltpu.with_memory_space_constraint(value, pltpu.HBM)
 
 
 def split_pieces(value, count):
@@ -94,23 +99,41 @@
     )(start, index, feat)
 
 
-def prepare_kernel(feat_ref, out_ref):
+def prepare_kernel(me_ref, feat_ref, out_ref):
     high, mid = split_pieces(feat_ref[...] * FEATURE_SCALE, 2)
     out_ref[...] = operand(high, mid, True).T
 
 
-def prepare_rows(feat, block=1024):
+def prepare_rows(me, feat, block=1024):
     depth, n = feat.shape
+    blocks = n // block
+    half = blocks // 2
     return pl.pallas_call(
         prepare_kernel,
-        grid=(n // block,),
-        in_specs=[pl.BlockSpec((depth, block), lambda i: (0, i))],
-        out_specs=pl.BlockSpec((block, 256), lambda i: (i, 0)),
-        out_shape=jax.ShapeDtypeStruct((n, 256), BF16),
-        compiler_params=params(60),
+        grid_spec=pltpu.PrefetchScalarGridSpec(
+            num_scalar_prefetch=1,
+            grid=(blocks,),
+            in_specs=[pl.BlockSpec((depth, block), lambda i, me: (0, (i + half * (1 - me[0])) % blocks))],
+            out_specs=pl.BlockSpec((block, 256), lambda i, me: (i, 0)),
+        ),
+        out_shape=pltpu.HBM((n, 256), BF16),
+        compiler_params=params(),
         cost_estimate=cost(n * 2**20 // 2, n * 1024),
         name="prepare_rows",
-    )(feat)
+    )(me, feat)
+
+
+def send_kernel(dir_ref, out_ref):
+    out_ref[...] = jnp.broadcast_to(dir_ref[...].astype(BF16)[None], out_ref.shape)
+
+
+def copies_of(direction, count):
+    return pl.pallas_call(
+        send_kernel,
+        out_shape=jax.ShapeDtypeStruct((count, *direction.shape), BF16),
+        compiler_params=params(),
+        name="direction_copies",
+    )(direction)
 
 
 VMEM = pl.BlockSpec(memory_space=pltpu.VMEM)
@@ -118,40 +141,57 @@
 HBM = pl.BlockSpec(memory_space=pltpu.HBM)
 
 
-def tile_kernel(rows_ref, got_ref, tile_ref, fit_ref, cen_ref, coef_ref):
-    @pl.when(pl.program_id(0) == 0)
-    def _():
-        parts, depth, width = got_ref.shape
-        share = depth - 2 * FEAT
-        for j in range(parts):
-            both = got_ref[j, share:]
-            cen_ref[:, j * width : (j + 1) * width] = operand(both[:FEAT], both[FEAT:], False)
-            coef_ref[j * share : (j + 1) * share] = got_ref[j, :share]
-
+def centre_kernel(got_ref, cen_ref, coef_ref):
+    parts, depth, width = got_ref.shape
+    share = depth - 2 * FEAT
+    for j in range(parts):
+        both = got_ref[j, share:]
+        cen_ref[:, j * width : (j + 1) * width] = operand(both[:FEAT], both[FEAT:], False)
+        coef_ref[j * share : (j + 1) * share] = got_ref[j, :share]
+
+
+def prepare_centres(got):
+    parts, depth, width = got.shape
+    return pl.pallas_call(
+        centre_kernel,
+        out_shape=[
+            jax.ShapeDtypeStruct((256, parts * width), BF16),
+            jax.ShapeDtypeStruct((parts * (depth - 2 * FEAT), OUTS), BF16),
+        ],
+        compiler_params=params(),
+        name="prepare_centres",
+    )(got)
+
+
+def tile_kernel(rows_ref, cen_ref, coef_ref, tile_ref, fit_ref):
     power = jnp.dot(rows_ref[...], cen_ref[...], preferred_element_type=F32)
     tile = jnp.exp2(power).astype(BF16)
     tile_ref[...] = tile
-    fit_ref[...] = jnp.dot(tile, coef_ref[...], preferred_element_type=F32)
-
-
-def tile_forward(rows_op, got, block=512):
-    n = rows_op.shape[0]
-    parts, depth, width = got.shape
-    m = parts * width
+    fit_ref[...] = jnp.dot(tile, coef_ref[...], preferred_element_type=F32).astype(fit_ref.dtype)
+
+
+def tile_forward(rows_op, half, cen_op, coef, fit_type, block=512):
+    n = rows_op.shape[0] // 2
+    m = cen_op.shape[1]
+    first = half * (n // block)
     return pl.pallas_call(
         tile_kernel,
         grid=(n // block,),
-        in_specs=[pl.BlockSpec((block, 256), lambda i: (i, 0)), pl.BlockSpec(got.shape, lambda i: (0, 0, 0))],
+        in_specs=[
+            pl.BlockSpec((block, 256), lambda i: (first + i, 0)),
+            pl.BlockSpec(cen_op.shape, lambda i: (0, 0)),
+            pl.BlockSpec(coef.shape, lambda i: (0, 0)),
+        ],
         out_specs=[pl.BlockSpec((block, m), lambda i: (i, 0)), pl.BlockSpec((block, OUTS), lambda i: (i, 0))],
-        out_shape=[jax.ShapeDtypeStruct((n, m), BF16), jax.ShapeDtypeStruct((n, OUTS), F32)],
-        scratch_shapes=[pltpu.VMEM((256, m), BF16), pltpu.VMEM((parts * (depth - 2 * FEAT), OUTS), BF16)],
-        compiler_params=params(56),
+        out_shape=[pltpu.HBM((n, m), BF16), jax.ShapeDtypeStruct((n, OUTS), fit_type)],
+        compiler_params=params(),
         cost_estimate=cost(2 * n * m * 384, 2 * n * m, n * m),
         name="tile_forward",
-    )(rows_op, got)
-
-
-def back_kernel(me_ref, tile_ref, mine_ref, came_ref, grad_ref, tile_here, fit_ref, total_ref, sems):
+    )(in_hbm(rows_op), cen_op, coef)
+
+
+def back_kernel(*refs, last):
+    tile_ref, fit_ref, *before, out_ref, tile_here, turned, total_ref, sems = refs
     blocks = sems.shape[0]
     block = tile_ref.shape[0] // blocks
     copies = [
@@ -160,48 +200,51 @@
     ]
     for copy in copies:
         copy.start()
-    me = me_ref[0]
-    parts, share, _ = mine_ref.shape
-    half = parts * share
+    parts, share, _ = fit_ref.shape
     for j in range(parts):
-        fit_ref[:, pl.ds(pl.multiple_of(me * half + j * share, share), share)] = mine_ref[j].T
-        fit_ref[:, pl.ds(pl.multiple_of((1 - me) * half + j * share, share), share)] = came_ref[j].T
+        turned[:, j * share : (j + 1) * share] = fit_ref[j].T
     for j in range(blocks):
         copies[j].wait()
         here = slice(j * block, (j + 1) * block)
-        part = jnp.dot(fit_ref[:, here], tile_here[here], preferred_element_type=F32)
-        if j == 0:
+        part = jnp.dot(turned[:, here], tile_here[here], preferred_element_type=F32)
+        if j or before:
+            part += total_ref[...] if j else before[0][...]
+        if j < blocks - 1:
             total_ref[...] = part
+        elif last:
+            out_ref[...] = part.T.astype(BF16)
         else:
-            total_ref[...] += part
-    grad_ref[...] = total_ref[...].T.astype(BF16)
-
-
-def backward(me, tile, mine, came, blocks=8):
+            out_ref[...] = part
+
+
+def backward(tile, fitted, before=None, blocks=4):
     n, m = tile.shape
-    return pl.pallas_call(
-        back_kernel,
-        in_specs=[SMEM, HBM, VMEM, VMEM],
+    last = before is not None
+    return pl.pallas_call(
+        functools.partial(back_kernel, last=last),
+        in_specs=[HBM, VMEM] + [VMEM] * last,
         out_specs=VMEM,
-        out_shape=jax.ShapeDtypeStruct((m, OUTS), BF16),
+        out_shape=jax.ShapeDtypeStruct((m, OUTS), BF16) if last else jax.ShapeDtypeStruct((OUTS, m), F32),
         scratch_shapes=[
             pltpu.VMEM((n, m), BF16),
             pltpu.VMEM((OUTS, n), BF16),
             pltpu.VMEM((OUTS, m), F32),
             pltpu.SemaphoreType.DMA((blocks,)),
         ],
-        compiler_params=params(53),
+        compiler_params=params(),
         cost_estimate=cost(2 * n * m * OUTS, 2 * n * m),
         name="tile_backward",
-    )(me, tile, mine, came)
+    )(in_hbm(tile), fitted, *([before] if last else []))
 
 
 def field_kernel(me_ref, pre_ref, mine_ref, came_ref, feat_ref, out_ref, pre_here, dir_here, sems):
     parts = out_ref.shape[0]
     width = out_ref.shape[1] - 2 * FEAT
+    blocks = sems.shape[0]
+    block = pre_ref.shape[0] // blocks
     copies = [
-        pltpu.make_async_copy(pre_ref.at[pl.ds(j * width, width)], pre_here.at[pl.ds(j * width, width)], sems.at[j])
-        for j in range(parts)
+        pltpu.make_async_copy(pre_ref.at[pl.ds(j * block, block)], pre_here.at[pl.ds(j * block, block)], sems.at[j])
+        for j in range(blocks)
     ]
     for copy in copies:
         copy.start()
@@ -212,13 +255,14 @@
         dir_here[pl.ds(pl.multiple_of((2 * j + 1 - me) * share, share), share)] = came_ref[j]
     for j in range(parts):
         out_ref[j, width:] = feat_ref[j]
-    for j in range(parts):
+    for j in range(blocks):
         copies[j].wait()
-        part = jnp.dot(pre_here[j * width : (j + 1) * width], dir_here[...], preferred_element_type=F32)
-        out_ref[j, :width] = part.astype(BF16)
-
-
-def field(me, precond, mine, came, feat_parts):
+        part = jnp.dot(pre_here[j * block : (j + 1) * block], dir_here[...], preferred_element_type=F32).astype(BF16)
+        for k in range(block // width):
+            out_ref[j * (block // width) + k, :width] = part[k * width : (k + 1) * width]
+
+
+def field(me, precond, mine, came, feat_parts, blocks=4):
     n, m = precond.shape
     parts = feat_parts.shape[0]
     return pl.pallas_call(
@@ -226,34 +270,48 @@
         in_specs=[SMEM, HBM, VMEM, VMEM, VMEM],
         out_specs=VMEM,
         out_shape=jax.ShapeDtypeStruct((parts, n // parts + 2 * FEAT, OUTS), BF16),
-        scratch_shapes=[pltpu.VMEM((n, m), BF16), pltpu.VMEM((m, OUTS), BF16), pltpu.SemaphoreType.DMA((parts,))],
-        compiler_params=params(57),
+        scratch_shapes=[pltpu.VMEM((n, m), BF16), pltpu.VMEM((m, OUTS), BF16), pltpu.SemaphoreType.DMA((blocks,))],
+        compiler_params=params(),
         cost_estimate=cost(2 * n * m * OUTS, 2 * n * m),
         name="precond_forward",
-    )(me, precond, mine, came, feat_parts)
-
-
-def image_kernel(pre_ref, grad_ref, out_ref):
-    part = jnp.dot(grad_ref[...].T, pre_ref[...], preferred_element_type=F32).T
-    chips, width = out_ref.shape[1:3]
-    for chip in range(chips):
-        for core in range(2):
-            first = (chip * 2 + core) * width
-            out_ref[core, chip] = part[first : first + width]
-
-
-def image_part(precond, grad, share, block=512):
+    )(me, in_hbm(precond), mine, came, feat_parts)
+
+
+def image_kernel(core_ref, pre_ref, grad_ref, out_ref, pre_here, sems):
+    core = core_ref[0]
+    chips, width, _ = out_ref.shape
+    copies = [
+        pltpu.make_async_copy(
+            pre_ref.at[:, pl.ds(pl.multiple_of((2 * j + core) * width, width), width)],
+            pre_here.at[j // 2, :, pl.ds(j % 2 * width, width)],
+            sems.at[j],
+        )
+        for j in range(chips)
+    ]
+    for copy in copies:
+        copy.start()
+    grad = grad_ref[...].T
+    for j in range(0, chips, 2):
+        copies[j].wait()
+        copies[j + 1].wait()
+        part = jnp.dot(grad, pre_here[j // 2], preferred_element_type=F32).T
+        out_ref[j] = part[:width]
+        out_ref[j + 1] = part[width:]
+
+
+def image_part(core, precond, grad, share):
     n, m = precond.shape
+    chips = m // share // 2
     return pl.pallas_call(
         image_kernel,
-        grid=(m // block,),
-        in_specs=[pl.BlockSpec((n, block), lambda i: (0, i)), pl.BlockSpec((n, OUTS), lambda i: (0, 0))],
-        out_specs=pl.BlockSpec((2, block // share // 2, share, OUTS), lambda i: (0, i, 0, 0)),
-        out_shape=jax.ShapeDtypeStruct((2, m // share // 2, share, OUTS), F32),
-        compiler_params=params(),
-        cost_estimate=cost(2 * n * m * OUTS, 2 * n * m),
+        in_specs=[SMEM, HBM, VMEM],
+        out_specs=VMEM,
+        out_shape=jax.ShapeDtypeStruct((chips, share, OUTS), F32),
+        scratch_shapes=[pltpu.VMEM((chips // 2, n, 2 * share), BF16), pltpu.SemaphoreType.DMA((chips,))],
+        compiler_params=params(),
+        cost_estimate=cost(n * m * OUTS, n * m),
         name="precond_backward",
-    )(precond, grad)
+    )(core, in_hbm(precond), grad)
 
 
 def numbers_kernel(part_ref, dir_ref, res_ref, image_ref, out_ref):
@@ -332,12 +390,8 @@
     return jnp.sum(parts.astype(F32), axis=0)
 
 
-def core_halves(part, send):
-    me = lax.axis_index("core")
-    mine = lax.dynamic_index_in_dim(part, me, 0, keepdims=False)
-    other = lax.dynamic_index_in_dim(part, 1 - me, 0, keepdims=False)
-    came = lax.ppermute(other.astype(send), "core", SWAP)
-    return (mine + came.astype(F32)).astype(BF16)
+def swapped(part):
+    return lax.ppermute(part, "core", SWAP)
 
 
 def on_device(train_rows, centre_index, precond, coefficients, residual, direction):
@@ -349,25 +403,36 @@
     start_row = (lax.axis_index(ROWS) * rows_here).astype(jnp.int32)
     share = cen_here // row_devices
 
-    dir_mine = gathered(direction.astype(BF16), CHIPS)
+    other = 1 - me
+    dir_mine = spread(copies_of(direction, cen_devices // 2), CHIPS)
+
     feat = train_rows.T
     picked = pick(start_row[None], centre_index[None], feat, row_devices)
     dir_mine, picked = lax.optimization_barrier((dir_mine, picked))
-    dir_came = lax.ppermute(dir_mine, "core", SWAP)
-    rows_op = prepare_rows(feat)
-    parts = spread(field(me, precond, dir_mine, dir_came, picked), ROWS)
+    rows_op = prepare_rows(me, feat)
+    parts = spread(field(me, precond, dir_mine, swapped(dir_mine), picked), ROWS)
     got = gathered(summed(parts).astype(BF16), ROWS)
-    tile, fit_part = tile_forward(rows_op, got)
-
-    half = core_halves(fit_part.reshape(2, cen_devices // 2, rows_here // cen_devices, OUTS), BF16)
-    fit_mine = gathered(summed(spread(half, CHIPS)).astype(BF16), CHIPS)
-    fit_came = lax.ppermute(fit_mine, "core", SWAP)
-
-    grad_part = backward(me, tile, fit_mine, fit_came).reshape(row_devices, share, OUTS)
-    grad_mine = summed(spread(grad_part, ROWS)) * float(rows_here * row_devices) ** (-0.5)
-    grad_low = gathered(grad_mine.astype(BF16), ROWS).reshape(cen_here, OUTS)
-
-    half = core_halves(image_part(precond, grad_low, direction.shape[0]), F32)
+    cen_op, coef = prepare_centres(got)
+
+    chips_shape = (cen_devices // 2, rows_here // cen_devices, OUTS)
+    tile_other, fit_other = tile_forward(rows_op, 0, cen_op, coef, BF16)
+    fit_came = swapped(fit_other)
+    tile_mine, fit_mine = tile_forward(rows_op, 1, cen_op, coef, F32)
+    fit_mine, fit_came = lax.optimization_barrier((fit_mine, fit_came))
+    half = (fit_mine + fit_came.astype(F32)).astype(BF16).reshape(chips_shape)
+    fitted = gathered(summed(spread(half, CHIPS)).astype(BF16), CHIPS)
+    fitted_came = swapped(fitted)
+    grad_mine = backward(tile_mine, fitted)
+    grad_mine, fitted_came = lax.optimization_barrier((grad_mine, fitted_came))
+    grad_part = backward(tile_other, fitted_came, grad_mine).reshape(row_devices, share, OUTS)
+
+    grad_sum = summed(spread(grad_part, ROWS)) * float(rows_here * row_devices) ** (-0.5)
+    grad_low = gathered(grad_sum.astype(BF16), ROWS).reshape(cen_here, OUTS)
+
+    image_came = swapped(image_part(other, precond, grad_low, direction.shape[0]))
+    image_mine = image_part(me, precond, grad_low, direction.shape[0])
+    image_mine, image_came = lax.optimization_barrier((image_mine, image_came))
+    half = (image_mine + image_came).astype(BF16)
     image, row = numbers(spread(half, CHIPS), direction, residual, row_devices * cen_devices)
     every = spread(row, (*ROWS, *CENT))
     return tuple(finish(every, image, coefficients, residual, direction))

time: 161 us -> 154 us (0.957)
  blocking collectives: 86.1 us -> 75.5 us
  waiting for transfers between devices: 11.5 us -> 16.7 us
  local copies, waits for them, and re-layouts: 8.04 us -> 4.45 us
  starting transfers between devices: 19.9 us -> 23.4 us
  other arithmetic: 2.45 us -> 0.36 us
    all_to_all x7 -> x6, blocking collectives: 86.1 us -> 75.5 us  [spread(): return lax.all_to_all(part, axes, 0, 0, tiled=True)]
    all_to_all x2 -> x3, waiting for transfers between devices: 5.68 us -> 15.5 us  [spread(): return lax.all_to_all(part, axes, 0, 0, tiled=True)]
    ppermute x4, waiting for transfers between devices: 5.77 us -> 1.17 us  [swapped(): return lax.ppermute(part, 'core', SWAP)]
    all_to_all x2 -> x3, starting transfers between devices: 9.74 us -> 13.8 us  [spread(): return lax.all_to_all(part, axes, 0, 0, tiled=True)]
    pallas_call x1, Pallas kernels: 5.35 us -> 3.06 us  [field(): pl.pallas_call(field_kernel, in_specs=[SMEM, HBM, VMEM, VMEM, VMEM], out_...]
    unnamed x22 -> x14, local copies, waits for them, and re-layouts: 4.97 us -> 2.77 us
    convert_element_type x4 -> x3, other arithmetic: 2.26 us -> 0.17 us  [the longest x1 0.1 us: on_device(): half = (fit_mine + fit_came.astype(F32)).astype(BF16).reshape(chips_shape)]
    pallas_call x3 -> x7, Pallas kernels: 11.4 us -> 13.4 us  [the longest x2 5.11 us: backward(): pl.pallas_call(functools.partial(back_kernel, last=last), in_specs=[HBM,...]
  transfers between devices with their start and end apart: 6 -> 7, of which waited for: 6 -> 4; matrix products, arithmetic and copies ran while one was open for 0% -> 0% of each run, Pallas kernels for 4% -> 10%
where the time goes in v4:
time: 154 us; the launch traced here: 153 us
  blocking collectives  75.5 us (49%)
  Pallas kernels  31.5 us (20%)
  starting transfers between devices  23.4 us (15%)
  waiting for transfers between devices  16.7 us (11%)
  local copies, waits for them, and re-layouts  4.45 us (3%)
    all_to_all x6, blocking collectives, spread(): return lax.all_to_all(part, axes, 0, 0, tiled=True)  75.5 us
    all_to_all x3, waiting for transfers between devices, spread(): return lax.all_to_all(part, axes, 0, 0, tiled=True)  15.5 us
    all_to_all x3, starting transfers between devices, spread(): return lax.all_to_all(part, axes, 0, 0, tiled=True)  13.8 us
    pallas_call x2, Pallas kernels, tile_forward(): pl.pallas_call(tile_kernel, grid=(n // block,), in_specs=[pl.BlockSpec((b...  11 us
    ppermute x4, starting transfers between devices, swapped(): return lax.ppermute(part, 'core', SWAP)  9.53 us
    pallas_call x2, Pallas kernels, backward(): pl.pallas_call(functools.partial(back_kernel, last=last), in_specs=[HBM,...  5.11 us
    pallas_call x2, Pallas kernels, image_part(): pl.pallas_call(image_kernel, in_specs=[SMEM, HBM, VMEM], out_specs=VMEM,...  5.06 us
  transfers between devices with their start and end apart: 7, of which 4 were waited for; matrix products, arithmetic and copies ran while one was open for 0% of the time, Pallas kernels for 10%

profile of v4, /device:TPU:1, one launch (start us, length us, event | category | flops | bytes accessed | tf_op | source)
XLA Modules:
  0.0 152.6 jit_solution(9958548011519733768)
XLA Ops:
  0.6 0.0 copy-start
  0.6 0.8 copy-done
  1.5 0.7 direction_copies.1
  2.2 5.9 %all-to-all-start = ((bf16[8,128,128]{2,1,0:T(8,128)(2,1)}), bf16[8,128,128]{2,1,0:T(8,128)(2,1)S(1)}, u32[]{:S(2)}, u32[]{:S(2)}) async-start(bf16[8,128,128]{2,1,0:T(8,128)(2,1)} %direction_copies.1), calls=%async_computation | async-start | bytes 524288 | tf_op jit(solution)/shard_map/all_to_all | solution.py:381
  8.1 0.0 copy-start.4
  8.1 1.2 copy-done.4
  9.3 0.0 copy-start.6
  9.3 0.7 copy-done.6
  10.0 2.8 %pick_centres.1.feat_ref = bf16[8,128,128]{2,1,0:T(8,128)(2,1)S(1)} custom-call(s32[1]{0:T(128)} %bitcast.2.start_ref, s32[1,1024]{1,0:T(1,128)S(1)} %bitcast.18, f32[64,4096]{1,0:T(8,128)S(1)} %bitcast.16), custom_call_target="tpu_custom_call" | custom-call | flops 4294967296 | bytes 1048576 | tf_op jit(solution)/shard_map/pick_centres/pallas_call | solution.py:85
  12.8 1.5 %all-to-all-done.mine_ref = bf16[8,128,128]{2,1,0:T(8,128)(2,1)S(1)} async-done(((bf16[8,128,128]{2,1,0:T(8,128)(2,1)}), bf16[8,128,128]{2,1,0:T(8,128)(2,1)S(1)}, u32[]{:S(2)}, u32[]{:S(2)}) %all-to-all-start) | async-done | bytes 262176 | tf_op jit(solution)/shard_map/all_to_all | solution.py:381
  14.4 1.9 %collective-permute-start = (bf16[8,128,128]{2,1,0:T(8,128)(2,1)S(1)}, bf16[8,128,128]{2,1,0:T(8,128)(2,1)S(1)}, u32[]{:S(2)}, u32[]{:S(2)}) collective-permute-start(bf16[8,128,128]{2,1,0:T(8,128)(2,1)S(1)} %all-to-all-done.mine_ref), channel_id=1, source_target_pairs={{0,1},{1,0},{2,3},{3,2},{4,5},{5,4},{6,7},{7,6},{8,9},{9,8},{10,11... | collective-permute-start | bytes 786440 | tf_op jit(solution)/shard_map/ppermute | solution.py:394
  16.3 1.2 collective-permute-done.came_ref
  17.5 0.0 copy-start.5
  17.5 3.1 %precond_forward.1 = bf16[8,256,128]{2,1,0:T(8,128)(2,1)S(1)} custom-call(s32[1]{0:T(128)} %bitcast.me_ref.core_ref, bf16[1024,2048]{1,0:T(8,128)(2,1)} %pre_ref.5, bf16[8,128,128]{2,1,0:T(8,128)(2,1)S(1)} %all-to-all-done.mine_ref, bf16[8,128,128]{2,1,0:T(8,128)(2,1)S(1)} %collective-permute-done.came_ref, bf16[8,128,128]{2,1,0:T(8,128)(2,1)S(1)} %pick_centres.1.feat_ref), custom_call_target="tpu_custom_call" | custom-call | flops 536870912 | bytes 4194304 | tf_op jit(solution)/shard_map/precond_forward/pallas_call | solution.py:268
  20.5 17.2 %all_to_all.51 = bf16[8,256,128]{2,1,0:T(8,128)(2,1)S(1)} all-to-all(bf16[8,256,128]{2,1,0:T(8,128)(2,1)S(1)} %precond_forward.1), channel_id=1, replica_groups=mesh['yh'=2,'z'=4,'yl'=2,'x'=4,'core'=2] {'yh','z'}, dimensions={0} | all-to-all | bytes 1048576 | tf_op jit(solution)/shard_map/all_to_all | solution.py:381
  37.7 0.1 reduce_sum.33
  37.8 0.9 broadcast_in_dim.30
  38.7 3.9 %all-to-all-start.2 = ((bf16[8,256,128]{2,1,0:T(8,128)(2,1)}), bf16[8,256,128]{2,1,0:T(8,128)(2,1)S(1)}, u32[]{:S(2)}, u32[]{:S(2)}) async-start(bf16[8,256,128]{2,1,0:T(8,128)(2,1)} %broadcast_in_dim.30), calls=%async_computation.2 | async-start | bytes 1048576 | tf_op jit(solution)/shard_map/all_to_all | solution.py:381
  42.6 0.0 copy-done.5
  42.6 2.4 %prepare_rows.1.rows_ref = bf16[4096,256]{1,0:T(8,128)(2,1)} custom-call(s32[1]{0:T(128)} %bitcast.me_ref.core_ref, f32[64,4096]{1,0:T(8,128)S(1)} %bitcast.17), custom_call_target="tpu_custom_call" | custom-call | flops 2147483648 | bytes 4194304 | tf_op jit(solution)/shard_map/prepare_rows/pallas_call | solution.py:111
  45.0 6.4 %all-to-all-done.2.got_ref = bf16[8,256,128]{2,1,0:T(8,128)(2,1)S(1)} async-done(((bf16[8,256,128]{2,1,0:T(8,128)(2,1)}), bf16[8,256,128]{2,1,0:T(8,128)(2,1)S(1)}, u32[]{:S(2)}, u32[]{:S(2)}) %all-to-all-start.2) | async-done | bytes 524320 | tf_op jit(solution)/shard_map/all_to_all | solution.py:381
  51.4 0.1 prepare_centres.1
  51.5 5.5 %tile_forward.2 = (bf16[2048,1024]{1,0:T(8,128)(2,1)}, bf16[2048,128]{1,0:T(8,128)(2,1)S(1)}) custom-call(bf16[4096,256]{1,0:T(8,128)(2,1)} %prepare_rows.1.rows_ref, bf16[256,1024]{1,0:T(8,128)(2,1)S(1)} %get-tuple-element.21.cen_ref, bf16[1024,128]{1,0:T(8,128)(2,1)S(1)} %get-tuple-element.22.coef_ref), custom_call_target="tpu_custom_call" | custom-call | flops 1610612736 | bytes 4194304 | tf_op jit(solution)/shard_map/tile_forward/pallas_call | solution.py:177
  57.0 3.3 %collective-permute-start.1 = (bf16[2048,128]{1,0:T(8,128)(2,1)S(1)}, bf16[2048,128]{1,0:T(8,128)(2,1)S(1)}, u32[]{:S(2)}, u32[]{:S(2)}) collective-permute-start(bf16[2048,128]{1,0:T(8,128)(2,1)S(1)} %get-tuple-element.26), channel_id=1, source_target_pairs={{0,1},{1,0},{2,3},{3,2},{4,5},{5,4},{6,7},{7,6},{8,9},{9,8},{10,11... | collective-permute-start | bytes 1572872 | tf_op jit(solution)/shard_map/ppermute | solution.py:394
  60.3 5.5 %tile_forward.3 = (bf16[2048,1024]{1,0:T(8,128)(2,1)}, f32[2048,128]{1,0:T(8,128)S(1)}) custom-call(bf16[4096,256]{1,0:T(8,128)(2,1)} %prepare_rows.1.rows_ref, bf16[256,1024]{1,0:T(8,128)(2,1)S(1)} %get-tuple-element.21.cen_ref, bf16[1024,128]{1,0:T(8,128)(2,1)S(1)} %get-tuple-element.22.coef_ref), custom_call_target="tpu_custom_call" | custom-call | flops 1610612736 | bytes 4194304 | tf_op jit(solution)/shard_map/tile_forward/pallas_call | solution.py:177
  65.9 0.0 collective-permute-done.1
  65.9 0.1 add_convert_fusion
  66.0 12.8 %all_to_all.52 = bf16[8,256,128]{2,1,0:T(8,128)(2,1)S(1)} all-to-all(bf16[8,256,128]{2,1,0:T(8,128)(2,1)S(1)} %bitcast.19), channel_id=1, replica_groups=mesh['yh'=2,'z'=4,'yl'=2,'x'=4,'core'=2] {'yl','x'}, dimensions={0} | all-to-all | bytes 1048576 | tf_op jit(solution)/shard_map/all_to_all | solution.py:381
  78.7 0.1 reduce_sum.34
  78.8 0.1 broadcast_in_dim.31
  78.9 11.6 %all_to_all.53.refs_1_ = bf16[8,256,128]{2,1,0:T(8,128)(2,1)S(1)} all-to-all(bf16[8,256,128]{2,1,0:T(8,128)(2,1)S(1)} %broadcast_in_dim.31), channel_id=1, replica_groups=mesh['yh'=2,'z'=4,'yl'=2,'x'=4,'core'=2] {'yl','x'}, dimensions={0} | all-to-all | bytes 1048576 | tf_op jit(solution)/shard_map/all_to_all | solution.py:381
  90.5 1.9 %collective-permute-start.2 = (bf16[8,256,128]{2,1,0:T(8,128)(2,1)S(1)}, bf16[8,256,128]{2,1,0:T(8,128)(2,1)S(1)}, u32[]{:S(2)}, u32[]{:S(2)}) collective-permute-start(bf16[8,256,128]{2,1,0:T(8,128)(2,1)S(1)} %all_to_all.53.refs_1_), channel_id=1, source_target_pairs={{0,1},{1,0},{2,3},{3,2},{4,5},{5,4},{6,7},{7,6},{8,9},{9,8},{10,11... | collective-permute-start | bytes 1572872 | tf_op jit(solution)/shard_map/ppermute | solution.py:394
  92.3 2.5 %tile_backward.2.refs_2_ = f32[128,1024]{1,0:T(8,128)S(1)} custom-call(bf16[2048,1024]{1,0:T(8,128)(2,1)} %get-tuple-element.24.refs_0_, bf16[8,256,128]{2,1,0:T(8,128)(2,1)S(1)} %all_to_all.53.refs_1_), custom_call_target="tpu_custom_call" | custom-call | flops 536870912 | bytes 4194304 | tf_op jit(solution)/shard_map/tile_backward/pallas_call | solution.py:223
  94.9 0.0 collective-permute-done.2.refs_1_
  94.9 2.6 %tile_backward.3 = bf16[1024,128]{1,0:T(8,128)(2,1)S(1)} custom-call(bf16[2048,1024]{1,0:T(8,128)(2,1)} %get-tuple-element.23.refs_0_, bf16[8,256,128]{2,1,0:T(8,128)(2,1)S(1)} %collective-permute-done.2.refs_1_, f32[128,1024]{1,0:T(8,128)S(1)} %tile_backward.2.refs_2_), custom_call_target="tpu_custom_call" | custom-call | flops 536870912 | bytes 4194304 | tf_op jit(solution)/shard_map/tile_backward/pallas_call | solution.py:223
  97.5 10.6 %all_to_all.54 = bf16[8,128,128]{2,1,0:T(8,128)(2,1)S(1)} all-to-all(bf16[8,128,128]{2,1,0:T(8,128)(2,1)S(1)} %bitcast.13), channel_id=1, replica_groups=mesh['yh'=2,'z'=4,'yl'=2,'x'=4,'core'=2] {'yh','z'}, dimensions={0} | all-to-all | bytes 524288 | tf_op jit(solution)/shard_map/all_to_all | solution.py:381
  108.1 0.7 broadcast_in_dim.32
  108.8 4.1 %all-to-all-start.6 = ((bf16[8,128,128]{2,1,0:T(8,128)(2,1)}), bf16[8,128,128]{2,1,0:T(8,128)(2,1)S(1)}, u32[]{:S(2)}, u32[]{:S(2)}) async-start(bf16[8,128,128]{2,1,0:T(8,128)(2,1)} %broadcast_in_dim.32), calls=%async_computation.6 | async-start | bytes 524288 | tf_op jit(solution)/shard_map/all_to_all | solution.py:381
  112.9 7.6 %all-to-all-done.6 = bf16[8,128,128]{2,1,0:T(8,128)(2,1)S(1)} async-done(((bf16[8,128,128]{2,1,0:T(8,128)(2,1)}), bf16[8,128,128]{2,1,0:T(8,128)(2,1)S(1)}, u32[]{:S(2)}, u32[]{:S(2)}) %all-to-all-start.6) | async-done | bytes 262176 | tf_op jit(solution)/shard_map/all_to_all | solution.py:381
  120.5 2.5 %precond_backward.3 = f32[8,128,128]{2,1,0:T(8,128)S(1)} custom-call(s32[1]{0:T(128)S(6)} %sub.3.core_ref, bf16[1024,2048]{1,0:T(8,128)(2,1)} %pre_ref.5, bf16[1024,128]{1,0:T(8,128)(2,1)S(1)} %bitcast.11), custom_call_target="tpu_custom_call" | custom-call | flops 268435456 | bytes 2097152 | tf_op jit(solution)/shard_map/precond_backward/pallas_call | solution.py:305
  123.0 0.0 copy-start.1
  123.0 0.0 copy-start.2
  123.1 0.0 copy-start.3
  123.1 2.4 %collective-permute-start.3 = (f32[8,128,128]{2,1,0:T(8,128)S(1)}, f32[8,128,128]{2,1,0:T(8,128)S(1)}, u32[]{:S(2)}, u32[]{:S(2)}) collective-permute-start(f32[8,128,128]{2,1,0:T(8,128)S(1)} %precond_backward.3), channel_id=1, source_target_pairs={{0,1},{1,0},{2,3},{3,2},{4,5},{5,4},{6,7},{7,6},{8,9},{9,8},{10,11... | collective-permute-start | bytes 1572872 | tf_op jit(solution)/shard_map/ppermute | solution.py:394
  125.5 2.5 %precond_backward.2 = f32[8,128,128]{2,1,0:T(8,128)S(1)} custom-call(s32[1]{0:T(128)} %bitcast.me_ref.core_ref, bf16[1024,2048]{1,0:T(8,128)(2,1)} %pre_ref.5, bf16[1024,128]{1,0:T(8,128)(2,1)S(1)} %bitcast.12), custom_call_target="tpu_custom_call" | custom-call | flops 268435456 | bytes 2097152 | tf_op jit(solution)/shard_map/precond_backward/pallas_call | solution.py:305
  128.0 0.0 collective-permute-done.3
  128.0 0.1 add_convert_fusion.1
  128.1 9.9 %all_to_all.55.part_ref = bf16[8,128,128]{2,1,0:T(8,128)(2,1)S(1)} all-to-all(bf16[8,128,128]{2,1,0:T(8,128)(2,1)S(1)} %add_convert_fusion.1), channel_id=1, replica_groups=mesh['yh'=2,'z'=4,'yl'=2,'x'=4,'core'=2] {'yl','x'}, dimensions={0} | all-to-all | bytes 524288 | tf_op jit(solution)/shard_map/all_to_all | solution.py:381
  138.0 0.0 copy-done.1
  138.0 0.0 copy-done.2
  138.0 0.2 image_numbers.1
  138.3 13.5 %all_to_all.56 = f32[128,1,128]{2,1,0:T(1,128)S(1)} all-to-all(f32[128,1,128]{2,1,0:T(1,128)S(1)} %bitcast.15), channel_id=1, replica_groups=mesh['yh'=2,'z'=4,'yl'=2,'x'=4,'core'=2] {'yh','z','yl','x','core'}, dimensions={0} | all-to-all | bytes 131072 | tf_op jit(solution)/shard_map/all_to_all | solution.py:381
  151.7 0.0 copy-done.3
  151.7 0.8 finish.1
  (2 shorter events, 0.0 us)
Async XLA Ops:
  0.6 0.8 copy-start
  2.2 12.2 %all-to-all-start = ((bf16[8,128,128]{2,1,0:T(8,128)(2,1)}), bf16[8,128,128]{2,1,0:T(8,128)(2,1)S(1)}, u32[]{:S(2)}, u32[]{:S(2)}) async-start(bf16[8,128,128]{2,1,0:T(8,128)(2,1)} %direction_copies.1), calls=%async_computation | async-start | bytes 524288 | tf_op jit(solution)/shard_map/all_to_all | solution.py:381
  8.1 1.2 copy-start.4
  9.3 0.7 copy-start.6
  14.4 3.1 %collective-permute-start = (bf16[8,128,128]{2,1,0:T(8,128)(2,1)S(1)}, bf16[8,128,128]{2,1,0:T(8,128)(2,1)S(1)}, u32[]{:S(2)}, u32[]{:S(2)}) collective-permute-start(bf16[8,128,128]{2,1,0:T(8,128)(2,1)S(1)} %all-to-all-done.mine_ref), channel_id=1, source_target_pairs={{0,1},{1,0},{2,3},{3,2},{4,5},{5,4},{6,7},{7,6},{8,9},{9,8},{10,11... | collective-permute-start | bytes 786440 | tf_op jit(solution)/shard_map/ppermute | solution.py:394
  17.5 25.1 %copy-start.5 = (f32[4096,64]{0,1:T(8,128)S(1)}, f32[4096,64]{0,1:T(8,128)}, u32[]{:S(2)}) copy-start(f32[4096,64]{0,1:T(8,128)} %param.6) | copy-start | bytes 3145732
  38.7 12.7 %all-to-all-start.2 = ((bf16[8,256,128]{2,1,0:T(8,128)(2,1)}), bf16[8,256,128]{2,1,0:T(8,128)(2,1)S(1)}, u32[]{:S(2)}, u32[]{:S(2)}) async-start(bf16[8,256,128]{2,1,0:T(8,128)(2,1)} %broadcast_in_dim.30), calls=%async_computation.2 | async-start | bytes 1048576 | tf_op jit(solution)/shard_map/all_to_all | solution.py:381
  57.0 8.9 %collective-permute-start.1 = (bf16[2048,128]{1,0:T(8,128)(2,1)S(1)}, bf16[2048,128]{1,0:T(8,128)(2,1)S(1)}, u32[]{:S(2)}, u32[]{:S(2)}) collective-permute-start(bf16[2048,128]{1,0:T(8,128)(2,1)S(1)} %get-tuple-element.26), channel_id=1, source_target_pairs={{0,1},{1,0},{2,3},{3,2},{4,5},{5,4},{6,7},{7,6},{8,9},{9,8},{10,11... | collective-permute-start | bytes 1572872 | tf_op jit(solution)/shard_map/ppermute | solution.py:394
  90.5 4.4 %collective-permute-start.2 = (bf16[8,256,128]{2,1,0:T(8,128)(2,1)S(1)}, bf16[8,256,128]{2,1,0:T(8,128)(2,1)S(1)}, u32[]{:S(2)}, u32[]{:S(2)}) collective-permute-start(bf16[8,256,128]{2,1,0:T(8,128)(2,1)S(1)} %all_to_all.53.refs_1_), channel_id=1, source_target_pairs={{0,1},{1,0},{2,3},{3,2},{4,5},{5,4},{6,7},{7,6},{8,9},{9,8},{10,11... | collective-permute-start | bytes 1572872 | tf_op jit(solution)/shard_map/ppermute | solution.py:394
  108.8 11.7 %all-to-all-start.6 = ((bf16[8,128,128]{2,1,0:T(8,128)(2,1)}), bf16[8,128,128]{2,1,0:T(8,128)(2,1)S(1)}, u32[]{:S(2)}, u32[]{:S(2)}) async-start(bf16[8,128,128]{2,1,0:T(8,128)(2,1)} %broadcast_in_dim.32), calls=%async_computation.6 | async-start | bytes 524288 | tf_op jit(solution)/shard_map/all_to_all | solution.py:381
  123.0 15.0 %copy-start.1 = (f32[128,128]{1,0:T(8,128)S(1)}, f32[128,128]{1,0:T(8,128)}, u32[]{:S(2)}) copy-start(f32[128,128]{1,0:T(8,128)} %dir_ref.5) | copy-start | bytes 196612
  123.0 15.0 %copy-start.2 = (f32[128,128]{1,0:T(8,128)S(1)}, f32[128,128]{1,0:T(8,128)}, u32[]{:S(2)}) copy-start(f32[128,128]{1,0:T(8,128)} %res_ref.3) | copy-start | bytes 196612
  123.1 28.7 %copy-start.3 = (f32[128,128]{1,0:T(8,128)S(1)}, f32[128,128]{1,0:T(8,128)}, u32[]{:S(2)}) copy-start(f32[128,128]{1,0:T(8,128)} %coef_ref.1) | copy-start | bytes 196612
  123.1 4.9 %collective-permute-start.3 = (f32[8,128,128]{2,1,0:T(8,128)S(1)}, f32[8,128,128]{2,1,0:T(8,128)S(1)}, u32[]{:S(2)}, u32[]{:S(2)}) collective-permute-start(f32[8,128,128]{2,1,0:T(8,128)S(1)} %precond_backward.3), channel_id=1, source_target_pairs={{0,1},{1,0},{2,3},{3,2},{4,5},{5,4},{6,7},{7,6},{8,9},{9,8},{10,11... | collective-permute-start | bytes 1572872 | tf_op jit(solution)/shard_map/ppermute | solution.py:394

commit v5 on v4

--- a/solution.py
+++ b/solution.py
@@ -141,53 +141,72 @@
 HBM = pl.BlockSpec(memory_space=pltpu.HBM)
 
 
-def centre_kernel(got_ref, cen_ref, coef_ref):
-    parts, depth, width = got_ref.shape
-    share = depth - 2 * FEAT
-    for j in range(parts):
-        both = got_ref[j, share:]
-        cen_ref[:, j * width : (j + 1) * width] = operand(both[:FEAT], both[FEAT:], False)
-        coef_ref[j * share : (j + 1) * share] = got_ref[j, :share]
-
-
-def prepare_centres(got):
-    parts, depth, width = got.shape
-    return pl.pallas_call(
-        centre_kernel,
-        out_shape=[
-            jax.ShapeDtypeStruct((256, parts * width), BF16),
+def tile_kernel(*refs, first):
+    if first:
+        rows_ref, got_ref, tile_ref, fit_ref, cen_ref, coef_ref, rows_here, tile_here, rows_sems, sems = refs
+    else:
+        rows_ref, cen_ref, coef_ref, tile_ref, fit_ref, rows_here, tile_here, rows_sems, sems = refs
+    blocks = sems.shape[0]
+    block = fit_ref.shape[0] // blocks
+    offset = 0 if first else fit_ref.shape[0]
+    loads = [
+        pltpu.make_async_copy(
+            rows_ref.at[pl.ds(offset + j * block, block)], rows_here.at[pl.ds(j * block, block)], rows_sems.at[j]
+        )
+        for j in range(blocks)
+    ]
+    for load in loads:
+        load.start()
+    if first:
+        parts, depth, width = got_ref.shape
+        share = depth - 2 * FEAT
+        for j in range(parts):
+            both = got_ref[j, share:]
+            cen_ref[:, j * width : (j + 1) * width] = operand(both[:FEAT], both[FEAT:], False)
+            coef_ref[j * share : (j + 1) * share] = got_ref[j, :share]
+    stores = []
+    for j in range(blocks):
+        loads[j].wait()
+        here = slice(j * block, (j + 1) * block)
+        power = jnp.dot(rows_here[here], cen_ref[...], preferred_element_type=F32)
+        tile = jnp.exp2(power).astype(BF16)
+        tile_here[here] = tile
+        place = pl.ds(j * block, block)
+        stores.append(pltpu.make_async_copy(tile_here.at[place], tile_ref.at[place], sems.at[j]))
+        stores[-1].start()
+        fit_ref[here] = jnp.dot(tile, coef_ref[...], preferred_element_type=F32).astype(fit_ref.dtype)
+    for store in stores:
+        store.wait()
+
+
+def tile_forward(rows_op, operands, fit_type, block=256):
+    n = rows_op.shape[0] // 2
+    first = len(operands) == 1
+    if first:
+        parts, depth, width = operands[0].shape
+        m = parts * width
+        more = [
+            jax.ShapeDtypeStruct((256, m), BF16),
             jax.ShapeDtypeStruct((parts * (depth - 2 * FEAT), OUTS), BF16),
+        ]
+    else:
+        m = operands[0].shape[1]
+        more = []
+    return pl.pallas_call(
+        functools.partial(tile_kernel, first=first),
+        in_specs=[HBM] + [VMEM] * len(operands),
+        out_specs=[HBM] + [VMEM] * (1 + len(more)),
+        out_shape=[pltpu.HBM((n, m), BF16), jax.ShapeDtypeStruct((n, OUTS), fit_type), *more],
+        scratch_shapes=[
+            pltpu.VMEM((n, 256), BF16),
+            pltpu.VMEM((n, m), BF16),
+            pltpu.SemaphoreType.DMA((n // block,)),
+            pltpu.SemaphoreType.DMA((n // block,)),
         ],
-        compiler_params=params(),
-        name="prepare_centres",
-    )(got)
-
-
-def tile_kernel(rows_ref, cen_ref, coef_ref, tile_ref, fit_ref):
-    power = jnp.dot(rows_ref[...], cen_ref[...], preferred_element_type=F32)
-    tile = jnp.exp2(power).astype(BF16)
-    tile_ref[...] = tile
-    fit_ref[...] = jnp.dot(tile, coef_ref[...], preferred_element_type=F32).astype(fit_ref.dtype)
-
-
-def tile_forward(rows_op, half, cen_op, coef, fit_type, block=512):
-    n = rows_op.shape[0] // 2
-    m = cen_op.shape[1]
-    first = half * (n // block)
-    return pl.pallas_call(
-        tile_kernel,
-        grid=(n // block,),
-        in_specs=[
-            pl.BlockSpec((block, 256), lambda i: (first + i, 0)),
-            pl.BlockSpec(cen_op.shape, lambda i: (0, 0)),
-            pl.BlockSpec(coef.shape, lambda i: (0, 0)),
-        ],
-        out_specs=[pl.BlockSpec((block, m), lambda i: (i, 0)), pl.BlockSpec((block, OUTS), lambda i: (i, 0))],
-        out_shape=[pltpu.HBM((n, m), BF16), jax.ShapeDtypeStruct((n, OUTS), fit_type)],
         compiler_params=params(),
         cost_estimate=cost(2 * n * m * 384, 2 * n * m, n * m),
         name="tile_forward",
-    )(in_hbm(rows_op), cen_op, coef)
+    )(in_hbm(rows_op), *operands)
 
 
 def back_kernel(*refs, last):
@@ -277,41 +296,28 @@
     )(me, in_hbm(precond), mine, came, feat_parts)
 
 
-def image_kernel(core_ref, pre_ref, grad_ref, out_ref, pre_here, sems):
+def image_kernel(core_ref, pre_ref, grad_ref, out_ref):
     core = core_ref[0]
     chips, width, _ = out_ref.shape
-    copies = [
-        pltpu.make_async_copy(
-            pre_ref.at[:, pl.ds(pl.multiple_of((2 * j + core) * width, width), width)],
-            pre_here.at[j // 2, :, pl.ds(j % 2 * width, width)],
-            sems.at[j],
-        )
-        for j in range(chips)
-    ]
-    for copy in copies:
-        copy.start()
     grad = grad_ref[...].T
     for j in range(0, chips, 2):
-        copies[j].wait()
-        copies[j + 1].wait()
-        part = jnp.dot(grad, pre_here[j // 2], preferred_element_type=F32).T
+        pair = [pre_ref[:, pl.ds(pl.multiple_of((2 * k + core) * width, width), width)] for k in (j, j + 1)]
+        part = jnp.dot(grad, jnp.concatenate(pair, axis=1), preferred_element_type=F32).T
         out_ref[j] = part[:width]
         out_ref[j + 1] = part[width:]
 
 
 def image_part(core, precond, grad, share):
     n, m = precond.shape
-    chips = m // share // 2
     return pl.pallas_call(
         image_kernel,
-        in_specs=[SMEM, HBM, VMEM],
+        in_specs=[SMEM, VMEM, VMEM],
         out_specs=VMEM,
-        out_shape=jax.ShapeDtypeStruct((chips, share, OUTS), F32),
-        scratch_shapes=[pltpu.VMEM((chips // 2, n, 2 * share), BF16), pltpu.SemaphoreType.DMA((chips,))],
+        out_shape=jax.ShapeDtypeStruct((m // share // 2, share, OUTS), F32),
         compiler_params=params(),
         cost_estimate=cost(n * m * OUTS, n * m),
         name="precond_backward",
-    )(core, in_hbm(precond), grad)
+    )(core, precond, grad)
 
 
 def numbers_kernel(part_ref, dir_ref, res_ref, image_ref, out_ref):
@@ -408,16 +414,15 @@
 
     feat = train_rows.T
     picked = pick(start_row[None], centre_index[None], feat, row_devices)
-    dir_mine, picked = lax.optimization_barrier((dir_mine, picked))
+    dir_mine, picked, other = lax.optimization_barrier((dir_mine, picked, other))
     rows_op = prepare_rows(me, feat)
     parts = spread(field(me, precond, dir_mine, swapped(dir_mine), picked), ROWS)
     got = gathered(summed(parts).astype(BF16), ROWS)
-    cen_op, coef = prepare_centres(got)
 
     chips_shape = (cen_devices // 2, rows_here // cen_devices, OUTS)
-    tile_other, fit_other = tile_forward(rows_op, 0, cen_op, coef, BF16)
+    tile_other, fit_other, cen_op, coef = tile_forward(rows_op, [got], BF16)
     fit_came = swapped(fit_other)
-    tile_mine, fit_mine = tile_forward(rows_op, 1, cen_op, coef, F32)
+    tile_mine, fit_mine = tile_forward(rows_op, [cen_op, coef], F32)
     fit_mine, fit_came = lax.optimization_barrier((fit_mine, fit_came))
     half = (fit_mine + fit_came.astype(F32)).astype(BF16).reshape(chips_shape)
     fitted = gathered(summed(spread(half, CHIPS)).astype(BF16), CHIPS)

time: 154 us -> 149 us (0.968)
  blocking collectives: 75.5 us -> 87 us
  waiting for transfers between devices: 16.7 us -> 9.72 us
  starting transfers between devices: 23.4 us -> 19.1 us
  Pallas kernels: 31.5 us -> 27.6 us
    all_to_all x6 -> x7, blocking collectives: 75.5 us -> 87 us  [spread(): return lax.all_to_all(part, axes, 0, 0, tiled=True)]
    all_to_all x3 -> x2, waiting for transfers between devices: 15.5 us -> 7.9 us  [spread(): return lax.all_to_all(part, axes, 0, 0, tiled=True)]
    all_to_all x3 -> x2, starting transfers between devices: 13.8 us -> 9.74 us  [spread(): return lax.all_to_all(part, axes, 0, 0, tiled=True)]
    pallas_call x5 -> x4, Pallas kernels: 16.2 us -> 12.3 us  [the longest x2 10.6 us: tile_forward(): pl.pallas_call(functools.partial(tile_kernel, first=first), in_specs=[HBM...]
  transfers between devices with their start and end apart: 7 -> 6, of which waited for: 4 -> 4; matrix products, arithmetic and copies ran while one was open for 0% -> 0% of each run, Pallas kernels for 10% -> 9%
where the time goes in v5:
time: 149 us; the launch traced here: 148 us
  blocking collectives  87 us (58%)
  Pallas kernels  27.6 us (19%)
  starting transfers between devices  19.1 us (13%)
  waiting for transfers between devices  9.72 us (7%)
  local copies, waits for them, and re-layouts  3.74 us (3%)
    all_to_all x7, blocking collectives, spread(): return lax.all_to_all(part, axes, 0, 0, tiled=True)  87 us
    pallas_call x2, Pallas kernels, tile_forward(): pl.pallas_call(functools.partial(tile_kernel, first=first), in_specs=[HBM...  10.6 us
    all_to_all x2, starting transfers between devices, spread(): return lax.all_to_all(part, axes, 0, 0, tiled=True)  9.74 us
    ppermute x4, starting transfers between devices, swapped(): return lax.ppermute(part, 'core', SWAP)  9.4 us
    all_to_all x2, waiting for transfers between devices, spread(): return lax.all_to_all(part, axes, 0, 0, tiled=True)  7.9 us
    pallas_call x2, Pallas kernels, backward(): pl.pallas_call(functools.partial(back_kernel, last=last), in_specs=[HBM,...  5.26 us
  transfers between devices with their start and end apart: 6, of which 4 were waited for; matrix products, arithmetic and copies ran while one was open for 0% of the time, Pallas kernels for 9%

profile of v5, /device:TPU:1, one launch (start us, length us, event | category | flops | bytes accessed | tf_op | source)
XLA Modules:
  0.0 148.4 jit_solution(1530090228244465107)
XLA Ops:
  0.6 0.0 copy-start.1
  0.6 0.8 copy-done.1
  1.5 0.7 direction_copies.1
  2.2 5.9 %all-to-all-start = ((bf16[8,128,128]{2,1,0:T(8,128)(2,1)}), bf16[8,128,128]{2,1,0:T(8,128)(2,1)S(1)}, u32[]{:S(2)}, u32[]{:S(2)}) async-start(bf16[8,128,128]{2,1,0:T(8,128)(2,1)} %direction_copies.1), calls=%async_computation | async-start | bytes 524288 | tf_op jit(solution)/shard_map/all_to_all | solution.py:387
  8.1 0.0 copy-start.5
  8.1 1.2 copy-done.5
  9.3 0.0 copy-start.7
  9.3 0.7 copy-done.7
  10.0 2.8 %pick_centres.1.feat_ref = bf16[8,128,128]{2,1,0:T(8,128)(2,1)S(1)} custom-call(s32[1]{0:T(128)} %bitcast.2.start_ref, s32[1,1024]{1,0:T(1,128)S(1)} %bitcast.18, f32[64,4096]{1,0:T(8,128)S(1)} %bitcast.16), custom_call_target="tpu_custom_call" | custom-call | flops 4294967296 | bytes 1048576 | tf_op jit(solution)/shard_map/pick_centres/pallas_call | solution.py:85
  12.8 0.0 copy-start.6
  12.8 1.5 %all-to-all-done.mine_ref = bf16[8,128,128]{2,1,0:T(8,128)(2,1)S(1)} async-done(((bf16[8,128,128]{2,1,0:T(8,128)(2,1)}), bf16[8,128,128]{2,1,0:T(8,128)(2,1)S(1)}, u32[]{:S(2)}, u32[]{:S(2)}) %all-to-all-start) | async-done | bytes 262176 | tf_op jit(solution)/shard_map/all_to_all | solution.py:387
  14.4 1.9 %collective-permute-start = (bf16[8,128,128]{2,1,0:T(8,128)(2,1)S(1)}, bf16[8,128,128]{2,1,0:T(8,128)(2,1)S(1)}, u32[]{:S(2)}, u32[]{:S(2)}) collective-permute-start(bf16[8,128,128]{2,1,0:T(8,128)(2,1)S(1)} %all-to-all-done.mine_ref), channel_id=1, source_target_pairs={{0,1},{1,0},{2,3},{3,2},{4,5},{5,4},{6,7},{7,6},{8,9},{9,8},{10,11... | collective-permute-start | bytes 786440 | tf_op jit(solution)/shard_map/ppermute | solution.py:400
  16.3 1.2 collective-permute-done.came_ref
  17.5 3.0 %precond_forward.1 = bf16[8,256,128]{2,1,0:T(8,128)(2,1)S(1)} custom-call(s32[1]{0:T(128)} %bitcast.me_ref.core_ref, bf16[1024,2048]{1,0:T(8,128)(2,1)} %pre_ref.5, bf16[8,128,128]{2,1,0:T(8,128)(2,1)S(1)} %all-to-all-done.mine_ref, bf16[8,128,128]{2,1,0:T(8,128)(2,1)S(1)} %collective-permute-done.came_ref, bf16[8,128,128]{2,1,0:T(8,128)(2,1)S(1)} %pick_centres.1.feat_ref), custom_call_target="tpu_custom_call" | custom-call | flops 536870912 | bytes 4194304 | tf_op jit(solution)/shard_map/precond_forward/pallas_call | solution.py:287
  20.5 17.2 %all_to_all.51 = bf16[8,256,128]{2,1,0:T(8,128)(2,1)S(1)} all-to-all(bf16[8,256,128]{2,1,0:T(8,128)(2,1)S(1)} %precond_forward.1), channel_id=1, replica_groups=mesh['yh'=2,'z'=4,'yl'=2,'x'=4,'core'=2] {'yh','z'}, dimensions={0} | all-to-all | bytes 1048576 | tf_op jit(solution)/shard_map/all_to_all | solution.py:387
  37.6 0.1 reduce_sum.33
  37.7 0.9 broadcast_in_dim.30
  38.6 3.9 %all-to-all-start.2 = ((bf16[8,256,128]{2,1,0:T(8,128)(2,1)}), bf16[8,256,128]{2,1,0:T(8,128)(2,1)S(1)}, u32[]{:S(2)}, u32[]{:S(2)}) async-start(bf16[8,256,128]{2,1,0:T(8,128)(2,1)} %broadcast_in_dim.30), calls=%async_computation.2 | async-start | bytes 1048576 | tf_op jit(solution)/shard_map/all_to_all | solution.py:387
  42.5 0.0 copy-done.6
  42.5 2.4 %prepare_rows.1.refs_0_ = bf16[4096,256]{1,0:T(8,128)(2,1)} custom-call(s32[1]{0:T(128)} %bitcast.me_ref.core_ref, f32[64,4096]{1,0:T(8,128)S(1)} %bitcast.17), custom_call_target="tpu_custom_call" | custom-call | flops 2147483648 | bytes 4194304 | tf_op jit(solution)/shard_map/prepare_rows/pallas_call | solution.py:111
  44.9 6.4 %all-to-all-done.2.refs_1_ = bf16[8,256,128]{2,1,0:T(8,128)(2,1)S(1)} async-done(((bf16[8,256,128]{2,1,0:T(8,128)(2,1)}), bf16[8,256,128]{2,1,0:T(8,128)(2,1)S(1)}, u32[]{:S(2)}, u32[]{:S(2)}) %all-to-all-start.2) | async-done | bytes 524320 | tf_op jit(solution)/shard_map/all_to_all | solution.py:387
  51.3 5.3 %tile_forward.2 = (bf16[2048,1024]{1,0:T(8,128)(2,1)}, bf16[2048,128]{1,0:T(8,128)(2,1)S(1)}, bf16[256,1024]{1,0:T(8,128)(2,1)S(1)}, bf16[1024,128]{1,0:T(8,128)(2,1)S(1)}) custom-call(bf16[4096,256]{1,0:T(8,128)(2,1)} %prepare_rows.1.refs_0_, bf16[8,256,128]{2,1,0:T(8,128)(2,1)S(1)} %all-to-all-done.2.refs_1_), custom_call_target="tpu_custom_call" | custom-call | flops 1610612736 | bytes 4194304 | tf_op jit(solution)/shard_map/tile_forward/pallas_call | solution.py:195
  56.5 3.4 %collective-permute-start.1 = (bf16[2048,128]{1,0:T(8,128)(2,1)S(1)}, bf16[2048,128]{1,0:T(8,128)(2,1)S(1)}, u32[]{:S(2)}, u32[]{:S(2)}) collective-permute-start(bf16[2048,128]{1,0:T(8,128)(2,1)S(1)} %get-tuple-element.27), channel_id=1, source_target_pairs={{0,1},{1,0},{2,3},{3,2},{4,5},{5,4},{6,7},{7,6},{8,9},{9,8},{10,11... | collective-permute-start | bytes 1572872 | tf_op jit(solution)/shard_map/ppermute | solution.py:400
  59.9 5.3 %tile_forward.3 = (bf16[2048,1024]{1,0:T(8,128)(2,1)}, f32[2048,128]{1,0:T(8,128)S(1)}) custom-call(bf16[4096,256]{1,0:T(8,128)(2,1)} %prepare_rows.1.refs_0_, bf16[256,1024]{1,0:T(8,128)(2,1)S(1)} %get-tuple-element.23.refs_1_, bf16[1024,128]{1,0:T(8,128)(2,1)S(1)} %get-tuple-element.24.refs_2_), custom_call_target="tpu_custom_call" | custom-call | flops 1610612736 | bytes 4194304 | tf_op jit(solution)/shard_map/tile_forward/pallas_call | solution.py:195
  65.3 0.0 collective-permute-done.1
  65.3 0.1 add_convert_fusion
  65.4 12.7 %all_to_all.52 = bf16[8,256,128]{2,1,0:T(8,128)(2,1)S(1)} all-to-all(bf16[8,256,128]{2,1,0:T(8,128)(2,1)S(1)} %bitcast.19), channel_id=1, replica_groups=mesh['yh'=2,'z'=4,'yl'=2,'x'=4,'core'=2] {'yl','x'}, dimensions={0} | all-to-all | bytes 1048576 | tf_op jit(solution)/shard_map/all_to_all | solution.py:387
  78.1 0.1 reduce_sum.34
  78.2 0.1 broadcast_in_dim.31
  78.3 11.6 %all_to_all.53.refs_1_ = bf16[8,256,128]{2,1,0:T(8,128)(2,1)S(1)} all-to-all(bf16[8,256,128]{2,1,0:T(8,128)(2,1)S(1)} %broadcast_in_dim.31), channel_id=1, replica_groups=mesh['yh'=2,'z'=4,'yl'=2,'x'=4,'core'=2] {'yl','x'}, dimensions={0} | all-to-all | bytes 1048576 | tf_op jit(solution)/shard_map/all_to_all | solution.py:387
  89.9 1.9 %collective-permute-start.2 = (bf16[8,256,128]{2,1,0:T(8,128)(2,1)S(1)}, bf16[8,256,128]{2,1,0:T(8,128)(2,1)S(1)}, u32[]{:S(2)}, u32[]{:S(2)}) collective-permute-start(bf16[8,256,128]{2,1,0:T(8,128)(2,1)S(1)} %all_to_all.53.refs_1_), channel_id=1, source_target_pairs={{0,1},{1,0},{2,3},{3,2},{4,5},{5,4},{6,7},{7,6},{8,9},{9,8},{10,11... | collective-permute-start | bytes 1572872 | tf_op jit(solution)/shard_map/ppermute | solution.py:400
  91.7 2.5 %tile_backward.2.refs_2_ = f32[128,1024]{1,0:T(8,128)S(1)} custom-call(bf16[2048,1024]{1,0:T(8,128)(2,1)} %get-tuple-element.25.refs_0_, bf16[8,256,128]{2,1,0:T(8,128)(2,1)S(1)} %all_to_all.53.refs_1_), custom_call_target="tpu_custom_call" | custom-call | flops 536870912 | bytes 4194304 | tf_op jit(solution)/shard_map/tile_backward/pallas_call | solution.py:242
  94.2 0.0 copy-start
  94.3 0.0 collective-permute-done.2.refs_1_
  94.3 2.7 %tile_backward.3 = bf16[1024,128]{1,0:T(8,128)(2,1)S(1)} custom-call(bf16[2048,1024]{1,0:T(8,128)(2,1)} %get-tuple-element.22.refs_0_, bf16[8,256,128]{2,1,0:T(8,128)(2,1)S(1)} %collective-permute-done.2.refs_1_, f32[128,1024]{1,0:T(8,128)S(1)} %tile_backward.2.refs_2_), custom_call_target="tpu_custom_call" | custom-call | flops 536870912 | bytes 4194304 | tf_op jit(solution)/shard_map/tile_backward/pallas_call | solution.py:242
  97.0 10.6 %all_to_all.54 = bf16[8,128,128]{2,1,0:T(8,128)(2,1)S(1)} all-to-all(bf16[8,128,128]{2,1,0:T(8,128)(2,1)S(1)} %bitcast.13), channel_id=1, replica_groups=mesh['yh'=2,'z'=4,'yl'=2,'x'=4,'core'=2] {'yh','z'}, dimensions={0} | all-to-all | bytes 524288 | tf_op jit(solution)/shard_map/all_to_all | solution.py:387
  107.7 11.5 %all_to_all.55 = bf16[8,128,128]{2,1,0:T(8,128)(2,1)S(1)} all-to-all(bf16[8,128,128]{2,1,0:T(8,128)(2,1)S(1)} %broadcast_in_dim.32), channel_id=1, replica_groups=mesh['yh'=2,'z'=4,'yl'=2,'x'=4,'core'=2] {'yh','z'}, dimensions={0} | all-to-all | bytes 524288 | tf_op jit(solution)/shard_map/all_to_all | solution.py:387
  119.2 0.0 copy-done
  119.2 0.9 precond_backward.3
  120.1 0.0 copy-start.2
  120.1 0.0 copy-start.3
  120.1 0.0 copy-start.4
  120.1 2.2 %collective-permute-start.3 = (f32[8,128,128]{2,1,0:T(8,128)S(1)}, f32[8,128,128]{2,1,0:T(8,128)S(1)}, u32[]{:S(2)}, u32[]{:S(2)}) collective-permute-start(f32[8,128,128]{2,1,0:T(8,128)S(1)} %precond_backward.3), channel_id=1, source_target_pairs={{0,1},{1,0},{2,3},{3,2},{4,5},{5,4},{6,7},{7,6},{8,9},{9,8},{10,11... | collective-permute-start | bytes 1572872 | tf_op jit(solution)/shard_map/ppermute | solution.py:400
  122.3 0.9 precond_backward.2
  123.2 0.7 collective-permute-done.3
  123.8 0.1 add_convert_fusion.1
  123.9 9.8 %all_to_all.56.part_ref = bf16[8,128,128]{2,1,0:T(8,128)(2,1)S(1)} all-to-all(bf16[8,128,128]{2,1,0:T(8,128)(2,1)S(1)} %add_convert_fusion.1), channel_id=1, replica_groups=mesh['yh'=2,'z'=4,'yl'=2,'x'=4,'core'=2] {'yl','x'}, dimensions={0} | all-to-all | bytes 524288 | tf_op jit(solution)/shard_map/all_to_all | solution.py:387
  133.7 0.0 copy-done.2
  133.7 0.0 copy-done.3
  133.7 0.2 image_numbers.1
  133.9 13.6 %all_to_all.57 = f32[128,1,128]{2,1,0:T(1,128)S(1)} all-to-all(f32[128,1,128]{2,1,0:T(1,128)S(1)} %bitcast.15), channel_id=1, replica_groups=mesh['yh'=2,'z'=4,'yl'=2,'x'=4,'core'=2] {'yh','z','yl','x','core'}, dimensions={0} | all-to-all | bytes 131072 | tf_op jit(solution)/shard_map/all_to_all | solution.py:387
  147.5 0.0 copy-done.4
  147.5 0.8 finish.1
  (3 shorter events, 0.1 us)
Async XLA Ops:
  0.6 0.8 copy-start.1
  2.2 12.2 %all-to-all-start = ((bf16[8,128,128]{2,1,0:T(8,128)(2,1)}), bf16[8,128,128]{2,1,0:T(8,128)(2,1)S(1)}, u32[]{:S(2)}, u32[]{:S(2)}) async-start(bf16[8,128,128]{2,1,0:T(8,128)(2,1)} %direction_copies.1), calls=%async_computation | async-start | bytes 524288 | tf_op jit(solution)/shard_map/all_to_all | solution.py:387
  8.1 1.2 copy-start.5
  9.3 0.7 copy-start.7
  12.8 29.6 %copy-start.6 = (f32[4096,64]{0,1:T(8,128)S(1)}, f32[4096,64]{0,1:T(8,128)}, u32[]{:S(2)}) copy-start(f32[4096,64]{0,1:T(8,128)} %param.6) | copy-start | bytes 3145732
  14.4 3.1 %collective-permute-start = (bf16[8,128,128]{2,1,0:T(8,128)(2,1)S(1)}, bf16[8,128,128]{2,1,0:T(8,128)(2,1)S(1)}, u32[]{:S(2)}, u32[]{:S(2)}) collective-permute-start(bf16[8,128,128]{2,1,0:T(8,128)(2,1)S(1)} %all-to-all-done.mine_ref), channel_id=1, source_target_pairs={{0,1},{1,0},{2,3},{3,2},{4,5},{5,4},{6,7},{7,6},{8,9},{9,8},{10,11... | collective-permute-start | bytes 786440 | tf_op jit(solution)/shard_map/ppermute | solution.py:400
  38.6 12.7 %all-to-all-start.2 = ((bf16[8,256,128]{2,1,0:T(8,128)(2,1)}), bf16[8,256,128]{2,1,0:T(8,128)(2,1)S(1)}, u32[]{:S(2)}, u32[]{:S(2)}) async-start(bf16[8,256,128]{2,1,0:T(8,128)(2,1)} %broadcast_in_dim.30), calls=%async_computation.2 | async-start | bytes 1048576 | tf_op jit(solution)/shard_map/all_to_all | solution.py:387
  56.5 8.7 %collective-permute-start.1 = (bf16[2048,128]{1,0:T(8,128)(2,1)S(1)}, bf16[2048,128]{1,0:T(8,128)(2,1)S(1)}, u32[]{:S(2)}, u32[]{:S(2)}) collective-permute-start(bf16[2048,128]{1,0:T(8,128)(2,1)S(1)} %get-tuple-element.27), channel_id=1, source_target_pairs={{0,1},{1,0},{2,3},{3,2},{4,5},{5,4},{6,7},{7,6},{8,9},{9,8},{10,11... | collective-permute-start | bytes 1572872 | tf_op jit(solution)/shard_map/ppermute | solution.py:400
  89.9 4.4 %collective-permute-start.2 = (bf16[8,256,128]{2,1,0:T(8,128)(2,1)S(1)}, bf16[8,256,128]{2,1,0:T(8,128)(2,1)S(1)}, u32[]{:S(2)}, u32[]{:S(2)}) collective-permute-start(bf16[8,256,128]{2,1,0:T(8,128)(2,1)S(1)} %all_to_all.53.refs_1_), channel_id=1, source_target_pairs={{0,1},{1,0},{2,3},{3,2},{4,5},{5,4},{6,7},{7,6},{8,9},{9,8},{10,11... | collective-permute-start | bytes 1572872 | tf_op jit(solution)/shard_map/ppermute | solution.py:400
  94.2 24.9 %copy-start = (bf16[1024,2048]{1,0:T(8,128)(2,1)S(1)}, bf16[1024,2048]{1,0:T(8,128)(2,1)}, u32[]{:S(2)}) copy-start(bf16[1024,2048]{1,0:T(8,128)(2,1)} %pre_ref.5) | copy-start | bytes 12582916
  120.1 13.6 %copy-start.2 = (f32[128,128]{1,0:T(8,128)S(1)}, f32[128,128]{1,0:T(8,128)}, u32[]{:S(2)}) copy-start(f32[128,128]{1,0:T(8,128)} %dir_ref.5) | copy-start | bytes 196612
  120.1 13.6 %copy-start.3 = (f32[128,128]{1,0:T(8,128)S(1)}, f32[128,128]{1,0:T(8,128)}, u32[]{:S(2)}) copy-start(f32[128,128]{1,0:T(8,128)} %res_ref.3) | copy-start | bytes 196612
  120.1 27.5 %copy-start.4 = (f32[128,128]{1,0:T(8,128)S(1)}, f32[128,128]{1,0:T(8,128)}, u32[]{:S(2)}) copy-start(f32[128,128]{1,0:T(8,128)} %coef_ref.1) | copy-start | bytes 196612
  120.1 3.7 %collective-permute-start.3 = (f32[8,128,128]{2,1,0:T(8,128)S(1)}, f32[8,128,128]{2,1,0:T(8,128)S(1)}, u32[]{:S(2)}, u32[]{:S(2)}) collective-permute-start(f32[8,128,128]{2,1,0:T(8,128)S(1)} %precond_backward.3), channel_id=1, source_target_pairs={{0,1},{1,0},{2,3},{3,2},{4,5},{5,4},{6,7},{7,6},{8,9},{9,8},{10,11... | collective-permute-start | bytes 1572872 | tf_op jit(solution)/shard_map/ppermute | solution.py:400

commit v6 on v5

--- a/solution.py
+++ b/solution.py
@@ -99,30 +99,6 @@
     )(start, index, feat)
 
 
-def prepare_kernel(me_ref, feat_ref, out_ref):
-    high, mid = split_pieces(feat_ref[...] * FEATURE_SCALE, 2)
-    out_ref[...] = operand(high, mid, True).T
-
-
-def prepare_rows(me, feat, block=1024):
-    depth, n = feat.shape
-    blocks = n // block
-    half = blocks // 2
-    return pl.pallas_call(
-        prepare_kernel,
-        grid_spec=pltpu.PrefetchScalarGridSpec(
-            num_scalar_prefetch=1,
-            grid=(blocks,),
-            in_specs=[pl.BlockSpec((depth, block), lambda i, me: (0, (i + half * (1 - me[0])) % blocks))],
-            out_specs=pl.BlockSpec((block, 256), lambda i, me: (i, 0)),
-        ),
-        out_shape=pltpu.HBM((n, 256), BF16),
-        compiler_params=params(),
-        cost_estimate=cost(n * 2**20 // 2, n * 1024),
-        name="prepare_rows",
-    )(me, feat)
-
-
 def send_kernel(dir_ref, out_ref):
     out_ref[...] = jnp.broadcast_to(dir_ref[...].astype(BF16)[None], out_ref.shape)
 
@@ -143,32 +119,24 @@
 
 def tile_kernel(*refs, first):
     if first:
-        rows_ref, got_ref, tile_ref, fit_ref, cen_ref, coef_ref, rows_here, tile_here, rows_sems, sems = refs
-    else:
-        rows_ref, cen_ref, coef_ref, tile_ref, fit_ref, rows_here, tile_here, rows_sems, sems = refs
-    blocks = sems.shape[0]
-    block = fit_ref.shape[0] // blocks
-    offset = 0 if first else fit_ref.shape[0]
-    loads = [
-        pltpu.make_async_copy(
-            rows_ref.at[pl.ds(offset + j * block, block)], rows_here.at[pl.ds(j * block, block)], rows_sems.at[j]
-        )
-        for j in range(blocks)
-    ]
-    for load in loads:
-        load.start()
-    if first:
+        half_ref, feat_ref, got_ref, tile_ref, fit_ref, cen_ref, coef_ref, tile_here, sems = refs
         parts, depth, width = got_ref.shape
         share = depth - 2 * FEAT
         for j in range(parts):
             both = got_ref[j, share:]
             cen_ref[:, j * width : (j + 1) * width] = operand(both[:FEAT], both[FEAT:], False)
             coef_ref[j * share : (j + 1) * share] = got_ref[j, :share]
+    else:
+        half_ref, feat_ref, cen_ref, coef_ref, tile_ref, fit_ref, tile_here, sems = refs
+    blocks = sems.shape[0]
+    n = fit_ref.shape[0]
+    block = n // blocks
     stores = []
     for j in range(blocks):
-        loads[j].wait()
         here = slice(j * block, (j + 1) * block)
-        power = jnp.dot(rows_here[here], cen_ref[...], preferred_element_type=F32)
+        place = pl.ds(pl.multiple_of(half_ref[0] * n + j * block, block), block)
+        high, mid = split_pieces(feat_ref[:, place] * FEATURE_SCALE, 2)
+        power = jnp.dot(operand(high, mid, True).T, cen_ref[...], preferred_element_type=F32)
         tile = jnp.exp2(power).astype(BF16)
         tile_here[here] = tile
         place = pl.ds(j * block, block)
@@ -179,8 +147,8 @@
         store.wait()
 
 
-def tile_forward(rows_op, operands, fit_type, block=256):
-    n = rows_op.shape[0] // 2
+def tile_forward(half, feat, operands, fit_type, block=256):
+    n = feat.shape[1] // 2
     first = len(operands) == 1
     if first:
         parts, depth, width = operands[0].shape
@@ -194,19 +162,14 @@
         more = []
     return pl.pallas_call(
         functools.partial(tile_kernel, first=first),
-        in_specs=[HBM] + [VMEM] * len(operands),
+        in_specs=[SMEM, VMEM] + [VMEM] * len(operands),
         out_specs=[HBM] + [VMEM] * (1 + len(more)),
         out_shape=[pltpu.HBM((n, m), BF16), jax.ShapeDtypeStruct((n, OUTS), fit_type), *more],
-        scratch_shapes=[
-            pltpu.VMEM((n, 256), BF16),
-            pltpu.VMEM((n, m), BF16),
-            pltpu.SemaphoreType.DMA((n // block,)),
-            pltpu.SemaphoreType.DMA((n // block,)),
-        ],
+        scratch_shapes=[pltpu.VMEM((n, m), BF16), pltpu.SemaphoreType.DMA((n // block,))],
         compiler_params=params(),
         cost_estimate=cost(2 * n * m * 384, 2 * n * m, n * m),
         name="tile_forward",
-    )(in_hbm(rows_op), *operands)
+    )(half, feat, *operands)
 
 
 def back_kernel(*refs, last):
@@ -415,14 +378,13 @@
     feat = train_rows.T
     picked = pick(start_row[None], centre_index[None], feat, row_devices)
     dir_mine, picked, other = lax.optimization_barrier((dir_mine, picked, other))
-    rows_op = prepare_rows(me, feat)
     parts = spread(field(me, precond, dir_mine, swapped(dir_mine), picked), ROWS)
     got = gathered(summed(parts).astype(BF16), ROWS)
 
     chips_shape = (cen_devices // 2, rows_here // cen_devices, OUTS)
-    tile_other, fit_other, cen_op, coef = tile_forward(rows_op, [got], BF16)
+    tile_other, fit_other, cen_op, coef = tile_forward(other, feat, [got], BF16)
     fit_came = swapped(fit_other)
-    tile_mine, fit_mine = tile_forward(rows_op, [cen_op, coef], F32)
+    tile_mine, fit_mine = tile_forward(me, feat, [cen_op, coef], F32)
     fit_mine, fit_came = lax.optimization_barrier((fit_mine, fit_came))
     half = (fit_mine + fit_came.astype(F32)).astype(BF16).reshape(chips_shape)
     fitted = gathered(summed(spread(half, CHIPS)).astype(BF16), CHIPS)

time: 149 us -> 144 us (0.966)
  blocking collectives: 87 us -> 100 us
  Pallas kernels: 27.6 us -> 21 us
  waiting for transfers between devices: 9.72 us -> 3.34 us
  starting transfers between devices: 19.1 us -> 14.9 us
    all_to_all x7 -> x8, blocking collectives: 87 us -> 100 us  [spread(): return lax.all_to_all(part, axes, 0, 0, tiled=True)]
    pallas_call x3 -> x2, Pallas kernels: 13 us -> 6.43 us  [tile_forward(): pl.pallas_call(functools.partial(tile_kernel, first=first), in_specs=[SME...]
    all_to_all x2 -> x1, waiting for transfers between devices: 7.9 us -> 1.51 us  [spread(): return lax.all_to_all(part, axes, 0, 0, tiled=True)]
    all_to_all x2 -> x1, starting transfers between devices: 9.74 us -> 5.86 us  [spread(): return lax.all_to_all(part, axes, 0, 0, tiled=True)]
  transfers between devices with their start and end apart: 6 -> 5, of which waited for: 4 -> 3; matrix products, arithmetic and copies ran while one was open for 0% -> 0% of each run, Pallas kernels for 9% -> 7%
where the time goes in v6:
time: 144 us; the launch traced here: 143 us
  blocking collectives  100 us (69%)
  Pallas kernels  21 us (15%)
  starting transfers between devices  14.9 us (10%)
  waiting for transfers between devices  3.34 us (2%)
  local copies, waits for them, and re-layouts  2.95 us (2%)
    all_to_all x8, blocking collectives, spread(): return lax.all_to_all(part, axes, 0, 0, tiled=True)  100 us
    ppermute x4, starting transfers between devices, swapped(): return lax.ppermute(part, 'core', SWAP)  9.03 us
    pallas_call x2, Pallas kernels, tile_forward(): pl.pallas_call(functools.partial(tile_kernel, first=first), in_specs=[SME...  6.43 us
    all_to_all x1, starting transfers between devices, spread(): return lax.all_to_all(part, axes, 0, 0, tiled=True)  5.86 us
    pallas_call x2, Pallas kernels, backward(): pl.pallas_call(functools.partial(back_kernel, last=last), in_specs=[HBM,...  5.26 us
    pallas_call x1, Pallas kernels, field(): pl.pallas_call(field_kernel, in_specs=[SMEM, HBM, VMEM, VMEM, VMEM], out_...  2.98 us
  transfers between devices with their start and end apart: 5, of which 3 were waited for; matrix products, arithmetic and copies ran while one was open for 0% of the time, Pallas kernels for 7%

profile of v6, /device:TPU:1, one launch (start us, length us, event | category | flops | bytes accessed | tf_op | source)
XLA Modules:
  0.0 143.4 jit_solution(8186754385804914922)
XLA Ops:
  0.6 0.0 copy-start.1
  0.6 0.8 copy-done.1
  1.5 0.7 direction_copies.1
  2.2 5.9 %all-to-all-start = ((bf16[8,128,128]{2,1,0:T(8,128)(2,1)}), bf16[8,128,128]{2,1,0:T(8,128)(2,1)S(1)}, u32[]{:S(2)}, u32[]{:S(2)}) async-start(bf16[8,128,128]{2,1,0:T(8,128)(2,1)} %direction_copies.1), calls=%async_computation | async-start | bytes 524288 | tf_op jit(solution)/shard_map/all_to_all | solution.py:350
  8.0 0.0 copy-start.5
  8.1 1.2 copy-done.5
  9.3 0.0 copy-start.7
  9.3 0.7 copy-done.7
  10.0 2.8 %pick_centres.1.feat_ref = bf16[8,128,128]{2,1,0:T(8,128)(2,1)S(1)} custom-call(s32[1]{0:T(128)} %bitcast.1.start_ref, s32[1,1024]{1,0:T(1,128)S(1)} %bitcast.19, f32[64,4096]{1,0:T(8,128)S(1)} %bitcast.16), custom_call_target="tpu_custom_call" | custom-call | flops 4294967296 | bytes 1048576 | tf_op jit(solution)/shard_map/pick_centres/pallas_call | solution.py:85
  12.8 0.0 copy-start.6
  12.8 1.5 %all-to-all-done.mine_ref = bf16[8,128,128]{2,1,0:T(8,128)(2,1)S(1)} async-done(((bf16[8,128,128]{2,1,0:T(8,128)(2,1)}), bf16[8,128,128]{2,1,0:T(8,128)(2,1)S(1)}, u32[]{:S(2)}, u32[]{:S(2)}) %all-to-all-start) | async-done | bytes 262176 | tf_op jit(solution)/shard_map/all_to_all | solution.py:350
  14.3 1.9 %collective-permute-start = (bf16[8,128,128]{2,1,0:T(8,128)(2,1)S(1)}, bf16[8,128,128]{2,1,0:T(8,128)(2,1)S(1)}, u32[]{:S(2)}, u32[]{:S(2)}) collective-permute-start(bf16[8,128,128]{2,1,0:T(8,128)(2,1)S(1)} %all-to-all-done.mine_ref), channel_id=1, source_target_pairs={{0,1},{1,0},{2,3},{3,2},{4,5},{5,4},{6,7},{7,6},{8,9},{9,8},{10,11... | collective-permute-start | bytes 786440 | tf_op jit(solution)/shard_map/ppermute | solution.py:363
  16.3 1.2 collective-permute-done.came_ref
  17.5 3.0 %precond_forward.1 = bf16[8,256,128]{2,1,0:T(8,128)(2,1)S(1)} custom-call(s32[1]{0:T(128)} %bitcast.me_ref.refs_0_.core_ref, bf16[1024,2048]{1,0:T(8,128)(2,1)} %pre_ref.5, bf16[8,128,128]{2,1,0:T(8,128)(2,1)S(1)} %all-to-all-done.mine_ref, bf16[8,128,128]{2,1,0:T(8,128)(2,1)S(1)} %collective-permute-done.came_ref, bf16[8,128,128]{2,1,0:T(8,128)(2,1)S(1)} %pick_centres.1.feat_ref), custom_call_target="tpu_custom_call" | custom-call | flops 536870912 | bytes 4194304 | tf_op jit(solution)/shard_map/precond_forward/pallas_call | solution.py:250
  20.4 17.2 %all_to_all.51 = bf16[8,256,128]{2,1,0:T(8,128)(2,1)S(1)} all-to-all(bf16[8,256,128]{2,1,0:T(8,128)(2,1)S(1)} %precond_forward.1), channel_id=1, replica_groups=mesh['yh'=2,'z'=4,'yl'=2,'x'=4,'core'=2] {'yh','z'}, dimensions={0} | all-to-all | bytes 1048576 | tf_op jit(solution)/shard_map/all_to_all | solution.py:350
  37.6 0.1 reduce_sum.33
  37.7 0.1 broadcast_in_dim.30
  37.8 13.2 %all_to_all.52.refs_2_ = bf16[8,256,128]{2,1,0:T(8,128)(2,1)S(1)} all-to-all(bf16[8,256,128]{2,1,0:T(8,128)(2,1)S(1)} %broadcast_in_dim.30), channel_id=1, replica_groups=mesh['yh'=2,'z'=4,'yl'=2,'x'=4,'core'=2] {'yh','z'}, dimensions={0} | all-to-all | bytes 1048576 | tf_op jit(solution)/shard_map/all_to_all | solution.py:350
  51.0 0.0 copy-done.6
  51.0 3.2 %tile_forward.2 = (bf16[2048,1024]{1,0:T(8,128)(2,1)}, bf16[2048,128]{1,0:T(8,128)(2,1)S(1)}, bf16[256,1024]{1,0:T(8,128)(2,1)S(1)}, bf16[1024,128]{1,0:T(8,128)(2,1)S(1)}) custom-call(s32[1]{0:T(128)S(6)} %sub.3.refs_0_.core_ref, f32[64,4096]{1,0:T(8,128)S(1)} %bitcast.17, bf16[8,256,128]{2,1,0:T(8,128)(2,1)S(1)} %all_to_all.52.refs_2_), custom_call_target="tpu_custom_call" | custom-call | flops 1610612736 | bytes 4194304 | tf_op jit(solution)/shard_map/tile_forward/pallas_call | solution.py:163
  54.2 3.0 %collective-permute-start.1 = (bf16[2048,128]{1,0:T(8,128)(2,1)S(1)}, bf16[2048,128]{1,0:T(8,128)(2,1)S(1)}, u32[]{:S(2)}, u32[]{:S(2)}) collective-permute-start(bf16[2048,128]{1,0:T(8,128)(2,1)S(1)} %get-tuple-element.28), channel_id=1, source_target_pairs={{0,1},{1,0},{2,3},{3,2},{4,5},{5,4},{6,7},{7,6},{8,9},{9,8},{10,11... | collective-permute-start | bytes 1572872 | tf_op jit(solution)/shard_map/ppermute | solution.py:363
  57.2 3.2 %tile_forward.3 = (bf16[2048,1024]{1,0:T(8,128)(2,1)}, f32[2048,128]{1,0:T(8,128)S(1)}) custom-call(s32[1]{0:T(128)} %bitcast.me_ref.refs_0_.core_ref, f32[64,4096]{1,0:T(8,128)S(1)} %bitcast.18, bf16[256,1024]{1,0:T(8,128)(2,1)S(1)} %get-tuple-element.24.refs_2_, bf16[1024,128]{1,0:T(8,128)(2,1)S(1)} %get-tuple-element.25.refs_3_), custom_call_target="tpu_custom_call" | custom-call | flops 1610612736 | bytes 4194304 | tf_op jit(solution)/shard_map/tile_forward/pallas_call | solution.py:163
  60.5 0.0 collective-permute-done.1
  60.5 0.1 add_convert_fusion
  60.6 12.8 %all_to_all.53 = bf16[8,256,128]{2,1,0:T(8,128)(2,1)S(1)} all-to-all(bf16[8,256,128]{2,1,0:T(8,128)(2,1)S(1)} %bitcast.20), channel_id=1, replica_groups=mesh['yh'=2,'z'=4,'yl'=2,'x'=4,'core'=2] {'yl','x'}, dimensions={0} | all-to-all | bytes 1048576 | tf_op jit(solution)/shard_map/all_to_all | solution.py:350
  73.3 0.1 reduce_sum.34
  73.4 0.1 broadcast_in_dim.31
  73.5 11.6 %all_to_all.54.refs_1_ = bf16[8,256,128]{2,1,0:T(8,128)(2,1)S(1)} all-to-all(bf16[8,256,128]{2,1,0:T(8,128)(2,1)S(1)} %broadcast_in_dim.31), channel_id=1, replica_groups=mesh['yh'=2,'z'=4,'yl'=2,'x'=4,'core'=2] {'yl','x'}, dimensions={0} | all-to-all | bytes 1048576 | tf_op jit(solution)/shard_map/all_to_all | solution.py:350
  85.1 1.9 %collective-permute-start.2 = (bf16[8,256,128]{2,1,0:T(8,128)(2,1)S(1)}, bf16[8,256,128]{2,1,0:T(8,128)(2,1)S(1)}, u32[]{:S(2)}, u32[]{:S(2)}) collective-permute-start(bf16[8,256,128]{2,1,0:T(8,128)(2,1)S(1)} %all_to_all.54.refs_1_), channel_id=1, source_target_pairs={{0,1},{1,0},{2,3},{3,2},{4,5},{5,4},{6,7},{7,6},{8,9},{9,8},{10,11... | collective-permute-start | bytes 1572872 | tf_op jit(solution)/shard_map/ppermute | solution.py:363
  87.0 2.5 %tile_backward.2.refs_2_ = f32[128,1024]{1,0:T(8,128)S(1)} custom-call(bf16[2048,1024]{1,0:T(8,128)(2,1)} %get-tuple-element.26.refs_0_, bf16[8,256,128]{2,1,0:T(8,128)(2,1)S(1)} %all_to_all.54.refs_1_), custom_call_target="tpu_custom_call" | custom-call | flops 536870912 | bytes 4194304 | tf_op jit(solution)/shard_map/tile_backward/pallas_call | solution.py:205
  89.5 0.0 copy-start
  89.5 0.0 collective-permute-done.2.refs_1_
  89.5 2.7 %tile_backward.3 = bf16[1024,128]{1,0:T(8,128)(2,1)S(1)} custom-call(bf16[2048,1024]{1,0:T(8,128)(2,1)} %get-tuple-element.23.refs_0_, bf16[8,256,128]{2,1,0:T(8,128)(2,1)S(1)} %collective-permute-done.2.refs_1_, f32[128,1024]{1,0:T(8,128)S(1)} %tile_backward.2.refs_2_), custom_call_target="tpu_custom_call" | custom-call | flops 536870912 | bytes 4194304 | tf_op jit(solution)/shard_map/tile_backward/pallas_call | solution.py:205
  92.2 10.2 %all_to_all.55 = bf16[8,128,128]{2,1,0:T(8,128)(2,1)S(1)} all-to-all(bf16[8,128,128]{2,1,0:T(8,128)(2,1)S(1)} %bitcast.13), channel_id=1, replica_groups=mesh['yh'=2,'z'=4,'yl'=2,'x'=4,'core'=2] {'yh','z'}, dimensions={0} | all-to-all | bytes 524288 | tf_op jit(solution)/shard_map/all_to_all | solution.py:350
  102.6 11.5 %all_to_all.56 = bf16[8,128,128]{2,1,0:T(8,128)(2,1)S(1)} all-to-all(bf16[8,128,128]{2,1,0:T(8,128)(2,1)S(1)} %broadcast_in_dim.32), channel_id=1, replica_groups=mesh['yh'=2,'z'=4,'yl'=2,'x'=4,'core'=2] {'yh','z'}, dimensions={0} | all-to-all | bytes 524288 | tf_op jit(solution)/shard_map/all_to_all | solution.py:350
  114.0 0.0 copy-done
  114.0 0.9 precond_backward.3
  114.9 0.0 copy-start.2
  114.9 0.0 copy-start.3
  114.9 0.0 copy-start.4
  115.0 2.2 %collective-permute-start.3 = (f32[8,128,128]{2,1,0:T(8,128)S(1)}, f32[8,128,128]{2,1,0:T(8,128)S(1)}, u32[]{:S(2)}, u32[]{:S(2)}) collective-permute-start(f32[8,128,128]{2,1,0:T(8,128)S(1)} %precond_backward.3), channel_id=1, source_target_pairs={{0,1},{1,0},{2,3},{3,2},{4,5},{5,4},{6,7},{7,6},{8,9},{9,8},{10,11... | collective-permute-start | bytes 1572872 | tf_op jit(solution)/shard_map/ppermute | solution.py:363
  117.1 0.9 precond_backward.2
  118.0 0.7 collective-permute-done.3
  118.7 0.1 add_convert_fusion.1
  118.7 9.8 %all_to_all.57.part_ref = bf16[8,128,128]{2,1,0:T(8,128)(2,1)S(1)} all-to-all(bf16[8,128,128]{2,1,0:T(8,128)(2,1)S(1)} %add_convert_fusion.1), channel_id=1, replica_groups=mesh['yh'=2,'z'=4,'yl'=2,'x'=4,'core'=2] {'yl','x'}, dimensions={0} | all-to-all | bytes 524288 | tf_op jit(solution)/shard_map/all_to_all | solution.py:350
  128.6 0.0 copy-done.2
  128.6 0.0 copy-done.3
  128.6 0.2 image_numbers.1
  128.8 13.7 %all_to_all.58 = f32[128,1,128]{2,1,0:T(1,128)S(1)} all-to-all(f32[128,1,128]{2,1,0:T(1,128)S(1)} %bitcast.15), channel_id=1, replica_groups=mesh['yh'=2,'z'=4,'yl'=2,'x'=4,'core'=2] {'yh','z','yl','x','core'}, dimensions={0} | all-to-all | bytes 131072 | tf_op jit(solution)/shard_map/all_to_all | solution.py:350
  142.5 0.0 copy-done.4
  142.5 0.8 finish.1
  (3 shorter events, 0.1 us)
Async XLA Ops:
  0.6 0.8 copy-start.1
  2.2 12.2 %all-to-all-start = ((bf16[8,128,128]{2,1,0:T(8,128)(2,1)}), bf16[8,128,128]{2,1,0:T(8,128)(2,1)S(1)}, u32[]{:S(2)}, u32[]{:S(2)}) async-start(bf16[8,128,128]{2,1,0:T(8,128)(2,1)} %direction_copies.1), calls=%async_computation | async-start | bytes 524288 | tf_op jit(solution)/shard_map/all_to_all | solution.py:350
  8.0 1.2 copy-start.5
  9.3 0.7 copy-start.7
  12.8 38.2 %copy-start.6 = (f32[4096,64]{0,1:T(8,128)S(1)}, f32[4096,64]{0,1:T(8,128)}, u32[]{:S(2)}) copy-start(f32[4096,64]{0,1:T(8,128)} %param.6) | copy-start | bytes 3145732
  14.3 3.1 %collective-permute-start = (bf16[8,128,128]{2,1,0:T(8,128)(2,1)S(1)}, bf16[8,128,128]{2,1,0:T(8,128)(2,1)S(1)}, u32[]{:S(2)}, u32[]{:S(2)}) collective-permute-start(bf16[8,128,128]{2,1,0:T(8,128)(2,1)S(1)} %all-to-all-done.mine_ref), channel_id=1, source_target_pairs={{0,1},{1,0},{2,3},{3,2},{4,5},{5,4},{6,7},{7,6},{8,9},{9,8},{10,11... | collective-permute-start | bytes 786440 | tf_op jit(solution)/shard_map/ppermute | solution.py:363
  54.2 6.3 %collective-permute-start.1 = (bf16[2048,128]{1,0:T(8,128)(2,1)S(1)}, bf16[2048,128]{1,0:T(8,128)(2,1)S(1)}, u32[]{:S(2)}, u32[]{:S(2)}) collective-permute-start(bf16[2048,128]{1,0:T(8,128)(2,1)S(1)} %get-tuple-element.28), channel_id=1, source_target_pairs={{0,1},{1,0},{2,3},{3,2},{4,5},{5,4},{6,7},{7,6},{8,9},{9,8},{10,11... | collective-permute-start | bytes 1572872 | tf_op jit(solution)/shard_map/ppermute | solution.py:363
  85.1 4.4 %collective-permute-start.2 = (bf16[8,256,128]{2,1,0:T(8,128)(2,1)S(1)}, bf16[8,256,128]{2,1,0:T(8,128)(2,1)S(1)}, u32[]{:S(2)}, u32[]{:S(2)}) collective-permute-start(bf16[8,256,128]{2,1,0:T(8,128)(2,1)S(1)} %all_to_all.54.refs_1_), channel_id=1, source_target_pairs={{0,1},{1,0},{2,3},{3,2},{4,5},{5,4},{6,7},{7,6},{8,9},{9,8},{10,11... | collective-permute-start | bytes 1572872 | tf_op jit(solution)/shard_map/ppermute | solution.py:363
  89.5 24.6 %copy-start = (bf16[1024,2048]{1,0:T(8,128)(2,1)S(1)}, bf16[1024,2048]{1,0:T(8,128)(2,1)}, u32[]{:S(2)}) copy-start(bf16[1024,2048]{1,0:T(8,128)(2,1)} %pre_ref.5) | copy-start | bytes 12582916
  114.9 13.6 %copy-start.2 = (f32[128,128]{1,0:T(8,128)S(1)}, f32[128,128]{1,0:T(8,128)}, u32[]{:S(2)}) copy-start(f32[128,128]{1,0:T(8,128)} %dir_ref.5) | copy-start | bytes 196612
  114.9 13.6 %copy-start.3 = (f32[128,128]{1,0:T(8,128)S(1)}, f32[128,128]{1,0:T(8,128)}, u32[]{:S(2)}) copy-start(f32[128,128]{1,0:T(8,128)} %res_ref.3) | copy-start | bytes 196612
  114.9 27.6 %copy-start.4 = (f32[128,128]{1,0:T(8,128)S(1)}, f32[128,128]{1,0:T(8,128)}, u32[]{:S(2)}) copy-start(f32[128,128]{1,0:T(8,128)} %coef_ref.1) | copy-start | bytes 196612
  115.0 3.7 %collective-permute-start.3 = (f32[8,128,128]{2,1,0:T(8,128)S(1)}, f32[8,128,128]{2,1,0:T(8,128)S(1)}, u32[]{:S(2)}, u32[]{:S(2)}) collective-permute-start(f32[8,128,128]{2,1,0:T(8,128)S(1)} %precond_backward.3), channel_id=1, source_target_pairs={{0,1},{1,0},{2,3},{3,2},{4,5},{5,4},{6,7},{7,6},{8,9},{9,8},{10,11... | collective-permute-start | bytes 1572872 | tf_op jit(solution)/shard_map/ppermute | solution.py:363

commit v7 on v6

--- a/solution.py
+++ b/solution.py
@@ -173,50 +173,30 @@
 
 
 def back_kernel(*refs, last):
-    tile_ref, fit_ref, *before, out_ref, tile_here, turned, total_ref, sems = refs
-    blocks = sems.shape[0]
-    block = tile_ref.shape[0] // blocks
-    copies = [
-        pltpu.make_async_copy(tile_ref.at[pl.ds(j * block, block)], tile_here.at[pl.ds(j * block, block)], sems.at[j])
-        for j in range(blocks)
-    ]
-    for copy in copies:
-        copy.start()
+    tile_ref, fit_ref, *before, out_ref, turned = refs
     parts, share, _ = fit_ref.shape
     for j in range(parts):
         turned[:, j * share : (j + 1) * share] = fit_ref[j].T
-    for j in range(blocks):
-        copies[j].wait()
-        here = slice(j * block, (j + 1) * block)
-        part = jnp.dot(turned[:, here], tile_here[here], preferred_element_type=F32)
-        if j or before:
-            part += total_ref[...] if j else before[0][...]
-        if j < blocks - 1:
-            total_ref[...] = part
-        elif last:
-            out_ref[...] = part.T.astype(BF16)
-        else:
-            out_ref[...] = part
-
-
-def backward(tile, fitted, before=None, blocks=4):
+    part = jnp.dot(turned[...], tile_ref[...], preferred_element_type=F32)
+    if last:
+        out_ref[...] = (part + before[0][...]).T.astype(BF16)
+    else:
+        out_ref[...] = part
+
+
+def backward(tile, fitted, before=None):
     n, m = tile.shape
     last = before is not None
     return pl.pallas_call(
         functools.partial(back_kernel, last=last),
-        in_specs=[HBM, VMEM] + [VMEM] * last,
+        in_specs=[VMEM, VMEM] + [VMEM] * last,
         out_specs=VMEM,
         out_shape=jax.ShapeDtypeStruct((m, OUTS), BF16) if last else jax.ShapeDtypeStruct((OUTS, m), F32),
-        scratch_shapes=[
-            pltpu.VMEM((n, m), BF16),
-            pltpu.VMEM((OUTS, n), BF16),
-            pltpu.VMEM((OUTS, m), F32),
-            pltpu.SemaphoreType.DMA((blocks,)),
-        ],
+        scratch_shapes=[pltpu.VMEM((OUTS, n), BF16)],
         compiler_params=params(),
         cost_estimate=cost(2 * n * m * OUTS, 2 * n * m),
         name="tile_backward",
-    )(in_hbm(tile), fitted, *([before] if last else []))
+    )(tile, fitted, *([before] if last else []))
 
 
 def field_kernel(me_ref, pre_ref, mine_ref, came_ref, feat_ref, out_ref, pre_here, dir_here, sems):

time: 144 us -> 144 us (level)
  local copies, waits for them, and re-layouts: 2.95 us -> 6.56 us
  Pallas kernels: 21 us -> 17.4 us
    pallas_call x2, Pallas kernels: 5.26 us -> 1.54 us  [backward(): pl.pallas_call(functools.partial(back_kernel, last=last), in_specs=[VMEM,...]
    unnamed x16 -> x20, local copies, waits for them, and re-layouts: 2.77 us -> 6.39 us
  transfers between devices with their start and end apart: 5 -> 5, of which waited for: 3 -> 3; matrix products, arithmetic and copies ran while one was open for 0% -> 0% of each run, Pallas kernels for 7% -> 5%
where the time goes in v7:
time: 144 us; the launch traced here: 143 us
  blocking collectives  100 us (69%)
  Pallas kernels  17.4 us (12%)
  starting transfers between devices  14.9 us (10%)
  local copies, waits for them, and re-layouts  6.56 us (5%)
  waiting for transfers between devices  3.33 us (2%)
    all_to_all x8, blocking collectives, spread(): return lax.all_to_all(part, axes, 0, 0, tiled=True)  100 us
    ppermute x4, starting transfers between devices, swapped(): return lax.ppermute(part, 'core', SWAP)  9.02 us
    pallas_call x2, Pallas kernels, tile_forward(): pl.pallas_call(functools.partial(tile_kernel, first=first), in_specs=[SME...  6.43 us
    unnamed x20, local copies, waits for them, and re-layouts  6.39 us
    all_to_all x1, starting transfers between devices, spread(): return lax.all_to_all(part, axes, 0, 0, tiled=True)  5.86 us
    pallas_call x1, Pallas kernels, field(): pl.pallas_call(field_kernel, in_specs=[SMEM, HBM, VMEM, VMEM, VMEM], out_...  2.98 us
  transfers between devices with their start and end apart: 5, of which 3 were waited for; matrix products, arithmetic and copies ran while one was open for 0% of the time, Pallas kernels for 5%

profile of v7, /device:TPU:1, one launch (start us, length us, event | category | flops | bytes accessed | tf_op | source)
XLA Modules:
  0.0 143.3 jit_solution(11886641656170051384)
XLA Ops:
  0.6 0.0 copy-start.3
  0.6 0.8 copy-done.3
  1.5 0.7 direction_copies.1
  2.2 5.9 %all-to-all-start = ((bf16[8,128,128]{2,1,0:T(8,128)(2,1)}), bf16[8,128,128]{2,1,0:T(8,128)(2,1)S(1)}, u32[]{:S(2)}, u32[]{:S(2)}) async-start(bf16[8,128,128]{2,1,0:T(8,128)(2,1)} %direction_copies.1), calls=%async_computation | async-start | bytes 524288 | tf_op jit(solution)/shard_map/all_to_all | solution.py:330
  8.1 0.0 copy-start.7
  8.1 1.2 copy-done.7
  9.3 0.0 copy-start.9
  9.3 0.7 copy-done.9
  10.0 2.9 %pick_centres.1.feat_ref = bf16[8,128,128]{2,1,0:T(8,128)(2,1)S(1)} custom-call(s32[1]{0:T(128)} %bitcast.1.start_ref, s32[1,1024]{1,0:T(1,128)S(1)} %bitcast.19, f32[64,4096]{1,0:T(8,128)S(1)} %bitcast.16), custom_call_target="tpu_custom_call" | custom-call | flops 4294967296 | bytes 1048576 | tf_op jit(solution)/shard_map/pick_centres/pallas_call | solution.py:85
  12.8 0.0 copy-start.8
  12.9 1.5 %all-to-all-done.mine_ref = bf16[8,128,128]{2,1,0:T(8,128)(2,1)S(1)} async-done(((bf16[8,128,128]{2,1,0:T(8,128)(2,1)}), bf16[8,128,128]{2,1,0:T(8,128)(2,1)S(1)}, u32[]{:S(2)}, u32[]{:S(2)}) %all-to-all-start) | async-done | bytes 262176 | tf_op jit(solution)/shard_map/all_to_all | solution.py:330
  14.4 1.9 %collective-permute-start = (bf16[8,128,128]{2,1,0:T(8,128)(2,1)S(1)}, bf16[8,128,128]{2,1,0:T(8,128)(2,1)S(1)}, u32[]{:S(2)}, u32[]{:S(2)}) collective-permute-start(bf16[8,128,128]{2,1,0:T(8,128)(2,1)S(1)} %all-to-all-done.mine_ref), channel_id=1, source_target_pairs={{0,1},{1,0},{2,3},{3,2},{4,5},{5,4},{6,7},{7,6},{8,9},{9,8},{10,11... | collective-permute-start | bytes 786440 | tf_op jit(solution)/shard_map/ppermute | solution.py:343
  16.3 1.2 collective-permute-done.came_ref
  17.5 3.0 %precond_forward.1 = bf16[8,256,128]{2,1,0:T(8,128)(2,1)S(1)} custom-call(s32[1]{0:T(128)} %bitcast.me_ref.refs_0_.core_ref, bf16[1024,2048]{1,0:T(8,128)(2,1)} %pre_ref.5, bf16[8,128,128]{2,1,0:T(8,128)(2,1)S(1)} %all-to-all-done.mine_ref, bf16[8,128,128]{2,1,0:T(8,128)(2,1)S(1)} %collective-permute-done.came_ref, bf16[8,128,128]{2,1,0:T(8,128)(2,1)S(1)} %pick_centres.1.feat_ref), custom_call_target="tpu_custom_call" | custom-call | flops 536870912 | bytes 4194304 | tf_op jit(solution)/shard_map/precond_forward/pallas_call | solution.py:230
  20.5 17.2 %all_to_all.51 = bf16[8,256,128]{2,1,0:T(8,128)(2,1)S(1)} all-to-all(bf16[8,256,128]{2,1,0:T(8,128)(2,1)S(1)} %precond_forward.1), channel_id=1, replica_groups=mesh['yh'=2,'z'=4,'yl'=2,'x'=4,'core'=2] {'yh','z'}, dimensions={0} | all-to-all | bytes 1048576 | tf_op jit(solution)/shard_map/all_to_all | solution.py:330
  37.6 0.1 reduce_sum.33
  37.7 0.1 broadcast_in_dim.30
  37.8 13.2 %all_to_all.52.refs_2_ = bf16[8,256,128]{2,1,0:T(8,128)(2,1)S(1)} all-to-all(bf16[8,256,128]{2,1,0:T(8,128)(2,1)S(1)} %broadcast_in_dim.30), channel_id=1, replica_groups=mesh['yh'=2,'z'=4,'yl'=2,'x'=4,'core'=2] {'yh','z'}, dimensions={0} | all-to-all | bytes 1048576 | tf_op jit(solution)/shard_map/all_to_all | solution.py:330
  51.0 0.0 copy-done.8
  51.0 3.2 %tile_forward.2 = (bf16[2048,1024]{1,0:T(8,128)(2,1)}, bf16[2048,128]{1,0:T(8,128)(2,1)S(1)}, bf16[256,1024]{1,0:T(8,128)(2,1)S(1)}, bf16[1024,128]{1,0:T(8,128)(2,1)S(1)}) custom-call(s32[1]{0:T(128)S(6)} %sub.3.refs_0_.core_ref, f32[64,4096]{1,0:T(8,128)S(1)} %bitcast.17, bf16[8,256,128]{2,1,0:T(8,128)(2,1)S(1)} %all_to_all.52.refs_2_), custom_call_target="tpu_custom_call" | custom-call | flops 1610612736 | bytes 4194304 | tf_op jit(solution)/shard_map/tile_forward/pallas_call | solution.py:163
  54.2 3.0 %collective-permute-start.1 = (bf16[2048,128]{1,0:T(8,128)(2,1)S(1)}, bf16[2048,128]{1,0:T(8,128)(2,1)S(1)}, u32[]{:S(2)}, u32[]{:S(2)}) collective-permute-start(bf16[2048,128]{1,0:T(8,128)(2,1)S(1)} %get-tuple-element.28), channel_id=1, source_target_pairs={{0,1},{1,0},{2,3},{3,2},{4,5},{5,4},{6,7},{7,6},{8,9},{9,8},{10,11... | collective-permute-start | bytes 1572872 | tf_op jit(solution)/shard_map/ppermute | solution.py:343
  57.3 3.2 %tile_forward.3 = (bf16[2048,1024]{1,0:T(8,128)(2,1)}, f32[2048,128]{1,0:T(8,128)S(1)}) custom-call(s32[1]{0:T(128)} %bitcast.me_ref.refs_0_.core_ref, f32[64,4096]{1,0:T(8,128)S(1)} %bitcast.18, bf16[256,1024]{1,0:T(8,128)(2,1)S(1)} %get-tuple-element.24.refs_2_, bf16[1024,128]{1,0:T(8,128)(2,1)S(1)} %get-tuple-element.25.refs_3_), custom_call_target="tpu_custom_call" | custom-call | flops 1610612736 | bytes 4194304 | tf_op jit(solution)/shard_map/tile_forward/pallas_call | solution.py:163
  60.5 0.0 collective-permute-done.1
  60.5 0.1 add_convert_fusion
  60.6 12.8 %all_to_all.53 = bf16[8,256,128]{2,1,0:T(8,128)(2,1)S(1)} all-to-all(bf16[8,256,128]{2,1,0:T(8,128)(2,1)S(1)} %bitcast.20), channel_id=1, replica_groups=mesh['yh'=2,'z'=4,'yl'=2,'x'=4,'core'=2] {'yl','x'}, dimensions={0} | all-to-all | bytes 1048576 | tf_op jit(solution)/shard_map/all_to_all | solution.py:330
  73.4 0.1 reduce_sum.34
  73.4 0.1 broadcast_in_dim.31
  73.5 11.6 %all_to_all.54.refs_1_ = bf16[8,256,128]{2,1,0:T(8,128)(2,1)S(1)} all-to-all(bf16[8,256,128]{2,1,0:T(8,128)(2,1)S(1)} %broadcast_in_dim.31), channel_id=1, replica_groups=mesh['yh'=2,'z'=4,'yl'=2,'x'=4,'core'=2] {'yl','x'}, dimensions={0} | all-to-all | bytes 1048576 | tf_op jit(solution)/shard_map/all_to_all | solution.py:330
  85.1 1.9 %collective-permute-start.2 = (bf16[8,256,128]{2,1,0:T(8,128)(2,1)S(1)}, bf16[8,256,128]{2,1,0:T(8,128)(2,1)S(1)}, u32[]{:S(2)}, u32[]{:S(2)}) collective-permute-start(bf16[8,256,128]{2,1,0:T(8,128)(2,1)S(1)} %all_to_all.54.refs_1_), channel_id=1, source_target_pairs={{0,1},{1,0},{2,3},{3,2},{4,5},{5,4},{6,7},{7,6},{8,9},{9,8},{10,11... | collective-permute-start | bytes 1572872 | tf_op jit(solution)/shard_map/ppermute | solution.py:343
  87.0 0.0 copy-start.1
  87.0 2.2 %copy-done.1 = bf16[2048,1024]{1,0:T(8,128)(2,1)S(1)} copy-done((bf16[2048,1024]{1,0:T(8,128)(2,1)S(1)}, bf16[2048,1024]{1,0:T(8,128)(2,1)}, u32[]{:S(2)}) %copy-start.1) | copy-done | bytes 4194328
  89.2 0.0 copy-start.2
  89.2 0.7 tile_backward.2.refs_2_
  89.9 0.0 copy-start
  89.9 0.0 collective-permute-done.2.refs_1_
  89.9 1.4 copy-done.2
  91.3 0.8 tile_backward.3
  92.2 10.2 %all_to_all.55 = bf16[8,128,128]{2,1,0:T(8,128)(2,1)S(1)} all-to-all(bf16[8,128,128]{2,1,0:T(8,128)(2,1)S(1)} %bitcast.13), channel_id=1, replica_groups=mesh['yh'=2,'z'=4,'yl'=2,'x'=4,'core'=2] {'yh','z'}, dimensions={0} | all-to-all | bytes 524288 | tf_op jit(solution)/shard_map/all_to_all | solution.py:330
  102.5 11.5 %all_to_all.56 = bf16[8,128,128]{2,1,0:T(8,128)(2,1)S(1)} all-to-all(bf16[8,128,128]{2,1,0:T(8,128)(2,1)S(1)} %broadcast_in_dim.32), channel_id=1, replica_groups=mesh['yh'=2,'z'=4,'yl'=2,'x'=4,'core'=2] {'yh','z'}, dimensions={0} | all-to-all | bytes 524288 | tf_op jit(solution)/shard_map/all_to_all | solution.py:330
  113.9 0.0 copy-done
  114.0 0.9 precond_backward.3
  114.8 0.0 copy-start.4
  114.8 0.0 copy-start.5
  114.9 0.0 copy-start.6
  114.9 2.2 %collective-permute-start.3 = (f32[8,128,128]{2,1,0:T(8,128)S(1)}, f32[8,128,128]{2,1,0:T(8,128)S(1)}, u32[]{:S(2)}, u32[]{:S(2)}) collective-permute-start(f32[8,128,128]{2,1,0:T(8,128)S(1)} %precond_backward.3), channel_id=1, source_target_pairs={{0,1},{1,0},{2,3},{3,2},{4,5},{5,4},{6,7},{7,6},{8,9},{9,8},{10,11... | collective-permute-start | bytes 1572872 | tf_op jit(solution)/shard_map/ppermute | solution.py:343
  117.0 0.9 precond_backward.2
  117.9 0.7 collective-permute-done.3
  118.6 0.1 add_convert_fusion.1
  118.6 9.8 %all_to_all.57.part_ref = bf16[8,128,128]{2,1,0:T(8,128)(2,1)S(1)} all-to-all(bf16[8,128,128]{2,1,0:T(8,128)(2,1)S(1)} %add_convert_fusion.1), channel_id=1, replica_groups=mesh['yh'=2,'z'=4,'yl'=2,'x'=4,'core'=2] {'yl','x'}, dimensions={0} | all-to-all | bytes 524288 | tf_op jit(solution)/shard_map/all_to_all | solution.py:330
  128.5 0.0 copy-done.4
  128.5 0.0 copy-done.5
  128.5 0.2 image_numbers.1
  128.7 13.7 %all_to_all.58 = f32[128,1,128]{2,1,0:T(1,128)S(1)} all-to-all(f32[128,1,128]{2,1,0:T(1,128)S(1)} %bitcast.15), channel_id=1, replica_groups=mesh['yh'=2,'z'=4,'yl'=2,'x'=4,'core'=2] {'yh','z','yl','x','core'}, dimensions={0} | all-to-all | bytes 131072 | tf_op jit(solution)/shard_map/all_to_all | solution.py:330
  142.4 0.0 copy-done.6
  142.4 0.8 finish.1
  (3 shorter events, 0.1 us)
Async XLA Ops:
  0.6 0.8 copy-start.3
  2.2 12.2 %all-to-all-start = ((bf16[8,128,128]{2,1,0:T(8,128)(2,1)}), bf16[8,128,128]{2,1,0:T(8,128)(2,1)S(1)}, u32[]{:S(2)}, u32[]{:S(2)}) async-start(bf16[8,128,128]{2,1,0:T(8,128)(2,1)} %direction_copies.1), calls=%async_computation | async-start | bytes 524288 | tf_op jit(solution)/shard_map/all_to_all | solution.py:330
  8.1 1.2 copy-start.7
  9.3 0.7 copy-start.9
  12.8 38.2 %copy-start.8 = (f32[4096,64]{0,1:T(8,128)S(1)}, f32[4096,64]{0,1:T(8,128)}, u32[]{:S(2)}) copy-start(f32[4096,64]{0,1:T(8,128)} %param.6) | copy-start | bytes 3145732
  14.4 3.1 %collective-permute-start = (bf16[8,128,128]{2,1,0:T(8,128)(2,1)S(1)}, bf16[8,128,128]{2,1,0:T(8,128)(2,1)S(1)}, u32[]{:S(2)}, u32[]{:S(2)}) collective-permute-start(bf16[8,128,128]{2,1,0:T(8,128)(2,1)S(1)} %all-to-all-done.mine_ref), channel_id=1, source_target_pairs={{0,1},{1,0},{2,3},{3,2},{4,5},{5,4},{6,7},{7,6},{8,9},{9,8},{10,11... | collective-permute-start | bytes 786440 | tf_op jit(solution)/shard_map/ppermute | solution.py:343
  54.2 6.3 %collective-permute-start.1 = (bf16[2048,128]{1,0:T(8,128)(2,1)S(1)}, bf16[2048,128]{1,0:T(8,128)(2,1)S(1)}, u32[]{:S(2)}, u32[]{:S(2)}) collective-permute-start(bf16[2048,128]{1,0:T(8,128)(2,1)S(1)} %get-tuple-element.28), channel_id=1, source_target_pairs={{0,1},{1,0},{2,3},{3,2},{4,5},{5,4},{6,7},{7,6},{8,9},{9,8},{10,11... | collective-permute-start | bytes 1572872 | tf_op jit(solution)/shard_map/ppermute | solution.py:343
  85.1 4.8 %collective-permute-start.2 = (bf16[8,256,128]{2,1,0:T(8,128)(2,1)S(1)}, bf16[8,256,128]{2,1,0:T(8,128)(2,1)S(1)}, u32[]{:S(2)}, u32[]{:S(2)}) collective-permute-start(bf16[8,256,128]{2,1,0:T(8,128)(2,1)S(1)} %all_to_all.54.refs_1_), channel_id=1, source_target_pairs={{0,1},{1,0},{2,3},{3,2},{4,5},{5,4},{6,7},{7,6},{8,9},{9,8},{10,11... | collective-permute-start | bytes 1572872 | tf_op jit(solution)/shard_map/ppermute | solution.py:343
  87.0 2.2 %copy-start.1 = (bf16[2048,1024]{1,0:T(8,128)(2,1)S(1)}, bf16[2048,1024]{1,0:T(8,128)(2,1)}, u32[]{:S(2)}) copy-start(bf16[2048,1024]{1,0:T(8,128)(2,1)} %get-tuple-element.26.refs_0_) | copy-start | bytes 12582916
  89.2 2.2 %copy-start.2 = (bf16[2048,1024]{1,0:T(8,128)(2,1)S(1)}, bf16[2048,1024]{1,0:T(8,128)(2,1)}, u32[]{:S(2)}) copy-start(bf16[2048,1024]{1,0:T(8,128)(2,1)} %get-tuple-element.23.refs_0_) | copy-start | bytes 12582916
  89.9 24.0 %copy-start = (bf16[1024,2048]{1,0:T(8,128)(2,1)S(1)}, bf16[1024,2048]{1,0:T(8,128)(2,1)}, u32[]{:S(2)}) copy-start(bf16[1024,2048]{1,0:T(8,128)(2,1)} %pre_ref.5) | copy-start | bytes 12582916
  114.8 13.6 %copy-start.4 = (f32[128,128]{1,0:T(8,128)S(1)}, f32[128,128]{1,0:T(8,128)}, u32[]{:S(2)}) copy-start(f32[128,128]{1,0:T(8,128)} %dir_ref.5) | copy-start | bytes 196612
  114.8 13.6 %copy-start.5 = (f32[128,128]{1,0:T(8,128)S(1)}, f32[128,128]{1,0:T(8,128)}, u32[]{:S(2)}) copy-start(f32[128,128]{1,0:T(8,128)} %res_ref.3) | copy-start | bytes 196612
  114.9 27.6 %copy-start.6 = (f32[128,128]{1,0:T(8,128)S(1)}, f32[128,128]{1,0:T(8,128)}, u32[]{:S(2)}) copy-start(f32[128,128]{1,0:T(8,128)} %coef_ref.1) | copy-start | bytes 196612
  114.9 3.7 %collective-permute-start.3 = (f32[8,128,128]{2,1,0:T(8,128)S(1)}, f32[8,128,128]{2,1,0:T(8,128)S(1)}, u32[]{:S(2)}, u32[]{:S(2)}) collective-permute-start(f32[8,128,128]{2,1,0:T(8,128)S(1)} %precond_backward.3), channel_id=1, source_target_pairs={{0,1},{1,0},{2,3},{3,2},{4,5},{5,4},{6,7},{7,6},{8,9},{9,8},{10,11... | collective-permute-start | bytes 1572872 | tf_op jit(solution)/shard_map/ppermute | solution.py:343

commit v8 on v7

--- a/solution.py
+++ b/solution.py
@@ -119,7 +119,7 @@
 
 def tile_kernel(*refs, first):
     if first:
-        half_ref, feat_ref, got_ref, tile_ref, fit_ref, cen_ref, coef_ref, tile_here, sems = refs
+        half_ref, feat_ref, got_ref, tile_ref, fit_ref, cen_ref, coef_ref = refs
         parts, depth, width = got_ref.shape
         share = depth - 2 * FEAT
         for j in range(parts):
@@ -127,27 +127,21 @@
             cen_ref[:, j * width : (j + 1) * width] = operand(both[:FEAT], both[FEAT:], False)
             coef_ref[j * share : (j + 1) * share] = got_ref[j, :share]
     else:
-        half_ref, feat_ref, cen_ref, coef_ref, tile_ref, fit_ref, tile_here, sems = refs
-    blocks = sems.shape[0]
+        half_ref, feat_ref, cen_ref, coef_ref, tile_ref, fit_ref = refs
     n = fit_ref.shape[0]
-    block = n // blocks
-    stores = []
+    block = 256
+    blocks = n // block
     for j in range(blocks):
         here = slice(j * block, (j + 1) * block)
         place = pl.ds(pl.multiple_of(half_ref[0] * n + j * block, block), block)
         high, mid = split_pieces(feat_ref[:, place] * FEATURE_SCALE, 2)
         power = jnp.dot(operand(high, mid, True).T, cen_ref[...], preferred_element_type=F32)
         tile = jnp.exp2(power).astype(BF16)
-        tile_here[here] = tile
-        place = pl.ds(j * block, block)
-        stores.append(pltpu.make_async_copy(tile_here.at[place], tile_ref.at[place], sems.at[j]))
-        stores[-1].start()
+        tile_ref[here] = tile
         fit_ref[here] = jnp.dot(tile, coef_ref[...], preferred_element_type=F32).astype(fit_ref.dtype)
-    for store in stores:
-        store.wait()
-
-
-def tile_forward(half, feat, operands, fit_type, block=256):
+
+
+def tile_forward(half, feat, operands, fit_type):
     n = feat.shape[1] // 2
     first = len(operands) == 1
     if first:
@@ -163,9 +157,8 @@
     return pl.pallas_call(
         functools.partial(tile_kernel, first=first),
         in_specs=[SMEM, VMEM] + [VMEM] * len(operands),
-        out_specs=[HBM] + [VMEM] * (1 + len(more)),
-        out_shape=[pltpu.HBM((n, m), BF16), jax.ShapeDtypeStruct((n, OUTS), fit_type), *more],
-        scratch_shapes=[pltpu.VMEM((n, m), BF16), pltpu.SemaphoreType.DMA((n // block,))],
+        out_specs=[VMEM] * (2 + len(more)),
+        out_shape=[jax.ShapeDtypeStruct((n, m), BF16), jax.ShapeDtypeStruct((n, OUTS), fit_type), *more],
         compiler_params=params(),
         cost_estimate=cost(2 * n * m * 384, 2 * n * m, n * m),
         name="tile_forward",
@@ -330,13 +323,22 @@
     return lax.all_to_all(part, axes, 0, 0, tiled=True)
 
 
-def gathered(part, axes):
-    count = math.prod(lax.axis_size(axis) for axis in axes)
-    return spread(jnp.broadcast_to(part[None], (count, *part.shape)), axes)
-
-
-def summed(parts):
-    return jnp.sum(parts.astype(F32), axis=0)
+def sum_kernel(parts_ref, out_ref, *, scale):
+    total = jnp.sum(parts_ref[...].astype(F32), axis=0)
+    if scale is not None:
+        total = total * scale
+    out_ref[...] = jnp.broadcast_to(total.astype(BF16)[None], out_ref.shape)
+
+
+def all_summed(parts, axes, scale=None):
+    own = spread(parts, axes)
+    copies = pl.pallas_call(
+        functools.partial(sum_kernel, scale=scale),
+        out_shape=jax.ShapeDtypeStruct(parts.shape, BF16),
+        compiler_params=params(8),
+        name="sum_copies",
+    )(own)
+    return spread(copies, axes)
 
 
 def swapped(part):
@@ -358,8 +360,7 @@
     feat = train_rows.T
     picked = pick(start_row[None], centre_index[None], feat, row_devices)
     dir_mine, picked, other = lax.optimization_barrier((dir_mine, picked, other))
-    parts = spread(field(me, precond, dir_mine, swapped(dir_mine), picked), ROWS)
-    got = gathered(summed(parts).astype(BF16), ROWS)
+    got = all_summed(field(me, precond, dir_mine, swapped(dir_mine), picked), ROWS)
 
     chips_shape = (cen_devices // 2, rows_here // cen_devices, OUTS)
     tile_other, fit_other, cen_op, coef = tile_forward(other, feat, [got], BF16)
@@ -367,14 +368,13 @@
     tile_mine, fit_mine = tile_forward(me, feat, [cen_op, coef], F32)
     fit_mine, fit_came = lax.optimization_barrier((fit_mine, fit_came))
     half = (fit_mine + fit_came.astype(F32)).astype(BF16).reshape(chips_shape)
-    fitted = gathered(summed(spread(half, CHIPS)).astype(BF16), CHIPS)
+    fitted = all_summed(half, CHIPS)
     fitted_came = swapped(fitted)
     grad_mine = backward(tile_mine, fitted)
     grad_mine, fitted_came = lax.optimization_barrier((grad_mine, fitted_came))
     grad_part = backward(tile_other, fitted_came, grad_mine).reshape(row_devices, share, OUTS)
 
-    grad_sum = summed(spread(grad_part, ROWS)) * float(rows_here * row_devices) ** (-0.5)
-    grad_low = gathered(grad_sum.astype(BF16), ROWS).reshape(cen_here, OUTS)
+    grad_low = all_summed(grad_part, ROWS, float(rows_here * row_devices) ** (-0.5)).reshape(cen_here, OUTS)
 
     image_came = swapped(image_part(other, precond, grad_low, direction.shape[0]))
     image_mine = image_part(me, precond, grad_low, direction.shape[0])

time: 144 us -> 139 us (0.965)
  local copies, waits for them, and re-layouts: 6.56 us -> 2.77 us
    unnamed x20 -> x16, local copies, waits for them, and re-layouts: 6.39 us -> 2.77 us
    pallas_call x2, Pallas kernels: 6.43 us -> 4.9 us  [tile_forward(): pl.pallas_call(functools.partial(tile_kernel, first=first), in_specs=[SME...]
  transfers between devices with their start and end apart: 5 -> 5, of which waited for: 3 -> 4; matrix products, arithmetic and copies ran while one was open for 0% -> 0% of each run, Pallas kernels for 5% -> 5%
where the time goes in v8:
time: 139 us
  blocking collectives  99.4 us (72%)
  Pallas kernels  16.1 us (12%)
  starting transfers between devices  15.3 us (11%)
  waiting for transfers between devices  4.09 us (3%)
  local copies, waits for them, and re-layouts  2.77 us (2%)
    all_to_all x8, blocking collectives, spread(): return lax.all_to_all(part, axes, 0, 0, tiled=True)  99.4 us
    ppermute x4, starting transfers between devices, swapped(): return lax.ppermute(part, 'core', SWAP)  9.46 us
    all_to_all x1, starting transfers between devices, spread(): return lax.all_to_all(part, axes, 0, 0, tiled=True)  5.86 us
    pallas_call x2, Pallas kernels, tile_forward(): pl.pallas_call(functools.partial(tile_kernel, first=first), in_specs=[SME...  4.9 us
    pallas_call x1, Pallas kernels, field(): pl.pallas_call(field_kernel, in_specs=[SMEM, HBM, VMEM, VMEM, VMEM], out_...  2.98 us
    pallas_call x1, Pallas kernels, pick(): pl.pallas_call(pick_kernel, grid=(n // block,), in_specs=[pl.BlockSpec(me...  2.85 us
  transfers between devices with their start and end apart: 5, of which 4 were waited for; matrix products, arithmetic and copies ran while one was open for 0% of the time, Pallas kernels for 5%

profile of v8, /device:TPU:1, one launch (start us, length us, event | category | flops | bytes accessed | tf_op | source)
XLA Modules:
  0.0 138.6 jit_solution(13722651397021263213)
XLA Ops:
  0.6 0.0 copy-start.1
  0.6 0.8 copy-done.1
  1.5 0.7 direction_copies.1
  2.2 5.9 %all-to-all-start = ((bf16[8,128,128]{2,1,0:T(8,128)(2,1)}), bf16[8,128,128]{2,1,0:T(8,128)(2,1)S(1)}, u32[]{:S(2)}, u32[]{:S(2)}) async-start(bf16[8,128,128]{2,1,0:T(8,128)(2,1)} %direction_copies.1), calls=%async_computation | async-start | bytes 524288 | tf_op jit(solution)/shard_map/all_to_all | solution.py:323
  8.1 0.0 copy-start.5
  8.1 1.2 copy-done.5
  9.3 0.0 copy-start.7
  9.3 0.7 copy-done.7
  10.0 2.9 %pick_centres.1.feat_ref = bf16[8,128,128]{2,1,0:T(8,128)(2,1)S(1)} custom-call(s32[1]{0:T(128)} %bitcast.1.start_ref, s32[1,1024]{1,0:T(1,128)S(1)} %bitcast.19, f32[64,4096]{1,0:T(8,128)S(1)} %bitcast.16), custom_call_target="tpu_custom_call" | custom-call | flops 4294967296 | bytes 1048576 | tf_op jit(solution)/shard_map/pick_centres/pallas_call | solution.py:85
  12.8 0.0 copy-start.6
  12.8 1.5 %all-to-all-done.mine_ref = bf16[8,128,128]{2,1,0:T(8,128)(2,1)S(1)} async-done(((bf16[8,128,128]{2,1,0:T(8,128)(2,1)}), bf16[8,128,128]{2,1,0:T(8,128)(2,1)S(1)}, u32[]{:S(2)}, u32[]{:S(2)}) %all-to-all-start) | async-done | bytes 262176 | tf_op jit(solution)/shard_map/all_to_all | solution.py:323
  14.3 1.9 %collective-permute-start = (bf16[8,128,128]{2,1,0:T(8,128)(2,1)S(1)}, bf16[8,128,128]{2,1,0:T(8,128)(2,1)S(1)}, u32[]{:S(2)}, u32[]{:S(2)}) collective-permute-start(bf16[8,128,128]{2,1,0:T(8,128)(2,1)S(1)} %all-to-all-done.mine_ref), channel_id=1, source_target_pairs={{0,1},{1,0},{2,3},{3,2},{4,5},{5,4},{6,7},{7,6},{8,9},{9,8},{10,11... | collective-permute-start | bytes 786440 | tf_op jit(solution)/shard_map/ppermute | solution.py:345
  16.3 1.2 collective-permute-done.came_ref
  17.5 3.0 %precond_forward.1 = bf16[8,256,128]{2,1,0:T(8,128)(2,1)S(1)} custom-call(s32[1]{0:T(128)} %bitcast.me_ref.refs_0_.core_ref, bf16[1024,2048]{1,0:T(8,128)(2,1)} %pre_ref.5, bf16[8,128,128]{2,1,0:T(8,128)(2,1)S(1)} %all-to-all-done.mine_ref, bf16[8,128,128]{2,1,0:T(8,128)(2,1)S(1)} %collective-permute-done.came_ref, bf16[8,128,128]{2,1,0:T(8,128)(2,1)S(1)} %pick_centres.1.feat_ref), custom_call_target="tpu_custom_call" | custom-call | flops 536870912 | bytes 4194304 | tf_op jit(solution)/shard_map/precond_forward/pallas_call | solution.py:223
  20.4 17.2 %all_to_all.51.parts_ref = bf16[8,256,128]{2,1,0:T(8,128)(2,1)S(1)} all-to-all(bf16[8,256,128]{2,1,0:T(8,128)(2,1)S(1)} %precond_forward.1), channel_id=1, replica_groups=mesh['yh'=2,'z'=4,'yl'=2,'x'=4,'core'=2] {'yh','z'}, dimensions={0} | all-to-all | bytes 1048576 | tf_op jit(solution)/shard_map/all_to_all | solution.py:323
  37.6 0.1 sum_copies.3
  37.7 13.2 %all_to_all.52.refs_2_ = bf16[8,256,128]{2,1,0:T(8,128)(2,1)S(1)} all-to-all(bf16[8,256,128]{2,1,0:T(8,128)(2,1)S(1)} %sum_copies.3), channel_id=1, replica_groups=mesh['yh'=2,'z'=4,'yl'=2,'x'=4,'core'=2] {'yh','z'}, dimensions={0} | all-to-all | bytes 1048576 | tf_op jit(solution)/shard_map/all_to_all | solution.py:323
  50.9 0.0 copy-done.6
  50.9 2.5 %tile_forward.2 = (bf16[2048,1024]{1,0:T(8,128)(2,1)S(1)}, bf16[2048,128]{1,0:T(8,128)(2,1)S(1)}, bf16[256,1024]{1,0:T(8,128)(2,1)S(1)}, bf16[1024,128]{1,0:T(8,128)(2,1)S(1)}) custom-call(s32[1]{0:T(128)S(6)} %sub.3.refs_0_.core_ref, f32[64,4096]{1,0:T(8,128)S(1)} %bitcast.17, bf16[8,256,128]{2,1,0:T(8,128)(2,1)S(1)} %all_to_all.52.refs_2_), custom_call_target="tpu_custom_call" | custom-call | flops 1610612736 | bytes 4194304 | tf_op jit(solution)/shard_map/tile_forward/pallas_call | solution.py:157
  53.4 3.0 %collective-permute-start.1 = (bf16[2048,128]{1,0:T(8,128)(2,1)S(1)}, bf16[2048,128]{1,0:T(8,128)(2,1)S(1)}, u32[]{:S(2)}, u32[]{:S(2)}) collective-permute-start(bf16[2048,128]{1,0:T(8,128)(2,1)S(1)} %get-tuple-element.28), channel_id=1, source_target_pairs={{0,1},{1,0},{2,3},{3,2},{4,5},{5,4},{6,7},{7,6},{8,9},{9,8},{10,11... | collective-permute-start | bytes 1572872 | tf_op jit(solution)/shard_map/ppermute | solution.py:345
  56.4 2.4 %tile_forward.3 = (bf16[2048,1024]{1,0:T(8,128)(2,1)S(1)}, f32[2048,128]{1,0:T(8,128)S(1)}) custom-call(s32[1]{0:T(128)} %bitcast.me_ref.refs_0_.core_ref, f32[64,4096]{1,0:T(8,128)S(1)} %bitcast.18, bf16[256,1024]{1,0:T(8,128)(2,1)S(1)} %get-tuple-element.24.refs_2_, bf16[1024,128]{1,0:T(8,128)(2,1)S(1)} %get-tuple-element.25.refs_3_), custom_call_target="tpu_custom_call" | custom-call | flops 1610612736 | bytes 4194304 | tf_op jit(solution)/shard_map/tile_forward/pallas_call | solution.py:157
  58.9 0.0 collective-permute-done.1
  58.9 0.1 add_convert_fusion
  59.0 12.8 %all_to_all.53.parts_ref = bf16[8,256,128]{2,1,0:T(8,128)(2,1)S(1)} all-to-all(bf16[8,256,128]{2,1,0:T(8,128)(2,1)S(1)} %bitcast.20), channel_id=1, replica_groups=mesh['yh'=2,'z'=4,'yl'=2,'x'=4,'core'=2] {'yl','x'}, dimensions={0} | all-to-all | bytes 1048576 | tf_op jit(solution)/shard_map/all_to_all | solution.py:323
  71.7 0.1 sum_copies.4
  71.8 11.6 %all_to_all.54.refs_1_ = bf16[8,256,128]{2,1,0:T(8,128)(2,1)S(1)} all-to-all(bf16[8,256,128]{2,1,0:T(8,128)(2,1)S(1)} %sum_copies.4), channel_id=1, replica_groups=mesh['yh'=2,'z'=4,'yl'=2,'x'=4,'core'=2] {'yl','x'}, dimensions={0} | all-to-all | bytes 1048576 | tf_op jit(solution)/shard_map/all_to_all | solution.py:323
  83.4 1.9 %collective-permute-start.2 = (bf16[8,256,128]{2,1,0:T(8,128)(2,1)S(1)}, bf16[8,256,128]{2,1,0:T(8,128)(2,1)S(1)}, u32[]{:S(2)}, u32[]{:S(2)}) collective-permute-start(bf16[8,256,128]{2,1,0:T(8,128)(2,1)S(1)} %all_to_all.54.refs_1_), channel_id=1, source_target_pairs={{0,1},{1,0},{2,3},{3,2},{4,5},{5,4},{6,7},{7,6},{8,9},{9,8},{10,11... | collective-permute-start | bytes 1572872 | tf_op jit(solution)/shard_map/ppermute | solution.py:345
  85.3 0.7 tile_backward.2.refs_2_
  86.0 0.0 copy-start
  86.0 0.8 collective-permute-done.2.refs_1_
  86.8 0.8 tile_backward.3
  87.7 10.2 %all_to_all.55.parts_ref = bf16[8,128,128]{2,1,0:T(8,128)(2,1)S(1)} all-to-all(bf16[8,128,128]{2,1,0:T(8,128)(2,1)S(1)} %bitcast.13), channel_id=1, replica_groups=mesh['yh'=2,'z'=4,'yl'=2,'x'=4,'core'=2] {'yh','z'}, dimensions={0} | all-to-all | bytes 524288 | tf_op jit(solution)/shard_map/all_to_all | solution.py:323
  97.9 10.9 %all_to_all.56 = bf16[8,128,128]{2,1,0:T(8,128)(2,1)S(1)} all-to-all(bf16[8,128,128]{2,1,0:T(8,128)(2,1)S(1)} %sum_copies.5), channel_id=1, replica_groups=mesh['yh'=2,'z'=4,'yl'=2,'x'=4,'core'=2] {'yh','z'}, dimensions={0} | all-to-all | bytes 524288 | tf_op jit(solution)/shard_map/all_to_all | solution.py:323
  108.7 0.0 copy-done
  108.7 0.9 precond_backward.3
  109.6 0.0 copy-start.2
  109.6 0.0 copy-start.3
  109.7 0.0 copy-start.4
  109.7 2.6 %collective-permute-start.3 = (f32[8,128,128]{2,1,0:T(8,128)S(1)}, f32[8,128,128]{2,1,0:T(8,128)S(1)}, u32[]{:S(2)}, u32[]{:S(2)}) collective-permute-start(f32[8,128,128]{2,1,0:T(8,128)S(1)} %precond_backward.3), channel_id=1, source_target_pairs={{0,1},{1,0},{2,3},{3,2},{4,5},{5,4},{6,7},{7,6},{8,9},{9,8},{10,11... | collective-permute-start | bytes 1572872 | tf_op jit(solution)/shard_map/ppermute | solution.py:345
  112.3 0.9 precond_backward.2
  113.2 0.7 collective-permute-done.3
  113.8 0.1 add_convert_fusion.1
  113.9 9.8 %all_to_all.57.part_ref = bf16[8,128,128]{2,1,0:T(8,128)(2,1)S(1)} all-to-all(bf16[8,128,128]{2,1,0:T(8,128)(2,1)S(1)} %add_convert_fusion.1), channel_id=1, replica_groups=mesh['yh'=2,'z'=4,'yl'=2,'x'=4,'core'=2] {'yl','x'}, dimensions={0} | all-to-all | bytes 524288 | tf_op jit(solution)/shard_map/all_to_all | solution.py:323
  123.7 0.0 copy-done.2
  123.7 0.0 copy-done.3
  123.7 0.2 image_numbers.1
  124.0 13.8 %all_to_all.58 = f32[128,1,128]{2,1,0:T(1,128)S(1)} all-to-all(f32[128,1,128]{2,1,0:T(1,128)S(1)} %bitcast.15), channel_id=1, replica_groups=mesh['yh'=2,'z'=4,'yl'=2,'x'=4,'core'=2] {'yh','z','yl','x','core'}, dimensions={0} | all-to-all | bytes 131072 | tf_op jit(solution)/shard_map/all_to_all | solution.py:323
  137.7 0.0 copy-done.4
  137.7 0.8 finish.1
  (1 shorter events, 0.0 us)
Async XLA Ops:
  0.6 0.8 copy-start.1
  2.2 12.2 %all-to-all-start = ((bf16[8,128,128]{2,1,0:T(8,128)(2,1)}), bf16[8,128,128]{2,1,0:T(8,128)(2,1)S(1)}, u32[]{:S(2)}, u32[]{:S(2)}) async-start(bf16[8,128,128]{2,1,0:T(8,128)(2,1)} %direction_copies.1), calls=%async_computation | async-start | bytes 524288 | tf_op jit(solution)/shard_map/all_to_all | solution.py:323
  8.1 1.2 copy-start.5
  9.3 0.7 copy-start.7
  12.8 38.1 %copy-start.6 = (f32[4096,64]{0,1:T(8,128)S(1)}, f32[4096,64]{0,1:T(8,128)}, u32[]{:S(2)}) copy-start(f32[4096,64]{0,1:T(8,128)} %param.6) | copy-start | bytes 3145732
  14.3 3.1 %collective-permute-start = (bf16[8,128,128]{2,1,0:T(8,128)(2,1)S(1)}, bf16[8,128,128]{2,1,0:T(8,128)(2,1)S(1)}, u32[]{:S(2)}, u32[]{:S(2)}) collective-permute-start(bf16[8,128,128]{2,1,0:T(8,128)(2,1)S(1)} %all-to-all-done.mine_ref), channel_id=1, source_target_pairs={{0,1},{1,0},{2,3},{3,2},{4,5},{5,4},{6,7},{7,6},{8,9},{9,8},{10,11... | collective-permute-start | bytes 786440 | tf_op jit(solution)/shard_map/ppermute | solution.py:345
  53.4 5.5 %collective-permute-start.1 = (bf16[2048,128]{1,0:T(8,128)(2,1)S(1)}, bf16[2048,128]{1,0:T(8,128)(2,1)S(1)}, u32[]{:S(2)}, u32[]{:S(2)}) collective-permute-start(bf16[2048,128]{1,0:T(8,128)(2,1)S(1)} %get-tuple-element.28), channel_id=1, source_target_pairs={{0,1},{1,0},{2,3},{3,2},{4,5},{5,4},{6,7},{7,6},{8,9},{9,8},{10,11... | collective-permute-start | bytes 1572872 | tf_op jit(solution)/shard_map/ppermute | solution.py:345
  83.4 3.4 %collective-permute-start.2 = (bf16[8,256,128]{2,1,0:T(8,128)(2,1)S(1)}, bf16[8,256,128]{2,1,0:T(8,128)(2,1)S(1)}, u32[]{:S(2)}, u32[]{:S(2)}) collective-permute-start(bf16[8,256,128]{2,1,0:T(8,128)(2,1)S(1)} %all_to_all.54.refs_1_), channel_id=1, source_target_pairs={{0,1},{1,0},{2,3},{3,2},{4,5},{5,4},{6,7},{7,6},{8,9},{9,8},{10,11... | collective-permute-start | bytes 1572872 | tf_op jit(solution)/shard_map/ppermute | solution.py:345
  86.0 22.7 %copy-start = (bf16[1024,2048]{1,0:T(8,128)(2,1)S(1)}, bf16[1024,2048]{1,0:T(8,128)(2,1)}, u32[]{:S(2)}) copy-start(bf16[1024,2048]{1,0:T(8,128)(2,1)} %pre_ref.5) | copy-start | bytes 12582916
  109.6 14.1 %copy-start.2 = (f32[128,128]{1,0:T(8,128)S(1)}, f32[128,128]{1,0:T(8,128)}, u32[]{:S(2)}) copy-start(f32[128,128]{1,0:T(8,128)} %dir_ref.5) | copy-start | bytes 196612
  109.6 14.1 %copy-start.3 = (f32[128,128]{1,0:T(8,128)S(1)}, f32[128,128]{1,0:T(8,128)}, u32[]{:S(2)}) copy-start(f32[128,128]{1,0:T(8,128)} %res_ref.3) | copy-start | bytes 196612
  109.7 28.1 %copy-start.4 = (f32[128,128]{1,0:T(8,128)S(1)}, f32[128,128]{1,0:T(8,128)}, u32[]{:S(2)}) copy-start(f32[128,128]{1,0:T(8,128)} %coef_ref.1) | copy-start | bytes 196612
  109.7 4.1 %collective-permute-start.3 = (f32[8,128,128]{2,1,0:T(8,128)S(1)}, f32[8,128,128]{2,1,0:T(8,128)S(1)}, u32[]{:S(2)}, u32[]{:S(2)}) collective-permute-start(f32[8,128,128]{2,1,0:T(8,128)S(1)} %precond_backward.3), channel_id=1, source_target_pairs={{0,1},{1,0},{2,3},{3,2},{4,5},{5,4},{6,7},{7,6},{8,9},{9,8},{10,11... | collective-permute-start | bytes 1572872 | tf_op jit(solution)/shard_map/ppermute | solution.py:345

commit v9 on v8

--- a/solution.py
+++ b/solution.py
@@ -21,6 +21,11 @@
 CENT = ("yl", "x", "core")
 FEATURE_SCALE = math.sqrt(2.0 * (2.0 / FEAT) * math.log2(math.e))
 SWAP = [(0, 1), (1, 0)]
+
+
+VMEM = pl.BlockSpec(memory_space=pltpu.VMEM)
+SMEM = pl.BlockSpec(memory_space=pltpu.SMEM)
+HBM = pl.BlockSpec(memory_space=pltpu.HBM)
 
 
 def params(limit=16):
@@ -58,45 +63,98 @@
     return jnp.concatenate([high, *middle, tail], axis=0)
 
 
-def pick_kernel(start_ref, index_ref, feat_ref, out_ref, total_ref):
-    step = pl.program_id(0)
-    block = feat_ref.shape[1]
-
-    @pl.when(step == 0)
-    def _():
-        total_ref[...] = jnp.zeros_like(total_ref)
-
-    table = jnp.concatenate(split_pieces(feat_ref[...] * FEATURE_SCALE, 2), axis=0)
-    wanted = index_ref[...] - (start_ref[0] + step * block)
-    place = lax.broadcasted_iota(jnp.int32, (block, wanted.shape[1]), 0)
-    choice = jnp.where(place == wanted, 1.0, 0.0).astype(BF16)
-    total_ref[...] += jnp.dot(table, choice, preferred_element_type=F32)
-
-    @pl.when(step == pl.num_programs(0) - 1)
-    def _():
-        for j in range(out_ref.shape[0]):
-            width = out_ref.shape[2]
-            out_ref[j] = total_ref[:, j * width : (j + 1) * width].astype(BF16)
-
-
-def pick(start, index, feat, parts, block=512):
+def pick_kernel(place_ref, index_hbm, feat_hbm, *refs, ring):
+    parts = refs[:ring]
+    feat_ref, index_ref, total_ref, sems = refs[ring:]
+    n = feat_ref.shape[1]
+    m = index_ref.shape[1]
+    pieces = sems.shape[0] - 1
+    wide = n // pieces
+    copies = [pltpu.make_async_copy(index_hbm, index_ref, sems.at[0])]
+    for j in range(pieces):
+        here = pl.ds(j * wide, wide)
+        copies.append(pltpu.make_async_copy(feat_hbm.at[:, here], feat_ref.at[:, here], sems.at[1 + j]))
+    for copy in copies:
+        copy.start()
+    copies[0].wait()
+    block = 512
+    for j in range(n // block):
+        if j * block % wide == 0:
+            copies[1 + j * block // wide].wait()
+        here = slice(j * block, (j + 1) * block)
+        table = jnp.concatenate(split_pieces(feat_ref[:, here] * FEATURE_SCALE, 2), axis=0)
+        wanted = index_ref[...] - (place_ref[0] + j * block)
+        row = lax.broadcasted_iota(jnp.int32, (block, m), 0)
+        choice = jnp.where(row == wanted, 1.0, 0.0).astype(BF16)
+        part = jnp.dot(table, choice, preferred_element_type=F32)
+        if j == 0:
+            total_ref[...] = part
+        else:
+            total_ref[...] += part
+    width = m // ring
+    for k in range(ring):
+        first = pl.multiple_of(lax.rem(place_ref[1] + k, ring) * width, width)
+        parts[k][...] = total_ref[:, pl.ds(first, width)].astype(BF16)
+
+
+def pick(place, index, feat, ring, pieces=4):
     depth, n = feat.shape
     m = index.shape[1]
     return pl.pallas_call(
-        pick_kernel,
-        grid=(n // block,),
-        in_specs=[
-            pl.BlockSpec(memory_space=pltpu.SMEM),
-            pl.BlockSpec((1, m), lambda i: (0, 0)),
-            pl.BlockSpec((depth, block), lambda i: (0, i)),
+        functools.partial(pick_kernel, ring=ring),
+        in_specs=[SMEM, HBM, HBM],
+        out_specs=[VMEM] * ring,
+        out_shape=[jax.ShapeDtypeStruct((2 * depth, m // ring), BF16)] * ring,
+        scratch_shapes=[
+            pltpu.VMEM(feat.shape, F32),
+            pltpu.VMEM((1, m), jnp.int32),
+            pltpu.VMEM((2 * depth, m), F32),
+            pltpu.SemaphoreType.DMA((1 + pieces,)),
         ],
-        out_specs=pl.BlockSpec((parts, 2 * depth, m // parts), lambda i: (0, 0, 0)),
-        out_shape=jax.ShapeDtypeStruct((parts, 2 * depth, m // parts), BF16),
-        scratch_shapes=[pltpu.VMEM((2 * depth, m), F32)],
         compiler_params=params(),
         cost_estimate=cost(2 * n * m * 128 * 4, n * depth * 4),
         name="pick_centres",
-    )(start, index, feat)
+    )(place, in_hbm(index), in_hbm(feat))
+
+
+def load_kernel(source, out_ref, sems):
+    pieces = sems.shape[0]
+    tall = source.shape[0] // pieces
+    copies = [
+        pltpu.make_async_copy(source.at[pl.ds(j * tall, tall)], out_ref.at[pl.ds(j * tall, tall)], sems.at[j])
+        for j in range(pieces)
+    ]
+    for copy in copies:
+        copy.start()
+    for copy in copies:
+        copy.wait()
+
+
+def loaded(source, pieces=2):
+    return pl.pallas_call(
+        load_kernel,
+        in_specs=[HBM],
+        out_specs=VMEM,
+        out_shape=jax.ShapeDtypeStruct(source.shape, source.dtype),
+        scratch_shapes=[pltpu.SemaphoreType.DMA((pieces,))],
+        compiler_params=params(8),
+        cost_estimate=cost(0, 2 * source.size),
+        name="precond_load",
+    )(in_hbm(source))
+
+
+def add_kernel(*refs):
+    *parts, out_ref = refs
+    out_ref[...] = sum(part[...].astype(F32) for part in parts).astype(BF16)
+
+
+def added(*parts):
+    return pl.pallas_call(
+        add_kernel,
+        out_shape=jax.ShapeDtypeStruct(parts[0].shape, BF16),
+        compiler_params=params(8),
+        name="features_sum",
+    )(*parts)
 
 
 def send_kernel(dir_ref, out_ref):
@@ -112,26 +170,18 @@
     )(direction)
 
 
-VMEM = pl.BlockSpec(memory_space=pltpu.VMEM)
-SMEM = pl.BlockSpec(memory_space=pltpu.SMEM)
-HBM = pl.BlockSpec(memory_space=pltpu.HBM)
-
-
-def tile_kernel(*refs, first):
+def tile_kernel(place_ref, half_ref, feat_ref, coef_ref, *refs, first):
+    tile_ref, fit_ref, cen_ref = refs[-3:] if first else (*refs[1:], refs[0])
     if first:
-        half_ref, feat_ref, got_ref, tile_ref, fit_ref, cen_ref, coef_ref = refs
-        parts, depth, width = got_ref.shape
-        share = depth - 2 * FEAT
-        for j in range(parts):
-            both = got_ref[j, share:]
-            cen_ref[:, j * width : (j + 1) * width] = operand(both[:FEAT], both[FEAT:], False)
-            coef_ref[j * share : (j + 1) * share] = got_ref[j, :share]
-    else:
-        half_ref, feat_ref, cen_ref, coef_ref, tile_ref, fit_ref = refs
+        parts = refs[:-3]
+        ring = len(parts)
+        width = parts[0].shape[1]
+        for k in range(ring):
+            start = pl.multiple_of(lax.rem(place_ref[1] + ring - k, ring) * width, width)
+            cen_ref[:, pl.ds(start, width)] = operand(parts[k][:FEAT], parts[k][FEAT:], False)
     n = fit_ref.shape[0]
     block = 256
-    blocks = n // block
-    for j in range(blocks):
+    for j in range(n // block):
         here = slice(j * block, (j + 1) * block)
         place = pl.ds(pl.multiple_of(half_ref[0] * n + j * block, block), block)
         high, mid = split_pieces(feat_ref[:, place] * FEATURE_SCALE, 2)
@@ -141,28 +191,19 @@
         fit_ref[here] = jnp.dot(tile, coef_ref[...], preferred_element_type=F32).astype(fit_ref.dtype)
 
 
-def tile_forward(half, feat, operands, fit_type):
-    n = feat.shape[1] // 2
-    first = len(operands) == 1
-    if first:
-        parts, depth, width = operands[0].shape
-        m = parts * width
-        more = [
-            jax.ShapeDtypeStruct((256, m), BF16),
-            jax.ShapeDtypeStruct((parts * (depth - 2 * FEAT), OUTS), BF16),
-        ]
-    else:
-        m = operands[0].shape[1]
-        more = []
+def tile_forward(place, half, feat, coef, centres, fit_type):
+    n, m = feat.shape[1] // 2, coef.shape[0]
+    first = len(centres) > 1
+    more = [jax.ShapeDtypeStruct((256, m), BF16)] * first
     return pl.pallas_call(
         functools.partial(tile_kernel, first=first),
-        in_specs=[SMEM, VMEM] + [VMEM] * len(operands),
+        in_specs=[SMEM, SMEM] + [VMEM] * (2 + len(centres)),
         out_specs=[VMEM] * (2 + len(more)),
         out_shape=[jax.ShapeDtypeStruct((n, m), BF16), jax.ShapeDtypeStruct((n, OUTS), fit_type), *more],
         compiler_params=params(),
         cost_estimate=cost(2 * n * m * 384, 2 * n * m, n * m),
         name="tile_forward",
-    )(half, feat, *operands)
+    )(place, half, feat, coef, *centres)
 
 
 def back_kernel(*refs, last):
@@ -192,44 +233,27 @@
     )(tile, fitted, *([before] if last else []))
 
 
-def field_kernel(me_ref, pre_ref, mine_ref, came_ref, feat_ref, out_ref, pre_here, dir_here, sems):
-    parts = out_ref.shape[0]
-    width = out_ref.shape[1] - 2 * FEAT
-    blocks = sems.shape[0]
-    block = pre_ref.shape[0] // blocks
-    copies = [
-        pltpu.make_async_copy(pre_ref.at[pl.ds(j * block, block)], pre_here.at[pl.ds(j * block, block)], sems.at[j])
-        for j in range(blocks)
-    ]
-    for copy in copies:
-        copy.start()
+def field_kernel(me_ref, pre_ref, mine_ref, came_ref, out_ref, dir_here):
     me = me_ref[0]
     chips, share, _ = mine_ref.shape
     for j in range(chips):
         dir_here[pl.ds(pl.multiple_of((2 * j + me) * share, share), share)] = mine_ref[j]
         dir_here[pl.ds(pl.multiple_of((2 * j + 1 - me) * share, share), share)] = came_ref[j]
-    for j in range(parts):
-        out_ref[j, width:] = feat_ref[j]
-    for j in range(blocks):
-        copies[j].wait()
-        part = jnp.dot(pre_here[j * block : (j + 1) * block], dir_here[...], preferred_element_type=F32).astype(BF16)
-        for k in range(block // width):
-            out_ref[j * (block // width) + k, :width] = part[k * width : (k + 1) * width]
-
-
-def field(me, precond, mine, came, feat_parts, blocks=4):
+    out_ref[...] = jnp.dot(pre_ref[...], dir_here[...], preferred_element_type=F32).astype(BF16)
+
+
+def field(me, precond, mine, came):
     n, m = precond.shape
-    parts = feat_parts.shape[0]
     return pl.pallas_call(
         field_kernel,
-        in_specs=[SMEM, HBM, VMEM, VMEM, VMEM],
+        in_specs=[SMEM, VMEM, VMEM, VMEM],
         out_specs=VMEM,
-        out_shape=jax.ShapeDtypeStruct((parts, n // parts + 2 * FEAT, OUTS), BF16),
-        scratch_shapes=[pltpu.VMEM((n, m), BF16), pltpu.VMEM((m, OUTS), BF16), pltpu.SemaphoreType.DMA((blocks,))],
+        out_shape=jax.ShapeDtypeStruct((n, OUTS), BF16),
+        scratch_shapes=[pltpu.VMEM((m, OUTS), BF16)],
         compiler_params=params(),
         cost_estimate=cost(2 * n * m * OUTS, 2 * n * m),
         name="precond_forward",
-    )(me, in_hbm(precond), mine, came, feat_parts)
+    )(me, precond, mine, came)
 
 
 def image_kernel(core_ref, pre_ref, grad_ref, out_ref):
@@ -330,15 +354,17 @@
     out_ref[...] = jnp.broadcast_to(total.astype(BF16)[None], out_ref.shape)
 
 
-def all_summed(parts, axes, scale=None):
-    own = spread(parts, axes)
-    copies = pl.pallas_call(
+def sum_copies(parts, scale=None):
+    return pl.pallas_call(
         functools.partial(sum_kernel, scale=scale),
         out_shape=jax.ShapeDtypeStruct(parts.shape, BF16),
         compiler_params=params(8),
         name="sum_copies",
-    )(own)
-    return spread(copies, axes)
+    )(parts)
+
+
+def all_summed(parts, axes, scale=None):
+    return spread(sum_copies(spread(parts, axes), scale), axes)
 
 
 def swapped(part):
@@ -351,21 +377,34 @@
     row_devices = lax.axis_size("yh") * lax.axis_size("z")
     cen_devices = lax.axis_size("yl") * lax.axis_size("x") * lax.axis_size("core")
     me = lax.axis_index("core").astype(jnp.int32)[None]
-    start_row = (lax.axis_index(ROWS) * rows_here).astype(jnp.int32)
+    other = 1 - me
+    ring = lax.axis_size("z")
+    place = jnp.stack([lax.axis_index(ROWS) * rows_here, lax.axis_index("z")]).astype(jnp.int32)
     share = cen_here // row_devices
 
-    other = 1 - me
+    def onward(part, by):
+        return lax.ppermute(part, "z", [(i, (i + by) % ring) for i in range(ring)])
+
     dir_mine = spread(copies_of(direction, cen_devices // 2), CHIPS)
 
     feat = train_rows.T
-    picked = pick(start_row[None], centre_index[None], feat, row_devices)
-    dir_mine, picked, other = lax.optimization_barrier((dir_mine, picked, other))
-    got = all_summed(field(me, precond, dir_mine, swapped(dir_mine), picked), ROWS)
+    picked = pick(place, centre_index[None], feat, ring)
+    dir_mine, *picked = lax.optimization_barrier((dir_mine, *picked))
+    came = [picked[0]] + [onward(picked[k], k) for k in range(1, ring)]
+    dir_mine, own_precond, other = lax.optimization_barrier((dir_mine, precond, other))
+    field_part = field(me, loaded(own_precond), dir_mine, swapped(dir_mine))
+    field_part, came[0] = lax.optimization_barrier((field_part, came[0]))
+    own = added(*came)
+    own = added(own, lax.ppermute(own, "yh", SWAP))
+    features = [own] + [onward(own, k) for k in range(1, ring)]
+    copies = sum_copies(spread(field_part.reshape(row_devices, share, OUTS), ROWS))
+    copies, features = lax.optimization_barrier((copies, features))
+    coef = spread(copies, ROWS).reshape(cen_here, OUTS)
 
     chips_shape = (cen_devices // 2, rows_here // cen_devices, OUTS)
-    tile_other, fit_other, cen_op, coef = tile_forward(other, feat, [got], BF16)
+    tile_other, fit_other, cen_op = tile_forward(place, other, feat, coef, features, BF16)
     fit_came = swapped(fit_other)
-    tile_mine, fit_mine = tile_forward(me, feat, [cen_op, coef], F32)
+    tile_mine, fit_mine = tile_forward(place, me, feat, coef, [cen_op], F32)
     fit_mine, fit_came = lax.optimization_barrier((fit_mine, fit_came))
     half = (fit_mine + fit_came.astype(F32)).astype(BF16).reshape(chips_shape)
     fitted = all_summed(half, CHIPS)

time: 139 us -> 152 us (1.094)
  starting transfers between devices: 15.3 us -> 35.8 us
  blocking collectives: 99.4 us -> 81.5 us
  waiting for transfers between devices: 4.09 us -> 13.8 us
  Pallas kernels: 16.1 us -> 18.8 us
  local copies, waits for them, and re-layouts: 2.77 us -> 0.87 us
    all_to_all x8 -> x7, blocking collectives: 99.4 us -> 81.5 us  [spread(): return lax.all_to_all(part, axes, 0, 0, tiled=True)]
    ppermute x0 -> x7, starting transfers between devices: none -> 11.2 us  [the longest x6 7.83 us: onward(): return lax.ppermute(part, 'z', [(i, (i + by) % ring) for i in range(ring)])]
    ppermute x0 -> x7, waiting for transfers between devices: none -> 9.3 us  [the longest x6 7.64 us: onward(): return lax.ppermute(part, 'z', [(i, (i + by) % ring) for i in range(ring)])]
    all_to_all x1 -> x2, starting transfers between devices: 5.86 us -> 13.2 us  [spread(): return lax.all_to_all(part, axes, 0, 0, tiled=True)]
    ppermute x4, starting transfers between devices: 9.46 us -> 11.4 us  [swapped(): return lax.ppermute(part, 'core', SWAP)]
    unnamed x16 -> x12, local copies, waits for them, and re-layouts: 2.77 us -> 0.87 us
    pallas_call x5 -> x8, Pallas kernels: 6.02 us -> 7.62 us  [the longest x1 3.16 us: pick(): pl.pallas_call(functools.partial(pick_kernel, ring=ring), in_specs=[SMEM,...]
    all_to_all x1 -> x2, waiting for transfers between devices: 1.51 us -> 3.05 us  [spread(): return lax.all_to_all(part, axes, 0, 0, tiled=True)]
  transfers between devices with their start and end apart: 5 -> 13, of which waited for: 4 -> 9; matrix products, arithmetic and copies ran while one was open for 0% -> 0% of each run, Pallas kernels for 5% -> 7%
where the time goes in v9:
time: 152 us
  blocking collectives  81.5 us (54%)
  starting transfers between devices  35.8 us (24%)
  Pallas kernels  18.8 us (12%)
  waiting for transfers between devices  13.8 us (9%)
    all_to_all x7, blocking collectives, spread(): return lax.all_to_all(part, axes, 0, 0, tiled=True)  81.5 us
    all_to_all x2, starting transfers between devices, spread(): return lax.all_to_all(part, axes, 0, 0, tiled=True)  13.2 us
    ppermute x4, starting transfers between devices, swapped(): return lax.ppermute(part, 'core', SWAP)  11.4 us
    ppermute x6, starting transfers between devices, onward(): return lax.ppermute(part, 'z', [(i, (i + by) % ring) for i in range(ring)])  7.83 us
    ppermute x6, waiting for transfers between devices, onward(): return lax.ppermute(part, 'z', [(i, (i + by) % ring) for i in range(ring)])  7.64 us
    pallas_call x2, Pallas kernels, tile_forward(): pl.pallas_call(functools.partial(tile_kernel, first=first), in_specs=[SME...  6.02 us
    ppermute x1, starting transfers between devices, on_device(): own = added(own, lax.ppermute(own, 'yh', SWAP))  3.36 us
    pallas_call x1, Pallas kernels, pick(): pl.pallas_call(functools.partial(pick_kernel, ring=ring), in_specs=[SMEM,...  3.16 us
  transfers between devices with their start and end apart: 13, of which 9 were waited for; matrix products, arithmetic and copies ran while one was open for 0% of the time, Pallas kernels for 7%

profile of v9, /device:TPU:1, one launch (start us, length us, event | category | flops | bytes accessed | tf_op | source)
XLA Modules:
  0.0 151.7 jit_solution(7513050092698461363)
XLA Ops:
  0.6 0.0 copy-start.1
  0.6 0.8 copy-done.1
  1.5 0.7 direction_copies.1
  2.2 5.9 %all-to-all-start = ((bf16[8,128,128]{2,1,0:T(8,128)(2,1)}), bf16[8,128,128]{2,1,0:T(8,128)(2,1)S(1)}, u32[]{:S(2)}, u32[]{:S(2)}) async-start(bf16[8,128,128]{2,1,0:T(8,128)(2,1)} %direction_copies.1), calls=%async_computation | async-start | bytes 524288 | tf_op jit(solution)/shard_map/all_to_all | solution.py:347
  8.1 0.1 pad_add_fusion.place_ref
  8.1 3.2 %pick_centres.1 = (bf16[128,256]{1,0:T(8,128)(2,1)S(1)}, bf16[128,256]{1,0:T(8,128)(2,1)S(1)}, bf16[128,256]{1,0:T(8,128)(2,1)S(1)}, bf16[128,256]{1,0:T(8,128)(2,1)S(1)}) custom-call(s32[2]{0:T(128)S(1)} %pad_add_fusion.place_ref, s32[1,1024]{1,0:T(1,128)} %bitcast.25, f32[64,4096]{1,0:T(8,128)} %bitcast.21), custom_call_target="tpu_custom_call" | custom-call | flops 4294967296 | bytes 1048576 | tf_op jit(solution)/shard_map/pick_centres/pallas_call | solution.py:103
  11.3 3.0 %all-to-all-done.mine_ref = bf16[8,128,128]{2,1,0:T(8,128)(2,1)S(1)} async-done(((bf16[8,128,128]{2,1,0:T(8,128)(2,1)}), bf16[8,128,128]{2,1,0:T(8,128)(2,1)S(1)}, u32[]{:S(2)}, u32[]{:S(2)}) %all-to-all-start) | async-done | bytes 262176 | tf_op jit(solution)/shard_map/all_to_all | solution.py:347
  14.4 1.9 %collective-permute-start = (bf16[8,128,128]{2,1,0:T(8,128)(2,1)S(1)}, bf16[8,128,128]{2,1,0:T(8,128)(2,1)S(1)}, u32[]{:S(2)}, u32[]{:S(2)}) collective-permute-start(bf16[8,128,128]{2,1,0:T(8,128)(2,1)S(1)} %all-to-all-done.mine_ref), channel_id=1, source_target_pairs={{0,1},{1,0},{2,3},{3,2},{4,5},{5,4},{6,7},{7,6},{8,9},{9,8},{10,11... | collective-permute-start | bytes 786440 | tf_op jit(solution)/shard_map/ppermute | solution.py:371
  16.3 2.2 %precond_load.1.pre_ref = bf16[1024,2048]{1,0:T(8,128)(2,1)S(1)} custom-call(bf16[1024,2048]{1,0:T(8,128)(2,1)} %pre_ref.3), custom_call_target="tpu_custom_call" | custom-call | bytes 4194304 | tf_op jit(solution)/shard_map/precond_load/pallas_call | solution.py:134
  18.6 0.0 copy-start.5
  18.6 0.0 collective-permute-done.came_ref
  18.6 2.0 %precond_forward.1 = bf16[1024,128]{1,0:T(8,128)(2,1)} custom-call(s32[1]{0:T(128)} %bitcast.me_ref.half_ref.core_ref, bf16[1024,2048]{1,0:T(8,128)(2,1)S(1)} %precond_load.1.pre_ref, bf16[8,128,128]{2,1,0:T(8,128)(2,1)S(1)} %all-to-all-done.mine_ref, bf16[8,128,128]{2,1,0:T(8,128)(2,1)S(1)} %collective-permute-done.came_ref), custom_call_target="tpu_custom_call" | custom-call | flops 536870912 | bytes 4194304 | tf_op jit(solution)/shard_map/precond_forward/pallas_call | solution.py:247
  20.6 7.4 %all-to-all-start.1 = ((bf16[8,128,128]{2,1,0:T(8,128)(2,1)}), bf16[8,128,128]{2,1,0:T(8,128)(2,1)S(1)}, u32[]{:S(2)}, u32[]{:S(2)}) async-start(bf16[8,128,128]{2,1,0:T(8,128)(2,1)} %bitcast.5), calls=%async_computation.1 | async-start | bytes 524288 | tf_op jit(solution)/shard_map/all_to_all | solution.py:347
  28.0 1.5 collective-permute-start.1
  29.4 2.4 %collective-permute-start.2 = (bf16[128,256]{1,0:T(8,128)(2,1)S(1)}, bf16[128,256]{1,0:T(8,128)(2,1)S(1)}, u32[]{:S(2)}, u32[]{:S(2)}) collective-permute-start(bf16[128,256]{1,0:T(8,128)(2,1)S(1)} %get-tuple-element.47), channel_id=1, source_target_pairs={{0,32},{16,48},{32,0},{48,16},{1,33},{17,49},{33,1},{49,17},{2,34}... | collective-permute-start | bytes 196616 | tf_op jit(solution)/shard_map/ppermute | solution.py:386
  31.8 1.2 collective-permute-start.3
  33.0 1.6 %collective-permute-done.1.refs_1_ = bf16[128,256]{1,0:T(8,128)(2,1)S(1)} collective-permute-done((bf16[128,256]{1,0:T(8,128)(2,1)S(1)}, bf16[128,256]{1,0:T(8,128)(2,1)S(1)}, u32[]{:S(2)}, u32[]{:S(2)}) %collective-permute-start.1) | collective-permute-done | bytes 65568 | tf_op jit(solution)/shard_map/ppermute | solution.py:386
  34.6 2.4 %collective-permute-done.2.refs_2_ = bf16[128,256]{1,0:T(8,128)(2,1)S(1)} collective-permute-done((bf16[128,256]{1,0:T(8,128)(2,1)S(1)}, bf16[128,256]{1,0:T(8,128)(2,1)S(1)}, u32[]{:S(2)}, u32[]{:S(2)}) %collective-permute-start.2) | collective-permute-done | bytes 65568 | tf_op jit(solution)/shard_map/ppermute | solution.py:386
  37.0 0.0 collective-permute-done.3.refs_3_
  37.0 3.4 %collective-permute-start.4 = (bf16[128,256]{1,0:T(8,128)(2,1)S(1)}, bf16[128,256]{1,0:T(8,128)(2,1)S(1)}, u32[]{:S(2)}, u32[]{:S(2)}) collective-permute-start(bf16[128,256]{1,0:T(8,128)(2,1)S(1)} %features_sum.2.refs_0_), channel_id=1, source_target_pairs={{0,64},{64,0},{1,65},{65,1},{2,66},{66,2},{3,67},{67,3},{4,68},{68... | collective-permute-start | bytes 196616 | tf_op jit(solution)/shard_map/ppermute | solution.py:398
  40.4 1.7 %collective-permute-done.4.refs_1_ = bf16[128,256]{1,0:T(8,128)(2,1)S(1)} collective-permute-done((bf16[128,256]{1,0:T(8,128)(2,1)S(1)}, bf16[128,256]{1,0:T(8,128)(2,1)S(1)}, u32[]{:S(2)}, u32[]{:S(2)}) %collective-permute-start.4) | collective-permute-done | bytes 65568 | tf_op jit(solution)/shard_map/ppermute | solution.py:398
  42.1 1.0 collective-permute-start.7
  43.0 1.2 collective-permute-start.6
  44.2 0.6 collective-permute-start.5
  44.9 0.0 all-to-all-done.1.parts_ref
  44.9 0.3 collective-permute-done.7.refs_3_
  45.3 2.4 %collective-permute-done.6.refs_2_ = bf16[128,256]{1,0:T(8,128)(2,1)S(1)} collective-permute-done((bf16[128,256]{1,0:T(8,128)(2,1)S(1)}, bf16[128,256]{1,0:T(8,128)(2,1)S(1)}, u32[]{:S(2)}, u32[]{:S(2)}) %collective-permute-start.6) | collective-permute-done | bytes 65568 | tf_op jit(solution)/shard_map/ppermute | solution.py:386
  47.7 0.9 collective-permute-done.5.refs_1_
  48.6 12.0 %all_to_all.51 = bf16[8,128,128]{2,1,0:T(8,128)(2,1)S(1)} all-to-all(bf16[8,128,128]{2,1,0:T(8,128)(2,1)S(1)} %sum_copies.3), channel_id=1, replica_groups=mesh['yh'=2,'z'=4,'yl'=2,'x'=4,'core'=2] {'yh','z'}, dimensions={0} | all-to-all | bytes 524288 | tf_op jit(solution)/shard_map/all_to_all | solution.py:347
  60.6 0.0 copy-done.5
  60.6 3.1 %tile_forward.2 = (bf16[2048,1024]{1,0:T(8,128)(2,1)S(1)}, bf16[2048,128]{1,0:T(8,128)(2,1)S(1)}, bf16[256,1024]{1,0:T(8,128)(2,1)S(1)}) custom-call(s32[2]{0:T(128)S(1)} %pad_add_fusion.place_ref, s32[1]{0:T(128)S(6)} %sub.3.half_ref.core_ref, f32[64,4096]{1,0:T(8,128)S(1)} %bitcast.22, bf16[1024,128]{1,0:T(8,128)(2,1)S(1)} %bitcast.18, ...), custom_call_target="tpu_custom_call" | custom-call | flops 1610612736 | bytes 4194304 | tf_op jit(solution)/shard_map/tile_forward/pallas_call | solution.py:198
  63.7 5.3 %collective-permute-start.8 = (bf16[2048,128]{1,0:T(8,128)(2,1)S(1)}, bf16[2048,128]{1,0:T(8,128)(2,1)S(1)}, u32[]{:S(2)}, u32[]{:S(2)}) collective-permute-start(bf16[2048,128]{1,0:T(8,128)(2,1)S(1)} %get-tuple-element.58), channel_id=1, source_target_pairs={{0,1},{1,0},{2,3},{3,2},{4,5},{5,4},{6,7},{7,6},{8,9},{9,8},{10,11... | collective-permute-start | bytes 1572872 | tf_op jit(solution)/shard_map/ppermute | solution.py:371
  69.0 3.0 %tile_forward.3 = (bf16[2048,1024]{1,0:T(8,128)(2,1)S(1)}, f32[2048,128]{1,0:T(8,128)S(1)}) custom-call(s32[2]{0:T(128)S(1)} %pad_add_fusion.place_ref, s32[1]{0:T(128)} %bitcast.me_ref.half_ref.core_ref, f32[64,4096]{1,0:T(8,128)S(1)} %bitcast.23, bf16[1024,128]{1,0:T(8,128)(2,1)S(1)} %bitcast.19, bf16[256,1024]{1,0:T(8,128)(2,1)S(1)} %get-tuple-element.55.refs_0_), custom_call_target="tpu_custom_call" | custom-call | flops 1610612736 | bytes 4194304 | tf_op jit(solution)/shard_map/tile_forward/pallas_call | solution.py:198
  72.0 0.0 collective-permute-done.8
  72.0 0.1 add_convert_fusion
  72.1 12.7 %all_to_all.52.parts_ref = bf16[8,256,128]{2,1,0:T(8,128)(2,1)S(1)} all-to-all(bf16[8,256,128]{2,1,0:T(8,128)(2,1)S(1)} %bitcast.24), channel_id=1, replica_groups=mesh['yh'=2,'z'=4,'yl'=2,'x'=4,'core'=2] {'yl','x'}, dimensions={0} | all-to-all | bytes 1048576 | tf_op jit(solution)/shard_map/all_to_all | solution.py:347
  84.8 0.1 sum_copies.4
  84.9 11.6 %all_to_all.53.refs_1_ = bf16[8,256,128]{2,1,0:T(8,128)(2,1)S(1)} all-to-all(bf16[8,256,128]{2,1,0:T(8,128)(2,1)S(1)} %sum_copies.4), channel_id=1, replica_groups=mesh['yh'=2,'z'=4,'yl'=2,'x'=4,'core'=2] {'yl','x'}, dimensions={0} | all-to-all | bytes 1048576 | tf_op jit(solution)/shard_map/all_to_all | solution.py:347
  96.5 1.9 %collective-permute-start.9 = (bf16[8,256,128]{2,1,0:T(8,128)(2,1)S(1)}, bf16[8,256,128]{2,1,0:T(8,128)(2,1)S(1)}, u32[]{:S(2)}, u32[]{:S(2)}) collective-permute-start(bf16[8,256,128]{2,1,0:T(8,128)(2,1)S(1)} %all_to_all.53.refs_1_), channel_id=1, source_target_pairs={{0,1},{1,0},{2,3},{3,2},{4,5},{5,4},{6,7},{7,6},{8,9},{9,8},{10,11... | collective-permute-start | bytes 1572872 | tf_op jit(solution)/shard_map/ppermute | solution.py:371
  98.4 0.7 tile_backward.2.refs_2_
  99.1 0.0 copy-start
  99.1 0.8 collective-permute-done.9.refs_1_
  99.9 0.8 tile_backward.3
  100.7 10.0 %all_to_all.54.parts_ref = bf16[8,128,128]{2,1,0:T(8,128)(2,1)S(1)} all-to-all(bf16[8,128,128]{2,1,0:T(8,128)(2,1)S(1)} %bitcast.16), channel_id=1, replica_groups=mesh['yh'=2,'z'=4,'yl'=2,'x'=4,'core'=2] {'yh','z'}, dimensions={0} | all-to-all | bytes 524288 | tf_op jit(solution)/shard_map/all_to_all | solution.py:347
  110.8 11.3 %all_to_all.55 = bf16[8,128,128]{2,1,0:T(8,128)(2,1)S(1)} all-to-all(bf16[8,128,128]{2,1,0:T(8,128)(2,1)S(1)} %sum_copies.5), channel_id=1, replica_groups=mesh['yh'=2,'z'=4,'yl'=2,'x'=4,'core'=2] {'yh','z'}, dimensions={0} | all-to-all | bytes 524288 | tf_op jit(solution)/shard_map/all_to_all | solution.py:347
  122.1 0.0 copy-done
  122.1 0.9 precond_backward.3
  122.9 0.0 copy-start.2
  123.0 0.0 copy-start.3
  123.0 0.0 copy-start.4
  123.0 2.2 %collective-permute-start.10 = (f32[8,128,128]{2,1,0:T(8,128)S(1)}, f32[8,128,128]{2,1,0:T(8,128)S(1)}, u32[]{:S(2)}, u32[]{:S(2)}) collective-permute-start(f32[8,128,128]{2,1,0:T(8,128)S(1)} %precond_backward.3), channel_id=1, source_target_pairs={{0,1},{1,0},{2,3},{3,2},{4,5},{5,4},{6,7},{7,6},{8,9},{9,8},{10,11... | collective-permute-start | bytes 1572872 | tf_op jit(solution)/shard_map/ppermute | solution.py:371
  125.2 0.9 precond_backward.2
  126.1 0.7 collective-permute-done.10
  126.7 0.1 add_convert_fusion.1
  126.8 9.8 %all_to_all.56.part_ref = bf16[8,128,128]{2,1,0:T(8,128)(2,1)S(1)} all-to-all(bf16[8,128,128]{2,1,0:T(8,128)(2,1)S(1)} %add_convert_fusion.1), channel_id=1, replica_groups=mesh['yh'=2,'z'=4,'yl'=2,'x'=4,'core'=2] {'yl','x'}, dimensions={0} | all-to-all | bytes 524288 | tf_op jit(solution)/shard_map/all_to_all | solution.py:347
  136.6 0.0 copy-done.2
  136.6 0.0 copy-done.3
  136.6 0.2 image_numbers.1
  136.9 14.0 %all_to_all.57 = f32[128,1,128]{2,1,0:T(1,128)S(1)} all-to-all(f32[128,1,128]{2,1,0:T(1,128)S(1)} %bitcast.20), channel_id=1, replica_groups=mesh['yh'=2,'z'=4,'yl'=2,'x'=4,'core'=2] {'yh','z','yl','x','core'}, dimensions={0} | all-to-all | bytes 131072 | tf_op jit(solution)/shard_map/all_to_all | solution.py:347
  150.9 0.0 copy-done.4
  150.9 0.8 finish.1
  (4 shorter events, 0.1 us)
Async XLA Ops:
  0.6 0.8 copy-start.1
  2.2 12.2 %all-to-all-start = ((bf16[8,128,128]{2,1,0:T(8,128)(2,1)}), bf16[8,128,128]{2,1,0:T(8,128)(2,1)S(1)}, u32[]{:S(2)}, u32[]{:S(2)}) async-start(bf16[8,128,128]{2,1,0:T(8,128)(2,1)} %direction_copies.1), calls=%async_computation | async-start | bytes 524288 | tf_op jit(solution)/shard_map/all_to_all | solution.py:347
  14.4 4.2 %collective-permute-start = (bf16[8,128,128]{2,1,0:T(8,128)(2,1)S(1)}, bf16[8,128,128]{2,1,0:T(8,128)(2,1)S(1)}, u32[]{:S(2)}, u32[]{:S(2)}) collective-permute-start(bf16[8,128,128]{2,1,0:T(8,128)(2,1)S(1)} %all-to-all-done.mine_ref), channel_id=1, source_target_pairs={{0,1},{1,0},{2,3},{3,2},{4,5},{5,4},{6,7},{7,6},{8,9},{9,8},{10,11... | collective-permute-start | bytes 786440 | tf_op jit(solution)/shard_map/ppermute | solution.py:371
  18.6 42.0 %copy-start.5 = (f32[4096,64]{0,1:T(8,128)S(1)}, f32[4096,64]{0,1:T(8,128)}, u32[]{:S(2)}) copy-start(f32[4096,64]{0,1:T(8,128)} %param.6) | copy-start | bytes 3145732
  20.6 24.3 %all-to-all-start.1 = ((bf16[8,128,128]{2,1,0:T(8,128)(2,1)}), bf16[8,128,128]{2,1,0:T(8,128)(2,1)S(1)}, u32[]{:S(2)}, u32[]{:S(2)}) async-start(bf16[8,128,128]{2,1,0:T(8,128)(2,1)} %bitcast.5), calls=%async_computation.1 | async-start | bytes 524288 | tf_op jit(solution)/shard_map/all_to_all | solution.py:347
  28.0 6.6 %collective-permute-start.1 = (bf16[128,256]{1,0:T(8,128)(2,1)S(1)}, bf16[128,256]{1,0:T(8,128)(2,1)S(1)}, u32[]{:S(2)}, u32[]{:S(2)}) collective-permute-start(bf16[128,256]{1,0:T(8,128)(2,1)S(1)} %get-tuple-element.46), channel_id=1, source_target_pairs={{0,16},{16,32},{32,48},{48,0},{1,17},{17,33},{33,49},{49,1},{2,18}... | collective-permute-start | bytes 196616 | tf_op jit(solution)/shard_map/ppermute | solution.py:386
  29.4 7.6 %collective-permute-start.2 = (bf16[128,256]{1,0:T(8,128)(2,1)S(1)}, bf16[128,256]{1,0:T(8,128)(2,1)S(1)}, u32[]{:S(2)}, u32[]{:S(2)}) collective-permute-start(bf16[128,256]{1,0:T(8,128)(2,1)S(1)} %get-tuple-element.47), channel_id=1, source_target_pairs={{0,32},{16,48},{32,0},{48,16},{1,33},{17,49},{33,1},{49,17},{2,34}... | collective-permute-start | bytes 196616 | tf_op jit(solution)/shard_map/ppermute | solution.py:386
  31.8 5.2 %collective-permute-start.3 = (bf16[128,256]{1,0:T(8,128)(2,1)S(1)}, bf16[128,256]{1,0:T(8,128)(2,1)S(1)}, u32[]{:S(2)}, u32[]{:S(2)}) collective-permute-start(bf16[128,256]{1,0:T(8,128)(2,1)S(1)} %get-tuple-element.48), channel_id=1, source_target_pairs={{0,48},{16,0},{32,16},{48,32},{1,49},{17,1},{33,17},{49,33},{2,50}... | collective-permute-start | bytes 196616 | tf_op jit(solution)/shard_map/ppermute | solution.py:386
  37.0 5.0 %collective-permute-start.4 = (bf16[128,256]{1,0:T(8,128)(2,1)S(1)}, bf16[128,256]{1,0:T(8,128)(2,1)S(1)}, u32[]{:S(2)}, u32[]{:S(2)}) collective-permute-start(bf16[128,256]{1,0:T(8,128)(2,1)S(1)} %features_sum.2.refs_0_), channel_id=1, source_target_pairs={{0,64},{64,0},{1,65},{65,1},{2,66},{66,2},{3,67},{67,3},{4,68},{68... | collective-permute-start | bytes 196616 | tf_op jit(solution)/shard_map/ppermute | solution.py:398
  42.1 3.2 %collective-permute-start.7 = (bf16[128,256]{1,0:T(8,128)(2,1)S(1)}, bf16[128,256]{1,0:T(8,128)(2,1)S(1)}, u32[]{:S(2)}, u32[]{:S(2)}) collective-permute-start(bf16[128,256]{1,0:T(8,128)(2,1)S(1)} %features_sum.3.refs_0_), channel_id=1, source_target_pairs={{0,48},{16,0},{32,16},{48,32},{1,49},{17,1},{33,17},{49,33},{2,50}... | collective-permute-start | bytes 196616 | tf_op jit(solution)/shard_map/ppermute | solution.py:386
  43.0 4.6 %collective-permute-start.6 = (bf16[128,256]{1,0:T(8,128)(2,1)S(1)}, bf16[128,256]{1,0:T(8,128)(2,1)S(1)}, u32[]{:S(2)}, u32[]{:S(2)}) collective-permute-start(bf16[128,256]{1,0:T(8,128)(2,1)S(1)} %features_sum.3.refs_0_), channel_id=1, source_target_pairs={{0,32},{16,48},{32,0},{48,16},{1,33},{17,49},{33,1},{49,17},{2,34}... | collective-permute-start | bytes 196616 | tf_op jit(solution)/shard_map/ppermute | solution.py:386
  44.2 4.3 %collective-permute-start.5 = (bf16[128,256]{1,0:T(8,128)(2,1)S(1)}, bf16[128,256]{1,0:T(8,128)(2,1)S(1)}, u32[]{:S(2)}, u32[]{:S(2)}) collective-permute-start(bf16[128,256]{1,0:T(8,128)(2,1)S(1)} %features_sum.3.refs_0_), channel_id=1, source_target_pairs={{0,16},{16,32},{32,48},{48,0},{1,17},{17,33},{33,49},{49,1},{2,18}... | collective-permute-start | bytes 196616 | tf_op jit(solution)/shard_map/ppermute | solution.py:386
  63.7 8.3 %collective-permute-start.8 = (bf16[2048,128]{1,0:T(8,128)(2,1)S(1)}, bf16[2048,128]{1,0:T(8,128)(2,1)S(1)}, u32[]{:S(2)}, u32[]{:S(2)}) collective-permute-start(bf16[2048,128]{1,0:T(8,128)(2,1)S(1)} %get-tuple-element.58), channel_id=1, source_target_pairs={{0,1},{1,0},{2,3},{3,2},{4,5},{5,4},{6,7},{7,6},{8,9},{9,8},{10,11... | collective-permute-start | bytes 1572872 | tf_op jit(solution)/shard_map/ppermute | solution.py:371
  96.5 3.4 %collective-permute-start.9 = (bf16[8,256,128]{2,1,0:T(8,128)(2,1)S(1)}, bf16[8,256,128]{2,1,0:T(8,128)(2,1)S(1)}, u32[]{:S(2)}, u32[]{:S(2)}) collective-permute-start(bf16[8,256,128]{2,1,0:T(8,128)(2,1)S(1)} %all_to_all.53.refs_1_), channel_id=1, source_target_pairs={{0,1},{1,0},{2,3},{3,2},{4,5},{5,4},{6,7},{7,6},{8,9},{9,8},{10,11... | collective-permute-start | bytes 1572872 | tf_op jit(solution)/shard_map/ppermute | solution.py:371
  99.1 22.9 %copy-start = (bf16[1024,2048]{1,0:T(8,128)(2,1)S(1)}, bf16[1024,2048]{1,0:T(8,128)(2,1)}, u32[]{:S(2)}) copy-start(bf16[1024,2048]{1,0:T(8,128)(2,1)} %pre_ref.3) | copy-start | bytes 12582916
  122.9 13.7 %copy-start.2 = (f32[128,128]{1,0:T(8,128)S(1)}, f32[128,128]{1,0:T(8,128)}, u32[]{:S(2)}) copy-start(f32[128,128]{1,0:T(8,128)} %dir_ref.5) | copy-start | bytes 196612
  123.0 13.7 %copy-start.3 = (f32[128,128]{1,0:T(8,128)S(1)}, f32[128,128]{1,0:T(8,128)}, u32[]{:S(2)}) copy-start(f32[128,128]{1,0:T(8,128)} %res_ref.3) | copy-start | bytes 196612
  123.0 27.9 %copy-start.4 = (f32[128,128]{1,0:T(8,128)S(1)}, f32[128,128]{1,0:T(8,128)}, u32[]{:S(2)}) copy-start(f32[128,128]{1,0:T(8,128)} %coef_ref.1) | copy-start | bytes 196612
  123.0 3.7 %collective-permute-start.10 = (f32[8,128,128]{2,1,0:T(8,128)S(1)}, f32[8,128,128]{2,1,0:T(8,128)S(1)}, u32[]{:S(2)}, u32[]{:S(2)}) collective-permute-start(f32[8,128,128]{2,1,0:T(8,128)S(1)} %precond_backward.3), channel_id=1, source_target_pairs={{0,1},{1,0},{2,3},{3,2},{4,5},{5,4},{6,7},{7,6},{8,9},{9,8},{10,11... | collective-permute-start | bytes 1572872 | tf_op jit(solution)/shard_map/ppermute | solution.py:371

commit v10 on v8

--- a/solution.py
+++ b/solution.py
@@ -21,6 +21,11 @@
 CENT = ("yl", "x", "core")
 FEATURE_SCALE = math.sqrt(2.0 * (2.0 / FEAT) * math.log2(math.e))
 SWAP = [(0, 1), (1, 0)]
+
+
+VMEM = pl.BlockSpec(memory_space=pltpu.VMEM)
+SMEM = pl.BlockSpec(memory_space=pltpu.SMEM)
+HBM = pl.BlockSpec(memory_space=pltpu.HBM)
 
 
 def params(limit=16):
@@ -99,22 +104,32 @@
     )(start, index, feat)
 
 
-def send_kernel(dir_ref, out_ref):
-    out_ref[...] = jnp.broadcast_to(dir_ref[...].astype(BF16)[None], out_ref.shape)
+def send_kernel(dir_hbm, out_hbm, dir_ref, low_ref, sems):
+    load = pltpu.make_async_copy(dir_hbm, dir_ref, sems.at[0])
+    load.start()
+    load.wait()
+    low_ref[...] = dir_ref[...].astype(BF16)
+    stores = [pltpu.make_async_copy(low_ref, out_hbm.at[j], sems.at[1 + j]) for j in range(out_hbm.shape[0])]
+    for store in stores:
+        store.start()
+    for store in stores:
+        store.wait()
 
 
 def copies_of(direction, count):
     return pl.pallas_call(
         send_kernel,
-        out_shape=jax.ShapeDtypeStruct((count, *direction.shape), BF16),
-        compiler_params=params(),
+        in_specs=[HBM],
+        out_specs=HBM,
+        out_shape=pltpu.HBM((count, *direction.shape), BF16),
+        scratch_shapes=[
+            pltpu.VMEM(direction.shape, F32),
+            pltpu.VMEM(direction.shape, BF16),
+            pltpu.SemaphoreType.DMA((1 + count,)),
+        ],
+        compiler_params=params(8),
         name="direction_copies",
-    )(direction)
-
-
-VMEM = pl.BlockSpec(memory_space=pltpu.VMEM)
-SMEM = pl.BlockSpec(memory_space=pltpu.SMEM)
-HBM = pl.BlockSpec(memory_space=pltpu.HBM)
+    )(in_hbm(direction))
 
 
 def tile_kernel(*refs, first):
@@ -192,44 +207,73 @@
     )(tile, fitted, *([before] if last else []))
 
 
-def field_kernel(me_ref, pre_ref, mine_ref, came_ref, feat_ref, out_ref, pre_here, dir_here, sems):
-    parts = out_ref.shape[0]
-    width = out_ref.shape[1] - 2 * FEAT
+def core_columns(pre_ref, here, core, width, count):
+    return jnp.concatenate(
+        [pre_ref[here, pl.ds(pl.multiple_of((2 * j + core) * width, width), width)] for j in range(count)], axis=1
+    )
+
+
+def field_first_kernel(core_ref, pre_hbm, dir_ref, out_ref, pre_ref, sems):
     blocks = sems.shape[0]
     block = pre_ref.shape[0] // blocks
     copies = [
-        pltpu.make_async_copy(pre_ref.at[pl.ds(j * block, block)], pre_here.at[pl.ds(j * block, block)], sems.at[j])
+        pltpu.make_async_copy(pre_hbm.at[pl.ds(j * block, block)], pre_ref.at[pl.ds(j * block, block)], sems.at[j])
         for j in range(blocks)
     ]
     for copy in copies:
         copy.start()
-    me = me_ref[0]
-    chips, share, _ = mine_ref.shape
-    for j in range(chips):
-        dir_here[pl.ds(pl.multiple_of((2 * j + me) * share, share), share)] = mine_ref[j]
-        dir_here[pl.ds(pl.multiple_of((2 * j + 1 - me) * share, share), share)] = came_ref[j]
-    for j in range(parts):
-        out_ref[j, width:] = feat_ref[j]
+    count, width, outs = dir_ref.shape
+    direction = dir_ref[...].reshape(count * width, outs)
     for j in range(blocks):
         copies[j].wait()
-        part = jnp.dot(pre_here[j * block : (j + 1) * block], dir_here[...], preferred_element_type=F32).astype(BF16)
-        for k in range(block // width):
-            out_ref[j * (block // width) + k, :width] = part[k * width : (k + 1) * width]
-
-
-def field(me, precond, mine, came, feat_parts, blocks=4):
+        here = slice(j * block, (j + 1) * block)
+        columns = core_columns(pre_ref, here, core_ref[0], width, count)
+        out_ref[here] = jnp.dot(columns, direction, preferred_element_type=F32)
+
+
+def field_first(core, precond, direction, blocks=4):
+    n, m = precond.shape
+    return pl.pallas_call(
+        field_first_kernel,
+        in_specs=[SMEM, HBM, VMEM],
+        out_specs=[VMEM, VMEM],
+        out_shape=[jax.ShapeDtypeStruct((n, OUTS), F32), jax.ShapeDtypeStruct((n, m), BF16)],
+        scratch_shapes=[pltpu.SemaphoreType.DMA((blocks,))],
+        compiler_params=params(),
+        cost_estimate=cost(n * m * OUTS, 4 * n * m),
+        name="precond_first",
+    )(core, in_hbm(precond), direction)
+
+
+def field_second_kernel(core_ref, pre_ref, dir_ref, before_ref, feat_ref, out_ref):
+    parts = out_ref.shape[0]
+    share = out_ref.shape[1] - 2 * FEAT
+    count, width, outs = dir_ref.shape
+    direction = dir_ref[...].reshape(count * width, outs)
+    block = 256
+    for j in range(pre_ref.shape[0] // block):
+        here = slice(j * block, (j + 1) * block)
+        columns = core_columns(pre_ref, here, core_ref[0], width, count)
+        part = jnp.dot(columns, direction, preferred_element_type=F32) + before_ref[here]
+        part = part.astype(BF16)
+        for k in range(block // share):
+            out_ref[j * (block // share) + k, :share] = part[k * share : (k + 1) * share]
+    for j in range(parts):
+        out_ref[j, share:] = feat_ref[j]
+
+
+def field_second(core, precond, direction, before, feat_parts):
     n, m = precond.shape
     parts = feat_parts.shape[0]
     return pl.pallas_call(
-        field_kernel,
-        in_specs=[SMEM, HBM, VMEM, VMEM, VMEM],
+        field_second_kernel,
+        in_specs=[SMEM, VMEM, VMEM, VMEM, VMEM],
         out_specs=VMEM,
         out_shape=jax.ShapeDtypeStruct((parts, n // parts + 2 * FEAT, OUTS), BF16),
-        scratch_shapes=[pltpu.VMEM((n, m), BF16), pltpu.VMEM((m, OUTS), BF16), pltpu.SemaphoreType.DMA((blocks,))],
-        compiler_params=params(),
-        cost_estimate=cost(2 * n * m * OUTS, 2 * n * m),
-        name="precond_forward",
-    )(me, in_hbm(precond), mine, came, feat_parts)
+        compiler_params=params(),
+        cost_estimate=cost(n * m * OUTS, n * m),
+        name="precond_second",
+    )(core, precond, direction, before, feat_parts)
 
 
 def image_kernel(core_ref, pre_ref, grad_ref, out_ref):
@@ -360,7 +404,10 @@
     feat = train_rows.T
     picked = pick(start_row[None], centre_index[None], feat, row_devices)
     dir_mine, picked, other = lax.optimization_barrier((dir_mine, picked, other))
-    got = all_summed(field(me, precond, dir_mine, swapped(dir_mine), picked), ROWS)
+    dir_came = swapped(dir_mine)
+    first, precond = field_first(me, precond, dir_mine)
+    first, dir_came = lax.optimization_barrier((first, dir_came))
+    got = all_summed(field_second(other, precond, dir_came, first, picked), ROWS)
 
     chips_shape = (cen_devices // 2, rows_here // cen_devices, OUTS)
     tile_other, fit_other, cen_op, coef = tile_forward(other, feat, [got], BF16)

time: 139 us -> 139 us (level)
  blocking collectives: 99.4 us -> 101 us
    pallas_call x2 -> x3, Pallas kernels: 3.69 us -> 4.91 us  [the longest x1 2.51 us: field_first(): pl.pallas_call(field_first_kernel, in_specs=[SMEM, HBM, VMEM], out_specs=...]
  transfers between devices with their start and end apart: 5 -> 5, of which waited for: 4 -> 3; matrix products, arithmetic and copies ran while one was open for 0% -> 0% of each run, Pallas kernels for 5% -> 7%
where the time goes in v10:
time: 139 us
  blocking collectives  101 us (73%)
  Pallas kernels  17.2 us (12%)
  starting transfers between devices  14.8 us (11%)
  waiting for transfers between devices  2.98 us (2%)
  local copies, waits for them, and re-layouts  1.93 us (1%)
    all_to_all x8, blocking collectives, spread(): return lax.all_to_all(part, axes, 0, 0, tiled=True)  101 us
    ppermute x4, starting transfers between devices, swapped(): return lax.ppermute(part, 'core', SWAP)  8.96 us
    all_to_all x1, starting transfers between devices, spread(): return lax.all_to_all(part, axes, 0, 0, tiled=True)  5.87 us
    pallas_call x2, Pallas kernels, tile_forward(): pl.pallas_call(functools.partial(tile_kernel, first=first), in_specs=[SME...  4.9 us
    pallas_call x1, Pallas kernels, pick(): pl.pallas_call(pick_kernel, grid=(n // block,), in_specs=[pl.BlockSpec(me...  2.84 us
  transfers between devices with their start and end apart: 5, of which 3 were waited for; matrix products, arithmetic and copies ran while one was open for 0% of the time, Pallas kernels for 7%

profile of v10, /device:TPU:1, one launch (start us, length us, event | category | flops | bytes accessed | tf_op | source)
XLA Modules:
  0.0 138.5 jit_solution(2296667823657620552)
XLA Ops:
  0.6 1.6 %direction_copies.1 = bf16[8,128,128]{2,1,0:T(8,128)(2,1)} custom-call(f32[128,128]{1,0:T(8,128)} %dir_ref.3), custom_call_target="tpu_custom_call" | custom-call | tf_op jit(solution)/shard_map/direction_copies/pallas_call | solution.py:120
  2.3 5.9 %all-to-all-start = ((bf16[8,128,128]{2,1,0:T(8,128)(2,1)}), bf16[8,128,128]{2,1,0:T(8,128)(2,1)S(1)}, u32[]{:S(2)}, u32[]{:S(2)}) async-start(bf16[8,128,128]{2,1,0:T(8,128)(2,1)} %direction_copies.1), calls=%async_computation | async-start | bytes 524288 | tf_op jit(solution)/shard_map/all_to_all | solution.py:367
  8.1 0.0 copy-start.3
  8.1 1.2 copy-done.3
  9.4 0.0 copy-start.5
  9.4 0.7 copy-done.5
  10.0 2.8 %pick_centres.1.feat_ref = bf16[8,128,128]{2,1,0:T(8,128)(2,1)S(1)} custom-call(s32[1]{0:T(128)} %bitcast.1.start_ref, s32[1,1024]{1,0:T(1,128)S(1)} %bitcast.19, f32[64,4096]{1,0:T(8,128)S(1)} %bitcast.16), custom_call_target="tpu_custom_call" | custom-call | flops 4294967296 | bytes 1048576 | tf_op jit(solution)/shard_map/pick_centres/pallas_call | solution.py:90
  12.9 1.5 %all-to-all-done.dir_ref = bf16[8,128,128]{2,1,0:T(8,128)(2,1)S(1)} async-done(((bf16[8,128,128]{2,1,0:T(8,128)(2,1)}), bf16[8,128,128]{2,1,0:T(8,128)(2,1)S(1)}, u32[]{:S(2)}, u32[]{:S(2)}) %all-to-all-start) | async-done | bytes 262176 | tf_op jit(solution)/shard_map/all_to_all | solution.py:367
  14.4 1.9 %collective-permute-start = (bf16[8,128,128]{2,1,0:T(8,128)(2,1)S(1)}, bf16[8,128,128]{2,1,0:T(8,128)(2,1)S(1)}, u32[]{:S(2)}, u32[]{:S(2)}) collective-permute-start(bf16[8,128,128]{2,1,0:T(8,128)(2,1)S(1)} %all-to-all-done.dir_ref), channel_id=1, source_target_pairs={{0,1},{1,0},{2,3},{3,2},{4,5},{5,4},{6,7},{7,6},{8,9},{9,8},{10,11... | collective-permute-start | bytes 786440 | tf_op jit(solution)/shard_map/ppermute | solution.py:389
  16.4 2.5 %precond_first.1 = (f32[1024,128]{1,0:T(8,128)S(1)}, bf16[1024,2048]{1,0:T(8,128)(2,1)S(1)}) custom-call(s32[1]{0:T(128)} %bitcast.core_ref.refs_0_, bf16[1024,2048]{1,0:T(8,128)(2,1)} %pre_hbm.1, bf16[8,128,128]{2,1,0:T(8,128)(2,1)S(1)} %all-to-all-done.dir_ref), custom_call_target="tpu_custom_call" | custom-call | flops 268435456 | bytes 8388608 | tf_op jit(solution)/shard_map/precond_first/pallas_call | solution.py:236
  18.9 0.0 collective-permute-done.dir_ref
  18.9 0.0 copy-start.4
  18.9 0.8 precond_second.1
  19.7 17.6 %all_to_all.51.parts_ref = bf16[8,256,128]{2,1,0:T(8,128)(2,1)S(1)} all-to-all(bf16[8,256,128]{2,1,0:T(8,128)(2,1)S(1)} %precond_second.1), channel_id=1, replica_groups=mesh['yh'=2,'z'=4,'yl'=2,'x'=4,'core'=2] {'yh','z'}, dimensions={0} | all-to-all | bytes 1048576 | tf_op jit(solution)/shard_map/all_to_all | solution.py:367
  37.3 0.1 sum_copies.3
  37.4 13.9 %all_to_all.52.refs_2_ = bf16[8,256,128]{2,1,0:T(8,128)(2,1)S(1)} all-to-all(bf16[8,256,128]{2,1,0:T(8,128)(2,1)S(1)} %sum_copies.3), channel_id=1, replica_groups=mesh['yh'=2,'z'=4,'yl'=2,'x'=4,'core'=2] {'yh','z'}, dimensions={0} | all-to-all | bytes 1048576 | tf_op jit(solution)/shard_map/all_to_all | solution.py:367
  51.3 0.0 copy-done.4
  51.3 2.5 %tile_forward.2 = (bf16[2048,1024]{1,0:T(8,128)(2,1)S(1)}, bf16[2048,128]{1,0:T(8,128)(2,1)S(1)}, bf16[256,1024]{1,0:T(8,128)(2,1)S(1)}, bf16[1024,128]{1,0:T(8,128)(2,1)S(1)}) custom-call(s32[1]{0:T(128)S(6)} %sub.3.core_ref.refs_0_, f32[64,4096]{1,0:T(8,128)S(1)} %bitcast.17, bf16[8,256,128]{2,1,0:T(8,128)(2,1)S(1)} %all_to_all.52.refs_2_), custom_call_target="tpu_custom_call" | custom-call | flops 1610612736 | bytes 4194304 | tf_op jit(solution)/shard_map/tile_forward/pallas_call | solution.py:172
  53.8 2.5 %collective-permute-start.1 = (bf16[2048,128]{1,0:T(8,128)(2,1)S(1)}, bf16[2048,128]{1,0:T(8,128)(2,1)S(1)}, u32[]{:S(2)}, u32[]{:S(2)}) collective-permute-start(bf16[2048,128]{1,0:T(8,128)(2,1)S(1)} %get-tuple-element.36), channel_id=1, source_target_pairs={{0,1},{1,0},{2,3},{3,2},{4,5},{5,4},{6,7},{7,6},{8,9},{9,8},{10,11... | collective-permute-start | bytes 1572872 | tf_op jit(solution)/shard_map/ppermute | solution.py:389
  56.3 2.4 %tile_forward.3 = (bf16[2048,1024]{1,0:T(8,128)(2,1)S(1)}, f32[2048,128]{1,0:T(8,128)S(1)}) custom-call(s32[1]{0:T(128)} %bitcast.core_ref.refs_0_, f32[64,4096]{1,0:T(8,128)S(1)} %bitcast.18, bf16[256,1024]{1,0:T(8,128)(2,1)S(1)} %get-tuple-element.32.refs_2_, bf16[1024,128]{1,0:T(8,128)(2,1)S(1)} %get-tuple-element.33.refs_3_), custom_call_target="tpu_custom_call" | custom-call | flops 1610612736 | bytes 4194304 | tf_op jit(solution)/shard_map/tile_forward/pallas_call | solution.py:172
  58.8 0.0 collective-permute-done.1
  58.8 0.1 add_convert_fusion
  58.9 12.7 %all_to_all.53.parts_ref = bf16[8,256,128]{2,1,0:T(8,128)(2,1)S(1)} all-to-all(bf16[8,256,128]{2,1,0:T(8,128)(2,1)S(1)} %bitcast.20), channel_id=1, replica_groups=mesh['yh'=2,'z'=4,'yl'=2,'x'=4,'core'=2] {'yl','x'}, dimensions={0} | all-to-all | bytes 1048576 | tf_op jit(solution)/shard_map/all_to_all | solution.py:367
  71.6 0.1 sum_copies.4
  71.7 11.6 %all_to_all.54.refs_1_ = bf16[8,256,128]{2,1,0:T(8,128)(2,1)S(1)} all-to-all(bf16[8,256,128]{2,1,0:T(8,128)(2,1)S(1)} %sum_copies.4), channel_id=1, replica_groups=mesh['yh'=2,'z'=4,'yl'=2,'x'=4,'core'=2] {'yl','x'}, dimensions={0} | all-to-all | bytes 1048576 | tf_op jit(solution)/shard_map/all_to_all | solution.py:367
  83.3 1.9 %collective-permute-start.2 = (bf16[8,256,128]{2,1,0:T(8,128)(2,1)S(1)}, bf16[8,256,128]{2,1,0:T(8,128)(2,1)S(1)}, u32[]{:S(2)}, u32[]{:S(2)}) collective-permute-start(bf16[8,256,128]{2,1,0:T(8,128)(2,1)S(1)} %all_to_all.54.refs_1_), channel_id=1, source_target_pairs={{0,1},{1,0},{2,3},{3,2},{4,5},{5,4},{6,7},{7,6},{8,9},{9,8},{10,11... | collective-permute-start | bytes 1572872 | tf_op jit(solution)/shard_map/ppermute | solution.py:389
  85.2 0.7 tile_backward.2.refs_2_
  85.9 0.8 collective-permute-done.2.refs_1_
  86.7 0.8 tile_backward.3
  87.5 10.2 %all_to_all.55.parts_ref = bf16[8,128,128]{2,1,0:T(8,128)(2,1)S(1)} all-to-all(bf16[8,128,128]{2,1,0:T(8,128)(2,1)S(1)} %bitcast.13), channel_id=1, replica_groups=mesh['yh'=2,'z'=4,'yl'=2,'x'=4,'core'=2] {'yh','z'}, dimensions={0} | all-to-all | bytes 524288 | tf_op jit(solution)/shard_map/all_to_all | solution.py:367
  97.7 10.9 %all_to_all.56 = bf16[8,128,128]{2,1,0:T(8,128)(2,1)S(1)} all-to-all(bf16[8,128,128]{2,1,0:T(8,128)(2,1)S(1)} %sum_copies.5), channel_id=1, replica_groups=mesh['yh'=2,'z'=4,'yl'=2,'x'=4,'core'=2] {'yh','z'}, dimensions={0} | all-to-all | bytes 524288 | tf_op jit(solution)/shard_map/all_to_all | solution.py:367
  108.6 0.9 precond_backward.3
  109.5 0.0 copy-start
  109.5 0.0 copy-start.1
  109.5 0.0 copy-start.2
  109.5 2.6 %collective-permute-start.3 = (f32[8,128,128]{2,1,0:T(8,128)S(1)}, f32[8,128,128]{2,1,0:T(8,128)S(1)}, u32[]{:S(2)}, u32[]{:S(2)}) collective-permute-start(f32[8,128,128]{2,1,0:T(8,128)S(1)} %precond_backward.3), channel_id=1, source_target_pairs={{0,1},{1,0},{2,3},{3,2},{4,5},{5,4},{6,7},{7,6},{8,9},{9,8},{10,11... | collective-permute-start | bytes 1572872 | tf_op jit(solution)/shard_map/ppermute | solution.py:389
  112.2 0.9 precond_backward.2
  113.0 0.7 collective-permute-done.3
  113.7 0.1 add_convert_fusion.1
  113.8 9.8 %all_to_all.57.part_ref = bf16[8,128,128]{2,1,0:T(8,128)(2,1)S(1)} all-to-all(bf16[8,128,128]{2,1,0:T(8,128)(2,1)S(1)} %add_convert_fusion.1), channel_id=1, replica_groups=mesh['yh'=2,'z'=4,'yl'=2,'x'=4,'core'=2] {'yl','x'}, dimensions={0} | all-to-all | bytes 524288 | tf_op jit(solution)/shard_map/all_to_all | solution.py:367
  123.6 0.0 copy-done
  123.6 0.0 copy-done.1
  123.6 0.2 image_numbers.1
  123.8 13.8 %all_to_all.58 = f32[128,1,128]{2,1,0:T(1,128)S(1)} all-to-all(f32[128,1,128]{2,1,0:T(1,128)S(1)} %bitcast.15), channel_id=1, replica_groups=mesh['yh'=2,'z'=4,'yl'=2,'x'=4,'core'=2] {'yh','z','yl','x','core'}, dimensions={0} | all-to-all | bytes 131072 | tf_op jit(solution)/shard_map/all_to_all | solution.py:367
  137.6 0.0 copy-done.2
  137.7 0.8 finish.1
  (1 shorter events, 0.0 us)
Async XLA Ops:
  2.3 12.2 %all-to-all-start = ((bf16[8,128,128]{2,1,0:T(8,128)(2,1)}), bf16[8,128,128]{2,1,0:T(8,128)(2,1)S(1)}, u32[]{:S(2)}, u32[]{:S(2)}) async-start(bf16[8,128,128]{2,1,0:T(8,128)(2,1)} %direction_copies.1), calls=%async_computation | async-start | bytes 524288 | tf_op jit(solution)/shard_map/all_to_all | solution.py:367
  8.1 1.2 copy-start.3
  9.4 0.7 copy-start.5
  14.4 4.5 %collective-permute-start = (bf16[8,128,128]{2,1,0:T(8,128)(2,1)S(1)}, bf16[8,128,128]{2,1,0:T(8,128)(2,1)S(1)}, u32[]{:S(2)}, u32[]{:S(2)}) collective-permute-start(bf16[8,128,128]{2,1,0:T(8,128)(2,1)S(1)} %all-to-all-done.dir_ref), channel_id=1, source_target_pairs={{0,1},{1,0},{2,3},{3,2},{4,5},{5,4},{6,7},{7,6},{8,9},{9,8},{10,11... | collective-permute-start | bytes 786440 | tf_op jit(solution)/shard_map/ppermute | solution.py:389
  18.9 32.4 %copy-start.4 = (f32[4096,64]{0,1:T(8,128)S(1)}, f32[4096,64]{0,1:T(8,128)}, u32[]{:S(2)}) copy-start(f32[4096,64]{0,1:T(8,128)} %param.6) | copy-start | bytes 3145732
  53.8 5.0 %collective-permute-start.1 = (bf16[2048,128]{1,0:T(8,128)(2,1)S(1)}, bf16[2048,128]{1,0:T(8,128)(2,1)S(1)}, u32[]{:S(2)}, u32[]{:S(2)}) collective-permute-start(bf16[2048,128]{1,0:T(8,128)(2,1)S(1)} %get-tuple-element.36), channel_id=1, source_target_pairs={{0,1},{1,0},{2,3},{3,2},{4,5},{5,4},{6,7},{7,6},{8,9},{9,8},{10,11... | collective-permute-start | bytes 1572872 | tf_op jit(solution)/shard_map/ppermute | solution.py:389
  83.3 3.4 %collective-permute-start.2 = (bf16[8,256,128]{2,1,0:T(8,128)(2,1)S(1)}, bf16[8,256,128]{2,1,0:T(8,128)(2,1)S(1)}, u32[]{:S(2)}, u32[]{:S(2)}) collective-permute-start(bf16[8,256,128]{2,1,0:T(8,128)(2,1)S(1)} %all_to_all.54.refs_1_), channel_id=1, source_target_pairs={{0,1},{1,0},{2,3},{3,2},{4,5},{5,4},{6,7},{7,6},{8,9},{9,8},{10,11... | collective-permute-start | bytes 1572872 | tf_op jit(solution)/shard_map/ppermute | solution.py:389
  109.5 14.1 %copy-start = (f32[128,128]{1,0:T(8,128)S(1)}, f32[128,128]{1,0:T(8,128)}, u32[]{:S(2)}) copy-start(f32[128,128]{1,0:T(8,128)} %dir_ref.3) | copy-start | bytes 196612
  109.5 14.1 %copy-start.1 = (f32[128,128]{1,0:T(8,128)S(1)}, f32[128,128]{1,0:T(8,128)}, u32[]{:S(2)}) copy-start(f32[128,128]{1,0:T(8,128)} %res_ref.3) | copy-start | bytes 196612
  109.5 28.1 %copy-start.2 = (f32[128,128]{1,0:T(8,128)S(1)}, f32[128,128]{1,0:T(8,128)}, u32[]{:S(2)}) copy-start(f32[128,128]{1,0:T(8,128)} %coef_ref.1) | copy-start | bytes 196612
  109.5 4.1 %collective-permute-start.3 = (f32[8,128,128]{2,1,0:T(8,128)S(1)}, f32[8,128,128]{2,1,0:T(8,128)S(1)}, u32[]{:S(2)}, u32[]{:S(2)}) collective-permute-start(f32[8,128,128]{2,1,0:T(8,128)S(1)} %precond_backward.3), channel_id=1, source_target_pairs={{0,1},{1,0},{2,3},{3,2},{4,5},{5,4},{6,7},{7,6},{8,9},{9,8},{10,11... | collective-permute-start | bytes 1572872 | tf_op jit(solution)/shard_map/ppermute | solution.py:389

commit v11 on v10

--- a/solution.py
+++ b/solution.py
@@ -17,7 +17,8 @@
 
 FINE = (("yh", 2), ("z", 4), ("yl", 2), ("x", 4), ("core", 2))
 ROWS = ("yh", "z")
-CHIPS = ("yl", "x")
+ROW_RING = ("z", "yh")
+CHIPS = ("x", "yl")
 CENT = ("yl", "x", "core")
 FEATURE_SCALE = math.sqrt(2.0 * (2.0 / FEAT) * math.log2(math.e))
 SWAP = [(0, 1), (1, 0)]
@@ -207,9 +208,17 @@
     )(tile, fitted, *([before] if last else []))
 
 
+def chip_at(place, count):
+    return place % 2 * (count // 2) + place // 2
+
+
 def core_columns(pre_ref, here, core, width, count):
     return jnp.concatenate(
-        [pre_ref[here, pl.ds(pl.multiple_of((2 * j + core) * width, width), width)] for j in range(count)], axis=1
+        [
+            pre_ref[here, pl.ds(pl.multiple_of((2 * chip_at(j, count) + core) * width, width), width)]
+            for j in range(count)
+        ],
+        axis=1,
     )
 
 
@@ -281,7 +290,9 @@
     chips, width, _ = out_ref.shape
     grad = grad_ref[...].T
     for j in range(0, chips, 2):
-        pair = [pre_ref[:, pl.ds(pl.multiple_of((2 * k + core) * width, width), width)] for k in (j, j + 1)]
+        pair = [
+            pre_ref[:, pl.ds(pl.multiple_of((2 * chip_at(k, chips) + core) * width, width), width)] for k in (j, j + 1)
+        ]
         part = jnp.dot(grad, jnp.concatenate(pair, axis=1), preferred_element_type=F32).T
         out_ref[j] = part[:width]
         out_ref[j + 1] = part[width:]
@@ -405,23 +416,23 @@
     picked = pick(start_row[None], centre_index[None], feat, row_devices)
     dir_mine, picked, other = lax.optimization_barrier((dir_mine, picked, other))
     dir_came = swapped(dir_mine)
-    first, precond = field_first(me, precond, dir_mine)
+    first, precond_here = field_first(me, precond, dir_mine)
     first, dir_came = lax.optimization_barrier((first, dir_came))
-    got = all_summed(field_second(other, precond, dir_came, first, picked), ROWS)
+    got = all_summed(field_second(other, precond_here, dir_came, first, picked), ROW_RING)
 
     chips_shape = (cen_devices // 2, rows_here // cen_devices, OUTS)
-    tile_other, fit_other, cen_op, coef = tile_forward(other, feat, [got], BF16)
+    tile_other, fit_other, cen_op, coef = tile_forward(other, feat, [got], F32)
     fit_came = swapped(fit_other)
     tile_mine, fit_mine = tile_forward(me, feat, [cen_op, coef], F32)
     fit_mine, fit_came = lax.optimization_barrier((fit_mine, fit_came))
-    half = (fit_mine + fit_came.astype(F32)).astype(BF16).reshape(chips_shape)
+    half = (fit_mine + fit_came).astype(BF16).reshape(chips_shape)
     fitted = all_summed(half, CHIPS)
     fitted_came = swapped(fitted)
     grad_mine = backward(tile_mine, fitted)
     grad_mine, fitted_came = lax.optimization_barrier((grad_mine, fitted_came))
     grad_part = backward(tile_other, fitted_came, grad_mine).reshape(row_devices, share, OUTS)
 
-    grad_low = all_summed(grad_part, ROWS, float(rows_here * row_devices) ** (-0.5)).reshape(cen_here, OUTS)
+    grad_low = all_summed(grad_part, ROW_RING, float(rows_here * row_devices) ** (-0.5)).reshape(cen_here, OUTS)
 
     image_came = swapped(image_part(other, precond, grad_low, direction.shape[0]))
     image_mine = image_part(me, precond, grad_low, direction.shape[0])

time: 139 us -> 138 us (level)
  blocking collectives: 101 us -> 98.8 us
    all_to_all x8, blocking collectives: 101 us -> 98.8 us  [spread(): return lax.all_to_all(part, axes, 0, 0, tiled=True)]
where the time goes in v11:
time: 138 us; the launch traced here: 137 us
  blocking collectives  98.8 us (72%)
  Pallas kernels  17.2 us (12%)
  starting transfers between devices  15.7 us (11%)
  waiting for transfers between devices  2.62 us (2%)
  local copies, waits for them, and re-layouts  1.94 us (1%)
    all_to_all x8, blocking collectives, spread(): return lax.all_to_all(part, axes, 0, 0, tiled=True)  98.8 us
    ppermute x4, starting transfers between devices, swapped(): return lax.ppermute(part, 'core', SWAP)  9.85 us
    all_to_all x1, starting transfers between devices, spread(): return lax.all_to_all(part, axes, 0, 0, tiled=True)  5.87 us
    pallas_call x2, Pallas kernels, tile_forward(): pl.pallas_call(functools.partial(tile_kernel, first=first), in_specs=[SME...  4.9 us
    pallas_call x1, Pallas kernels, pick(): pl.pallas_call(pick_kernel, grid=(n // block,), in_specs=[pl.BlockSpec(me...  2.84 us
  transfers between devices with their start and end apart: 5, of which 3 were waited for; matrix products, arithmetic and copies ran while one was open for 0% of the time, Pallas kernels for 7%

profile of v11, /device:TPU:1, one launch (start us, length us, event | category | flops | bytes accessed | tf_op | source)
XLA Modules:
  0.0 137.3 jit_solution(8591525895409185724)
XLA Ops:
  0.6 1.6 %direction_copies.1 = bf16[8,128,128]{2,1,0:T(8,128)(2,1)} custom-call(f32[128,128]{1,0:T(8,128)} %dir_ref.3), custom_call_target="tpu_custom_call" | custom-call | tf_op jit(solution)/shard_map/direction_copies/pallas_call | solution.py:121
  2.3 5.9 %all-to-all-start = ((bf16[8,128,128]{2,1,0:T(8,128)(2,1)}), bf16[8,128,128]{2,1,0:T(8,128)(2,1)S(1)}, u32[]{:S(2)}, u32[]{:S(2)}) async-start(bf16[8,128,128]{2,1,0:T(8,128)(2,1)} %direction_copies.1), calls=%async_computation | async-start | bytes 524288 | tf_op jit(solution)/shard_map/all_to_all | solution.py:378
  8.1 0.0 copy-start.4
  8.1 1.2 copy-done.4
  9.4 0.0 copy-start.6
  9.4 0.7 copy-done.6
  10.0 2.8 %pick_centres.1.feat_ref = bf16[8,128,128]{2,1,0:T(8,128)(2,1)S(1)} custom-call(s32[1]{0:T(128)} %bitcast.1.start_ref, s32[1,1024]{1,0:T(1,128)S(1)} %bitcast.19, f32[64,4096]{1,0:T(8,128)S(1)} %bitcast.16), custom_call_target="tpu_custom_call" | custom-call | flops 4294967296 | bytes 1048576 | tf_op jit(solution)/shard_map/pick_centres/pallas_call | solution.py:91
  12.9 1.2 all-to-all-done.dir_ref
  14.1 2.2 %collective-permute-start = (bf16[8,128,128]{2,1,0:T(8,128)(2,1)S(1)}, bf16[8,128,128]{2,1,0:T(8,128)(2,1)S(1)}, u32[]{:S(2)}, u32[]{:S(2)}) collective-permute-start(bf16[8,128,128]{2,1,0:T(8,128)(2,1)S(1)} %all-to-all-done.dir_ref), channel_id=1, source_target_pairs={{0,1},{1,0},{2,3},{3,2},{4,5},{5,4},{6,7},{7,6},{8,9},{9,8},{10,11... | collective-permute-start | bytes 786440 | tf_op jit(solution)/shard_map/ppermute | solution.py:400
  16.3 2.5 %precond_first.1 = (f32[1024,128]{1,0:T(8,128)S(1)}, bf16[1024,2048]{1,0:T(8,128)(2,1)S(1)}) custom-call(s32[1]{0:T(128)} %bitcast.core_ref.refs_0_, bf16[1024,2048]{1,0:T(8,128)(2,1)} %pre_ref.3, bf16[8,128,128]{2,1,0:T(8,128)(2,1)S(1)} %all-to-all-done.dir_ref), custom_call_target="tpu_custom_call" | custom-call | flops 268435456 | bytes 8388608 | tf_op jit(solution)/shard_map/precond_first/pallas_call | solution.py:245
  18.8 0.0 collective-permute-done.dir_ref
  18.8 0.0 copy-start.5
  18.8 0.8 precond_second.1
  19.6 18.6 %all_to_all.51.parts_ref = bf16[8,256,128]{2,1,0:T(8,128)(2,1)S(1)} all-to-all(bf16[8,256,128]{2,1,0:T(8,128)(2,1)S(1)} %precond_second.1), channel_id=1, replica_groups=mesh['yh'=2,'z'=4,'yl'=2,'x'=4,'core'=2] {'z','yh'}, dimensions={0} | all-to-all | bytes 1048576 | tf_op jit(solution)/shard_map/all_to_all | solution.py:378
  38.2 0.1 sum_copies.3
  38.3 12.8 %all_to_all.52.refs_2_ = bf16[8,256,128]{2,1,0:T(8,128)(2,1)S(1)} all-to-all(bf16[8,256,128]{2,1,0:T(8,128)(2,1)S(1)} %sum_copies.3), channel_id=1, replica_groups=mesh['yh'=2,'z'=4,'yl'=2,'x'=4,'core'=2] {'z','yh'}, dimensions={0} | all-to-all | bytes 1048576 | tf_op jit(solution)/shard_map/all_to_all | solution.py:378
  51.1 0.0 copy-done.5
  51.1 2.5 %tile_forward.2 = (bf16[2048,1024]{1,0:T(8,128)(2,1)S(1)}, f32[2048,128]{1,0:T(8,128)S(1)}, bf16[256,1024]{1,0:T(8,128)(2,1)S(1)}, bf16[1024,128]{1,0:T(8,128)(2,1)S(1)}) custom-call(s32[1]{0:T(128)S(6)} %sub.3.core_ref.refs_0_, f32[64,4096]{1,0:T(8,128)S(1)} %bitcast.17, bf16[8,256,128]{2,1,0:T(8,128)(2,1)S(1)} %all_to_all.52.refs_2_), custom_call_target="tpu_custom_call" | custom-call | flops 1610612736 | bytes 4194304 | tf_op jit(solution)/shard_map/tile_forward/pallas_call | solution.py:173
  53.6 2.2 %collective-permute-start.1 = (f32[2048,128]{1,0:T(8,128)S(1)}, f32[2048,128]{1,0:T(8,128)S(1)}, u32[]{:S(2)}, u32[]{:S(2)}) collective-permute-start(f32[2048,128]{1,0:T(8,128)S(1)} %get-tuple-element.36), channel_id=1, source_target_pairs={{0,1},{1,0},{2,3},{3,2},{4,5},{5,4},{6,7},{7,6},{8,9},{9,8},{10,11... | collective-permute-start | bytes 3145736 | tf_op jit(solution)/shard_map/ppermute | solution.py:400
  55.8 2.4 %tile_forward.3 = (bf16[2048,1024]{1,0:T(8,128)(2,1)S(1)}, f32[2048,128]{1,0:T(8,128)S(1)}) custom-call(s32[1]{0:T(128)} %bitcast.core_ref.refs_0_, f32[64,4096]{1,0:T(8,128)S(1)} %bitcast.18, bf16[256,1024]{1,0:T(8,128)(2,1)S(1)} %get-tuple-element.32.refs_2_, bf16[1024,128]{1,0:T(8,128)(2,1)S(1)} %get-tuple-element.33.refs_3_), custom_call_target="tpu_custom_call" | custom-call | flops 1610612736 | bytes 4194304 | tf_op jit(solution)/shard_map/tile_forward/pallas_call | solution.py:173
  58.2 0.0 collective-permute-done.1
  58.3 0.2 add_convert_fusion
  58.4 12.0 %all_to_all.53.parts_ref = bf16[8,256,128]{2,1,0:T(8,128)(2,1)S(1)} all-to-all(bf16[8,256,128]{2,1,0:T(8,128)(2,1)S(1)} %bitcast.20), channel_id=1, replica_groups=mesh['yh'=2,'z'=4,'yl'=2,'x'=4,'core'=2] {'x','yl'}, dimensions={0} | all-to-all | bytes 1048576 | tf_op jit(solution)/shard_map/all_to_all | solution.py:378
  70.4 0.1 sum_copies.4
  70.5 10.5 %all_to_all.54.refs_1_ = bf16[8,256,128]{2,1,0:T(8,128)(2,1)S(1)} all-to-all(bf16[8,256,128]{2,1,0:T(8,128)(2,1)S(1)} %sum_copies.4), channel_id=1, replica_groups=mesh['yh'=2,'z'=4,'yl'=2,'x'=4,'core'=2] {'x','yl'}, dimensions={0} | all-to-all | bytes 1048576 | tf_op jit(solution)/shard_map/all_to_all | solution.py:378
  81.0 2.7 %collective-permute-start.2 = (bf16[8,256,128]{2,1,0:T(8,128)(2,1)S(1)}, bf16[8,256,128]{2,1,0:T(8,128)(2,1)S(1)}, u32[]{:S(2)}, u32[]{:S(2)}) collective-permute-start(bf16[8,256,128]{2,1,0:T(8,128)(2,1)S(1)} %all_to_all.54.refs_1_), channel_id=1, source_target_pairs={{0,1},{1,0},{2,3},{3,2},{4,5},{5,4},{6,7},{7,6},{8,9},{9,8},{10,11... | collective-permute-start | bytes 1572872 | tf_op jit(solution)/shard_map/ppermute | solution.py:400
  83.7 0.7 tile_backward.2.refs_2_
  84.5 0.0 copy-start
  84.5 0.8 collective-permute-done.2.refs_1_
  85.3 0.8 tile_backward.3
  86.1 10.6 %all_to_all.55.parts_ref = bf16[8,128,128]{2,1,0:T(8,128)(2,1)S(1)} all-to-all(bf16[8,128,128]{2,1,0:T(8,128)(2,1)S(1)} %bitcast.13), channel_id=1, replica_groups=mesh['yh'=2,'z'=4,'yl'=2,'x'=4,'core'=2] {'z','yh'}, dimensions={0} | all-to-all | bytes 524288 | tf_op jit(solution)/shard_map/all_to_all | solution.py:378
  96.7 10.5 %all_to_all.56 = bf16[8,128,128]{2,1,0:T(8,128)(2,1)S(1)} all-to-all(bf16[8,128,128]{2,1,0:T(8,128)(2,1)S(1)} %sum_copies.5), channel_id=1, replica_groups=mesh['yh'=2,'z'=4,'yl'=2,'x'=4,'core'=2] {'z','yh'}, dimensions={0} | all-to-all | bytes 524288 | tf_op jit(solution)/shard_map/all_to_all | solution.py:378
  107.2 0.0 copy-done
  107.2 0.9 precond_backward.3
  108.1 0.0 copy-start.1
  108.1 0.0 copy-start.2
  108.1 0.0 copy-start.3
  108.1 2.7 %collective-permute-start.3 = (f32[8,128,128]{2,1,0:T(8,128)S(1)}, f32[8,128,128]{2,1,0:T(8,128)S(1)}, u32[]{:S(2)}, u32[]{:S(2)}) collective-permute-start(f32[8,128,128]{2,1,0:T(8,128)S(1)} %precond_backward.3), channel_id=1, source_target_pairs={{0,1},{1,0},{2,3},{3,2},{4,5},{5,4},{6,7},{7,6},{8,9},{9,8},{10,11... | collective-permute-start | bytes 1572872 | tf_op jit(solution)/shard_map/ppermute | solution.py:400
  110.8 0.9 precond_backward.2
  111.7 0.7 collective-permute-done.3
  112.3 0.1 add_convert_fusion.1
  112.4 8.4 %all_to_all.57.part_ref = bf16[8,128,128]{2,1,0:T(8,128)(2,1)S(1)} all-to-all(bf16[8,128,128]{2,1,0:T(8,128)(2,1)S(1)} %add_convert_fusion.1), channel_id=1, replica_groups=mesh['yh'=2,'z'=4,'yl'=2,'x'=4,'core'=2] {'x','yl'}, dimensions={0} | all-to-all | bytes 524288 | tf_op jit(solution)/shard_map/all_to_all | solution.py:378
  120.8 0.0 copy-done.1
  120.8 0.0 copy-done.2
  120.8 0.2 image_numbers.1
  121.0 15.4 %all_to_all.58 = f32[128,1,128]{2,1,0:T(1,128)S(1)} all-to-all(f32[128,1,128]{2,1,0:T(1,128)S(1)} %bitcast.15), channel_id=1, replica_groups=mesh['yh'=2,'z'=4,'yl'=2,'x'=4,'core'=2] {'yh','z','yl','x','core'}, dimensions={0} | all-to-all | bytes 131072 | tf_op jit(solution)/shard_map/all_to_all | solution.py:378
  136.4 0.0 copy-done.3
  136.4 0.8 finish.1
  (1 shorter events, 0.0 us)
Async XLA Ops:
  2.3 11.8 %all-to-all-start = ((bf16[8,128,128]{2,1,0:T(8,128)(2,1)}), bf16[8,128,128]{2,1,0:T(8,128)(2,1)S(1)}, u32[]{:S(2)}, u32[]{:S(2)}) async-start(bf16[8,128,128]{2,1,0:T(8,128)(2,1)} %direction_copies.1), calls=%async_computation | async-start | bytes 524288 | tf_op jit(solution)/shard_map/all_to_all | solution.py:378
  8.1 1.2 copy-start.4
  9.4 0.7 copy-start.6
  14.1 4.8 %collective-permute-start = (bf16[8,128,128]{2,1,0:T(8,128)(2,1)S(1)}, bf16[8,128,128]{2,1,0:T(8,128)(2,1)S(1)}, u32[]{:S(2)}, u32[]{:S(2)}) collective-permute-start(bf16[8,128,128]{2,1,0:T(8,128)(2,1)S(1)} %all-to-all-done.dir_ref), channel_id=1, source_target_pairs={{0,1},{1,0},{2,3},{3,2},{4,5},{5,4},{6,7},{7,6},{8,9},{9,8},{10,11... | collective-permute-start | bytes 786440 | tf_op jit(solution)/shard_map/ppermute | solution.py:400
  18.8 32.3 %copy-start.5 = (f32[4096,64]{0,1:T(8,128)S(1)}, f32[4096,64]{0,1:T(8,128)}, u32[]{:S(2)}) copy-start(f32[4096,64]{0,1:T(8,128)} %param.6) | copy-start | bytes 3145732
  53.6 4.7 %collective-permute-start.1 = (f32[2048,128]{1,0:T(8,128)S(1)}, f32[2048,128]{1,0:T(8,128)S(1)}, u32[]{:S(2)}, u32[]{:S(2)}) collective-permute-start(f32[2048,128]{1,0:T(8,128)S(1)} %get-tuple-element.36), channel_id=1, source_target_pairs={{0,1},{1,0},{2,3},{3,2},{4,5},{5,4},{6,7},{7,6},{8,9},{9,8},{10,11... | collective-permute-start | bytes 3145736 | tf_op jit(solution)/shard_map/ppermute | solution.py:400
  81.0 4.2 %collective-permute-start.2 = (bf16[8,256,128]{2,1,0:T(8,128)(2,1)S(1)}, bf16[8,256,128]{2,1,0:T(8,128)(2,1)S(1)}, u32[]{:S(2)}, u32[]{:S(2)}) collective-permute-start(bf16[8,256,128]{2,1,0:T(8,128)(2,1)S(1)} %all_to_all.54.refs_1_), channel_id=1, source_target_pairs={{0,1},{1,0},{2,3},{3,2},{4,5},{5,4},{6,7},{7,6},{8,9},{9,8},{10,11... | collective-permute-start | bytes 1572872 | tf_op jit(solution)/shard_map/ppermute | solution.py:400
  84.5 22.7 %copy-start = (bf16[1024,2048]{1,0:T(8,128)(2,1)S(1)}, bf16[1024,2048]{1,0:T(8,128)(2,1)}, u32[]{:S(2)}) copy-start(bf16[1024,2048]{1,0:T(8,128)(2,1)} %pre_ref.3) | copy-start | bytes 12582916
  108.1 12.7 %copy-start.1 = (f32[128,128]{1,0:T(8,128)S(1)}, f32[128,128]{1,0:T(8,128)}, u32[]{:S(2)}) copy-start(f32[128,128]{1,0:T(8,128)} %dir_ref.3) | copy-start | bytes 196612
  108.1 12.7 %copy-start.2 = (f32[128,128]{1,0:T(8,128)S(1)}, f32[128,128]{1,0:T(8,128)}, u32[]{:S(2)}) copy-start(f32[128,128]{1,0:T(8,128)} %res_ref.3) | copy-start | bytes 196612
  108.1 28.3 %copy-start.3 = (f32[128,128]{1,0:T(8,128)S(1)}, f32[128,128]{1,0:T(8,128)}, u32[]{:S(2)}) copy-start(f32[128,128]{1,0:T(8,128)} %coef_ref.1) | copy-start | bytes 196612
  108.1 4.2 %collective-permute-start.3 = (f32[8,128,128]{2,1,0:T(8,128)S(1)}, f32[8,128,128]{2,1,0:T(8,128)S(1)}, u32[]{:S(2)}, u32[]{:S(2)}) collective-permute-start(f32[8,128,128]{2,1,0:T(8,128)S(1)} %precond_backward.3), channel_id=1, source_target_pairs={{0,1},{1,0},{2,3},{3,2},{4,5},{5,4},{6,7},{7,6},{8,9},{9,8},{10,11... | collective-permute-start | bytes 1572872 | tf_op jit(solution)/shard_map/ppermute | solution.py:400

commit v12 on v11

--- a/solution.py
+++ b/solution.py
@@ -181,27 +181,31 @@
     )(half, feat, *operands)
 
 
+def side_by_side(parts_ref):
+    return jnp.concatenate([parts_ref[j] for j in range(parts_ref.shape[0])], axis=1)
+
+
 def back_kernel(*refs, last):
-    tile_ref, fit_ref, *before, out_ref, turned = refs
-    parts, share, _ = fit_ref.shape
-    for j in range(parts):
-        turned[:, j * share : (j + 1) * share] = fit_ref[j].T
-    part = jnp.dot(turned[...], tile_ref[...], preferred_element_type=F32)
+    tile_ref, fit_ref, *before, out_ref = refs
+    part = jnp.dot(side_by_side(fit_ref), tile_ref[...], preferred_element_type=F32)
     if last:
-        out_ref[...] = (part + before[0][...]).T.astype(BF16)
+        part = (part + before[0][...]).astype(BF16)
+        share = out_ref.shape[2]
+        for j in range(out_ref.shape[0]):
+            out_ref[j] = part[:, j * share : (j + 1) * share]
     else:
         out_ref[...] = part
 
 
-def backward(tile, fitted, before=None):
+def backward(tile, fitted, parts, before=None):
     n, m = tile.shape
     last = before is not None
+    whole = jax.ShapeDtypeStruct((parts, OUTS, m // parts), BF16)
     return pl.pallas_call(
         functools.partial(back_kernel, last=last),
         in_specs=[VMEM, VMEM] + [VMEM] * last,
         out_specs=VMEM,
-        out_shape=jax.ShapeDtypeStruct((m, OUTS), BF16) if last else jax.ShapeDtypeStruct((OUTS, m), F32),
-        scratch_shapes=[pltpu.VMEM((OUTS, n), BF16)],
+        out_shape=whole if last else jax.ShapeDtypeStruct((OUTS, m), F32),
         compiler_params=params(),
         cost_estimate=cost(2 * n * m * OUTS, 2 * n * m),
         name="tile_backward",
@@ -288,7 +292,7 @@
 def image_kernel(core_ref, pre_ref, grad_ref, out_ref):
     core = core_ref[0]
     chips, width, _ = out_ref.shape
-    grad = grad_ref[...].T
+    grad = side_by_side(grad_ref)
     for j in range(0, chips, 2):
         pair = [
             pre_ref[:, pl.ds(pl.multiple_of((2 * chip_at(k, chips) + core) * width, width), width)] for k in (j, j + 1)
@@ -378,21 +382,23 @@
     return lax.all_to_all(part, axes, 0, 0, tiled=True)
 
 
-def sum_kernel(parts_ref, out_ref, *, scale):
+def sum_kernel(parts_ref, out_ref, *, scale, turn):
     total = jnp.sum(parts_ref[...].astype(F32), axis=0)
     if scale is not None:
         total = total * scale
+    if turn:
+        total = total.T
     out_ref[...] = jnp.broadcast_to(total.astype(BF16)[None], out_ref.shape)
 
 
-def all_summed(parts, axes, scale=None):
-    own = spread(parts, axes)
+def all_summed(parts, axes, scale=None, turn=False):
+    count, first, second = parts.shape
     copies = pl.pallas_call(
-        functools.partial(sum_kernel, scale=scale),
-        out_shape=jax.ShapeDtypeStruct(parts.shape, BF16),
+        functools.partial(sum_kernel, scale=scale, turn=turn),
+        out_shape=jax.ShapeDtypeStruct((count, second, first) if turn else parts.shape, BF16),
         compiler_params=params(8),
         name="sum_copies",
-    )(own)
+    )(spread(parts, axes))
     return spread(copies, axes)
 
 
@@ -426,13 +432,12 @@
     tile_mine, fit_mine = tile_forward(me, feat, [cen_op, coef], F32)
     fit_mine, fit_came = lax.optimization_barrier((fit_mine, fit_came))
     half = (fit_mine + fit_came).astype(BF16).reshape(chips_shape)
-    fitted = all_summed(half, CHIPS)
+    fitted = all_summed(half, CHIPS, turn=True)
     fitted_came = swapped(fitted)
-    grad_mine = backward(tile_mine, fitted)
+    grad_mine = backward(tile_mine, fitted, row_devices)
     grad_mine, fitted_came = lax.optimization_barrier((grad_mine, fitted_came))
-    grad_part = backward(tile_other, fitted_came, grad_mine).reshape(row_devices, share, OUTS)
-
-    grad_low = all_summed(grad_part, ROW_RING, float(rows_here * row_devices) ** (-0.5)).reshape(cen_here, OUTS)
+    grad_part = backward(tile_other, fitted_came, row_devices, grad_mine)
+    grad_low = all_summed(grad_part, ROW_RING, float(rows_here * row_devices) ** (-0.5))
 
     image_came = swapped(image_part(other, precond, grad_low, direction.shape[0]))
     image_mine = image_part(me, precond, grad_low, direction.shape[0])

time: 138 us -> 138 us (level)
  no operation moved by 1% of the time
where the time goes in v12:
time: 138 us; the launch traced here: 137 us
  blocking collectives  98.8 us (72%)
  Pallas kernels  17.4 us (13%)
  starting transfers between devices  15.7 us (11%)
  waiting for transfers between devices  2.52 us (2%)
  local copies, waits for them, and re-layouts  1.94 us (1%)
    all_to_all x8, blocking collectives, spread(): return lax.all_to_all(part, axes, 0, 0, tiled=True)  98.8 us
    ppermute x4, starting transfers between devices, swapped(): return lax.ppermute(part, 'core', SWAP)  9.86 us
    all_to_all x1, starting transfers between devices, spread(): return lax.all_to_all(part, axes, 0, 0, tiled=True)  5.87 us
    pallas_call x2, Pallas kernels, tile_forward(): pl.pallas_call(functools.partial(tile_kernel, first=first), in_specs=[SME...  4.9 us
    pallas_call x1, Pallas kernels, pick(): pl.pallas_call(pick_kernel, grid=(n // block,), in_specs=[pl.BlockSpec(me...  2.84 us
  transfers between devices with their start and end apart: 5, of which 3 were waited for; matrix products, arithmetic and copies ran while one was open for 0% of the time, Pallas kernels for 7%

profile of v12, /device:TPU:1, one launch (start us, length us, event | category | flops | bytes accessed | tf_op | source)
XLA Modules:
  0.0 137.4 jit_solution(17338254531083234832)
XLA Ops:
  0.6 1.6 %direction_copies.1 = bf16[8,128,128]{2,1,0:T(8,128)(2,1)} custom-call(f32[128,128]{1,0:T(8,128)} %dir_ref.3), custom_call_target="tpu_custom_call" | custom-call | tf_op jit(solution)/shard_map/direction_copies/pallas_call | solution.py:121
  2.3 5.9 %all-to-all-start = ((bf16[8,128,128]{2,1,0:T(8,128)(2,1)}), bf16[8,128,128]{2,1,0:T(8,128)(2,1)S(1)}, u32[]{:S(2)}, u32[]{:S(2)}) async-start(bf16[8,128,128]{2,1,0:T(8,128)(2,1)} %direction_copies.1), calls=%async_computation | async-start | bytes 524288 | tf_op jit(solution)/shard_map/all_to_all | solution.py:382
  8.1 0.0 copy-start.4
  8.1 1.2 copy-done.4
  9.4 0.0 copy-start.6
  9.4 0.7 copy-done.6
  10.0 2.8 %pick_centres.1.feat_ref = bf16[8,128,128]{2,1,0:T(8,128)(2,1)S(1)} custom-call(s32[1]{0:T(128)} %bitcast.1.start_ref, s32[1,1024]{1,0:T(1,128)S(1)} %bitcast.14, f32[64,4096]{1,0:T(8,128)S(1)} %bitcast.11), custom_call_target="tpu_custom_call" | custom-call | flops 4294967296 | bytes 1048576 | tf_op jit(solution)/shard_map/pick_centres/pallas_call | solution.py:91
  12.9 1.2 all-to-all-done.dir_ref
  14.1 2.2 %collective-permute-start = (bf16[8,128,128]{2,1,0:T(8,128)(2,1)S(1)}, bf16[8,128,128]{2,1,0:T(8,128)(2,1)S(1)}, u32[]{:S(2)}, u32[]{:S(2)}) collective-permute-start(bf16[8,128,128]{2,1,0:T(8,128)(2,1)S(1)} %all-to-all-done.dir_ref), channel_id=1, source_target_pairs={{0,1},{1,0},{2,3},{3,2},{4,5},{5,4},{6,7},{7,6},{8,9},{9,8},{10,11... | collective-permute-start | bytes 786440 | tf_op jit(solution)/shard_map/ppermute | solution.py:406
  16.3 2.5 %precond_first.1 = (f32[1024,128]{1,0:T(8,128)S(1)}, bf16[1024,2048]{1,0:T(8,128)(2,1)S(1)}) custom-call(s32[1]{0:T(128)} %bitcast.core_ref.refs_0_, bf16[1024,2048]{1,0:T(8,128)(2,1)} %pre_ref.3, bf16[8,128,128]{2,1,0:T(8,128)(2,1)S(1)} %all-to-all-done.dir_ref), custom_call_target="tpu_custom_call" | custom-call | flops 268435456 | bytes 8388608 | tf_op jit(solution)/shard_map/precond_first/pallas_call | solution.py:249
  18.8 0.0 collective-permute-done.dir_ref
  18.8 0.0 copy-start.5
  18.8 0.8 precond_second.1
  19.6 18.6 %all_to_all.51.parts_ref = bf16[8,256,128]{2,1,0:T(8,128)(2,1)S(1)} all-to-all(bf16[8,256,128]{2,1,0:T(8,128)(2,1)S(1)} %precond_second.1), channel_id=1, replica_groups=mesh['yh'=2,'z'=4,'yl'=2,'x'=4,'core'=2] {'z','yh'}, dimensions={0} | all-to-all | bytes 1048576 | tf_op jit(solution)/shard_map/all_to_all | solution.py:382
  38.2 0.1 sum_copies.3
  38.3 12.8 %all_to_all.52.refs_2_ = bf16[8,256,128]{2,1,0:T(8,128)(2,1)S(1)} all-to-all(bf16[8,256,128]{2,1,0:T(8,128)(2,1)S(1)} %sum_copies.3), channel_id=1, replica_groups=mesh['yh'=2,'z'=4,'yl'=2,'x'=4,'core'=2] {'z','yh'}, dimensions={0} | all-to-all | bytes 1048576 | tf_op jit(solution)/shard_map/all_to_all | solution.py:382
  51.1 0.0 copy-done.5
  51.1 2.5 %tile_forward.2 = (bf16[2048,1024]{1,0:T(8,128)(2,1)S(1)}, f32[2048,128]{1,0:T(8,128)S(1)}, bf16[256,1024]{1,0:T(8,128)(2,1)S(1)}, bf16[1024,128]{1,0:T(8,128)(2,1)S(1)}) custom-call(s32[1]{0:T(128)S(6)} %sub.3.core_ref.refs_0_, f32[64,4096]{1,0:T(8,128)S(1)} %bitcast.12, bf16[8,256,128]{2,1,0:T(8,128)(2,1)S(1)} %all_to_all.52.refs_2_), custom_call_target="tpu_custom_call" | custom-call | flops 1610612736 | bytes 4194304 | tf_op jit(solution)/shard_map/tile_forward/pallas_call | solution.py:173
  53.6 2.2 %collective-permute-start.1 = (f32[2048,128]{1,0:T(8,128)S(1)}, f32[2048,128]{1,0:T(8,128)S(1)}, u32[]{:S(2)}, u32[]{:S(2)}) collective-permute-start(f32[2048,128]{1,0:T(8,128)S(1)} %get-tuple-element.36), channel_id=1, source_target_pairs={{0,1},{1,0},{2,3},{3,2},{4,5},{5,4},{6,7},{7,6},{8,9},{9,8},{10,11... | collective-permute-start | bytes 3145736 | tf_op jit(solution)/shard_map/ppermute | solution.py:406
  55.8 2.4 %tile_forward.3 = (bf16[2048,1024]{1,0:T(8,128)(2,1)S(1)}, f32[2048,128]{1,0:T(8,128)S(1)}) custom-call(s32[1]{0:T(128)} %bitcast.core_ref.refs_0_, f32[64,4096]{1,0:T(8,128)S(1)} %bitcast.13, bf16[256,1024]{1,0:T(8,128)(2,1)S(1)} %get-tuple-element.32.refs_2_, bf16[1024,128]{1,0:T(8,128)(2,1)S(1)} %get-tuple-element.33.refs_3_), custom_call_target="tpu_custom_call" | custom-call | flops 1610612736 | bytes 4194304 | tf_op jit(solution)/shard_map/tile_forward/pallas_call | solution.py:173
  58.2 0.0 collective-permute-done.1
  58.3 0.2 add_convert_fusion
  58.4 12.0 %all_to_all.53.parts_ref = bf16[8,256,128]{2,1,0:T(8,128)(2,1)S(1)} all-to-all(bf16[8,256,128]{2,1,0:T(8,128)(2,1)S(1)} %bitcast.15), channel_id=1, replica_groups=mesh['yh'=2,'z'=4,'yl'=2,'x'=4,'core'=2] {'x','yl'}, dimensions={0} | all-to-all | bytes 1048576 | tf_op jit(solution)/shard_map/all_to_all | solution.py:382
  70.4 0.1 sum_copies.4
  70.6 10.5 %all_to_all.54.refs_1_ = bf16[8,128,256]{2,1,0:T(8,128)(2,1)S(1)} all-to-all(bf16[8,128,256]{2,1,0:T(8,128)(2,1)S(1)} %sum_copies.4), channel_id=1, replica_groups=mesh['yh'=2,'z'=4,'yl'=2,'x'=4,'core'=2] {'x','yl'}, dimensions={0} | all-to-all | bytes 1048576 | tf_op jit(solution)/shard_map/all_to_all | solution.py:382
  81.1 2.7 %collective-permute-start.2 = (bf16[8,128,256]{2,1,0:T(8,128)(2,1)S(1)}, bf16[8,128,256]{2,1,0:T(8,128)(2,1)S(1)}, u32[]{:S(2)}, u32[]{:S(2)}) collective-permute-start(bf16[8,128,256]{2,1,0:T(8,128)(2,1)S(1)} %all_to_all.54.refs_1_), channel_id=1, source_target_pairs={{0,1},{1,0},{2,3},{3,2},{4,5},{5,4},{6,7},{7,6},{8,9},{9,8},{10,11... | collective-permute-start | bytes 1572872 | tf_op jit(solution)/shard_map/ppermute | solution.py:406
  83.8 0.7 tile_backward.2.refs_2_
  84.5 0.0 copy-start
  84.5 0.8 collective-permute-done.2.refs_1_
  85.3 0.7 tile_backward.3
  86.1 10.5 %all_to_all.55.parts_ref = bf16[8,128,128]{2,1,0:T(8,128)(2,1)S(1)} all-to-all(bf16[8,128,128]{2,1,0:T(8,128)(2,1)S(1)} %tile_backward.3), channel_id=1, replica_groups=mesh['yh'=2,'z'=4,'yl'=2,'x'=4,'core'=2] {'z','yh'}, dimensions={0} | all-to-all | bytes 524288 | tf_op jit(solution)/shard_map/all_to_all | solution.py:382
  96.7 10.5 %all_to_all.56.grad_ref = bf16[8,128,128]{2,1,0:T(8,128)(2,1)S(1)} all-to-all(bf16[8,128,128]{2,1,0:T(8,128)(2,1)S(1)} %sum_copies.5), channel_id=1, replica_groups=mesh['yh'=2,'z'=4,'yl'=2,'x'=4,'core'=2] {'z','yh'}, dimensions={0} | all-to-all | bytes 524288 | tf_op jit(solution)/shard_map/all_to_all | solution.py:382
  107.2 0.0 copy-done
  107.2 1.0 precond_backward.3
  108.2 0.0 copy-start.1
  108.2 0.0 copy-start.2
  108.2 0.0 copy-start.3
  108.2 2.7 %collective-permute-start.3 = (f32[8,128,128]{2,1,0:T(8,128)S(1)}, f32[8,128,128]{2,1,0:T(8,128)S(1)}, u32[]{:S(2)}, u32[]{:S(2)}) collective-permute-start(f32[8,128,128]{2,1,0:T(8,128)S(1)} %precond_backward.3), channel_id=1, source_target_pairs={{0,1},{1,0},{2,3},{3,2},{4,5},{5,4},{6,7},{7,6},{8,9},{9,8},{10,11... | collective-permute-start | bytes 1572872 | tf_op jit(solution)/shard_map/ppermute | solution.py:406
  110.9 1.0 precond_backward.2
  111.9 0.5 collective-permute-done.3
  112.4 0.1 add_convert_fusion.1
  112.5 8.4 %all_to_all.57.part_ref = bf16[8,128,128]{2,1,0:T(8,128)(2,1)S(1)} all-to-all(bf16[8,128,128]{2,1,0:T(8,128)(2,1)S(1)} %add_convert_fusion.1), channel_id=1, replica_groups=mesh['yh'=2,'z'=4,'yl'=2,'x'=4,'core'=2] {'x','yl'}, dimensions={0} | all-to-all | bytes 524288 | tf_op jit(solution)/shard_map/all_to_all | solution.py:382
  120.9 0.0 copy-done.1
  120.9 0.0 copy-done.2
  120.9 0.2 image_numbers.1
  121.1 15.4 %all_to_all.58 = f32[128,1,128]{2,1,0:T(1,128)S(1)} all-to-all(f32[128,1,128]{2,1,0:T(1,128)S(1)} %bitcast.10), channel_id=1, replica_groups=mesh['yh'=2,'z'=4,'yl'=2,'x'=4,'core'=2] {'yh','z','yl','x','core'}, dimensions={0} | all-to-all | bytes 131072 | tf_op jit(solution)/shard_map/all_to_all | solution.py:382
  136.5 0.0 copy-done.3
  136.5 0.8 finish.1
  (1 shorter events, 0.0 us)
Async XLA Ops:
  2.3 11.8 %all-to-all-start = ((bf16[8,128,128]{2,1,0:T(8,128)(2,1)}), bf16[8,128,128]{2,1,0:T(8,128)(2,1)S(1)}, u32[]{:S(2)}, u32[]{:S(2)}) async-start(bf16[8,128,128]{2,1,0:T(8,128)(2,1)} %direction_copies.1), calls=%async_computation | async-start | bytes 524288 | tf_op jit(solution)/shard_map/all_to_all | solution.py:382
  8.1 1.2 copy-start.4
  9.4 0.7 copy-start.6
  14.1 4.8 %collective-permute-start = (bf16[8,128,128]{2,1,0:T(8,128)(2,1)S(1)}, bf16[8,128,128]{2,1,0:T(8,128)(2,1)S(1)}, u32[]{:S(2)}, u32[]{:S(2)}) collective-permute-start(bf16[8,128,128]{2,1,0:T(8,128)(2,1)S(1)} %all-to-all-done.dir_ref), channel_id=1, source_target_pairs={{0,1},{1,0},{2,3},{3,2},{4,5},{5,4},{6,7},{7,6},{8,9},{9,8},{10,11... | collective-permute-start | bytes 786440 | tf_op jit(solution)/shard_map/ppermute | solution.py:406
  18.8 32.3 %copy-start.5 = (f32[4096,64]{0,1:T(8,128)S(1)}, f32[4096,64]{0,1:T(8,128)}, u32[]{:S(2)}) copy-start(f32[4096,64]{0,1:T(8,128)} %param.6) | copy-start | bytes 3145732
  53.6 4.7 %collective-permute-start.1 = (f32[2048,128]{1,0:T(8,128)S(1)}, f32[2048,128]{1,0:T(8,128)S(1)}, u32[]{:S(2)}, u32[]{:S(2)}) collective-permute-start(f32[2048,128]{1,0:T(8,128)S(1)} %get-tuple-element.36), channel_id=1, source_target_pairs={{0,1},{1,0},{2,3},{3,2},{4,5},{5,4},{6,7},{7,6},{8,9},{9,8},{10,11... | collective-permute-start | bytes 3145736 | tf_op jit(solution)/shard_map/ppermute | solution.py:406
  81.1 4.2 %collective-permute-start.2 = (bf16[8,128,256]{2,1,0:T(8,128)(2,1)S(1)}, bf16[8,128,256]{2,1,0:T(8,128)(2,1)S(1)}, u32[]{:S(2)}, u32[]{:S(2)}) collective-permute-start(bf16[8,128,256]{2,1,0:T(8,128)(2,1)S(1)} %all_to_all.54.refs_1_), channel_id=1, source_target_pairs={{0,1},{1,0},{2,3},{3,2},{4,5},{5,4},{6,7},{7,6},{8,9},{9,8},{10,11... | collective-permute-start | bytes 1572872 | tf_op jit(solution)/shard_map/ppermute | solution.py:406
  84.5 22.7 %copy-start = (bf16[1024,2048]{1,0:T(8,128)(2,1)S(1)}, bf16[1024,2048]{1,0:T(8,128)(2,1)}, u32[]{:S(2)}) copy-start(bf16[1024,2048]{1,0:T(8,128)(2,1)} %pre_ref.3) | copy-start | bytes 12582916
  108.2 12.7 %copy-start.1 = (f32[128,128]{1,0:T(8,128)S(1)}, f32[128,128]{1,0:T(8,128)}, u32[]{:S(2)}) copy-start(f32[128,128]{1,0:T(8,128)} %dir_ref.3) | copy-start | bytes 196612
  108.2 12.7 %copy-start.2 = (f32[128,128]{1,0:T(8,128)S(1)}, f32[128,128]{1,0:T(8,128)}, u32[]{:S(2)}) copy-start(f32[128,128]{1,0:T(8,128)} %res_ref.3) | copy-start | bytes 196612
  108.2 28.3 %copy-start.3 = (f32[128,128]{1,0:T(8,128)S(1)}, f32[128,128]{1,0:T(8,128)}, u32[]{:S(2)}) copy-start(f32[128,128]{1,0:T(8,128)} %coef_ref.1) | copy-start | bytes 196612
  108.2 4.2 %collective-permute-start.3 = (f32[8,128,128]{2,1,0:T(8,128)S(1)}, f32[8,128,128]{2,1,0:T(8,128)S(1)}, u32[]{:S(2)}, u32[]{:S(2)}) collective-permute-start(f32[8,128,128]{2,1,0:T(8,128)S(1)} %precond_backward.3), channel_id=1, source_target_pairs={{0,1},{1,0},{2,3},{3,2},{4,5},{5,4},{6,7},{7,6},{8,9},{9,8},{10,11... | collective-permute-start | bytes 1572872 | tf_op jit(solution)/shard_map/ppermute | solution.py:406

commit v13 on v12

--- a/solution.py
+++ b/solution.py
@@ -444,7 +444,7 @@
     image_mine, image_came = lax.optimization_barrier((image_mine, image_came))
     half = (image_mine + image_came).astype(BF16)
     image, row = numbers(spread(half, CHIPS), direction, residual, row_devices * cen_devices)
-    every = spread(row, (*ROWS, *CENT))
+    every = spread(row, ("core", *ROW_RING, *CHIPS))
     return tuple(finish(every, image, coefficients, residual, direction))
 
 

time: 138 us -> 138 us (level)
  no operation moved by 1% of the time
where the time goes in v13:
time: 138 us; the launch traced here: 137 us
  blocking collectives  98.8 us (72%)
  Pallas kernels  17.4 us (13%)
  starting transfers between devices  15.7 us (11%)
  waiting for transfers between devices  2.52 us (2%)
  local copies, waits for them, and re-layouts  1.94 us (1%)
    all_to_all x8, blocking collectives, spread(): return lax.all_to_all(part, axes, 0, 0, tiled=True)  98.8 us
    ppermute x4, starting transfers between devices, swapped(): return lax.ppermute(part, 'core', SWAP)  9.86 us
    all_to_all x1, starting transfers between devices, spread(): return lax.all_to_all(part, axes, 0, 0, tiled=True)  5.87 us
    pallas_call x2, Pallas kernels, tile_forward(): pl.pallas_call(functools.partial(tile_kernel, first=first), in_specs=[SME...  4.9 us
    pallas_call x1, Pallas kernels, pick(): pl.pallas_call(pick_kernel, grid=(n // block,), in_specs=[pl.BlockSpec(me...  2.84 us
  transfers between devices with their start and end apart: 5, of which 3 were waited for; matrix products, arithmetic and copies ran while one was open for 0% of the time, Pallas kernels for 7%

profile of v13, /device:TPU:1, one launch (start us, length us, event | category | flops | bytes accessed | tf_op | source)
XLA Modules:
  0.0 137.4 jit_solution(3327051917931160792)
XLA Ops:
  0.6 1.6 %direction_copies.1 = bf16[8,128,128]{2,1,0:T(8,128)(2,1)} custom-call(f32[128,128]{1,0:T(8,128)} %dir_ref.3), custom_call_target="tpu_custom_call" | custom-call | tf_op jit(solution)/shard_map/direction_copies/pallas_call | solution.py:121
  2.3 5.9 %all-to-all-start = ((bf16[8,128,128]{2,1,0:T(8,128)(2,1)}), bf16[8,128,128]{2,1,0:T(8,128)(2,1)S(1)}, u32[]{:S(2)}, u32[]{:S(2)}) async-start(bf16[8,128,128]{2,1,0:T(8,128)(2,1)} %direction_copies.1), calls=%async_computation | async-start | bytes 524288 | tf_op jit(solution)/shard_map/all_to_all | solution.py:382
  8.1 0.0 copy-start.4
  8.1 1.2 copy-done.4
  9.4 0.0 copy-start.6
  9.4 0.7 copy-done.6
  10.0 2.8 %pick_centres.1.feat_ref = bf16[8,128,128]{2,1,0:T(8,128)(2,1)S(1)} custom-call(s32[1]{0:T(128)} %bitcast.1.start_ref, s32[1,1024]{1,0:T(1,128)S(1)} %bitcast.14, f32[64,4096]{1,0:T(8,128)S(1)} %bitcast.11), custom_call_target="tpu_custom_call" | custom-call | flops 4294967296 | bytes 1048576 | tf_op jit(solution)/shard_map/pick_centres/pallas_call | solution.py:91
  12.9 1.2 all-to-all-done.dir_ref
  14.1 2.2 %collective-permute-start = (bf16[8,128,128]{2,1,0:T(8,128)(2,1)S(1)}, bf16[8,128,128]{2,1,0:T(8,128)(2,1)S(1)}, u32[]{:S(2)}, u32[]{:S(2)}) collective-permute-start(bf16[8,128,128]{2,1,0:T(8,128)(2,1)S(1)} %all-to-all-done.dir_ref), channel_id=1, source_target_pairs={{0,1},{1,0},{2,3},{3,2},{4,5},{5,4},{6,7},{7,6},{8,9},{9,8},{10,11... | collective-permute-start | bytes 786440 | tf_op jit(solution)/shard_map/ppermute | solution.py:406
  16.3 2.5 %precond_first.1 = (f32[1024,128]{1,0:T(8,128)S(1)}, bf16[1024,2048]{1,0:T(8,128)(2,1)S(1)}) custom-call(s32[1]{0:T(128)} %bitcast.core_ref.refs_0_, bf16[1024,2048]{1,0:T(8,128)(2,1)} %pre_ref.3, bf16[8,128,128]{2,1,0:T(8,128)(2,1)S(1)} %all-to-all-done.dir_ref), custom_call_target="tpu_custom_call" | custom-call | flops 268435456 | bytes 8388608 | tf_op jit(solution)/shard_map/precond_first/pallas_call | solution.py:249
  18.8 0.0 collective-permute-done.dir_ref
  18.8 0.0 copy-start.5
  18.8 0.8 precond_second.1
  19.6 18.6 %all_to_all.51.parts_ref = bf16[8,256,128]{2,1,0:T(8,128)(2,1)S(1)} all-to-all(bf16[8,256,128]{2,1,0:T(8,128)(2,1)S(1)} %precond_second.1), channel_id=1, replica_groups=mesh['yh'=2,'z'=4,'yl'=2,'x'=4,'core'=2] {'z','yh'}, dimensions={0} | all-to-all | bytes 1048576 | tf_op jit(solution)/shard_map/all_to_all | solution.py:382
  38.2 0.1 sum_copies.3
  38.3 12.8 %all_to_all.52.refs_2_ = bf16[8,256,128]{2,1,0:T(8,128)(2,1)S(1)} all-to-all(bf16[8,256,128]{2,1,0:T(8,128)(2,1)S(1)} %sum_copies.3), channel_id=1, replica_groups=mesh['yh'=2,'z'=4,'yl'=2,'x'=4,'core'=2] {'z','yh'}, dimensions={0} | all-to-all | bytes 1048576 | tf_op jit(solution)/shard_map/all_to_all | solution.py:382
  51.1 0.0 copy-done.5
  51.1 2.5 %tile_forward.2 = (bf16[2048,1024]{1,0:T(8,128)(2,1)S(1)}, f32[2048,128]{1,0:T(8,128)S(1)}, bf16[256,1024]{1,0:T(8,128)(2,1)S(1)}, bf16[1024,128]{1,0:T(8,128)(2,1)S(1)}) custom-call(s32[1]{0:T(128)S(6)} %sub.3.core_ref.refs_0_, f32[64,4096]{1,0:T(8,128)S(1)} %bitcast.12, bf16[8,256,128]{2,1,0:T(8,128)(2,1)S(1)} %all_to_all.52.refs_2_), custom_call_target="tpu_custom_call" | custom-call | flops 1610612736 | bytes 4194304 | tf_op jit(solution)/shard_map/tile_forward/pallas_call | solution.py:173
  53.6 2.2 %collective-permute-start.1 = (f32[2048,128]{1,0:T(8,128)S(1)}, f32[2048,128]{1,0:T(8,128)S(1)}, u32[]{:S(2)}, u32[]{:S(2)}) collective-permute-start(f32[2048,128]{1,0:T(8,128)S(1)} %get-tuple-element.36), channel_id=1, source_target_pairs={{0,1},{1,0},{2,3},{3,2},{4,5},{5,4},{6,7},{7,6},{8,9},{9,8},{10,11... | collective-permute-start | bytes 3145736 | tf_op jit(solution)/shard_map/ppermute | solution.py:406
  55.8 2.4 %tile_forward.3 = (bf16[2048,1024]{1,0:T(8,128)(2,1)S(1)}, f32[2048,128]{1,0:T(8,128)S(1)}) custom-call(s32[1]{0:T(128)} %bitcast.core_ref.refs_0_, f32[64,4096]{1,0:T(8,128)S(1)} %bitcast.13, bf16[256,1024]{1,0:T(8,128)(2,1)S(1)} %get-tuple-element.32.refs_2_, bf16[1024,128]{1,0:T(8,128)(2,1)S(1)} %get-tuple-element.33.refs_3_), custom_call_target="tpu_custom_call" | custom-call | flops 1610612736 | bytes 4194304 | tf_op jit(solution)/shard_map/tile_forward/pallas_call | solution.py:173
  58.2 0.0 collective-permute-done.1
  58.3 0.2 add_convert_fusion
  58.4 12.0 %all_to_all.53.parts_ref = bf16[8,256,128]{2,1,0:T(8,128)(2,1)S(1)} all-to-all(bf16[8,256,128]{2,1,0:T(8,128)(2,1)S(1)} %bitcast.15), channel_id=1, replica_groups=mesh['yh'=2,'z'=4,'yl'=2,'x'=4,'core'=2] {'x','yl'}, dimensions={0} | all-to-all | bytes 1048576 | tf_op jit(solution)/shard_map/all_to_all | solution.py:382
  70.4 0.1 sum_copies.4
  70.6 10.5 %all_to_all.54.refs_1_ = bf16[8,128,256]{2,1,0:T(8,128)(2,1)S(1)} all-to-all(bf16[8,128,256]{2,1,0:T(8,128)(2,1)S(1)} %sum_copies.4), channel_id=1, replica_groups=mesh['yh'=2,'z'=4,'yl'=2,'x'=4,'core'=2] {'x','yl'}, dimensions={0} | all-to-all | bytes 1048576 | tf_op jit(solution)/shard_map/all_to_all | solution.py:382
  81.1 2.7 %collective-permute-start.2 = (bf16[8,128,256]{2,1,0:T(8,128)(2,1)S(1)}, bf16[8,128,256]{2,1,0:T(8,128)(2,1)S(1)}, u32[]{:S(2)}, u32[]{:S(2)}) collective-permute-start(bf16[8,128,256]{2,1,0:T(8,128)(2,1)S(1)} %all_to_all.54.refs_1_), channel_id=1, source_target_pairs={{0,1},{1,0},{2,3},{3,2},{4,5},{5,4},{6,7},{7,6},{8,9},{9,8},{10,11... | collective-permute-start | bytes 1572872 | tf_op jit(solution)/shard_map/ppermute | solution.py:406
  83.8 0.7 tile_backward.2.refs_2_
  84.5 0.0 copy-start
  84.5 0.8 collective-permute-done.2.refs_1_
  85.3 0.7 tile_backward.3
  86.1 10.5 %all_to_all.55.parts_ref = bf16[8,128,128]{2,1,0:T(8,128)(2,1)S(1)} all-to-all(bf16[8,128,128]{2,1,0:T(8,128)(2,1)S(1)} %tile_backward.3), channel_id=1, replica_groups=mesh['yh'=2,'z'=4,'yl'=2,'x'=4,'core'=2] {'z','yh'}, dimensions={0} | all-to-all | bytes 524288 | tf_op jit(solution)/shard_map/all_to_all | solution.py:382
  96.7 10.5 %all_to_all.56.grad_ref = bf16[8,128,128]{2,1,0:T(8,128)(2,1)S(1)} all-to-all(bf16[8,128,128]{2,1,0:T(8,128)(2,1)S(1)} %sum_copies.5), channel_id=1, replica_groups=mesh['yh'=2,'z'=4,'yl'=2,'x'=4,'core'=2] {'z','yh'}, dimensions={0} | all-to-all | bytes 524288 | tf_op jit(solution)/shard_map/all_to_all | solution.py:382
  107.2 0.0 copy-done
  107.2 1.0 precond_backward.3
  108.2 0.0 copy-start.1
  108.2 0.0 copy-start.2
  108.2 0.0 copy-start.3
  108.2 2.7 %collective-permute-start.3 = (f32[8,128,128]{2,1,0:T(8,128)S(1)}, f32[8,128,128]{2,1,0:T(8,128)S(1)}, u32[]{:S(2)}, u32[]{:S(2)}) collective-permute-start(f32[8,128,128]{2,1,0:T(8,128)S(1)} %precond_backward.3), channel_id=1, source_target_pairs={{0,1},{1,0},{2,3},{3,2},{4,5},{5,4},{6,7},{7,6},{8,9},{9,8},{10,11... | collective-permute-start | bytes 1572872 | tf_op jit(solution)/shard_map/ppermute | solution.py:406
  110.9 1.0 precond_backward.2
  111.9 0.5 collective-permute-done.3
  112.4 0.1 add_convert_fusion.1
  112.5 8.4 %all_to_all.57.part_ref = bf16[8,128,128]{2,1,0:T(8,128)(2,1)S(1)} all-to-all(bf16[8,128,128]{2,1,0:T(8,128)(2,1)S(1)} %add_convert_fusion.1), channel_id=1, replica_groups=mesh['yh'=2,'z'=4,'yl'=2,'x'=4,'core'=2] {'x','yl'}, dimensions={0} | all-to-all | bytes 524288 | tf_op jit(solution)/shard_map/all_to_all | solution.py:382
  120.9 0.0 copy-done.1
  120.9 0.0 copy-done.2
  120.9 0.2 image_numbers.1
  121.1 15.4 %all_to_all.58 = f32[128,1,128]{2,1,0:T(1,128)S(1)} all-to-all(f32[128,1,128]{2,1,0:T(1,128)S(1)} %bitcast.10), channel_id=1, replica_groups=mesh['yh'=2,'z'=4,'yl'=2,'x'=4,'core'=2] {'core','z','yh','x','yl'}, dimensions={0} | all-to-all | bytes 131072 | tf_op jit(solution)/shard_map/all_to_all | solution.py:382
  136.5 0.0 copy-done.3
  136.5 0.8 finish.1
  (1 shorter events, 0.0 us)
Async XLA Ops:
  2.3 11.8 %all-to-all-start = ((bf16[8,128,128]{2,1,0:T(8,128)(2,1)}), bf16[8,128,128]{2,1,0:T(8,128)(2,1)S(1)}, u32[]{:S(2)}, u32[]{:S(2)}) async-start(bf16[8,128,128]{2,1,0:T(8,128)(2,1)} %direction_copies.1), calls=%async_computation | async-start | bytes 524288 | tf_op jit(solution)/shard_map/all_to_all | solution.py:382
  8.1 1.2 copy-start.4
  9.4 0.7 copy-start.6
  14.1 4.8 %collective-permute-start = (bf16[8,128,128]{2,1,0:T(8,128)(2,1)S(1)}, bf16[8,128,128]{2,1,0:T(8,128)(2,1)S(1)}, u32[]{:S(2)}, u32[]{:S(2)}) collective-permute-start(bf16[8,128,128]{2,1,0:T(8,128)(2,1)S(1)} %all-to-all-done.dir_ref), channel_id=1, source_target_pairs={{0,1},{1,0},{2,3},{3,2},{4,5},{5,4},{6,7},{7,6},{8,9},{9,8},{10,11... | collective-permute-start | bytes 786440 | tf_op jit(solution)/shard_map/ppermute | solution.py:406
  18.8 32.3 %copy-start.5 = (f32[4096,64]{0,1:T(8,128)S(1)}, f32[4096,64]{0,1:T(8,128)}, u32[]{:S(2)}) copy-start(f32[4096,64]{0,1:T(8,128)} %param.6) | copy-start | bytes 3145732
  53.6 4.7 %collective-permute-start.1 = (f32[2048,128]{1,0:T(8,128)S(1)}, f32[2048,128]{1,0:T(8,128)S(1)}, u32[]{:S(2)}, u32[]{:S(2)}) collective-permute-start(f32[2048,128]{1,0:T(8,128)S(1)} %get-tuple-element.36), channel_id=1, source_target_pairs={{0,1},{1,0},{2,3},{3,2},{4,5},{5,4},{6,7},{7,6},{8,9},{9,8},{10,11... | collective-permute-start | bytes 3145736 | tf_op jit(solution)/shard_map/ppermute | solution.py:406
  81.1 4.2 %collective-permute-start.2 = (bf16[8,128,256]{2,1,0:T(8,128)(2,1)S(1)}, bf16[8,128,256]{2,1,0:T(8,128)(2,1)S(1)}, u32[]{:S(2)}, u32[]{:S(2)}) collective-permute-start(bf16[8,128,256]{2,1,0:T(8,128)(2,1)S(1)} %all_to_all.54.refs_1_), channel_id=1, source_target_pairs={{0,1},{1,0},{2,3},{3,2},{4,5},{5,4},{6,7},{7,6},{8,9},{9,8},{10,11... | collective-permute-start | bytes 1572872 | tf_op jit(solution)/shard_map/ppermute | solution.py:406
  84.5 22.7 %copy-start = (bf16[1024,2048]{1,0:T(8,128)(2,1)S(1)}, bf16[1024,2048]{1,0:T(8,128)(2,1)}, u32[]{:S(2)}) copy-start(bf16[1024,2048]{1,0:T(8,128)(2,1)} %pre_ref.3) | copy-start | bytes 12582916
  108.2 12.7 %copy-start.1 = (f32[128,128]{1,0:T(8,128)S(1)}, f32[128,128]{1,0:T(8,128)}, u32[]{:S(2)}) copy-start(f32[128,128]{1,0:T(8,128)} %dir_ref.3) | copy-start | bytes 196612
  108.2 12.7 %copy-start.2 = (f32[128,128]{1,0:T(8,128)S(1)}, f32[128,128]{1,0:T(8,128)}, u32[]{:S(2)}) copy-start(f32[128,128]{1,0:T(8,128)} %res_ref.3) | copy-start | bytes 196612
  108.2 28.3 %copy-start.3 = (f32[128,128]{1,0:T(8,128)S(1)}, f32[128,128]{1,0:T(8,128)}, u32[]{:S(2)}) copy-start(f32[128,128]{1,0:T(8,128)} %coef_ref.1) | copy-start | bytes 196612
  108.2 4.2 %collective-permute-start.3 = (f32[8,128,128]{2,1,0:T(8,128)S(1)}, f32[8,128,128]{2,1,0:T(8,128)S(1)}, u32[]{:S(2)}, u32[]{:S(2)}) collective-permute-start(f32[8,128,128]{2,1,0:T(8,128)S(1)} %precond_backward.3), channel_id=1, source_target_pairs={{0,1},{1,0},{2,3},{3,2},{4,5},{5,4},{6,7},{7,6},{8,9},{9,8},{10,11... | collective-permute-start | bytes 1572872 | tf_op jit(solution)/shard_map/ppermute | solution.py:406
